TPU v7x, 32 devices: a whole 2x2x4 slice. The times are simulated.
32 devices in a mesh: groups: 2 (over x), pool: 8 (over z, y), tp: 2 (over core).
Axes of the slice: x: 2, y: 2, z: 4, core: 2. Of those that a mesh axis runs over, the one named last changes fastest.
Arguments:
- tokens: bfloat16 [2048, 5120], P(('groups', 'pool'), 'tp'), parts along dimension 0, may hold values from -6 to 6
- row_adapters: int32 [2048, 1], P(('groups', 'pool')), parts along dimension 0, may hold values from 0 to 7; in each aligned block of 128 rows (0 to 127, 128 to 255, ...) at most 32 rows name the same one
- positions: int32 [2048], P(('groups', 'pool')), parts along dimension 0, may hold values from 0 to 4095
- key_value_weight: bfloat16 [5120, 2048], P('tp'), may hold values from -0.078125 to 0.078125
- adapter_down: bfloat16 [8, 5120, 128], P('pool', 'tp'), may hold values from -0.078125 to 0.078125
- adapter_up: bfloat16 [8, 128, 2048], P('pool'), may hold values from -0.5 to 0.5
- ranks: int32 [8], P('pool'), may hold values from 16 to 128, as said below
- key_norm_gain: bfloat16 [128], replicated, may hold values from 0.099609375 to 1.8984375
Outputs:
- kv_entries: bfloat16 [2048, 8, 2, 128], P(('groups', 'pool'), 'tp'), parts along dimension 0
There are 2 independent parts, one for each index of `groups`. A program takes and returns all parts, laid end to end along the dimension named above; an argument that names none is the same for every part. Nothing has to cross between parts.
Inputs may be any that keep to these rules, and one draw needn't show every extreme that they name: `row_adapters`: in the rows of one device (aligned blocks of 128 rows) no adapter is named by more than 32 rows, a bound that some block reaches. `ranks`: each rank is 128 // 8 times 1, 2, 4 or 8; some adapter has rank 128 and some 128 // 8.
All inputs are finite; a program needn't handle non-finite values.
Results may differ from a plain program's by a relative error of at most 0.001.
Values may be sent and summed in bfloat16 or wider, within the bound.
No kernel may reach another device: no remote copies, remote signals or barrier semaphores. Data moves between devices by JAX's collectives and lax.ppermute only.
A program may use at most 64 MiB of HBM per device.

v0:
```python
import jax
import jax.numpy as jnp
from jax import lax
from jax.sharding import PartitionSpec as P

ALPHA = 32


rope_theta = 1000000.0
norm_eps = 1e-06


def rotate_keys(keys, positions):
    head_size = keys.shape[-1]
    half_dim = head_size // 2
    exponent = jnp.arange(half_dim, dtype=jnp.float32) * (2.0 / head_size)
    frequency = jnp.power(jnp.float32(rope_theta), -exponent)
    angles = positions.astype(jnp.float32)[:, None] * frequency[None, :]
    cosine = jnp.cos(angles)[:, None, :]
    sine = jnp.sin(angles)[:, None, :]
    lower = keys[..., :half_dim]
    upper = keys[..., half_dim:]
    return jnp.concatenate([lower * cosine - upper * sine, upper * cosine + lower * sine], axis=-1)


def finish_rows(projected, positions, key_norm_gain):
    head_size = key_norm_gain.shape[0]
    row_count = projected.shape[0]
    shaped = projected.reshape(row_count, -1, 2, head_size)
    keys = shaped[:, :, 0, :]
    values_part = shaped[:, :, 1, :]
    mean_square = jnp.mean(keys * keys, axis=-1, keepdims=True)
    normed = keys * lax.rsqrt(mean_square + norm_eps) * key_norm_gain.astype(jnp.float32)
    rotated = rotate_keys(normed, positions)
    return jnp.stack([rotated, values_part], axis=2).astype(jnp.bfloat16)


def body(
    tokens,
    row_adapters,
    positions,
    key_value_weight,
    adapter_down,
    adapter_up,
    ranks,
    key_norm_gain,
):
    pool_size = lax.axis_size("pool")
    tp_size = lax.axis_size("tp")
    row_count = tokens.shape[0]
    half_width = tokens.shape[1]
    local_rows = adapter_down.shape[0]
    adapter_count = local_rows * pool_size
    col_count = key_value_weight.shape[1]
    rank_extent = adapter_down.shape[2]
    slot_depth = max(2, 2 * row_count // adapter_count)
    row_adapter = row_adapters[:, 0]
    same_adapter = row_adapter[:, None] == row_adapter[None, :]
    earlier = jnp.arange(row_count)[None, :] < jnp.arange(row_count)[:, None]
    slot_index = jnp.sum(jnp.logical_and(same_adapter, earlier), axis=1)
    slot_place = row_adapter * slot_depth + slot_index
    picker = (
        slot_place[None, :] == jnp.arange(adapter_count * slot_depth, dtype=jnp.int32)[:, None]
    ).astype(tokens.dtype)
    outgoing = jnp.dot(picker, tokens, preferred_element_type=jnp.float32).astype(jnp.bfloat16)
    outgoing = outgoing.reshape(pool_size, local_rows, slot_depth, half_width)
    base_projected = jnp.dot(tokens, key_value_weight, preferred_element_type=jnp.float32)
    rank_mask = (jnp.arange(rank_extent, dtype=jnp.int32)[None, :] < ranks[:, None]).astype(
        jnp.float32
    )
    factor = rank_mask * (jnp.float32(ALPHA) / ranks.astype(jnp.float32))[:, None]
    col_start = lax.axis_index("tp") * (col_count // tp_size)
    up_factor_columns = lax.dynamic_slice_in_dim(
        adapter_up, col_start, col_count // tp_size, 2
    ).astype(jnp.float32)
    rank_reduced = jnp.einsum(
        "pjmd,jdr->pjmr",
        lax.all_to_all(outgoing, "pool", split_axis=0, concat_axis=0, tiled=True),
        adapter_down,
        preferred_element_type=jnp.float32,
    )
    rank_reduced = rank_reduced * factor[None, :, None, :]
    rank_reduced = lax.psum(rank_reduced, "tp")
    adapter_term = jnp.einsum(
        "hozf,ofe->hoze", rank_reduced, up_factor_columns, precision=lax.Precision.HIGHEST
    )
    incoming_sum = lax.all_to_all(adapter_term, "pool", split_axis=0, concat_axis=0, tiled=True)
    returned = incoming_sum.reshape(adapter_count * slot_depth, incoming_sum.shape[-1])
    row_delta = jnp.take(returned, slot_place, axis=0)
    head_sums = lax.psum_scatter(base_projected, "tp", scatter_dimension=1, tiled=True)
    head_sums = head_sums + row_delta
    return finish_rows(head_sums, positions, key_norm_gain)


def solution(mesh):
    return jax.shard_map(
        body,
        mesh=mesh,
        in_specs=(
            P(("groups", "pool"), "tp"),
            P(("groups", "pool"), None),
            P(("groups", "pool")),
            P("tp", None),
            P("pool", "tp", None),
            P("pool", None, None),
            P("pool"),
            P(),
        ),
        out_specs=P(("groups", "pool"), "tp", None, None),
        check_vma=False,
    )
```

profile of v0, /device:TPU:0, one launch (start us, length us, event | category | flops | bytes accessed | tf_op | source)
XLA Modules:
  0.0 113.6 jit_solution(8861597765508502517)
XLA Ops:
  6.5 0.0 copy-start
  6.5 0.9 convert_reduce_fusion
  7.4 0.7 multiply_add_fusion
  8.1 0.0 copy-done
  8.1 1.6 %convolution_convert_fusion = bf16[256,2560]{1,0:T(8,128)(2,1)} fusion(bf16[128,2560]{1,0:T(8,128)(2,1)S(1)} %copy-done, s32[128]{0:T(128)S(1)} %multiply_add_fusion), kind=kOutput, calls=%fused_computation.1 | convolution fusion | flops 168460288 | bytes 1966592 | tf_op jit(solution)/shard_map/dot_general | solution.py:65
  9.7 0.0 copy-start.1
  9.7 7.4 %all-to-all-start = ((bf16[8,1,32,2560]{3,2,1,0:T(8,128)(2,1)}), bf16[8,1,32,2560]{3,2,1,0:T(8,128)(2,1)S(1)}, u32[]{:S(2)}, u32[]{:S(2)}) async-start(bf16[8,1,32,2560]{3,2,1,0:T(8,128)(2,1)} %bitcast.6), calls=%async_computation.1 | async-start | bytes 2621440 | tf_op jit(solution)/shard_map/all_to_all | solution.py:78
  17.1 0.0 all-reduce.2.cloned.1.call-start
  17.8 30.6 %all-to-all-done = bf16[8,1,32,2560]{3,2,1,0:T(8,128)(2,1)S(1)} async-done(((bf16[8,1,32,2560]{3,2,1,0:T(8,128)(2,1)}), bf16[8,1,32,2560]{3,2,1,0:T(8,128)(2,1)S(1)}, u32[]{:S(2)}, u32[]{:S(2)}) %all-to-all-start) | async-done | bytes 1310752 | tf_op jit(solution)/shard_map/all_to_all | solution.py:78
  48.5 0.0 copy-done.1
  48.5 1.1 %fusion.8 = f32[8,32,128]{2,1,0:T(8,128)} fusion(bf16[8,1,32,2560]{3,2,1,0:T(8,128)(2,1)S(1)} %all-to-all-done, bf16[1,2560,128]{2,1,0:T(8,128)(2,1)S(1)} %copy-done.1, f32[128]{0:T(128)S(1)} %compare_select_fusion.1), kind=kOutput, calls=%fused_computation.7 | convolution fusion | flops 167804928 | bytes 2097664 | tf_op jit(solution)/shard_map/pjmd,jdr->pjmr/dot_general | solution.py:76
  49.6 0.0 all-reduce.2.cloned.1.call-update
  49.7 0.0 copy-start.2
  49.7 0.0 reduce-scatter.2.cloned.1.call-start
  49.7 6.5 %fusion.17 = f32[128,2048]{1,0:T(8,128)} fusion(bf16[128,2560]{1,0:T(8,128)(2,1)S(1)} %copy-done, bf16[2560,2048]{1,0:T(8,128)(2,1)} %param.11), kind=kOutput, calls=%fused_computation.35 | convolution fusion | flops 1342177280 | bytes 12189696 | tf_op jit(solution)/shard_map/dot_general | solution.py:67
  56.2 0.0 reduce-scatter.2.cloned.1.call-update
  56.3 10.5 %all-reduce.2.cloned.1.call-done = f32[8,32,128]{2,1,0:T(8,128)} async-done(((f32[8,32,128]{2,1,0:T(8,128)}), f32[8,32,128]{2,1,0:T(8,128)}) %all-reduce.2.cloned.1.call-update) | async-done | bytes 131088 | tf_op jit(solution)/shard_map/psum | solution.py:83
  66.8 0.0 copy-done.2
  66.8 2.5 %convolution_bitcast_fusion = f32[8,1,32,1024]{3,2,1,0:T(8,128)} fusion(f32[8,32,128]{2,1,0:T(8,128)} %all-reduce.2.cloned.1.call-done, bf16[1,128,2048]{2,1,0:T(8,128)(2,1)S(1)} %copy-done.2, s32[]{:T(128)S(6)} %select_n.15), kind=kOutput, calls=%fused_computation.2 | convolution fusion | flops 402653184 | bytes 1441796 | tf_op jit(solution)/shard_map/hozf,ofe->hoze/dot_general | solution.py:84
  69.3 0.0 copy-start.4
  69.3 0.0 copy-start.5
  69.3 0.0 copy-start.3
  69.3 5.9 %all-to-all-start.1 = ((f32[8,1,32,1024]{3,2,1,0:T(8,128)}), f32[8,1,32,1024]{3,2,1,0:T(8,128)S(1)}, u32[]{:S(2)}, u32[]{:S(2)}) async-start(f32[8,1,32,1024]{3,2,1,0:T(8,128)} %convolution_bitcast_fusion), calls=%async_computation.2 | async-start | bytes 2097152 | tf_op jit(solution)/shard_map/all_to_all | solution.py:87
  75.2 0.0 copy-done.4
  75.2 0.0 copy-done.5
  75.2 0.0 copy-done.3
  75.3 0.3 multiply_cosine_fusion
  75.6 25.8 %all-to-all-done.1 = f32[8,1,32,1024]{3,2,1,0:T(8,128)S(1)} async-done(((f32[8,1,32,1024]{3,2,1,0:T(8,128)}), f32[8,1,32,1024]{3,2,1,0:T(8,128)S(1)}, u32[]{:S(2)}, u32[]{:S(2)}) %all-to-all-start.1) | async-done | bytes 1048608 | tf_op jit(solution)/shard_map/all_to_all | solution.py:87
  101.4 0.8 gather_fusion
  102.2 0.0 reduce-scatter.2.cloned.1.call-done
  102.3 1.2 %select_add_fusion = f32[128,1024]{1,0:T(8,128)S(1)} fusion(f32[128,1024]{1,0:T(8,128)} %reduce-scatter.2.cloned.1.call-done, f32[128,1024]{1,0:T(8,128)S(1)} %gather_fusion, pred[128]{0:T(512)(128)(4,1)S(1)} %get-tuple-element.5), kind=kLoop, calls=%fused_computation.9 | loop fusion | flops 262144 | bytes 1572992 | tf_op jit(solution)/shard_map/add | solution.py:91
  103.4 0.4 reshape.120
  103.9 0.2 slice.19
  104.1 0.3 slice.28
  104.4 0.2 multiply_reduce_fusion
  104.6 0.2 multiply_multiply_fusion
  104.8 0.3 subtract_convert_fusion
  105.1 0.2 maximum_bitcast_fusion
  105.3 0.2 copy.24
  105.5 1.3 %pad_maximum_fusion = bf16[128,4,2,128]{3,2,1,0:T(2,128)(2,1)} fusion(bf16[128,4,1,128]{3,2,1,0:T(2,128)(2,1)S(1)} %slice.28, bf16[128,4,1,128]{3,2,1,0:T(2,128)(2,1)S(1)} %copy.24), kind=kLoop, calls=%fused_computation.11 | loop fusion | flops 524288 | bytes 524288 | tf_op jit(solution)/shard_map/stack | solution.py:35
  (7 shorter events, 0.1 us)
Async XLA Ops:
  6.5 1.6 %copy-start = (bf16[128,2560]{1,0:T(8,128)(2,1)S(1)}, bf16[128,2560]{1,0:T(8,128)(2,1)}, u32[]{:S(2)}) copy-start(bf16[128,2560]{1,0:T(8,128)(2,1)} %param.8) | copy-start | bytes 1966084
  9.7 38.8 %copy-start.1 = (bf16[1,2560,128]{2,1,0:T(8,128)(2,1)S(1)}, bf16[1,2560,128]{2,1,0:T(8,128)(2,1)}, u32[]{:S(2)}) copy-start(bf16[1,2560,128]{2,1,0:T(8,128)(2,1)} %param.12) | copy-start | bytes 1966084
  9.7 38.8 %all-to-all-start = ((bf16[8,1,32,2560]{3,2,1,0:T(8,128)(2,1)}), bf16[8,1,32,2560]{3,2,1,0:T(8,128)(2,1)S(1)}, u32[]{:S(2)}, u32[]{:S(2)}) async-start(bf16[8,1,32,2560]{3,2,1,0:T(8,128)(2,1)} %bitcast.6), calls=%async_computation.1 | async-start | bytes 2621440 | tf_op jit(solution)/shard_map/all_to_all | solution.py:78
  17.1 49.7 %all-reduce.2.cloned.1.call-start = ((), (), s32[]{:S(2)}) async-start(), calls=%async_computation.4 | async-start | bytes 262144 | tf_op jit(solution)/shard_map/psum | solution.py:83
  49.7 17.1 %copy-start.2 = (bf16[1,128,2048]{2,1,0:T(8,128)(2,1)S(1)}, bf16[1,128,2048]{2,1,0:T(8,128)(2,1)}, u32[]{:S(2)}) copy-start(bf16[1,128,2048]{2,1,0:T(8,128)(2,1)} %param.13) | copy-start | bytes 1572868
  49.7 52.6 %reduce-scatter.2.cloned.1.call-start = ((), (), s32[]{:S(2)}) async-start(), calls=%async_computation.3 | async-start | bytes 1572864 | tf_op jit(solution)/shard_map/reduce_scatter | solution.py:90
  69.3 5.9 %copy-start.4 = (bf16[128]{0:T(256)(128)(2,1)S(1)}, bf16[128]{0:T(256)(128)(2,1)}, u32[]{:S(2)}) copy-start(bf16[128]{0:T(256)(128)(2,1)} %param.15) | copy-start | bytes 772
  69.3 5.9 %copy-start.5 = (s32[128]{0:T(128)S(1)}, s32[128]{0:T(128)}, u32[]{:S(2)}) copy-start(s32[128]{0:T(128)} %param.10) | copy-start | bytes 1540
  69.3 6.0 %copy-start.3 = (s32[128,1]{0,1:T(1,128)S(1)}, s32[128,1]{0,1:T(1,128)}, u32[]{:S(2)}) copy-start(s32[128,1]{0,1:T(1,128)} %param.9) | copy-start | bytes 1540
  69.3 32.1 %all-to-all-start.1 = ((f32[8,1,32,1024]{3,2,1,0:T(8,128)}), f32[8,1,32,1024]{3,2,1,0:T(8,128)S(1)}, u32[]{:S(2)}, u32[]{:S(2)}) async-start(f32[8,1,32,1024]{3,2,1,0:T(8,128)} %convolution_bitcast_fusion), calls=%async_computation.2 | async-start | bytes 2097152 | tf_op jit(solution)/shard_map/all_to_all | solution.py:87
Sparse Core Ops, SparseCore 0:
  49.8 16.9 all-reduce.1
  69.0 9.7 reduce-scatter.1
where the time goes:
time: 114 us
  waiting for transfers between devices  67 us (59%)
  between operations  14.3 us (13%)
  starting transfers between devices  13.4 us (12%)
  matrix products  11.7 us (10%)
  other arithmetic  5.27 us (5%)
  local copies, waits for them, and re-layouts  1.93 us (2%)
    all_to_all x1, waiting for transfers between devices, body(): lax.all_to_all(outgoing, 'pool', split_axis=0, concat_axis=0, tiled=True)  30.6 us
    all_to_all x1, waiting for transfers between devices, body(): lax.all_to_all(adapter_term, 'pool', split_axis=0, concat_axis=0, tiled=T...  25.8 us
    psum x1, waiting for transfers between devices, body(): rank_reduced = lax.psum(rank_reduced, 'tp')  10.5 us
    all_to_all x1, starting transfers between devices, body(): lax.all_to_all(outgoing, 'pool', split_axis=0, concat_axis=0, tiled=True)  7.41 us
    dot_general x1, matrix products, body(): jnp.dot(tokens, key_value_weight, preferred_element_type=jnp.float32)  6.52 us
    all_to_all x1, starting transfers between devices, body(): lax.all_to_all(adapter_term, 'pool', split_axis=0, concat_axis=0, tiled=T...  5.9 us
    dot_general x1, matrix products, body(): jnp.einsum('hozf,ofe->hoze', rank_reduced, up_factor_columns, precision=l...  2.5 us
  transfers between devices with their start and end apart: 4, of which 3 were waited for; matrix products, arithmetic and copies ran while one was open for 9% of the time, Pallas kernels for 0%

commit v1 on v0

v1 whole, which is shorter than its diff:
```python
import functools

import jax
import jax.numpy as jnp
from jax import lax
from jax.experimental import pallas as pl
from jax.experimental.pallas import tpu as pltpu
from jax.sharding import PartitionSpec as P

ALPHA = 32
ROPE_THETA = 1000000.0
NORM_EPS = 1e-06
VMEM_LIMIT = 48 * 1024 * 1024

VMEM = pl.BlockSpec(memory_space=pltpu.VMEM)


def params(**kw):
    return pltpu.CompilerParams(vmem_limit_bytes=VMEM_LIMIT, **kw)


def cost(flops, bytes_accessed):
    return pl.CostEstimate(flops=flops, bytes_accessed=bytes_accessed, transcendentals=0)


def slot_places(adapter, me_ref, local, depth):
    rows = adapter.shape[0]
    r0 = lax.broadcasted_iota(jnp.int32, (rows, rows), 0)
    r1 = lax.broadcasted_iota(jnp.int32, (rows, rows), 1)
    column = jnp.broadcast_to(adapter, (rows, rows))
    row = jnp.sum(jnp.where(r0 == r1, column, 0), axis=0, keepdims=True)
    slot = jnp.sum(jnp.where((column == row) & (r0 < r1), 1, 0), axis=0, keepdims=True)
    holder = row // local
    return ((holder ^ me_ref[0]) * local + (row - holder * local)) * depth + slot


def pick_kernel(local, depth, me_ref, adapter_ref, tokens_ref, *outs):
    rows = tokens_ref.shape[0]
    place = slot_places(adapter_ref[...], me_ref, local, depth)
    size = local * depth
    slots = len(outs) * size
    picker = jnp.where(
        lax.broadcasted_iota(jnp.int32, (slots, rows), 0) == place, 1.0, 0.0
    ).astype(jnp.bfloat16)
    width = tokens_ref.shape[1]
    step = 512
    for at in range(0, width, step):
        block = jnp.dot(
            picker, tokens_ref[:, at : at + step], preferred_element_type=jnp.float32
        )
        for j, out in enumerate(outs):
            out[:, at : at + step] = block[j * size : (j + 1) * size].astype(jnp.bfloat16)


def down_kernel(local, depth, factor_ref, down_ref, *refs):
    count = len(refs) // 2
    ins, outs = refs[:count], refs[count:]
    for a in range(local):
        rows = jnp.concatenate([x[a * depth : (a + 1) * depth, :] for x in ins], axis=0)
        low = jnp.dot(rows, down_ref[a], preferred_element_type=jnp.float32)
        low = low * factor_ref[a : a + 1, :]
        for j, out in enumerate(outs):
            out[a * depth : (a + 1) * depth, :] = low[j * depth : (j + 1) * depth]


def halves(x):
    high = x.astype(jnp.bfloat16)
    low = (x - high.astype(jnp.float32)).astype(jnp.bfloat16)
    return high, low


def return_kernel(local, depth, me_ref, adapter_ref, *refs):
    ins, out = refs[:-1], refs[-1]
    place = slot_places(adapter_ref[...], me_ref, local, depth)
    slots = len(ins) * local * depth
    picker = jnp.where(
        lax.broadcasted_iota(jnp.int32, (slots, place.shape[1]), 0) == place, 1.0, 0.0
    ).astype(jnp.bfloat16)
    slot = jnp.concatenate([x[...] for x in ins], axis=0)
    high, low = halves(slot)
    rest = (slot - high.astype(jnp.float32) - low.astype(jnp.float32)).astype(jnp.bfloat16)
    total = None
    for part in (rest, low, high):
        term = lax.dot_general(
            picker, part, (((0,), (0,)), ((), ())), preferred_element_type=jnp.float32
        )
        total = term if total is None else total + term
    out[...] = total


def base_kernel(half_ref, tokens_ref, weight_ref, out_ref):
    @pl.when(pl.program_id(0) == 0)
    def _():
        out_ref[...] = jnp.zeros_like(out_ref)

    out_ref[...] += jnp.dot(
        tokens_ref[...], weight_ref[...], preferred_element_type=jnp.float32
    )


def base_half(tokens, weight, half, columns):
    rows, width = tokens.shape
    step = 512
    return pl.pallas_call(
        base_kernel,
        grid_spec=pltpu.PrefetchScalarGridSpec(
            num_scalar_prefetch=1,
            grid=(width // step,),
            in_specs=[
                pl.BlockSpec((rows, step), lambda k, h: (0, k)),
                pl.BlockSpec((step, columns), lambda k, h: (k, h[0])),
            ],
            out_specs=pl.BlockSpec((rows, columns), lambda k, h: (0, 0)),
        ),
        out_shape=jax.ShapeDtypeStruct((rows, columns), jnp.float32),
        compiler_params=params(),
        cost_estimate=cost(2 * rows * width * columns, 2 * width * (rows + columns)),
        name="base_half",
    )(half, tokens, weight)


def finish_kernel(
    adapter_ref, mine_ref, other_ref, low_ref, low_other_ref, up_ref, cos_ref, sin_ref, gain_ref, out_ref
):
    rows, columns = mine_ref.shape
    count, rank, _ = up_ref.shape
    head = cos_ref.shape[1]
    high, low = halves(low_ref[...] + low_other_ref[...])
    both = jnp.concatenate([high, low], axis=0)
    adapter = jnp.concatenate([adapter_ref[...], adapter_ref[...]], axis=0)
    blocks = [
        jnp.where(adapter == a, both, jnp.zeros_like(both)) for a in range(count)
    ]
    spread = jnp.concatenate(blocks, axis=1)
    cosine, sine, gain = cos_ref[...], sin_ref[...], gain_ref[...]
    for at in range(0, columns, 2 * head):
        up = up_ref[:, :, at : at + 2 * head].reshape(count * rank, 2 * head)
        delta = jnp.dot(spread, up, preferred_element_type=jnp.float32)
        delta = delta[:rows] + delta[rows:]
        projected = mine_ref[:, at : at + 2 * head] + other_ref[:, at : at + 2 * head] + delta
        key, value = projected[:, :head], projected[:, head:]
        mean = jnp.mean(key * key, axis=1, keepdims=True)
        normed = key * lax.rsqrt(mean + NORM_EPS) * gain
        rotated = normed * cosine + pltpu.roll(normed, head // 2, 1) * sine
        out_ref[:, at : at + head] = rotated.astype(jnp.bfloat16)
        out_ref[:, at + head : at + 2 * head] = value.astype(jnp.bfloat16)


def body(
    tokens,
    row_adapters,
    positions,
    key_value_weight,
    adapter_down,
    adapter_up,
    ranks,
    key_norm_gain,
):
    pool_size = lax.axis_size("pool")
    tp_size = lax.axis_size("tp")
    rows, width = tokens.shape
    local = adapter_down.shape[0]
    adapters = local * pool_size
    columns = key_value_weight.shape[1] // tp_size
    rank = adapter_down.shape[2]
    head = key_norm_gain.shape[0]
    depth = max(2, 2 * rows // adapters)
    size = local * depth
    f32, bf16 = jnp.float32, jnp.bfloat16

    me = lax.axis_index("pool").astype(jnp.int32)[None]
    core = lax.axis_index("tp").astype(jnp.int32)[None]
    smem = pl.BlockSpec(memory_space=pltpu.SMEM)

    own_up = lax.dynamic_slice_in_dim(adapter_up, core[0] * columns, columns, 2)
    ups = lax.all_gather(own_up, "pool", axis=0, tiled=True)

    picked = pl.pallas_call(
        functools.partial(pick_kernel, local, depth),
        in_specs=[smem, VMEM, VMEM],
        out_specs=[VMEM] * pool_size,
        out_shape=[jax.ShapeDtypeStruct((size, width), bf16)] * pool_size,
        compiler_params=params(),
        cost_estimate=cost(2 * pool_size * size * rows * width, 2 * (rows + pool_size * size) * width),
        name="pick",
    )(me, row_adapters, tokens)

    def across(x, j):
        return lax.ppermute(x, "pool", [(p, p ^ j) for p in range(pool_size)])

    def swap(x):
        return lax.ppermute(x, "tp", [(c, (c + 1) % tp_size) for c in range(tp_size)])

    arrived = [picked[0]] + [None] * (pool_size - 1)
    for j in range(pool_size - 1, 0, -1):
        arrived[j] = across(picked[j], j)

    theirs = base_half(tokens, key_value_weight, 1 - core, columns)
    mine = base_half(tokens, key_value_weight, core, columns)
    other = swap(theirs)

    mask = (jnp.arange(rank, dtype=jnp.int32)[None, :] < ranks[:, None]).astype(f32)
    factor = mask * (f32(ALPHA) / ranks.astype(f32))[:, None]

    half_dim = head // 2
    frequency = jnp.power(
        f32(ROPE_THETA), -jnp.arange(half_dim, dtype=f32) * (2.0 / head)
    )
    angles = positions.astype(f32)[:, None] * frequency[None, :]
    cosine, sine = jnp.cos(angles), jnp.sin(angles)
    cosine = jnp.concatenate([cosine, cosine], axis=1)
    sine = jnp.concatenate([-sine, sine], axis=1)

    low = pl.pallas_call(
        functools.partial(down_kernel, local, depth),
        in_specs=[VMEM] * (2 + pool_size),
        out_specs=[VMEM] * pool_size,
        out_shape=[jax.ShapeDtypeStruct((size, rank), f32)] * pool_size,
        compiler_params=params(),
        cost_estimate=cost(2 * pool_size * size * rank * width, 2 * (pool_size * size + rank) * width),
        name="down",
    )(factor, adapter_down, *arrived)

    back = [low[0]] + [None] * (pool_size - 1)
    for j in range(pool_size - 1, 0, -1):
        back[j] = across(low[j], j)
    row_low = pl.pallas_call(
        functools.partial(return_kernel, local, depth),
        in_specs=[smem] + [VMEM] * (1 + pool_size),
        out_specs=VMEM,
        out_shape=jax.ShapeDtypeStruct((rows, rank), f32),
        compiler_params=params(),
        cost_estimate=cost(6 * pool_size * size * rank * rows, 4 * pool_size * size * rank),
        name="collect",
    )(me, row_adapters, *back)
    row_low_other = swap(row_low)

    out = pl.pallas_call(
        finish_kernel,
        in_specs=[VMEM] * 9,
        out_specs=VMEM,
        out_shape=jax.ShapeDtypeStruct((rows, columns), bf16),
        compiler_params=params(),
        cost_estimate=cost(4 * rows * adapters * rank * columns, 2 * adapters * rank * columns),
        name="finish",
    )(
        row_adapters,
        mine,
        other,
        row_low,
        row_low_other,
        ups,
        cosine,
        sine,
        key_norm_gain.astype(f32)[None, :],
    )
    return out.reshape(rows, columns // (2 * head), 2, head)


def solution(mesh):
    return jax.shard_map(
        body,
        mesh=mesh,
        in_specs=(
            P(("groups", "pool"), "tp"),
            P(("groups", "pool"), None),
            P(("groups", "pool")),
            P("tp", None),
            P("pool", "tp", None),
            P("pool", None, None),
            P("pool"),
            P(),
        ),
        out_specs=P(("groups", "pool"), "tp", None, None),
        check_vma=False,
    )
```

time: 114 us -> 89.4 us (0.78)
  waiting for transfers between devices: 67 us -> 26.1 us
  starting transfers between devices: 13.4 us -> 29.5 us
  Pallas kernels: 0 us -> 11.9 us
  matrix products: 11.7 us -> 0 us
  other arithmetic: 5.27 us -> 1.09 us
  local copies, waits for them, and re-layouts: 1.93 us -> 6.09 us
    all_to_all x2 -> x0, waiting for transfers between devices: 56.5 us -> none  [the longest x1 30.6 us: body(): lax.all_to_all(outgoing, 'pool', split_axis=0, concat_axis=0, tiled=True)]
    ppermute x0 -> x16, starting transfers between devices: none -> 29.5 us  [the longest x14 29.4 us: across(): return lax.ppermute(x, 'pool', [(p, p ^ j) for p in range(pool_size)])]
    ppermute x0 -> x16, waiting for transfers between devices: none -> 24.1 us  [the longest x14 24.1 us: across(): return lax.ppermute(x, 'pool', [(p, p ^ j) for p in range(pool_size)])]
    all_to_all x2 -> x0, starting transfers between devices: 13.3 us -> none  [the longest x1 7.41 us: body(): lax.all_to_all(outgoing, 'pool', split_axis=0, concat_axis=0, tiled=True)]
    pallas_call x0 -> x6, Pallas kernels: none -> 11.9 us  [the longest x2 9.55 us: base_half(): pl.pallas_call(base_kernel, grid_spec=pltpu.PrefetchScalarGridSpec(num_sc...]
    dot_general x4 -> x0, matrix products: 11.7 us -> none  [the longest x1 6.52 us: body(): jnp.dot(tokens, key_value_weight, preferred_element_type=jnp.float32)]
    psum x1 -> x0, waiting for transfers between devices: 10.5 us -> none  [body(): rank_reduced = lax.psum(rank_reduced, 'tp')]
    unnamed x12 -> x13, local copies, waits for them, and re-layouts: 0.03 us -> 4.49 us
  transfers between devices with their start and end apart: 4 -> 17, of which waited for: 3 -> 5; matrix products, arithmetic and copies ran while one was open for 9% -> 2% of each run, Pallas kernels for 0% -> 12%
where the time goes in v1:
time: 89.4 us; the launch traced here: 89 us
  starting transfers between devices  29.5 us (33%)
  waiting for transfers between devices  26.1 us (29%)
  between operations  14.3 us (16%)
  Pallas kernels  11.9 us (13%)
  local copies, waits for them, and re-layouts  6.09 us (7%)
  other arithmetic  1.09 us (1%)
    ppermute x14, starting transfers between devices, across(): return lax.ppermute(x, 'pool', [(p, p ^ j) for p in range(pool_size)])  29.4 us
    ppermute x14, waiting for transfers between devices, across(): return lax.ppermute(x, 'pool', [(p, p ^ j) for p in range(pool_size)])  24.1 us
    pallas_call x2, Pallas kernels, base_half(): pl.pallas_call(base_kernel, grid_spec=pltpu.PrefetchScalarGridSpec(num_sc...  9.55 us
    unnamed x13, local copies, waits for them, and re-layouts  4.49 us
    all_gather x1, waiting for transfers between devices, body(): ups = lax.all_gather(own_up, 'pool', axis=0, tiled=True)  1.9 us
  transfers between devices with their start and end apart: 17, of which 5 were waited for; matrix products, arithmetic and copies ran while one was open for 2% of the time, Pallas kernels for 12%

profile of v1, /device:TPU:0, one launch (start us, length us, event | category | flops | bytes accessed | tf_op | source)
XLA Modules:
  0.0 89.0 jit_solution(10132950035173316964)
XLA Ops:
  6.5 0.0 copy-start
  6.5 0.0 copy-start.2
  6.5 0.0 copy-start.5
  6.5 0.0 all-gather.2.cloned.1.call-start
  6.6 1.0 %copy-done = bf16[1,128,2048]{2,1,0:T(8,128)(2,1)S(1)} copy-done((bf16[1,128,2048]{2,1,0:T(8,128)(2,1)S(1)}, bf16[1,128,2048]{2,1,0:T(8,128)(2,1)}, u32[]{:S(2)}) %copy-start) | copy-done | bytes 524312
  7.6 0.7 constant_dynamic-slice_fusion
  8.3 0.0 all-gather.2.cloned.1.call-update
  8.3 0.8 copy.14.adapter_ref
  9.1 0.0 copy-start.1
  9.1 1.1 %copy-done.1 = bf16[128,2560]{1,0:T(8,128)(2,1)S(1)} copy-done((bf16[128,2560]{1,0:T(8,128)(2,1)S(1)}, bf16[128,2560]{1,0:T(8,128)(2,1)}, u32[]{:S(2)}) %copy-start.1) | copy-done | bytes 655384
  10.2 0.0 copy-start.4
  10.2 0.6 pick.1
  10.8 3.0 %collective-permute-start.1 = (bf16[32,2560]{1,0:T(8,128)(2,1)S(1)}, bf16[32,2560]{1,0:T(8,128)(2,1)S(1)}, u32[]{:S(2)}, u32[]{:S(2)}) collective-permute-start(bf16[32,2560]{1,0:T(8,128)(2,1)S(1)} %get-tuple-element.22), channel_id=1, source_target_pairs={{0,2},{2,0},{4,6},{6,4},{8,10},{10,8},{12,14},{14,12},{1,3},{3,1},... | collective-permute-start | bytes 491528 | tf_op jit(solution)/shard_map/ppermute | solution.py:189
  13.8 1.6 %collective-permute-start.2 = (bf16[32,2560]{1,0:T(8,128)(2,1)S(1)}, bf16[32,2560]{1,0:T(8,128)(2,1)S(1)}, u32[]{:S(2)}, u32[]{:S(2)}) collective-permute-start(bf16[32,2560]{1,0:T(8,128)(2,1)S(1)} %get-tuple-element.23), channel_id=1, source_target_pairs={{0,4},{2,6},{4,0},{6,2},{8,12},{10,14},{12,8},{14,10},{1,5},{3,7},... | collective-permute-start | bytes 491528 | tf_op jit(solution)/shard_map/ppermute | solution.py:189
  15.4 0.0 collective-permute-start.3
  15.4 3.0 %collective-permute-start.4 = (bf16[32,2560]{1,0:T(8,128)(2,1)S(1)}, bf16[32,2560]{1,0:T(8,128)(2,1)S(1)}, u32[]{:S(2)}, u32[]{:S(2)}) collective-permute-start(bf16[32,2560]{1,0:T(8,128)(2,1)S(1)} %get-tuple-element.25), channel_id=1, source_target_pairs={{0,8},{2,10},{4,12},{6,14},{8,0},{10,2},{12,4},{14,6},{1,9},{3,11}... | collective-permute-start | bytes 491528 | tf_op jit(solution)/shard_map/ppermute | solution.py:189
  18.4 1.3 %collective-permute-start.5 = (bf16[32,2560]{1,0:T(8,128)(2,1)S(1)}, bf16[32,2560]{1,0:T(8,128)(2,1)S(1)}, u32[]{:S(2)}, u32[]{:S(2)}) collective-permute-start(bf16[32,2560]{1,0:T(8,128)(2,1)S(1)} %get-tuple-element.26), channel_id=1, source_target_pairs={{0,10},{2,8},{4,14},{6,12},{8,2},{10,0},{12,6},{14,4},{1,11},{3,9}... | collective-permute-start | bytes 491528 | tf_op jit(solution)/shard_map/ppermute | solution.py:189
  20.3 0.7 convert_element_type.9
  21.0 0.0 collective-permute-done.1.refs_1_
  21.1 3.7 %collective-permute-start.6 = (bf16[32,2560]{1,0:T(8,128)(2,1)S(1)}, bf16[32,2560]{1,0:T(8,128)(2,1)S(1)}, u32[]{:S(2)}, u32[]{:S(2)}) collective-permute-start(bf16[32,2560]{1,0:T(8,128)(2,1)S(1)} %get-tuple-element.27), channel_id=1, source_target_pairs={{0,12},{2,14},{4,8},{6,10},{8,4},{10,6},{12,0},{14,2},{1,13},{3,15... | collective-permute-start | bytes 491528 | tf_op jit(solution)/shard_map/ppermute | solution.py:189
  24.7 5.5 %collective-permute-done.2.refs_2_ = bf16[32,2560]{1,0:T(8,128)(2,1)S(1)} collective-permute-done((bf16[32,2560]{1,0:T(8,128)(2,1)S(1)}, bf16[32,2560]{1,0:T(8,128)(2,1)S(1)}, u32[]{:S(2)}, u32[]{:S(2)}) %collective-permute-start.2) | collective-permute-done | bytes 163872 | tf_op jit(solution)/shard_map/ppermute | solution.py:189
  30.2 0.0 collective-permute-start.7
  30.2 4.8 %base_half.3 = f32[128,1024]{1,0:T(8,128)S(1)} custom-call(s32[1]{0:T(128)S(6)} %sub.3.half_ref, bf16[128,2560]{1,0:T(8,128)(2,1)S(1)} %copy-done.1, bf16[2560,2048]{1,0:T(8,128)(2,1)} %weight_ref.3), custom_call_target="tpu_custom_call" | custom-call | flops 671088640 | bytes 5898240 | tf_op jit(solution)/shard_map/base_half/pallas_call | solution.py:104
  35.0 0.0 collective-permute-done.3.refs_3_
  35.0 0.1 collective-permute-start
  35.1 0.0 collective-permute-done.4.refs_4_
  35.1 14.1 %collective-permute-done.5.refs_5_ = bf16[32,2560]{1,0:T(8,128)(2,1)S(1)} collective-permute-done((bf16[32,2560]{1,0:T(8,128)(2,1)S(1)}, bf16[32,2560]{1,0:T(8,128)(2,1)S(1)}, u32[]{:S(2)}, u32[]{:S(2)}) %collective-permute-start.5) | collective-permute-done | bytes 163872 | tf_op jit(solution)/shard_map/ppermute | solution.py:189
  49.2 0.0 collective-permute-done.6.refs_6_
  49.2 0.0 collective-permute-done.7.refs_7_
  49.2 0.0 copy-done.4
  49.2 0.5 down.1
  49.7 7.4 %collective-permute-start.10 = (f32[32,128]{1,0:T(8,128)S(1)}, f32[32,128]{1,0:T(8,128)S(1)}, u32[]{:S(2)}, u32[]{:S(2)}) collective-permute-start(f32[32,128]{1,0:T(8,128)S(1)} %get-tuple-element.32), channel_id=1, source_target_pairs={{0,6},{2,4},{4,2},{6,0},{8,14},{10,12},{12,10},{14,8},{1,7},{3,5},... | collective-permute-start | bytes 49160 | tf_op jit(solution)/shard_map/ppermute | solution.py:189
  57.1 2.0 %collective-permute-start.11 = (f32[32,128]{1,0:T(8,128)S(1)}, f32[32,128]{1,0:T(8,128)S(1)}, u32[]{:S(2)}, u32[]{:S(2)}) collective-permute-start(f32[32,128]{1,0:T(8,128)S(1)} %get-tuple-element.33), channel_id=1, source_target_pairs={{0,8},{2,10},{4,12},{6,14},{8,0},{10,2},{12,4},{14,6},{1,9},{3,11}... | collective-permute-start | bytes 49160 | tf_op jit(solution)/shard_map/ppermute | solution.py:189
  59.1 1.8 %collective-permute-start.12 = (f32[32,128]{1,0:T(8,128)S(1)}, f32[32,128]{1,0:T(8,128)S(1)}, u32[]{:S(2)}, u32[]{:S(2)}) collective-permute-start(f32[32,128]{1,0:T(8,128)S(1)} %get-tuple-element.34), channel_id=1, source_target_pairs={{0,10},{2,8},{4,14},{6,12},{8,2},{10,0},{12,6},{14,4},{1,11},{3,9}... | collective-permute-start | bytes 49160 | tf_op jit(solution)/shard_map/ppermute | solution.py:189
  60.9 0.3 fusion
  61.2 3.5 %collective-permute-start.13 = (f32[32,128]{1,0:T(8,128)S(1)}, f32[32,128]{1,0:T(8,128)S(1)}, u32[]{:S(2)}, u32[]{:S(2)}) collective-permute-start(f32[32,128]{1,0:T(8,128)S(1)} %get-tuple-element.35), channel_id=1, source_target_pairs={{0,12},{2,14},{4,8},{6,10},{8,4},{10,6},{12,0},{14,2},{1,13},{3,15... | collective-permute-start | bytes 49160 | tf_op jit(solution)/shard_map/ppermute | solution.py:189
  64.7 0.0 collective-permute-done.10.refs_3_
  64.7 0.4 collective-permute-start.14
  65.2 0.0 collective-permute-done.11.refs_4_
  65.2 1.4 %collective-permute-start.8 = (f32[32,128]{1,0:T(8,128)S(1)}, f32[32,128]{1,0:T(8,128)S(1)}, u32[]{:S(2)}, u32[]{:S(2)}) collective-permute-start(f32[32,128]{1,0:T(8,128)S(1)} %get-tuple-element.30), channel_id=1, source_target_pairs={{0,2},{2,0},{4,6},{6,4},{8,10},{10,8},{12,14},{14,12},{1,3},{3,1},... | collective-permute-start | bytes 49160 | tf_op jit(solution)/shard_map/ppermute | solution.py:189
  66.6 0.0 collective-permute-done.12.refs_5_
  66.6 0.3 collective-permute-start.9
  66.9 0.0 copy-done.5
  66.9 0.3 collective-permute-done.13.refs_6_
  67.2 4.2 %collective-permute-done.14.refs_7_ = f32[32,128]{1,0:T(8,128)S(1)} collective-permute-done((f32[32,128]{1,0:T(8,128)S(1)}, f32[32,128]{1,0:T(8,128)S(1)}, u32[]{:S(2)}, u32[]{:S(2)}) %collective-permute-start.14) | collective-permute-done | bytes 16416 | tf_op jit(solution)/shard_map/ppermute | solution.py:189
  71.4 0.0 collective-permute-done.8.refs_1_
  71.4 0.0 collective-permute-done.9.refs_2_
  71.4 0.4 collect.1.low_ref
  71.8 0.1 collective-permute-start.15
  71.9 0.1 pad_maximum_fusion
  72.0 0.0 copy-done.2
  72.0 4.8 %base_half.2.mine_ref = f32[128,1024]{1,0:T(8,128)S(1)} custom-call(s32[1]{0:T(128)} %bitcast.half_ref, bf16[128,2560]{1,0:T(8,128)(2,1)S(1)} %copy-done.2, bf16[2560,2048]{1,0:T(8,128)(2,1)} %weight_ref.3), custom_call_target="tpu_custom_call" | custom-call | flops 671088640 | bytes 5898240 | tf_op jit(solution)/shard_map/base_half/pallas_call | solution.py:104
  76.8 0.0 collective-permute-done.15.low_other_ref
  76.8 0.0 collective-permute-done.other_ref
  76.8 1.9 %all-gather.2.cloned.1.call-done.up_ref = bf16[8,128,1024]{2,1,0:T(8,128)(2,1)} async-done(((bf16[1,128,1024]{2,1,0:T(8,128)(2,1)}), bf16[8,128,1024]{2,1,0:T(8,128)(2,1)}) %all-gather.2.cloned.1.call-update) | async-done | bytes 2097168 | tf_op jit(solution)/shard_map/all_gather | solution.py:176
  78.7 0.0 copy-start.3
  78.7 1.6 %copy-done.3 = bf16[8,128,1024]{2,1,0:T(8,128)(2,1)S(1)} copy-done((bf16[8,128,1024]{2,1,0:T(8,128)(2,1)S(1)}, bf16[8,128,1024]{2,1,0:T(8,128)(2,1)}, u32[]{:S(2)}) %copy-start.3) | copy-done | bytes 2097176
  80.3 0.9 %finish.1 = bf16[128,1024]{1,0:T(8,128)(2,1)S(1)} custom-call(s32[128,1]{1,0:T(8,128)S(1)} %copy.14.adapter_ref, f32[128,1024]{1,0:T(8,128)S(1)} %base_half.2.mine_ref, f32[128,1024]{1,0:T(8,128)S(1)} %collective-permute-done.other_ref, f32[128,128]{1,0:T(8,128)S(1)} %collect.1.low_ref, f32[128,128]{1,0:T(8,128)S(1)} %collective-permute-done.15.low_other_ref, ...), custom_call_target="tpu_custom_call" | custom-call | flops 536870912 | bytes 2097152 | tf_op jit(solution)/shard_map/finish/pallas_call | solution.py:238
  81.2 0.9 reshape.28
  (3 shorter events, 0.0 us)
Async XLA Ops:
  6.5 1.1 %copy-start = (bf16[1,128,2048]{2,1,0:T(8,128)(2,1)S(1)}, bf16[1,128,2048]{2,1,0:T(8,128)(2,1)}, u32[]{:S(2)}) copy-start(bf16[1,128,2048]{2,1,0:T(8,128)(2,1)} %param.13) | copy-start | bytes 1572868
  6.5 65.5 %copy-start.2 = (bf16[128,2560]{1,0:T(8,128)(2,1)S(1)}, bf16[128,2560]{1,0:T(8,128)(2,1)}, u32[]{:S(2)}) copy-start(bf16[128,2560]{1,0:T(8,128)(2,1)} %tokens_ref.5) | copy-start | bytes 1966084
  6.5 60.3 %copy-start.5 = (bf16[128]{0:T(256)(128)(2,1)S(1)}, bf16[128]{0:T(256)(128)(2,1)}, u32[]{:S(2)}) copy-start(bf16[128]{0:T(256)(128)(2,1)} %param.15) | copy-start | bytes 772
  6.5 72.2 %all-gather.2.cloned.1.call-start = ((), (), s32[]{:S(2)}) async-start(), calls=%async_computation | async-start | bytes 2359296 | tf_op jit(solution)/shard_map/all_gather | solution.py:176
  9.1 1.1 %copy-start.1 = (bf16[128,2560]{1,0:T(8,128)(2,1)S(1)}, bf16[128,2560]{1,0:T(8,128)(2,1)}, u32[]{:S(2)}) copy-start(bf16[128,2560]{1,0:T(8,128)(2,1)} %tokens_ref.5) | copy-start | bytes 1966084
  10.2 39.0 %copy-start.4 = (bf16[1,2560,128]{2,1,0:T(8,128)(2,1)S(1)}, bf16[1,2560,128]{2,1,0:T(8,128)(2,1)}, u32[]{:S(2)}) copy-start(bf16[1,2560,128]{2,1,0:T(8,128)(2,1)} %down_ref.1) | copy-start | bytes 1966084
  10.8 10.3 %collective-permute-start.1 = (bf16[32,2560]{1,0:T(8,128)(2,1)S(1)}, bf16[32,2560]{1,0:T(8,128)(2,1)S(1)}, u32[]{:S(2)}, u32[]{:S(2)}) collective-permute-start(bf16[32,2560]{1,0:T(8,128)(2,1)S(1)} %get-tuple-element.22), channel_id=1, source_target_pairs={{0,2},{2,0},{4,6},{6,4},{8,10},{10,8},{12,14},{14,12},{1,3},{3,1},... | collective-permute-start | bytes 491528 | tf_op jit(solution)/shard_map/ppermute | solution.py:189
  13.8 16.4 %collective-permute-start.2 = (bf16[32,2560]{1,0:T(8,128)(2,1)S(1)}, bf16[32,2560]{1,0:T(8,128)(2,1)S(1)}, u32[]{:S(2)}, u32[]{:S(2)}) collective-permute-start(bf16[32,2560]{1,0:T(8,128)(2,1)S(1)} %get-tuple-element.23), channel_id=1, source_target_pairs={{0,4},{2,6},{4,0},{6,2},{8,12},{10,14},{12,8},{14,10},{1,5},{3,7},... | collective-permute-start | bytes 491528 | tf_op jit(solution)/shard_map/ppermute | solution.py:189
  15.4 19.6 %collective-permute-start.3 = (bf16[32,2560]{1,0:T(8,128)(2,1)S(1)}, bf16[32,2560]{1,0:T(8,128)(2,1)S(1)}, u32[]{:S(2)}, u32[]{:S(2)}) collective-permute-start(bf16[32,2560]{1,0:T(8,128)(2,1)S(1)} %get-tuple-element.24), channel_id=1, source_target_pairs={{0,6},{2,4},{4,2},{6,0},{8,14},{10,12},{12,10},{14,8},{1,7},{3,5},... | collective-permute-start | bytes 491528 | tf_op jit(solution)/shard_map/ppermute | solution.py:189
  15.4 19.7 %collective-permute-start.4 = (bf16[32,2560]{1,0:T(8,128)(2,1)S(1)}, bf16[32,2560]{1,0:T(8,128)(2,1)S(1)}, u32[]{:S(2)}, u32[]{:S(2)}) collective-permute-start(bf16[32,2560]{1,0:T(8,128)(2,1)S(1)} %get-tuple-element.25), channel_id=1, source_target_pairs={{0,8},{2,10},{4,12},{6,14},{8,0},{10,2},{12,4},{14,6},{1,9},{3,11}... | collective-permute-start | bytes 491528 | tf_op jit(solution)/shard_map/ppermute | solution.py:189
  18.4 30.8 %collective-permute-start.5 = (bf16[32,2560]{1,0:T(8,128)(2,1)S(1)}, bf16[32,2560]{1,0:T(8,128)(2,1)S(1)}, u32[]{:S(2)}, u32[]{:S(2)}) collective-permute-start(bf16[32,2560]{1,0:T(8,128)(2,1)S(1)} %get-tuple-element.26), channel_id=1, source_target_pairs={{0,10},{2,8},{4,14},{6,12},{8,2},{10,0},{12,6},{14,4},{1,11},{3,9}... | collective-permute-start | bytes 491528 | tf_op jit(solution)/shard_map/ppermute | solution.py:189
  21.1 28.1 %collective-permute-start.6 = (bf16[32,2560]{1,0:T(8,128)(2,1)S(1)}, bf16[32,2560]{1,0:T(8,128)(2,1)S(1)}, u32[]{:S(2)}, u32[]{:S(2)}) collective-permute-start(bf16[32,2560]{1,0:T(8,128)(2,1)S(1)} %get-tuple-element.27), channel_id=1, source_target_pairs={{0,12},{2,14},{4,8},{6,10},{8,4},{10,6},{12,0},{14,2},{1,13},{3,15... | collective-permute-start | bytes 491528 | tf_op jit(solution)/shard_map/ppermute | solution.py:189
  30.2 19.0 %collective-permute-start.7 = (bf16[32,2560]{1,0:T(8,128)(2,1)S(1)}, bf16[32,2560]{1,0:T(8,128)(2,1)S(1)}, u32[]{:S(2)}, u32[]{:S(2)}) collective-permute-start(bf16[32,2560]{1,0:T(8,128)(2,1)S(1)} %get-tuple-element.28), channel_id=1, source_target_pairs={{0,14},{2,12},{4,10},{6,8},{8,6},{10,4},{12,2},{14,0},{1,15},{3,13... | collective-permute-start | bytes 491528 | tf_op jit(solution)/shard_map/ppermute | solution.py:189
  35.0 41.8 %collective-permute-start = (f32[128,1024]{1,0:T(8,128)S(1)}, f32[128,1024]{1,0:T(8,128)S(1)}, u32[]{:S(2)}, u32[]{:S(2)}) collective-permute-start(f32[128,1024]{1,0:T(8,128)S(1)} %base_half.3), channel_id=1, source_target_pairs={{0,1},{1,0},{2,3},{3,2},{4,5},{5,4},{6,7},{7,6},{8,9},{9,8},{10,11... | collective-permute-start | bytes 1572872 | tf_op jit(solution)/shard_map/ppermute | solution.py:192
  49.7 15.0 %collective-permute-start.10 = (f32[32,128]{1,0:T(8,128)S(1)}, f32[32,128]{1,0:T(8,128)S(1)}, u32[]{:S(2)}, u32[]{:S(2)}) collective-permute-start(f32[32,128]{1,0:T(8,128)S(1)} %get-tuple-element.32), channel_id=1, source_target_pairs={{0,6},{2,4},{4,2},{6,0},{8,14},{10,12},{12,10},{14,8},{1,7},{3,5},... | collective-permute-start | bytes 49160 | tf_op jit(solution)/shard_map/ppermute | solution.py:189
  57.1 8.0 %collective-permute-start.11 = (f32[32,128]{1,0:T(8,128)S(1)}, f32[32,128]{1,0:T(8,128)S(1)}, u32[]{:S(2)}, u32[]{:S(2)}) collective-permute-start(f32[32,128]{1,0:T(8,128)S(1)} %get-tuple-element.33), channel_id=1, source_target_pairs={{0,8},{2,10},{4,12},{6,14},{8,0},{10,2},{12,4},{14,6},{1,9},{3,11}... | collective-permute-start | bytes 49160 | tf_op jit(solution)/shard_map/ppermute | solution.py:189
  59.1 7.5 %collective-permute-start.12 = (f32[32,128]{1,0:T(8,128)S(1)}, f32[32,128]{1,0:T(8,128)S(1)}, u32[]{:S(2)}, u32[]{:S(2)}) collective-permute-start(f32[32,128]{1,0:T(8,128)S(1)} %get-tuple-element.34), channel_id=1, source_target_pairs={{0,10},{2,8},{4,14},{6,12},{8,2},{10,0},{12,6},{14,4},{1,11},{3,9}... | collective-permute-start | bytes 49160 | tf_op jit(solution)/shard_map/ppermute | solution.py:189
  61.2 6.0 %collective-permute-start.13 = (f32[32,128]{1,0:T(8,128)S(1)}, f32[32,128]{1,0:T(8,128)S(1)}, u32[]{:S(2)}, u32[]{:S(2)}) collective-permute-start(f32[32,128]{1,0:T(8,128)S(1)} %get-tuple-element.35), channel_id=1, source_target_pairs={{0,12},{2,14},{4,8},{6,10},{8,4},{10,6},{12,0},{14,2},{1,13},{3,15... | collective-permute-start | bytes 49160 | tf_op jit(solution)/shard_map/ppermute | solution.py:189
  64.7 6.7 %collective-permute-start.14 = (f32[32,128]{1,0:T(8,128)S(1)}, f32[32,128]{1,0:T(8,128)S(1)}, u32[]{:S(2)}, u32[]{:S(2)}) collective-permute-start(f32[32,128]{1,0:T(8,128)S(1)} %get-tuple-element.36), channel_id=1, source_target_pairs={{0,14},{2,12},{4,10},{6,8},{8,6},{10,4},{12,2},{14,0},{1,15},{3,13... | collective-permute-start | bytes 49160 | tf_op jit(solution)/shard_map/ppermute | solution.py:189
  65.2 6.3 %collective-permute-start.8 = (f32[32,128]{1,0:T(8,128)S(1)}, f32[32,128]{1,0:T(8,128)S(1)}, u32[]{:S(2)}, u32[]{:S(2)}) collective-permute-start(f32[32,128]{1,0:T(8,128)S(1)} %get-tuple-element.30), channel_id=1, source_target_pairs={{0,2},{2,0},{4,6},{6,4},{8,10},{10,8},{12,14},{14,12},{1,3},{3,1},... | collective-permute-start | bytes 49160 | tf_op jit(solution)/shard_map/ppermute | solution.py:189
  66.6 4.8 %collective-permute-start.9 = (f32[32,128]{1,0:T(8,128)S(1)}, f32[32,128]{1,0:T(8,128)S(1)}, u32[]{:S(2)}, u32[]{:S(2)}) collective-permute-start(f32[32,128]{1,0:T(8,128)S(1)} %get-tuple-element.31), channel_id=1, source_target_pairs={{0,4},{2,6},{4,0},{6,2},{8,12},{10,14},{12,8},{14,10},{1,5},{3,7},... | collective-permute-start | bytes 49160 | tf_op jit(solution)/shard_map/ppermute | solution.py:189
  71.8 5.0 %collective-permute-start.15 = (f32[128,128]{1,0:T(8,128)S(1)}, f32[128,128]{1,0:T(8,128)S(1)}, u32[]{:S(2)}, u32[]{:S(2)}) collective-permute-start(f32[128,128]{1,0:T(8,128)S(1)} %collect.1.low_ref), channel_id=1, source_target_pairs={{0,1},{1,0},{2,3},{3,2},{4,5},{5,4},{6,7},{7,6},{8,9},{9,8},{10,11... | collective-permute-start | bytes 196616 | tf_op jit(solution)/shard_map/ppermute | solution.py:192
  78.7 1.6 %copy-start.3 = (bf16[8,128,1024]{2,1,0:T(8,128)(2,1)S(1)}, bf16[8,128,1024]{2,1,0:T(8,128)(2,1)}, u32[]{:S(2)}) copy-start(bf16[8,128,1024]{2,1,0:T(8,128)(2,1)} %all-gather.2.cloned.1.call-done.up_ref) | copy-start | bytes 6291460
Sparse Core Ops, SparseCore 0:
  9.5 69.1 all-gather.1

commit v2 on v1

v2 whole, which is shorter than its diff:
```python
import functools

import jax
import jax.numpy as jnp
from jax import lax
from jax.experimental import pallas as pl
from jax.experimental.pallas import tpu as pltpu
from jax.sharding import PartitionSpec as P

ALPHA = 32
ROPE_THETA = 1000000.0
NORM_EPS = 1e-06
VMEM_LIMIT = 48 * 1024 * 1024
LANES = 128

VMEM = pl.BlockSpec(memory_space=pltpu.VMEM)
SMEM = pl.BlockSpec(memory_space=pltpu.SMEM)


def params(**kw):
    return pltpu.CompilerParams(vmem_limit_bytes=VMEM_LIMIT, **kw)


def cost(flops, bytes_accessed):
    return pl.CostEstimate(flops=flops, bytes_accessed=bytes_accessed, transcendentals=0)


def iota(shape, dim):
    return lax.broadcasted_iota(jnp.int32, shape, dim)


def to_column(row):
    n = row.shape[1]
    return jnp.sum(
        jnp.where(iota((n, n), 0) == iota((n, n), 1), row, 0), axis=1, keepdims=True
    )


def slot_places(row, me, pool, local, depth):
    n = row.shape[1]
    column = to_column(row)
    earlier = (column == row) & (iota((n, n), 0) < iota((n, n), 1))
    slot = jnp.sum(jnp.where(earlier, 1, 0), axis=0, keepdims=True)
    holder = row // local
    apart = holder ^ me
    buffer, far = apart % (pool // 2), apart // (pool // 2)
    return ((buffer * 2 + far) * local + (row - holder * local)) * depth + slot


def halves(x):
    high = x.astype(jnp.bfloat16)
    low = (x - high.astype(jnp.float32)).astype(jnp.bfloat16)
    return high, low


def pick_kernel(pool, local, depth, me_ref, adapter_ref, tokens_ref, *outs):
    rows, width = tokens_ref.shape
    place = slot_places(adapter_ref[...], me_ref[0], pool, local, depth)
    size = outs[0].shape[0]
    slots = len(outs) * size
    picker = jnp.where(iota((slots, rows), 0) == place, 1.0, 0.0).astype(jnp.bfloat16)
    step = 512
    for at in range(0, width, step):
        block = jnp.dot(
            picker, tokens_ref[:, at : at + step], preferred_element_type=jnp.float32
        )
        for j, out in enumerate(outs):
            out[:, at : at + step] = block[j * size : (j + 1) * size].astype(jnp.bfloat16)


def base_kernel(half_ref, tokens_ref, weight_ref, out_ref):
    @pl.when(pl.program_id(0) == 0)
    def _():
        out_ref[...] = jnp.zeros_like(out_ref)

    out_ref[...] += jnp.dot(
        tokens_ref[...], weight_ref[...], preferred_element_type=jnp.float32
    )


def base_half(tokens, weight, half, columns):
    rows, width = tokens.shape
    step = 512
    return pl.pallas_call(
        base_kernel,
        grid_spec=pltpu.PrefetchScalarGridSpec(
            num_scalar_prefetch=1,
            grid=(width // step,),
            in_specs=[
                pl.BlockSpec((rows, step), lambda k, h: (0, k)),
                pl.BlockSpec((step, columns), lambda k, h: (k, h[0])),
            ],
            out_specs=pl.BlockSpec((rows, columns), lambda k, h: (0, 0)),
        ),
        out_shape=jax.ShapeDtypeStruct((rows, columns), jnp.float32),
        compiler_params=params(),
        cost_estimate=cost(2 * rows * width * columns, 2 * width * (rows + columns)),
        name="base_half",
    )(half, tokens, weight)


def down_kernel(buffers, groups, local, depth, group_ref, down_ref, *refs):
    ins, shares, out = refs[:buffers], refs[buffers : buffers + groups], refs[-1]
    rank = out.shape[1]
    share = shares[0].shape[1]
    total = None
    for k in range(groups):
        at = pl.multiple_of((group_ref[0] ^ k) * share, share)
        rows = jnp.concatenate([x[:, pl.ds(at, share)] for x in ins], axis=0)
        factors = [down_ref[a, pl.ds(at, share), :] for a in range(local)]
        factors += [shares[k][a] for a in range(local)]
        term = jnp.dot(
            rows, jnp.concatenate(factors, axis=1), preferred_element_type=jnp.float32
        )
        total = term if total is None else total + term
    which = (iota((total.shape[0], 1), 0) // depth) % (2 * local)
    low = total[:, :rank]
    for i in range(1, 2 * local):
        low = jnp.where(which == i, total[:, i * rank : (i + 1) * rank], low)
    out[...] = low


def up_kernel(
    buffers, groups, local, depth, group_ref, core_ref, low_ref, other_ref, factor_ref, up_ref, *refs
):
    shares, outs, term_ref = refs[:groups], refs[groups : groups + buffers], refs[-1]
    rows, rank = low_ref.shape
    size = rows // buffers
    columns = term_ref.shape[1]
    share = columns // groups
    which = (iota((rows, 1), 0) // depth) % (2 * local)
    low = low_ref[...] + other_ref[...]
    for a in range(local):
        low = jnp.where(which == a, low * factor_ref[a : a + 1, :], low)
    both = jnp.concatenate(halves(low), axis=0)
    which = jnp.concatenate([which, which], axis=0)
    spread = jnp.concatenate(
        [jnp.where(which == i, both, jnp.zeros_like(both)) for i in range(2 * local)], axis=1
    )
    for k in range(groups):
        at = pl.multiple_of((group_ref[0] ^ k) * share, share)
        own_at = pl.multiple_of(core_ref[0] * columns + at, share)
        factors = [up_ref[a, :, pl.ds(own_at, share)] for a in range(local)]
        factors += [shares[k][a] for a in range(local)]
        term = jnp.dot(
            spread, jnp.concatenate(factors, axis=0), preferred_element_type=jnp.float32
        )
        term_ref[:, pl.ds(at, share)] = term[:rows] + term[rows:]
    for j, out in enumerate(outs):
        term = term_ref[j * size : (j + 1) * size, :]
        top = jnp.max(jnp.abs(term), axis=1, keepdims=True)
        exponent = jnp.ceil(jnp.log2(jnp.maximum(top, 1e-30)) + 1e-3)
        code = jnp.round(term * jnp.exp2(15.0 - exponent))
        code = jnp.clip(code, -32767.0, 32767.0)
        out[:, :columns] = code.astype(jnp.int32).astype(jnp.int16)
        out[:, columns:] = jnp.broadcast_to(
            exponent.astype(jnp.int32), (size, LANES)
        ).astype(jnp.int16)


def finish_kernel(
    buffers, pool, local, depth, me_ref, adapter_ref, mine_ref, other_ref, cos_ref, sin_ref, gain_ref, *refs
):
    ins, out_ref = refs[:buffers], refs[-1]
    rows, columns = mine_ref.shape
    head = cos_ref.shape[1]
    place = to_column(slot_places(adapter_ref[...], me_ref[0], pool, local, depth))
    slots = buffers * ins[0].shape[0]
    picker = jnp.where(iota((rows, slots), 1) == place, 1.0, 0.0).astype(jnp.bfloat16)

    def picked(at, size):
        code = jnp.concatenate([x[:, at : at + size] for x in ins], axis=0).astype(jnp.int32)
        high = (code >> 8).astype(jnp.float32).astype(jnp.bfloat16)
        low = (code & 255).astype(jnp.float32).astype(jnp.bfloat16)
        high = jnp.dot(picker, high, preferred_element_type=jnp.float32)
        low = jnp.dot(picker, low, preferred_element_type=jnp.float32)
        return high * 256.0 + low

    scale = jnp.exp2(picked(columns, LANES)[:, :1] - 15.0)
    cosine, sine, gain = cos_ref[...], sin_ref[...], gain_ref[...]
    for at in range(0, columns, 2 * head):
        projected = mine_ref[:, at : at + 2 * head] + other_ref[:, at : at + 2 * head]
        projected = projected + picked(at, 2 * head) * scale
        key, value = projected[:, :head], projected[:, head:]
        mean = jnp.mean(key * key, axis=1, keepdims=True)
        normed = key * lax.rsqrt(mean + NORM_EPS) * gain
        rotated = normed * cosine + pltpu.roll(normed, head // 2, 1) * sine
        out_ref[:, at : at + head] = rotated.astype(jnp.bfloat16)
        out_ref[:, at + head : at + 2 * head] = value.astype(jnp.bfloat16)


def body(
    tokens,
    row_adapters,
    positions,
    key_value_weight,
    adapter_down,
    adapter_up,
    ranks,
    key_norm_gain,
):
    pool = lax.axis_size("pool")
    groups = lax.axis_size("groups")
    cores = lax.axis_size("tp")
    rows, width = tokens.shape
    local = adapter_down.shape[0]
    adapters = local * pool
    columns = key_value_weight.shape[1] // cores
    rank = adapter_down.shape[2]
    head = key_norm_gain.shape[0]
    depth = max(2, 2 * rows // adapters)
    buffers = pool // 2
    size = 2 * local * depth
    f32, bf16 = jnp.float32, jnp.bfloat16

    me = lax.axis_index("pool").astype(jnp.int32)[None]
    core = lax.axis_index("tp").astype(jnp.int32)[None]
    group = lax.axis_index("groups").astype(jnp.int32)[None]

    def exchange(x, axis, count, j):
        return lax.ppermute(x, axis, [(p, p ^ j) for p in range(count)])

    def hand_round(share):
        return [share] + [exchange(share, "groups", groups, k) for k in range(1, groups)]

    mask = (jnp.arange(rank, dtype=jnp.int32)[None, :] < ranks[:, None]).astype(f32)
    factor = mask * (f32(ALPHA) / ranks.astype(f32))[:, None]

    down_share = width // groups
    down_part = lax.dynamic_slice_in_dim(adapter_down, group[0] * down_share, down_share, 1)
    far_down = exchange(down_part, "pool", pool, pool // 2)
    up_share = columns // groups
    up_part = lax.dynamic_slice_in_dim(
        adapter_up, core[0] * columns + group[0] * up_share, up_share, 2
    )
    up_part = (up_part.astype(f32) * factor[:, :, None]).astype(bf16)
    far_up = exchange(up_part, "pool", pool, pool // 2)

    adapter_row = row_adapters.reshape(1, rows)
    picked = pl.pallas_call(
        functools.partial(pick_kernel, pool, local, depth),
        in_specs=[SMEM, VMEM, VMEM],
        out_specs=[VMEM] * buffers,
        out_shape=[jax.ShapeDtypeStruct((size, width), bf16)] * buffers,
        compiler_params=params(),
        cost_estimate=cost(2 * buffers * size * rows * width, 2 * (rows + buffers * size) * width),
        name="pick",
    )(me, adapter_row, tokens)
    arrived = [picked[0]] + [None] * (buffers - 1)
    for j in range(buffers - 1, 0, -1):
        arrived[j] = exchange(picked[j], "pool", pool, j)

    far_downs = hand_round(far_down)
    far_ups = hand_round(far_up)

    theirs = base_half(tokens, key_value_weight, 1 - core, columns)
    mine = base_half(tokens, key_value_weight, core, columns)
    other = exchange(theirs, "tp", cores, 1)

    half_dim = head // 2
    frequency = jnp.power(
        f32(ROPE_THETA), -jnp.arange(half_dim, dtype=f32) * (2.0 / head)
    )
    angles = positions.astype(f32)[:, None] * frequency[None, :]
    cosine, sine = jnp.cos(angles), jnp.sin(angles)
    cosine = jnp.concatenate([cosine, cosine], axis=1)
    sine = jnp.concatenate([-sine, sine], axis=1)

    arrived, mine, cosine, sine = lax.optimization_barrier((arrived, mine, cosine, sine))
    slots = buffers * size
    low = pl.pallas_call(
        functools.partial(down_kernel, buffers, groups, local, depth),
        in_specs=[SMEM] + [VMEM] * (1 + buffers + groups),
        out_specs=VMEM,
        out_shape=jax.ShapeDtypeStruct((slots, rank), f32),
        compiler_params=params(),
        cost_estimate=cost(4 * local * slots * rank * width, 2 * (slots + rank) * width),
        name="down",
    )(group, adapter_down, *arrived, *far_downs)
    low_other = exchange(low, "tp", cores, 1)

    terms = pl.pallas_call(
        functools.partial(up_kernel, buffers, groups, local, depth),
        in_specs=[SMEM] * 2 + [VMEM] * (4 + groups),
        out_specs=[VMEM] * buffers,
        out_shape=[jax.ShapeDtypeStruct((size, columns + LANES), jnp.int16)] * buffers,
        scratch_shapes=[pltpu.VMEM((slots, columns), f32)],
        compiler_params=params(),
        cost_estimate=cost(8 * local * slots * rank * columns, 2 * slots * columns),
        name="up",
    )(group, core, low, low_other, factor, adapter_up, *far_ups)
    returned = [terms[0]] + [None] * (buffers - 1)
    for j in range(buffers - 1, 0, -1):
        returned[j] = exchange(terms[j], "pool", pool, j)

    out = pl.pallas_call(
        functools.partial(finish_kernel, buffers, pool, local, depth),
        in_specs=[SMEM] + [VMEM] * (6 + buffers),
        out_specs=VMEM,
        out_shape=jax.ShapeDtypeStruct((rows, columns), bf16),
        compiler_params=params(),
        cost_estimate=cost(4 * rows * slots * columns, 2 * slots * columns),
        name="finish",
    )(
        me,
        adapter_row,
        mine,
        other,
        cosine,
        sine,
        key_norm_gain.astype(f32)[None, :],
        *returned,
    )
    return out.reshape(rows, columns // (2 * head), 2, head)


def solution(mesh):
    return jax.shard_map(
        body,
        mesh=mesh,
        in_specs=(
            P(("groups", "pool"), "tp"),
            P(("groups", "pool"), None),
            P(("groups", "pool")),
            P("tp", None),
            P("pool", "tp", None),
            P("pool", None, None),
            P("pool"),
            P(),
        ),
        out_specs=P(("groups", "pool"), "tp", None, None),
        check_vma=False,
    )
```

time: 89.4 us -> 62.6 us (0.70)
  starting transfers between devices: 29.5 us -> 15.1 us
  between operations: 14.3 us -> 0.86 us
  other arithmetic: 1.09 us -> 2.08 us
    ppermute x16 -> x12, starting transfers between devices: 29.5 us -> 15.1 us  [exchange(): return lax.ppermute(x, axis, [(p, p ^ j) for p in range(count)])]
    ppermute x16 -> x12, waiting for transfers between devices: 24.1 us -> 26.5 us  [exchange(): return lax.ppermute(x, axis, [(p, p ^ j) for p in range(count)])]
    all_gather x1 -> x0, waiting for transfers between devices: 1.9 us -> none  [body(): ups = lax.all_gather(own_up, 'pool', axis=0, tiled=True)]
    unnamed x13 -> x16, local copies, waits for them, and re-layouts: 4.49 us -> 2.85 us
    convert_element_type x0 -> x1, other arithmetic: none -> 0.99 us  [body(): up_part = (up_part.astype(f32) * factor[:, :, None]).astype(bf16)]
    dynamic_slice x1, local copies, waits for them, and re-layouts: 0.72 us -> 1.71 us  [body(): lax.dynamic_slice_in_dim(adapter_down, group[0] * down_share, down_share, 1)]
  transfers between devices with their start and end apart: 17 -> 12, of which waited for: 5 -> 5; matrix products, arithmetic and copies ran while one was open for 2% -> 6% of each run, Pallas kernels for 12% -> 18%
where the time goes in v2:
time: 62.6 us; the launch traced here: 62.2 us
  waiting for transfers between devices  26.5 us (42%)
  starting transfers between devices  15.1 us (24%)
  Pallas kernels  12.3 us (20%)
  local copies, waits for them, and re-layouts  5.44 us (9%)
  other arithmetic  2.08 us (3%)
  between operations  0.86 us (1%)
    ppermute x12, waiting for transfers between devices, exchange(): return lax.ppermute(x, axis, [(p, p ^ j) for p in range(count)])  26.5 us
    ppermute x12, starting transfers between devices, exchange(): return lax.ppermute(x, axis, [(p, p ^ j) for p in range(count)])  15.1 us
    pallas_call x2, Pallas kernels, base_half(): pl.pallas_call(base_kernel, grid_spec=pltpu.PrefetchScalarGridSpec(num_sc...  9.63 us
    unnamed x16, local copies, waits for them, and re-layouts  2.85 us
    dynamic_slice x1, local copies, waits for them, and re-layouts, body(): lax.dynamic_slice_in_dim(adapter_down, group[0] * down_share, down_share, 1)  1.71 us
  transfers between devices with their start and end apart: 12, of which 5 were waited for; matrix products, arithmetic and copies ran while one was open for 6% of the time, Pallas kernels for 18%

profile of v2, /device:TPU:0, one launch (start us, length us, event | category | flops | bytes accessed | tf_op | source)
XLA Modules:
  0.0 62.2 jit_solution(4706086718275275955)
XLA Ops:
  0.0 0.0 copy-start
  0.0 1.1 %copy-done = bf16[128,2560]{1,0:T(8,128)(2,1)S(1)} copy-done((bf16[128,2560]{1,0:T(8,128)(2,1)S(1)}, bf16[128,2560]{1,0:T(8,128)(2,1)}, u32[]{:S(2)}) %copy-start) | copy-done | bytes 655384
  1.1 0.0 copy-start.5
  1.1 0.7 %copy-done.5 = s32[128,1]{0,1:T(1,128)S(1)} copy-done((s32[128,1]{0,1:T(1,128)S(1)}, s32[128,1]{0,1:T(1,128)}, u32[]{:S(2)}) %copy-start.5) | copy-done | bytes 536
  1.7 0.0 copy-start.2
  1.7 0.6 pick.1
  2.3 3.0 %collective-permute-start = (bf16[64,2560]{1,0:T(8,128)(2,1)S(1)}, bf16[64,2560]{1,0:T(8,128)(2,1)S(1)}, u32[]{:S(2)}, u32[]{:S(2)}) collective-permute-start(bf16[64,2560]{1,0:T(8,128)(2,1)S(1)} %get-tuple-element.21), channel_id=1, source_target_pairs={{0,2},{2,0},{4,6},{6,4},{8,10},{10,8},{12,14},{14,12},{1,3},{3,1},... | collective-permute-start | bytes 983048 | tf_op jit(solution)/shard_map/ppermute | solution.py:221
  5.4 1.6 %collective-permute-start.1 = (bf16[64,2560]{1,0:T(8,128)(2,1)S(1)}, bf16[64,2560]{1,0:T(8,128)(2,1)S(1)}, u32[]{:S(2)}, u32[]{:S(2)}) collective-permute-start(bf16[64,2560]{1,0:T(8,128)(2,1)S(1)} %get-tuple-element.22), channel_id=1, source_target_pairs={{0,4},{2,6},{4,0},{6,2},{8,12},{10,14},{12,8},{14,10},{1,5},{3,7},... | collective-permute-start | bytes 983048 | tf_op jit(solution)/shard_map/ppermute | solution.py:221
  7.0 0.0 collective-permute-start.2
  7.0 1.7 %constant_dynamic-slice_fusion = bf16[1,1280,128]{2,1,0:T(8,128)(2,1)} fusion(bf16[1,2560,128]{2,1,0:T(8,128)(2,1)} %down_ref.1, s32[]{:T(128)S(6)} %select_n.6), kind=kLoop, calls=%fused_computation.9 | loop fusion | bytes 655364 | tf_op jit(solution)/shard_map/dynamic_slice | solution.py:230
  8.7 3.0 %collective-permute-start.4 = (bf16[1,1280,128]{2,1,0:T(8,128)(2,1)}, bf16[1,1280,128]{2,1,0:T(8,128)(2,1)S(1)}, u32[]{:S(2)}, u32[]{:S(2)}) collective-permute-start(bf16[1,1280,128]{2,1,0:T(8,128)(2,1)} %constant_dynamic-slice_fusion), channel_id=1, source_target_pairs={{0,8},{2,10},{4,12},{6,14},{8,0},{10,2},{12,4},{14,6},{1,9},{3,11}... | collective-permute-start | bytes 983048 | tf_op jit(solution)/shard_map/ppermute | solution.py:221
  12.3 1.0 %multiply_convert_fusion = bf16[1,128,512]{2,1,0:T(8,128)(2,1)S(1)} fusion(f32[128]{0:T(128)S(1)} %compare_select_fusion, bf16[1,128,2048]{2,1,0:T(8,128)(2,1)} %up_ref.1, s32[]{:T(128)S(6)} %select_n.7), kind=kLoop, calls=%fused_computation | loop fusion | flops 196608 | bytes 262660 | tf_op jit(solution)/shard_map/convert_element_type | solution.py:236
  13.4 0.1 collective-permute-start.7
  13.4 0.7 %convert_element_type.14 = f32[128]{0:T(128)S(1)} convert(s32[128]{0:T(128)} %param.10) | non-fusion elementwise | flops 128 | bytes 1024 | tf_op jit(solution)/shard_map/convert_element_type | solution.py:264
  14.1 15.1 %collective-permute-done.4.refs_4_ = bf16[1,1280,128]{2,1,0:T(8,128)(2,1)S(1)} collective-permute-done((bf16[1,1280,128]{2,1,0:T(8,128)(2,1)}, bf16[1,1280,128]{2,1,0:T(8,128)(2,1)S(1)}, u32[]{:S(2)}, u32[]{:S(2)}) %collective-permute-start.4) | collective-permute-done | bytes 327712 | tf_op jit(solution)/shard_map/ppermute | solution.py:221
  29.2 1.5 %collective-permute-start.5 = (bf16[1,1280,128]{2,1,0:T(8,128)(2,1)S(1)}, bf16[1,1280,128]{2,1,0:T(8,128)(2,1)S(1)}, u32[]{:S(2)}, u32[]{:S(2)}) collective-permute-start(bf16[1,1280,128]{2,1,0:T(8,128)(2,1)S(1)} %collective-permute-done.4.refs_4_), channel_id=1, source_target_pairs={{0,16},{16,0},{1,17},{17,1},{2,18},{18,2},{3,19},{19,3},{4,20},{20... | collective-permute-start | bytes 983048 | tf_op jit(solution)/shard_map/ppermute | solution.py:221
  30.7 0.3 fusion
  31.0 0.0 copy-start.1
  31.1 1.1 %copy-done.1 = bf16[128,2560]{1,0:T(8,128)(2,1)S(1)} copy-done((bf16[128,2560]{1,0:T(8,128)(2,1)S(1)}, bf16[128,2560]{1,0:T(8,128)(2,1)}, u32[]{:S(2)}) %copy-start.1) | copy-done | bytes 655384
  32.1 0.0 copy-start.3
  32.1 0.0 copy-start.4
  32.1 4.9 %base_half.2.mine_ref = f32[128,1024]{1,0:T(8,128)S(1)} custom-call(s32[1]{0:T(128)} %bitcast.2.half_ref.core_ref, bf16[128,2560]{1,0:T(8,128)(2,1)S(1)} %copy-done.1, bf16[2560,2048]{1,0:T(8,128)(2,1)} %weight_ref.3), custom_call_target="tpu_custom_call" | custom-call | flops 671088640 | bytes 5898240 | tf_op jit(solution)/shard_map/base_half/pallas_call | solution.py:84
  37.0 0.0 copy-done.2
  37.0 0.0 copy-start.7
  37.0 0.0 copy-start.6
  37.0 4.8 %base_half.3 = f32[128,1024]{1,0:T(8,128)S(1)} custom-call(s32[1]{0:T(128)S(6)} %sub.3.half_ref, bf16[128,2560]{1,0:T(8,128)(2,1)S(1)} %copy-done.2, bf16[2560,2048]{1,0:T(8,128)(2,1)} %weight_ref.3), custom_call_target="tpu_custom_call" | custom-call | flops 671088640 | bytes 5898240 | tf_op jit(solution)/shard_map/base_half/pallas_call | solution.py:84
  41.8 0.0 collective-permute-done.7.refs_0_
  41.8 0.1 collective-permute-start.3
  41.9 0.1 pad_maximum_fusion
  42.0 0.0 collective-permute-done.refs_1_
  42.0 0.6 collective-permute-start.8
  42.6 0.0 collective-permute-done.1.refs_2_
  42.6 0.0 collective-permute-done.2.refs_3_
  42.6 0.0 collective-permute-done.5.refs_5_
  42.6 0.0 copy-done.3
  42.6 0.5 down.1.low_ref
  43.2 0.3 collective-permute-start.6
  43.5 4.5 %collective-permute-done.8.refs_1_ = bf16[1,128,512]{2,1,0:T(8,128)(2,1)S(1)} collective-permute-done((bf16[1,128,512]{2,1,0:T(8,128)(2,1)S(1)}, bf16[1,128,512]{2,1,0:T(8,128)(2,1)S(1)}, u32[]{:S(2)}, u32[]{:S(2)}) %collective-permute-start.8) | collective-permute-done | bytes 131104 | tf_op jit(solution)/shard_map/ppermute | solution.py:221
  48.0 0.0 collective-permute-done.6.other_ref
  48.0 0.0 copy-done.4
  48.0 0.8 %up.1 = (s16[64,1152]{1,0:T(8,128)(2,1)S(1)}, s16[64,1152]{1,0:T(8,128)(2,1)S(1)}, s16[64,1152]{1,0:T(8,128)(2,1)S(1)}, s16[64,1152]{1,0:T(8,128)(2,1)S(1)}) custom-call(s32[1]{0:T(128)} %bitcast.4.group_ref, s32[1]{0:T(128)} %bitcast.2.half_ref.core_ref, f32[256,128]{1,0:T(8,128)S(1)} %down.1.low_ref, f32[256,128]{1,0:T(8,128)S(1)} %collective-permute-done.6.other_ref, ...), custom_call_target="tpu_custom_call" | custom-call | flops 268435456 | bytes 524288 | tf_op jit(solution)/shard_map/up/pallas_call | solution.py:282
  48.8 3.4 %collective-permute-start.10 = (s16[64,1152]{1,0:T(8,128)(2,1)S(1)}, s16[64,1152]{1,0:T(8,128)(2,1)S(1)}, u32[]{:S(2)}, u32[]{:S(2)}) collective-permute-start(s16[64,1152]{1,0:T(8,128)(2,1)S(1)} %get-tuple-element.33), channel_id=1, source_target_pairs={{0,4},{2,6},{4,0},{6,2},{8,12},{10,14},{12,8},{14,10},{1,5},{3,7},... | collective-permute-start | bytes 442376 | tf_op jit(solution)/shard_map/ppermute | solution.py:221
  52.2 0.0 collective-permute-start.11
  52.2 1.5 %collective-permute-start.9 = (s16[64,1152]{1,0:T(8,128)(2,1)S(1)}, s16[64,1152]{1,0:T(8,128)(2,1)S(1)}, u32[]{:S(2)}, u32[]{:S(2)}) collective-permute-start(s16[64,1152]{1,0:T(8,128)(2,1)S(1)} %get-tuple-element.32), channel_id=1, source_target_pairs={{0,2},{2,0},{4,6},{6,4},{8,10},{10,8},{12,14},{14,12},{1,3},{3,1},... | collective-permute-start | bytes 442376 | tf_op jit(solution)/shard_map/ppermute | solution.py:221
  53.7 0.0 copy-done.7
  53.7 0.0 collective-permute-done.3.other_ref
  53.7 3.1 %collective-permute-done.10.refs_2_ = s16[64,1152]{1,0:T(8,128)(2,1)S(1)} collective-permute-done((s16[64,1152]{1,0:T(8,128)(2,1)S(1)}, s16[64,1152]{1,0:T(8,128)(2,1)S(1)}, u32[]{:S(2)}, u32[]{:S(2)}) %collective-permute-start.10) | collective-permute-done | bytes 147488 | tf_op jit(solution)/shard_map/ppermute | solution.py:221
  56.9 2.2 %collective-permute-done.11.refs_3_ = s16[64,1152]{1,0:T(8,128)(2,1)S(1)} collective-permute-done((s16[64,1152]{1,0:T(8,128)(2,1)S(1)}, s16[64,1152]{1,0:T(8,128)(2,1)S(1)}, u32[]{:S(2)}, u32[]{:S(2)}) %collective-permute-start.11) | collective-permute-done | bytes 147488 | tf_op jit(solution)/shard_map/ppermute | solution.py:221
  59.1 1.4 %collective-permute-done.9.refs_1_ = s16[64,1152]{1,0:T(8,128)(2,1)S(1)} collective-permute-done((s16[64,1152]{1,0:T(8,128)(2,1)S(1)}, s16[64,1152]{1,0:T(8,128)(2,1)S(1)}, u32[]{:S(2)}, u32[]{:S(2)}) %collective-permute-start.9) | collective-permute-done | bytes 147488 | tf_op jit(solution)/shard_map/ppermute | solution.py:221
  60.5 0.0 copy-done.6
  60.5 0.8 %finish.1 = bf16[128,1024]{1,0:T(8,128)(2,1)S(1)} custom-call(s32[1]{0:T(128)} %bitcast.me_ref, s32[1,128]{1,0:T(1,128)S(1)} %bitcast.12, f32[128,1024]{1,0:T(8,128)S(1)} %base_half.2.mine_ref, f32[128,1024]{1,0:T(8,128)S(1)} %collective-permute-done.3.other_ref, f32[128,128]{1,0:T(8,128)S(1)} %get-tuple-element.25.cos_ref, ...), custom_call_target="tpu_custom_call" | custom-call | flops 134217728 | bytes 524288 | tf_op jit(solution)/shard_map/finish/pallas_call | solution.py:296
  61.3 0.9 %reshape.39 = bf16[128,4,2,128]{3,2,1,0:T(2,128)(2,1)} reshape(bf16[128,1024]{1,0:T(8,128)(2,1)S(1)} %finish.1) | data formatting | bytes 524288 | tf_op jit(solution)/shard_map/reshape | solution.py:314
  (4 shorter events, 0.0 us)
Async XLA Ops:
  0.0 1.1 %copy-start = (bf16[128,2560]{1,0:T(8,128)(2,1)S(1)}, bf16[128,2560]{1,0:T(8,128)(2,1)}, u32[]{:S(2)}) copy-start(bf16[128,2560]{1,0:T(8,128)(2,1)} %tokens_ref.5) | copy-start | bytes 1966084
  1.1 0.7 %copy-start.5 = (s32[128,1]{0,1:T(1,128)S(1)}, s32[128,1]{0,1:T(1,128)}, u32[]{:S(2)}) copy-start(s32[128,1]{0,1:T(1,128)} %param.9) | copy-start | bytes 1540
  1.7 35.3 %copy-start.2 = (bf16[128,2560]{1,0:T(8,128)(2,1)S(1)}, bf16[128,2560]{1,0:T(8,128)(2,1)}, u32[]{:S(2)}) copy-start(bf16[128,2560]{1,0:T(8,128)(2,1)} %tokens_ref.5) | copy-start | bytes 1966084
  2.3 39.7 %collective-permute-start = (bf16[64,2560]{1,0:T(8,128)(2,1)S(1)}, bf16[64,2560]{1,0:T(8,128)(2,1)S(1)}, u32[]{:S(2)}, u32[]{:S(2)}) collective-permute-start(bf16[64,2560]{1,0:T(8,128)(2,1)S(1)} %get-tuple-element.21), channel_id=1, source_target_pairs={{0,2},{2,0},{4,6},{6,4},{8,10},{10,8},{12,14},{14,12},{1,3},{3,1},... | collective-permute-start | bytes 983048 | tf_op jit(solution)/shard_map/ppermute | solution.py:221
  5.4 37.3 %collective-permute-start.1 = (bf16[64,2560]{1,0:T(8,128)(2,1)S(1)}, bf16[64,2560]{1,0:T(8,128)(2,1)S(1)}, u32[]{:S(2)}, u32[]{:S(2)}) collective-permute-start(bf16[64,2560]{1,0:T(8,128)(2,1)S(1)} %get-tuple-element.22), channel_id=1, source_target_pairs={{0,4},{2,6},{4,0},{6,2},{8,12},{10,14},{12,8},{14,10},{1,5},{3,7},... | collective-permute-start | bytes 983048 | tf_op jit(solution)/shard_map/ppermute | solution.py:221
  7.0 35.7 %collective-permute-start.2 = (bf16[64,2560]{1,0:T(8,128)(2,1)S(1)}, bf16[64,2560]{1,0:T(8,128)(2,1)S(1)}, u32[]{:S(2)}, u32[]{:S(2)}) collective-permute-start(bf16[64,2560]{1,0:T(8,128)(2,1)S(1)} %get-tuple-element.23), channel_id=1, source_target_pairs={{0,6},{2,4},{4,2},{6,0},{8,14},{10,12},{12,10},{14,8},{1,7},{3,5},... | collective-permute-start | bytes 983048 | tf_op jit(solution)/shard_map/ppermute | solution.py:221
  8.7 20.6 %collective-permute-start.4 = (bf16[1,1280,128]{2,1,0:T(8,128)(2,1)}, bf16[1,1280,128]{2,1,0:T(8,128)(2,1)S(1)}, u32[]{:S(2)}, u32[]{:S(2)}) collective-permute-start(bf16[1,1280,128]{2,1,0:T(8,128)(2,1)} %constant_dynamic-slice_fusion), channel_id=1, source_target_pairs={{0,8},{2,10},{4,12},{6,14},{8,0},{10,2},{12,4},{14,6},{1,9},{3,11}... | collective-permute-start | bytes 983048 | tf_op jit(solution)/shard_map/ppermute | solution.py:221
  13.4 28.5 %collective-permute-start.7 = (bf16[1,128,512]{2,1,0:T(8,128)(2,1)S(1)}, bf16[1,128,512]{2,1,0:T(8,128)(2,1)S(1)}, u32[]{:S(2)}, u32[]{:S(2)}) collective-permute-start(bf16[1,128,512]{2,1,0:T(8,128)(2,1)S(1)} %multiply_convert_fusion), channel_id=1, source_target_pairs={{0,8},{2,10},{4,12},{6,14},{8,0},{10,2},{12,4},{14,6},{1,9},{3,11}... | collective-permute-start | bytes 393224 | tf_op jit(solution)/shard_map/ppermute | solution.py:221
  29.2 13.4 %collective-permute-start.5 = (bf16[1,1280,128]{2,1,0:T(8,128)(2,1)S(1)}, bf16[1,1280,128]{2,1,0:T(8,128)(2,1)S(1)}, u32[]{:S(2)}, u32[]{:S(2)}) collective-permute-start(bf16[1,1280,128]{2,1,0:T(8,128)(2,1)S(1)} %collective-permute-done.4.refs_4_), channel_id=1, source_target_pairs={{0,16},{16,0},{1,17},{17,1},{2,18},{18,2},{3,19},{19,3},{4,20},{20... | collective-permute-start | bytes 983048 | tf_op jit(solution)/shard_map/ppermute | solution.py:221
  31.0 1.1 %copy-start.1 = (bf16[128,2560]{1,0:T(8,128)(2,1)S(1)}, bf16[128,2560]{1,0:T(8,128)(2,1)}, u32[]{:S(2)}) copy-start(bf16[128,2560]{1,0:T(8,128)(2,1)} %tokens_ref.5) | copy-start | bytes 1966084
  32.1 10.5 %copy-start.3 = (bf16[1,2560,128]{2,1,0:T(8,128)(2,1)S(1)}, bf16[1,2560,128]{2,1,0:T(8,128)(2,1)}, u32[]{:S(2)}) copy-start(bf16[1,2560,128]{2,1,0:T(8,128)(2,1)} %down_ref.1) | copy-start | bytes 1966084
  32.1 15.9 %copy-start.4 = (bf16[1,128,2048]{2,1,0:T(8,128)(2,1)S(1)}, bf16[1,128,2048]{2,1,0:T(8,128)(2,1)}, u32[]{:S(2)}) copy-start(bf16[1,128,2048]{2,1,0:T(8,128)(2,1)} %up_ref.1) | copy-start | bytes 1572868
  37.0 16.7 %copy-start.7 = (bf16[128]{0:T(256)(128)(2,1)S(1)}, bf16[128]{0:T(256)(128)(2,1)}, u32[]{:S(2)}) copy-start(bf16[128]{0:T(256)(128)(2,1)} %param.15) | copy-start | bytes 772
  37.0 23.5 %copy-start.6 = (s32[128,1]{0,1:T(1,128)S(1)}, s32[128,1]{0,1:T(1,128)}, u32[]{:S(2)}) copy-start(s32[128,1]{0,1:T(1,128)} %param.9) | copy-start | bytes 1540
  41.8 11.9 %collective-permute-start.3 = (f32[128,1024]{1,0:T(8,128)S(1)}, f32[128,1024]{1,0:T(8,128)S(1)}, u32[]{:S(2)}, u32[]{:S(2)}) collective-permute-start(f32[128,1024]{1,0:T(8,128)S(1)} %base_half.3), channel_id=1, source_target_pairs={{0,1},{1,0},{2,3},{3,2},{4,5},{5,4},{6,7},{7,6},{8,9},{9,8},{10,11... | collective-permute-start | bytes 1572872 | tf_op jit(solution)/shard_map/ppermute | solution.py:221
  42.0 6.0 %collective-permute-start.8 = (bf16[1,128,512]{2,1,0:T(8,128)(2,1)S(1)}, bf16[1,128,512]{2,1,0:T(8,128)(2,1)S(1)}, u32[]{:S(2)}, u32[]{:S(2)}) collective-permute-start(bf16[1,128,512]{2,1,0:T(8,128)(2,1)S(1)} %collective-permute-done.7.refs_0_), channel_id=1, source_target_pairs={{0,16},{16,0},{1,17},{17,1},{2,18},{18,2},{3,19},{19,3},{4,20},{20... | collective-permute-start | bytes 393224 | tf_op jit(solution)/shard_map/ppermute | solution.py:221
  43.2 4.8 %collective-permute-start.6 = (f32[256,128]{1,0:T(8,128)S(1)}, f32[256,128]{1,0:T(8,128)S(1)}, u32[]{:S(2)}, u32[]{:S(2)}) collective-permute-start(f32[256,128]{1,0:T(8,128)S(1)} %down.1.low_ref), channel_id=1, source_target_pairs={{0,1},{1,0},{2,3},{3,2},{4,5},{5,4},{6,7},{7,6},{8,9},{9,8},{10,11... | collective-permute-start | bytes 393224 | tf_op jit(solution)/shard_map/ppermute | solution.py:221
  48.8 8.1 %collective-permute-start.10 = (s16[64,1152]{1,0:T(8,128)(2,1)S(1)}, s16[64,1152]{1,0:T(8,128)(2,1)S(1)}, u32[]{:S(2)}, u32[]{:S(2)}) collective-permute-start(s16[64,1152]{1,0:T(8,128)(2,1)S(1)} %get-tuple-element.33), channel_id=1, source_target_pairs={{0,4},{2,6},{4,0},{6,2},{8,12},{10,14},{12,8},{14,10},{1,5},{3,7},... | collective-permute-start | bytes 442376 | tf_op jit(solution)/shard_map/ppermute | solution.py:221
  52.2 6.9 %collective-permute-start.11 = (s16[64,1152]{1,0:T(8,128)(2,1)S(1)}, s16[64,1152]{1,0:T(8,128)(2,1)S(1)}, u32[]{:S(2)}, u32[]{:S(2)}) collective-permute-start(s16[64,1152]{1,0:T(8,128)(2,1)S(1)} %get-tuple-element.34), channel_id=1, source_target_pairs={{0,6},{2,4},{4,2},{6,0},{8,14},{10,12},{12,10},{14,8},{1,7},{3,5},... | collective-permute-start | bytes 442376 | tf_op jit(solution)/shard_map/ppermute | solution.py:221
  52.2 8.3 %collective-permute-start.9 = (s16[64,1152]{1,0:T(8,128)(2,1)S(1)}, s16[64,1152]{1,0:T(8,128)(2,1)S(1)}, u32[]{:S(2)}, u32[]{:S(2)}) collective-permute-start(s16[64,1152]{1,0:T(8,128)(2,1)S(1)} %get-tuple-element.32), channel_id=1, source_target_pairs={{0,2},{2,0},{4,6},{6,4},{8,10},{10,8},{12,14},{14,12},{1,3},{3,1},... | collective-permute-start | bytes 442376 | tf_op jit(solution)/shard_map/ppermute | solution.py:221

commit v3 on v2

--- a/solution.py
+++ b/solution.py
@@ -14,6 +14,7 @@
 LANES = 128
 
 VMEM = pl.BlockSpec(memory_space=pltpu.VMEM)
+HBM = pl.BlockSpec(memory_space=pltpu.HBM)
 SMEM = pl.BlockSpec(memory_space=pltpu.SMEM)
 
 
@@ -23,6 +24,10 @@
 
 def cost(flops, bytes_accessed):
     return pl.CostEstimate(flops=flops, bytes_accessed=bytes_accessed, transcendentals=0)
+
+
+def in_hbm(x):
+    return pltpu.with_memory_space_constraint(x, pltpu.HBM)
 
 
 def iota(shape, dim):
@@ -53,14 +58,57 @@
     return high, low
 
 
-def pick_kernel(pool, local, depth, me_ref, adapter_ref, tokens_ref, *outs):
+def prepare_kernel(
+    local, group_ref, core_ref, ranks_ref, down_ref, up_ref, down_out, up_out, up_own, sems
+):
+    down_share, up_share = down_out.shape[1], up_out.shape[2]
+    rank, columns = up_out.shape[1], up_ref.shape[2] // lax.axis_size("tp")
+    at = pl.multiple_of(group_ref[0] * down_share, down_share)
+    up_at = pl.multiple_of(core_ref[0] * columns + group_ref[0] * up_share, up_share)
+    down_copy = pltpu.make_async_copy(
+        down_ref.at[:, pl.ds(at, down_share), :], down_out, sems.at[0]
+    )
+    up_copy = pltpu.make_async_copy(
+        up_ref.at[:, :, pl.ds(up_at, up_share)], up_own, sems.at[1]
+    )
+    down_copy.start()
+    up_copy.start()
+    up_copy.wait()
+    for a in range(local):
+        used = jnp.full((rank, 1), ranks_ref[a], jnp.int32)
+        factor = jnp.where(
+            iota((rank, 1), 0) < used, jnp.float32(ALPHA) / used.astype(jnp.float32), 0.0
+        )
+        up_out[a] = (up_own[a].astype(jnp.float32) * factor).astype(jnp.bfloat16)
+    down_copy.wait()
+
+
+def pick_kernel(
+    pool, local, depth, me_ref, adapter_hbm, tokens_hbm, *refs
+):
+    outs, (adapter_ref, tokens_ref, adapter_sem, sems) = refs[:-4], refs[-4:]
     rows, width = tokens_ref.shape
+    step = width // sems.shape[0]
+    adapter_copy = pltpu.make_async_copy(adapter_hbm, adapter_ref, adapter_sem)
+    adapter_copy.start()
+    copies = [
+        pltpu.make_async_copy(
+            tokens_hbm.at[:, pl.ds(i * step, step)],
+            tokens_ref.at[:, pl.ds(i * step, step)],
+            sems.at[i],
+        )
+        for i in range(sems.shape[0])
+    ]
+    for copy in copies:
+        copy.start()
+    adapter_copy.wait()
     place = slot_places(adapter_ref[...], me_ref[0], pool, local, depth)
     size = outs[0].shape[0]
     slots = len(outs) * size
     picker = jnp.where(iota((slots, rows), 0) == place, 1.0, 0.0).astype(jnp.bfloat16)
-    step = 512
-    for at in range(0, width, step):
+    for i, copy in enumerate(copies):
+        copy.wait()
+        at = i * step
         block = jnp.dot(
             picker, tokens_ref[:, at : at + step], preferred_element_type=jnp.float32
         )
@@ -68,35 +116,41 @@
             out[:, at : at + step] = block[j * size : (j + 1) * size].astype(jnp.bfloat16)
 
 
-def base_kernel(half_ref, tokens_ref, weight_ref, out_ref):
-    @pl.when(pl.program_id(0) == 0)
-    def _():
-        out_ref[...] = jnp.zeros_like(out_ref)
-
-    out_ref[...] += jnp.dot(
-        tokens_ref[...], weight_ref[...], preferred_element_type=jnp.float32
-    )
-
-
-def base_half(tokens, weight, half, columns):
-    rows, width = tokens.shape
-    step = 512
-    return pl.pallas_call(
-        base_kernel,
-        grid_spec=pltpu.PrefetchScalarGridSpec(
-            num_scalar_prefetch=1,
-            grid=(width // step,),
-            in_specs=[
-                pl.BlockSpec((rows, step), lambda k, h: (0, k)),
-                pl.BlockSpec((step, columns), lambda k, h: (k, h[0])),
-            ],
-            out_specs=pl.BlockSpec((rows, columns), lambda k, h: (0, 0)),
-        ),
-        out_shape=jax.ShapeDtypeStruct((rows, columns), jnp.float32),
-        compiler_params=params(),
-        cost_estimate=cost(2 * rows * width * columns, 2 * width * (rows + columns)),
-        name="base_half",
-    )(half, tokens, weight)
+def base_kernel(
+    core_ref, tokens_hbm, weight_hbm, theirs_ref, mine_ref, tokens_ref, weight_ref, tokens_sem, sems
+):
+    rows, columns = mine_ref.shape
+    steps = sems.shape[1]
+    step = tokens_ref.shape[1] // steps
+    copies = []
+    for half in range(2):
+        start = (1 - core_ref[0] if half == 0 else core_ref[0]) * columns
+        start = pl.multiple_of(start, columns)
+        for k in range(steps):
+            copies.append(
+                pltpu.make_async_copy(
+                    weight_hbm.at[pl.ds(k * step, step), pl.ds(start, columns)],
+                    weight_ref.at[half, pl.ds(k * step, step), :],
+                    sems.at[half, k],
+                )
+            )
+    tokens_copy = pltpu.make_async_copy(tokens_hbm, tokens_ref, tokens_sem)
+    tokens_copy.start()
+    for copy in copies:
+        copy.start()
+    tokens_copy.wait()
+    for half, out in enumerate((theirs_ref, mine_ref)):
+        for k in range(steps):
+            copies[half * steps + k].wait()
+            term = jnp.dot(
+                tokens_ref[:, k * step : (k + 1) * step],
+                weight_ref[half, k * step : (k + 1) * step, :],
+                preferred_element_type=jnp.float32,
+            )
+            if k == 0:
+                out[...] = term
+            else:
+                out[...] += term
 
 
 def down_kernel(buffers, groups, local, depth, group_ref, down_ref, *refs):
@@ -185,8 +239,8 @@
         mean = jnp.mean(key * key, axis=1, keepdims=True)
         normed = key * lax.rsqrt(mean + NORM_EPS) * gain
         rotated = normed * cosine + pltpu.roll(normed, head // 2, 1) * sine
-        out_ref[:, at : at + head] = rotated.astype(jnp.bfloat16)
-        out_ref[:, at + head : at + 2 * head] = value.astype(jnp.bfloat16)
+        entry = jnp.stack([rotated, value], axis=1)
+        out_ref[:, at // (2 * head)] = entry.astype(jnp.bfloat16)
 
 
 def body(
@@ -227,36 +281,66 @@
     factor = mask * (f32(ALPHA) / ranks.astype(f32))[:, None]
 
     down_share = width // groups
-    down_part = lax.dynamic_slice_in_dim(adapter_down, group[0] * down_share, down_share, 1)
+    up_share = columns // groups
+    down_part, up_part = pl.pallas_call(
+        functools.partial(prepare_kernel, local),
+        in_specs=[SMEM] * 3 + [HBM] * 2,
+        out_specs=[VMEM] * 2,
+        out_shape=[
+            jax.ShapeDtypeStruct((local, down_share, rank), bf16),
+            jax.ShapeDtypeStruct((local, rank, up_share), bf16),
+        ],
+        scratch_shapes=[
+            pltpu.VMEM((local, rank, up_share), bf16),
+            pltpu.SemaphoreType.DMA((2,)),
+        ],
+        compiler_params=params(),
+        cost_estimate=cost(local * rank * up_share, 4 * local * rank * (down_share + up_share)),
+        name="prepare",
+    )(group, core, ranks, in_hbm(adapter_down), in_hbm(adapter_up))
     far_down = exchange(down_part, "pool", pool, pool // 2)
-    up_share = columns // groups
-    up_part = lax.dynamic_slice_in_dim(
-        adapter_up, core[0] * columns + group[0] * up_share, up_share, 2
-    )
-    up_part = (up_part.astype(f32) * factor[:, :, None]).astype(bf16)
     far_up = exchange(up_part, "pool", pool, pool // 2)
 
     adapter_row = row_adapters.reshape(1, rows)
+    steps = 5
+    tokens_now, _, _ = lax.optimization_barrier((tokens, down_part, up_part))
     picked = pl.pallas_call(
         functools.partial(pick_kernel, pool, local, depth),
-        in_specs=[SMEM, VMEM, VMEM],
+        in_specs=[SMEM, HBM, HBM],
         out_specs=[VMEM] * buffers,
         out_shape=[jax.ShapeDtypeStruct((size, width), bf16)] * buffers,
+        scratch_shapes=[
+            pltpu.VMEM((1, rows), jnp.int32),
+            pltpu.VMEM((rows, width), bf16),
+            pltpu.SemaphoreType.DMA,
+            pltpu.SemaphoreType.DMA((steps,)),
+        ],
         compiler_params=params(),
         cost_estimate=cost(2 * buffers * size * rows * width, 2 * (rows + buffers * size) * width),
         name="pick",
-    )(me, adapter_row, tokens)
+    )(me, in_hbm(adapter_row), in_hbm(tokens_now))
     arrived = [picked[0]] + [None] * (buffers - 1)
     for j in range(buffers - 1, 0, -1):
         arrived[j] = exchange(picked[j], "pool", pool, j)
 
+    theirs, mine = pl.pallas_call(
+        base_kernel,
+        in_specs=[SMEM, HBM, HBM],
+        out_specs=[VMEM] * 2,
+        out_shape=[jax.ShapeDtypeStruct((rows, columns), f32)] * 2,
+        scratch_shapes=[
+            pltpu.VMEM((rows, width), bf16),
+            pltpu.VMEM((2, width, columns), bf16),
+            pltpu.SemaphoreType.DMA,
+            pltpu.SemaphoreType.DMA((2, steps)),
+        ],
+        compiler_params=params(),
+        cost_estimate=cost(4 * rows * width * columns, 4 * width * columns),
+        name="base",
+    )(core, in_hbm(tokens), in_hbm(key_value_weight))
+    far_down, far_up, theirs = lax.optimization_barrier((far_down, far_up, theirs))
     far_downs = hand_round(far_down)
     far_ups = hand_round(far_up)
-
-    theirs = base_half(tokens, key_value_weight, 1 - core, columns)
-    mine = base_half(tokens, key_value_weight, core, columns)
-    other = exchange(theirs, "tp", cores, 1)
-
     half_dim = head // 2
     frequency = jnp.power(
         f32(ROPE_THETA), -jnp.arange(half_dim, dtype=f32) * (2.0 / head)
@@ -266,7 +350,10 @@
     cosine = jnp.concatenate([cosine, cosine], axis=1)
     sine = jnp.concatenate([-sine, sine], axis=1)
 
-    arrived, mine, cosine, sine = lax.optimization_barrier((arrived, mine, cosine, sine))
+    arrived, far_ups, theirs, mine, cosine, sine = lax.optimization_barrier(
+        (arrived, far_ups, theirs, mine, cosine, sine)
+    )
+    other = exchange(theirs, "tp", cores, 1)
     slots = buffers * size
     low = pl.pallas_call(
         functools.partial(down_kernel, buffers, groups, local, depth),
@@ -297,7 +384,7 @@
         functools.partial(finish_kernel, buffers, pool, local, depth),
         in_specs=[SMEM] + [VMEM] * (6 + buffers),
         out_specs=VMEM,
-        out_shape=jax.ShapeDtypeStruct((rows, columns), bf16),
+        out_shape=jax.ShapeDtypeStruct((rows, columns // (2 * head), 2, head), bf16),
         compiler_params=params(),
         cost_estimate=cost(4 * rows * slots * columns, 2 * slots * columns),
         name="finish",
@@ -311,7 +398,7 @@
         key_norm_gain.astype(f32)[None, :],
         *returned,
     )
-    return out.reshape(rows, columns // (2 * head), 2, head)
+    return out
 
 
 def solution(mesh):

time: 62.6 us -> 54.1 us (0.86)
  local copies, waits for them, and re-layouts: 5.44 us -> 0.01 us
  starting transfers between devices: 15.1 us -> 13.4 us
  other arithmetic: 2.08 us -> 1.09 us
    unnamed x16 -> x8, local copies, waits for them, and re-layouts: 2.85 us -> 0.01 us
    pallas_call x2, Pallas kernels: 9.63 us -> 7.26 us  [the longest x1 6.2 us: body(): pl.pallas_call(base_kernel, in_specs=[SMEM, HBM, HBM], out_specs=[VMEM] *...]
    dynamic_slice x1 -> x0, local copies, waits for them, and re-layouts: 1.71 us -> none  [body(): lax.dynamic_slice_in_dim(adapter_down, group[0] * down_share, down_share, 1)]
    ppermute x12, starting transfers between devices: 15.1 us -> 13.4 us  [exchange(): return lax.ppermute(x, axis, [(p, p ^ j) for p in range(count)])]
    pallas_call x1, Pallas kernels: 0.59 us -> 2.17 us  [body(): pl.pallas_call(functools.partial(pick_kernel, pool, local, depth), in_spe...]
    pallas_call x1, Pallas kernels: 0.77 us -> 1.8 us  [body(): pl.pallas_call(functools.partial(finish_kernel, buffers, pool, local, dep...]
    convert_element_type x1 -> x0, other arithmetic: 0.99 us -> none  [body(): up_part = (up_part.astype(f32) * factor[:, :, None]).astype(bf16)]
    reshape x1 -> x0, local copies, waits for them, and re-layouts: 0.88 us -> none  [body(): return out.reshape(rows, columns // (2 * head), 2, head)]
  transfers between devices with their start and end apart: 12 -> 12, of which waited for: 5 -> 8; matrix products, arithmetic and copies ran while one was open for 6% -> 2% of each run, Pallas kernels for 18% -> 18%
where the time goes in v3:
time: 54.1 us; the launch traced here: 53.9 us
  waiting for transfers between devices  26 us (48%)
  starting transfers between devices  13.4 us (25%)
  Pallas kernels  12.5 us (23%)
  other arithmetic  1.09 us (2%)
  between operations  0.9 us (2%)
    ppermute x12, waiting for transfers between devices, exchange(): return lax.ppermute(x, axis, [(p, p ^ j) for p in range(count)])  26 us
    ppermute x12, starting transfers between devices, exchange(): return lax.ppermute(x, axis, [(p, p ^ j) for p in range(count)])  13.4 us
    pallas_call x1, Pallas kernels, body(): pl.pallas_call(base_kernel, in_specs=[SMEM, HBM, HBM], out_specs=[VMEM] *...  6.2 us
    pallas_call x1, Pallas kernels, body(): pl.pallas_call(functools.partial(pick_kernel, pool, local, depth), in_spe...  2.17 us
    pallas_call x1, Pallas kernels, body(): pl.pallas_call(functools.partial(finish_kernel, buffers, pool, local, dep...  1.8 us
  transfers between devices with their start and end apart: 12, of which 8 were waited for; matrix products, arithmetic and copies ran while one was open for 2% of the time, Pallas kernels for 18%

profile of v3, /device:TPU:0, one launch (start us, length us, event | category | flops | bytes accessed | tf_op | source)
XLA Modules:
  0.0 53.9 jit_solution(16183268833992739766)
XLA Ops:
  0.0 0.0 copy-start
  0.0 0.0 copy-start.1
  0.0 0.0 copy-start.2
  0.0 0.0 copy-start.3
  0.8 1.1 %prepare.1 = (bf16[1,1280,128]{2,1,0:T(8,128)(2,1)S(1)}, bf16[1,128,512]{2,1,0:T(8,128)(2,1)S(1)}) custom-call(s32[1]{0:T(128)} %bitcast.2.group_ref, s32[1]{0:T(128)} %bitcast.3.core_ref, s32[1]{0:T(128)} %copy.9.ranks_ref, bf16[1,2560,128]{2,1,0:T(8,128)(2,1)} %down_ref.3, bf16[1,128,2048]{2,1,0:T(8,128)(2,1)} %up_ref.3), custom_call_target="tpu_custom_call" | custom-call | flops 65536 | bytes 917504 | tf_op jit(solution)/shard_map/prepare/pallas_call | solution.py:285
  1.8 4.1 %collective-permute-start.3 = (bf16[1,1280,128]{2,1,0:T(8,128)(2,1)S(1)}, bf16[1,1280,128]{2,1,0:T(8,128)(2,1)S(1)}, u32[]{:S(2)}, u32[]{:S(2)}) collective-permute-start(bf16[1,1280,128]{2,1,0:T(8,128)(2,1)S(1)} %get-tuple-element.31), channel_id=1, source_target_pairs={{0,8},{2,10},{4,12},{6,14},{8,0},{10,2},{12,4},{14,6},{1,9},{3,11}... | collective-permute-start | bytes 983048 | tf_op jit(solution)/shard_map/ppermute | solution.py:275
  5.9 0.1 collective-permute-start.4
  6.0 2.2 %pick.1 = (bf16[64,2560]{1,0:T(8,128)(2,1)S(1)}, bf16[64,2560]{1,0:T(8,128)(2,1)S(1)}, bf16[64,2560]{1,0:T(8,128)(2,1)S(1)}, bf16[64,2560]{1,0:T(8,128)(2,1)S(1)}) custom-call(s32[1]{0:T(128)} %bitcast.me_ref, s32[1,128]{1,0:T(1,128)} %bitcast.10, bf16[128,2560]{1,0:T(8,128)(2,1)} %tokens_hbm.2), custom_call_target="tpu_custom_call" | custom-call | flops 167772160 | bytes 1966080 | tf_op jit(solution)/shard_map/pick/pallas_call | solution.py:307
  8.2 1.9 %collective-permute-start = (bf16[64,2560]{1,0:T(8,128)(2,1)S(1)}, bf16[64,2560]{1,0:T(8,128)(2,1)S(1)}, u32[]{:S(2)}, u32[]{:S(2)}) collective-permute-start(bf16[64,2560]{1,0:T(8,128)(2,1)S(1)} %get-tuple-element.35), channel_id=1, source_target_pairs={{0,2},{2,0},{4,6},{6,4},{8,10},{10,8},{12,14},{14,12},{1,3},{3,1},... | collective-permute-start | bytes 983048 | tf_op jit(solution)/shard_map/ppermute | solution.py:275
  10.1 1.6 %collective-permute-start.1 = (bf16[64,2560]{1,0:T(8,128)(2,1)S(1)}, bf16[64,2560]{1,0:T(8,128)(2,1)S(1)}, u32[]{:S(2)}, u32[]{:S(2)}) collective-permute-start(bf16[64,2560]{1,0:T(8,128)(2,1)S(1)} %get-tuple-element.36), channel_id=1, source_target_pairs={{0,4},{2,6},{4,0},{6,2},{8,12},{10,14},{12,8},{14,10},{1,5},{3,7},... | collective-permute-start | bytes 983048 | tf_op jit(solution)/shard_map/ppermute | solution.py:275
  11.6 0.1 collective-permute-start.2
  11.8 0.7 %convert_element_type.8 = f32[128]{0:T(128)S(1)} convert(s32[128]{0:T(128)} %param.10) | non-fusion elementwise | flops 128 | bytes 1024 | tf_op jit(solution)/shard_map/convert_element_type | solution.py:348
  12.4 6.2 %base.1 = (f32[128,1024]{1,0:T(8,128)S(1)}, f32[128,1024]{1,0:T(8,128)S(1)}) custom-call(s32[1]{0:T(128)} %bitcast.3.core_ref, bf16[128,2560]{1,0:T(8,128)(2,1)} %tokens_hbm.2, bf16[2560,2048]{1,0:T(8,128)(2,1)} %weight_hbm.1), custom_call_target="tpu_custom_call" | custom-call | flops 1342177280 | bytes 10485760 | tf_op jit(solution)/shard_map/base/pallas_call | solution.py:326
  18.6 7.8 %collective-permute-done.4.refs_0_ = bf16[1,128,512]{2,1,0:T(8,128)(2,1)S(1)} collective-permute-done((bf16[1,128,512]{2,1,0:T(8,128)(2,1)S(1)}, bf16[1,128,512]{2,1,0:T(8,128)(2,1)S(1)}, u32[]{:S(2)}, u32[]{:S(2)}) %collective-permute-start.4) | collective-permute-done | bytes 131104 | tf_op jit(solution)/shard_map/ppermute | solution.py:275
  26.4 0.0 collective-permute-done.3.refs_4_
  26.4 1.5 %collective-permute-start.5 = (bf16[1,128,512]{2,1,0:T(8,128)(2,1)S(1)}, bf16[1,128,512]{2,1,0:T(8,128)(2,1)S(1)}, u32[]{:S(2)}, u32[]{:S(2)}) collective-permute-start(bf16[1,128,512]{2,1,0:T(8,128)(2,1)S(1)} %collective-permute-done.4.refs_0_), channel_id=1, source_target_pairs={{0,16},{16,0},{1,17},{17,1},{2,18},{18,2},{3,19},{19,3},{4,20},{20... | collective-permute-start | bytes 393224 | tf_op jit(solution)/shard_map/ppermute | solution.py:275
  27.9 0.5 collective-permute-start.7
  28.4 0.3 fusion
  28.7 0.1 pad_maximum_fusion
  28.8 0.0 collective-permute-done.refs_1_
  28.9 0.5 collective-permute-done.1.refs_2_
  29.4 5.0 %collective-permute-done.2.refs_3_ = bf16[64,2560]{1,0:T(8,128)(2,1)S(1)} collective-permute-done((bf16[64,2560]{1,0:T(8,128)(2,1)S(1)}, bf16[64,2560]{1,0:T(8,128)(2,1)S(1)}, u32[]{:S(2)}, u32[]{:S(2)}) %collective-permute-start.2) | collective-permute-done | bytes 327712 | tf_op jit(solution)/shard_map/ppermute | solution.py:275
  34.4 0.0 collective-permute-done.5.refs_1_
  34.4 0.0 collective-permute-start.6
  34.4 3.7 %collective-permute-done.7.refs_5_ = bf16[1,1280,128]{2,1,0:T(8,128)(2,1)S(1)} collective-permute-done((bf16[1,1280,128]{2,1,0:T(8,128)(2,1)S(1)}, bf16[1,1280,128]{2,1,0:T(8,128)(2,1)S(1)}, u32[]{:S(2)}, u32[]{:S(2)}) %collective-permute-start.7) | collective-permute-done | bytes 327712 | tf_op jit(solution)/shard_map/ppermute | solution.py:275
  38.0 0.0 copy-done
  38.0 0.5 down.1.low_ref
  38.6 0.1 collective-permute-start.8
  38.7 1.3 %collective-permute-done.8.other_ref = f32[256,128]{1,0:T(8,128)S(1)} collective-permute-done((f32[256,128]{1,0:T(8,128)S(1)}, f32[256,128]{1,0:T(8,128)S(1)}, u32[]{:S(2)}, u32[]{:S(2)}) %collective-permute-start.8) | collective-permute-done | bytes 131104 | tf_op jit(solution)/shard_map/ppermute | solution.py:275
  40.0 0.0 copy-done.1
  40.0 0.8 %up.1 = (s16[64,1152]{1,0:T(8,128)(2,1)S(1)}, s16[64,1152]{1,0:T(8,128)(2,1)S(1)}, s16[64,1152]{1,0:T(8,128)(2,1)S(1)}, s16[64,1152]{1,0:T(8,128)(2,1)S(1)}) custom-call(s32[1]{0:T(128)} %bitcast.2.group_ref, s32[1]{0:T(128)} %bitcast.3.core_ref, f32[256,128]{1,0:T(8,128)S(1)} %down.1.low_ref, f32[256,128]{1,0:T(8,128)S(1)} %collective-permute-done.8.other_ref, ...), custom_call_target="tpu_custom_call" | custom-call | flops 268435456 | bytes 524288 | tf_op jit(solution)/shard_map/up/pallas_call | solution.py:369
  40.8 1.5 %collective-permute-start.10 = (s16[64,1152]{1,0:T(8,128)(2,1)S(1)}, s16[64,1152]{1,0:T(8,128)(2,1)S(1)}, u32[]{:S(2)}, u32[]{:S(2)}) collective-permute-start(s16[64,1152]{1,0:T(8,128)(2,1)S(1)} %get-tuple-element.55), channel_id=1, source_target_pairs={{0,4},{2,6},{4,0},{6,2},{8,12},{10,14},{12,8},{14,10},{1,5},{3,7},... | collective-permute-start | bytes 442376 | tf_op jit(solution)/shard_map/ppermute | solution.py:275
  42.3 1.3 %collective-permute-start.11 = (s16[64,1152]{1,0:T(8,128)(2,1)S(1)}, s16[64,1152]{1,0:T(8,128)(2,1)S(1)}, u32[]{:S(2)}, u32[]{:S(2)}) collective-permute-start(s16[64,1152]{1,0:T(8,128)(2,1)S(1)} %get-tuple-element.56), channel_id=1, source_target_pairs={{0,6},{2,4},{4,2},{6,0},{8,14},{10,12},{12,10},{14,8},{1,7},{3,5},... | collective-permute-start | bytes 442376 | tf_op jit(solution)/shard_map/ppermute | solution.py:275
  43.5 0.8 %collective-permute-start.9 = (s16[64,1152]{1,0:T(8,128)(2,1)S(1)}, s16[64,1152]{1,0:T(8,128)(2,1)S(1)}, u32[]{:S(2)}, u32[]{:S(2)}) collective-permute-start(s16[64,1152]{1,0:T(8,128)(2,1)S(1)} %get-tuple-element.54), channel_id=1, source_target_pairs={{0,2},{2,0},{4,6},{6,4},{8,10},{10,8},{12,14},{14,12},{1,3},{3,1},... | collective-permute-start | bytes 442376 | tf_op jit(solution)/shard_map/ppermute | solution.py:275
  44.3 0.0 copy-done.3
  44.3 3.2 %collective-permute-done.10.refs_2_ = s16[64,1152]{1,0:T(8,128)(2,1)S(1)} collective-permute-done((s16[64,1152]{1,0:T(8,128)(2,1)S(1)}, s16[64,1152]{1,0:T(8,128)(2,1)S(1)}, u32[]{:S(2)}, u32[]{:S(2)}) %collective-permute-start.10) | collective-permute-done | bytes 147488 | tf_op jit(solution)/shard_map/ppermute | solution.py:275
  47.5 3.2 %collective-permute-done.11.refs_3_ = s16[64,1152]{1,0:T(8,128)(2,1)S(1)} collective-permute-done((s16[64,1152]{1,0:T(8,128)(2,1)S(1)}, s16[64,1152]{1,0:T(8,128)(2,1)S(1)}, u32[]{:S(2)}, u32[]{:S(2)}) %collective-permute-start.11) | collective-permute-done | bytes 147488 | tf_op jit(solution)/shard_map/ppermute | solution.py:275
  50.7 1.4 %collective-permute-done.9.refs_1_ = s16[64,1152]{1,0:T(8,128)(2,1)S(1)} collective-permute-done((s16[64,1152]{1,0:T(8,128)(2,1)S(1)}, s16[64,1152]{1,0:T(8,128)(2,1)S(1)}, u32[]{:S(2)}, u32[]{:S(2)}) %collective-permute-start.9) | collective-permute-done | bytes 147488 | tf_op jit(solution)/shard_map/ppermute | solution.py:275
  52.1 0.0 collective-permute-done.6.other_ref
  52.1 0.0 copy-done.2
  52.1 1.8 %finish.1 = bf16[128,4,2,128]{3,2,1,0:T(2,128)(2,1)} custom-call(s32[1]{0:T(128)} %bitcast.me_ref, s32[1,128]{1,0:T(1,128)S(1)} %bitcast.11, f32[128,1024]{1,0:T(8,128)S(1)} %get-tuple-element.42.mine_ref, f32[128,1024]{1,0:T(8,128)S(1)} %collective-permute-done.6.other_ref, f32[128,128]{1,0:T(8,128)S(1)} %get-tuple-element.44.cos_ref, ...), custom_call_target="tpu_custom_call" | custom-call | flops 134217728 | bytes 524288 | tf_op jit(solution)/shard_map/finish/pallas_call | solution.py:383
  (3 shorter events, 0.0 us)
Async XLA Ops:
  0.0 38.0 %copy-start = (bf16[1,2560,128]{2,1,0:T(8,128)(2,1)S(1)}, bf16[1,2560,128]{2,1,0:T(8,128)(2,1)}, u32[]{:S(2)}) copy-start(bf16[1,2560,128]{2,1,0:T(8,128)(2,1)} %down_ref.3) | copy-start | bytes 1966084
  0.0 40.0 %copy-start.1 = (bf16[1,128,2048]{2,1,0:T(8,128)(2,1)S(1)}, bf16[1,128,2048]{2,1,0:T(8,128)(2,1)}, u32[]{:S(2)}) copy-start(bf16[1,128,2048]{2,1,0:T(8,128)(2,1)} %up_ref.3) | copy-start | bytes 1572868
  0.0 52.1 %copy-start.2 = (s32[128,1]{0,1:T(1,128)S(1)}, s32[128,1]{0,1:T(1,128)}, u32[]{:S(2)}) copy-start(s32[128,1]{0,1:T(1,128)} %param.9) | copy-start | bytes 1540
  0.0 44.3 %copy-start.3 = (bf16[128]{0:T(256)(128)(2,1)S(1)}, bf16[128]{0:T(256)(128)(2,1)}, u32[]{:S(2)}) copy-start(bf16[128]{0:T(256)(128)(2,1)} %param.15) | copy-start | bytes 772
  1.8 24.6 %collective-permute-start.3 = (bf16[1,1280,128]{2,1,0:T(8,128)(2,1)S(1)}, bf16[1,1280,128]{2,1,0:T(8,128)(2,1)S(1)}, u32[]{:S(2)}, u32[]{:S(2)}) collective-permute-start(bf16[1,1280,128]{2,1,0:T(8,128)(2,1)S(1)} %get-tuple-element.31), channel_id=1, source_target_pairs={{0,8},{2,10},{4,12},{6,14},{8,0},{10,2},{12,4},{14,6},{1,9},{3,11}... | collective-permute-start | bytes 983048 | tf_op jit(solution)/shard_map/ppermute | solution.py:275
  5.9 20.4 %collective-permute-start.4 = (bf16[1,128,512]{2,1,0:T(8,128)(2,1)S(1)}, bf16[1,128,512]{2,1,0:T(8,128)(2,1)S(1)}, u32[]{:S(2)}, u32[]{:S(2)}) collective-permute-start(bf16[1,128,512]{2,1,0:T(8,128)(2,1)S(1)} %get-tuple-element.32), channel_id=1, source_target_pairs={{0,8},{2,10},{4,12},{6,14},{8,0},{10,2},{12,4},{14,6},{1,9},{3,11}... | collective-permute-start | bytes 393224 | tf_op jit(solution)/shard_map/ppermute | solution.py:275
  8.2 20.6 %collective-permute-start = (bf16[64,2560]{1,0:T(8,128)(2,1)S(1)}, bf16[64,2560]{1,0:T(8,128)(2,1)S(1)}, u32[]{:S(2)}, u32[]{:S(2)}) collective-permute-start(bf16[64,2560]{1,0:T(8,128)(2,1)S(1)} %get-tuple-element.35), channel_id=1, source_target_pairs={{0,2},{2,0},{4,6},{6,4},{8,10},{10,8},{12,14},{14,12},{1,3},{3,1},... | collective-permute-start | bytes 983048 | tf_op jit(solution)/shard_map/ppermute | solution.py:275
  10.1 19.3 %collective-permute-start.1 = (bf16[64,2560]{1,0:T(8,128)(2,1)S(1)}, bf16[64,2560]{1,0:T(8,128)(2,1)S(1)}, u32[]{:S(2)}, u32[]{:S(2)}) collective-permute-start(bf16[64,2560]{1,0:T(8,128)(2,1)S(1)} %get-tuple-element.36), channel_id=1, source_target_pairs={{0,4},{2,6},{4,0},{6,2},{8,12},{10,14},{12,8},{14,10},{1,5},{3,7},... | collective-permute-start | bytes 983048 | tf_op jit(solution)/shard_map/ppermute | solution.py:275
  11.6 22.7 %collective-permute-start.2 = (bf16[64,2560]{1,0:T(8,128)(2,1)S(1)}, bf16[64,2560]{1,0:T(8,128)(2,1)S(1)}, u32[]{:S(2)}, u32[]{:S(2)}) collective-permute-start(bf16[64,2560]{1,0:T(8,128)(2,1)S(1)} %get-tuple-element.37), channel_id=1, source_target_pairs={{0,6},{2,4},{4,2},{6,0},{8,14},{10,12},{12,10},{14,8},{1,7},{3,5},... | collective-permute-start | bytes 983048 | tf_op jit(solution)/shard_map/ppermute | solution.py:275
  26.4 8.0 %collective-permute-start.5 = (bf16[1,128,512]{2,1,0:T(8,128)(2,1)S(1)}, bf16[1,128,512]{2,1,0:T(8,128)(2,1)S(1)}, u32[]{:S(2)}, u32[]{:S(2)}) collective-permute-start(bf16[1,128,512]{2,1,0:T(8,128)(2,1)S(1)} %collective-permute-done.4.refs_0_), channel_id=1, source_target_pairs={{0,16},{16,0},{1,17},{17,1},{2,18},{18,2},{3,19},{19,3},{4,20},{20... | collective-permute-start | bytes 393224 | tf_op jit(solution)/shard_map/ppermute | solution.py:275
  27.9 10.1 %collective-permute-start.7 = (bf16[1,1280,128]{2,1,0:T(8,128)(2,1)S(1)}, bf16[1,1280,128]{2,1,0:T(8,128)(2,1)S(1)}, u32[]{:S(2)}, u32[]{:S(2)}) collective-permute-start(bf16[1,1280,128]{2,1,0:T(8,128)(2,1)S(1)} %collective-permute-done.3.refs_4_), channel_id=1, source_target_pairs={{0,16},{16,0},{1,17},{17,1},{2,18},{18,2},{3,19},{19,3},{4,20},{20... | collective-permute-start | bytes 983048 | tf_op jit(solution)/shard_map/ppermute | solution.py:275
  34.4 17.7 %collective-permute-start.6 = (f32[128,1024]{1,0:T(8,128)S(1)}, f32[128,1024]{1,0:T(8,128)S(1)}, u32[]{:S(2)}, u32[]{:S(2)}) collective-permute-start(f32[128,1024]{1,0:T(8,128)S(1)} %get-tuple-element.43), channel_id=1, source_target_pairs={{0,1},{1,0},{2,3},{3,2},{4,5},{5,4},{6,7},{7,6},{8,9},{9,8},{10,11... | collective-permute-start | bytes 1572872 | tf_op jit(solution)/shard_map/ppermute | solution.py:275
  38.6 1.4 %collective-permute-start.8 = (f32[256,128]{1,0:T(8,128)S(1)}, f32[256,128]{1,0:T(8,128)S(1)}, u32[]{:S(2)}, u32[]{:S(2)}) collective-permute-start(f32[256,128]{1,0:T(8,128)S(1)} %down.1.low_ref), channel_id=1, source_target_pairs={{0,1},{1,0},{2,3},{3,2},{4,5},{5,4},{6,7},{7,6},{8,9},{9,8},{10,11... | collective-permute-start | bytes 393224 | tf_op jit(solution)/shard_map/ppermute | solution.py:275
  40.8 6.8 %collective-permute-start.10 = (s16[64,1152]{1,0:T(8,128)(2,1)S(1)}, s16[64,1152]{1,0:T(8,128)(2,1)S(1)}, u32[]{:S(2)}, u32[]{:S(2)}) collective-permute-start(s16[64,1152]{1,0:T(8,128)(2,1)S(1)} %get-tuple-element.55), channel_id=1, source_target_pairs={{0,4},{2,6},{4,0},{6,2},{8,12},{10,14},{12,8},{14,10},{1,5},{3,7},... | collective-permute-start | bytes 442376 | tf_op jit(solution)/shard_map/ppermute | solution.py:275
  42.3 8.4 %collective-permute-start.11 = (s16[64,1152]{1,0:T(8,128)(2,1)S(1)}, s16[64,1152]{1,0:T(8,128)(2,1)S(1)}, u32[]{:S(2)}, u32[]{:S(2)}) collective-permute-start(s16[64,1152]{1,0:T(8,128)(2,1)S(1)} %get-tuple-element.56), channel_id=1, source_target_pairs={{0,6},{2,4},{4,2},{6,0},{8,14},{10,12},{12,10},{14,8},{1,7},{3,5},... | collective-permute-start | bytes 442376 | tf_op jit(solution)/shard_map/ppermute | solution.py:275
  43.5 8.5 %collective-permute-start.9 = (s16[64,1152]{1,0:T(8,128)(2,1)S(1)}, s16[64,1152]{1,0:T(8,128)(2,1)S(1)}, u32[]{:S(2)}, u32[]{:S(2)}) collective-permute-start(s16[64,1152]{1,0:T(8,128)(2,1)S(1)} %get-tuple-element.54), channel_id=1, source_target_pairs={{0,2},{2,0},{4,6},{6,4},{8,10},{10,8},{12,14},{14,12},{1,3},{3,1},... | collective-permute-start | bytes 442376 | tf_op jit(solution)/shard_map/ppermute | solution.py:275

commit v4 on v3

--- a/solution.py
+++ b/solution.py
@@ -52,35 +52,46 @@
     return ((buffer * 2 + far) * local + (row - holder * local)) * depth + slot
 
 
+def far_first(count):
+    return sorted(range(1, count), key=lambda j: (-bin(j).count("1"), j))
+
+
+def return_order(count):
+    order = far_first(count)
+    return order[-1:] + order[:-1]
+
+
 def halves(x):
     high = x.astype(jnp.bfloat16)
     low = (x - high.astype(jnp.float32)).astype(jnp.bfloat16)
     return high, low
 
 
-def prepare_kernel(
-    local, group_ref, core_ref, ranks_ref, down_ref, up_ref, down_out, up_out, up_own, sems
-):
-    down_share, up_share = down_out.shape[1], up_out.shape[2]
-    rank, columns = up_out.shape[1], up_ref.shape[2] // lax.axis_size("tp")
-    at = pl.multiple_of(group_ref[0] * down_share, down_share)
-    up_at = pl.multiple_of(core_ref[0] * columns + group_ref[0] * up_share, up_share)
-    down_copy = pltpu.make_async_copy(
-        down_ref.at[:, pl.ds(at, down_share), :], down_out, sems.at[0]
-    )
-    up_copy = pltpu.make_async_copy(
-        up_ref.at[:, :, pl.ds(up_at, up_share)], up_own, sems.at[1]
-    )
-    down_copy.start()
-    up_copy.start()
-    up_copy.wait()
+def down_share_kernel(group_ref, down_hbm, out_ref, sem):
+    share = out_ref.shape[1]
+    at = pl.multiple_of(group_ref[0] * share, share)
+    copy = pltpu.make_async_copy(down_hbm.at[:, pl.ds(at, share), :], out_ref, sem)
+    copy.start()
+    copy.wait()
+
+
+def up_share_kernel(cores, group_ref, core_ref, ranks_ref, up_hbm, out_ref, factor_ref, own_ref, sem):
+    local, rank, share = out_ref.shape
+    at = core_ref[0] * (up_hbm.shape[2] // cores) + group_ref[0] * share
+    copy = pltpu.make_async_copy(
+        up_hbm.at[:, :, pl.ds(pl.multiple_of(at, share), share)], own_ref, sem
+    )
+    copy.start()
+    copy.wait()
     for a in range(local):
-        used = jnp.full((rank, 1), ranks_ref[a], jnp.int32)
-        factor = jnp.where(
-            iota((rank, 1), 0) < used, jnp.float32(ALPHA) / used.astype(jnp.float32), 0.0
-        )
-        up_out[a] = (up_own[a].astype(jnp.float32) * factor).astype(jnp.bfloat16)
-    down_copy.wait()
+        used = ranks_ref[a]
+
+        def factor(shape, dim):
+            scale = jnp.float32(ALPHA) / jnp.full(shape, used, jnp.int32).astype(jnp.float32)
+            return jnp.where(iota(shape, dim) < used, scale, 0.0)
+
+        factor_ref[a : a + 1, :] = factor((1, rank), 1)
+        out_ref[a] = (own_ref[a].astype(jnp.float32) * factor((rank, 1), 0)).astype(jnp.bfloat16)
 
 
 def pick_kernel(
@@ -154,7 +165,9 @@
 
 
 def down_kernel(buffers, groups, local, depth, group_ref, down_ref, *refs):
-    ins, shares, out = refs[:buffers], refs[buffers : buffers + groups], refs[-1]
+    order = [0] + far_first(buffers)
+    ins = [refs[order.index(j)] for j in range(buffers)]
+    shares, out = refs[buffers : buffers + groups], refs[-1]
     rank = out.shape[1]
     share = shares[0].shape[1]
     total = None
@@ -215,7 +228,8 @@
 def finish_kernel(
     buffers, pool, local, depth, me_ref, adapter_ref, mine_ref, other_ref, cos_ref, sin_ref, gain_ref, *refs
 ):
-    ins, out_ref = refs[:buffers], refs[-1]
+    order = [0] + return_order(buffers)
+    ins, out_ref = [refs[order.index(j)] for j in range(buffers)], refs[-1]
     rows, columns = mine_ref.shape
     head = cos_ref.shape[1]
     place = to_column(slot_places(adapter_ref[...], me_ref[0], pool, local, depth))
@@ -277,33 +291,22 @@
     def hand_round(share):
         return [share] + [exchange(share, "groups", groups, k) for k in range(1, groups)]
 
-    mask = (jnp.arange(rank, dtype=jnp.int32)[None, :] < ranks[:, None]).astype(f32)
-    factor = mask * (f32(ALPHA) / ranks.astype(f32))[:, None]
-
     down_share = width // groups
-    up_share = columns // groups
-    down_part, up_part = pl.pallas_call(
-        functools.partial(prepare_kernel, local),
-        in_specs=[SMEM] * 3 + [HBM] * 2,
-        out_specs=[VMEM] * 2,
-        out_shape=[
-            jax.ShapeDtypeStruct((local, down_share, rank), bf16),
-            jax.ShapeDtypeStruct((local, rank, up_share), bf16),
-        ],
-        scratch_shapes=[
-            pltpu.VMEM((local, rank, up_share), bf16),
-            pltpu.SemaphoreType.DMA((2,)),
-        ],
-        compiler_params=params(),
-        cost_estimate=cost(local * rank * up_share, 4 * local * rank * (down_share + up_share)),
-        name="prepare",
-    )(group, core, ranks, in_hbm(adapter_down), in_hbm(adapter_up))
+    down_part = pl.pallas_call(
+        down_share_kernel,
+        in_specs=[SMEM, HBM],
+        out_specs=VMEM,
+        out_shape=jax.ShapeDtypeStruct((local, down_share, rank), bf16),
+        scratch_shapes=[pltpu.SemaphoreType.DMA],
+        compiler_params=params(),
+        cost_estimate=cost(0, 4 * local * rank * down_share),
+        name="down_share",
+    )(group, in_hbm(adapter_down))
     far_down = exchange(down_part, "pool", pool, pool // 2)
-    far_up = exchange(up_part, "pool", pool, pool // 2)
 
     adapter_row = row_adapters.reshape(1, rows)
     steps = 5
-    tokens_now, _, _ = lax.optimization_barrier((tokens, down_part, up_part))
+    tokens_now, _ = lax.optimization_barrier((tokens, down_part))
     picked = pl.pallas_call(
         functools.partial(pick_kernel, pool, local, depth),
         in_specs=[SMEM, HBM, HBM],
@@ -319,9 +322,28 @@
         cost_estimate=cost(2 * buffers * size * rows * width, 2 * (rows + buffers * size) * width),
         name="pick",
     )(me, in_hbm(adapter_row), in_hbm(tokens_now))
-    arrived = [picked[0]] + [None] * (buffers - 1)
-    for j in range(buffers - 1, 0, -1):
-        arrived[j] = exchange(picked[j], "pool", pool, j)
+    order = far_first(buffers)
+    arrived = [picked[0]] + [exchange(picked[j], "pool", pool, j) for j in order]
+
+    up_share = columns // groups
+    ranks_now, adapter_up_now, _ = lax.optimization_barrier((ranks, adapter_up, picked))
+    up_part, factor = pl.pallas_call(
+        functools.partial(up_share_kernel, cores),
+        in_specs=[SMEM] * 3 + [HBM],
+        out_specs=[VMEM] * 2,
+        out_shape=[
+            jax.ShapeDtypeStruct((local, rank, up_share), bf16),
+            jax.ShapeDtypeStruct((local, rank), f32),
+        ],
+        scratch_shapes=[
+            pltpu.VMEM((local, rank, up_share), bf16),
+            pltpu.SemaphoreType.DMA,
+        ],
+        compiler_params=params(),
+        cost_estimate=cost(local * rank * up_share, 4 * local * rank * up_share),
+        name="up_share",
+    )(group, core, ranks_now, in_hbm(adapter_up_now))
+    far_up = exchange(up_part, "pool", pool, pool // 2)
 
     theirs, mine = pl.pallas_call(
         base_kernel,
@@ -338,8 +360,9 @@
         cost_estimate=cost(4 * rows * width * columns, 4 * width * columns),
         name="base",
     )(core, in_hbm(tokens), in_hbm(key_value_weight))
-    far_down, far_up, theirs = lax.optimization_barrier((far_down, far_up, theirs))
+    far_down, theirs = lax.optimization_barrier((far_down, theirs))
     far_downs = hand_round(far_down)
+    far_up, _ = lax.optimization_barrier((far_up, far_down))
     far_ups = hand_round(far_up)
     half_dim = head // 2
     frequency = jnp.power(
@@ -376,9 +399,8 @@
         cost_estimate=cost(8 * local * slots * rank * columns, 2 * slots * columns),
         name="up",
     )(group, core, low, low_other, factor, adapter_up, *far_ups)
-    returned = [terms[0]] + [None] * (buffers - 1)
-    for j in range(buffers - 1, 0, -1):
-        returned[j] = exchange(terms[j], "pool", pool, j)
+    order = return_order(buffers)
+    returned = [terms[0]] + [exchange(terms[j], "pool", pool, j) for j in order]
 
     out = pl.pallas_call(
         functools.partial(finish_kernel, buffers, pool, local, depth),

time: 54.1 us -> 49.9 us (0.922)
  waiting for transfers between devices: 26 us -> 18 us
  starting transfers between devices: 13.4 us -> 15.5 us
  Pallas kernels: 12.5 us -> 14.3 us
    ppermute x12, waiting for transfers between devices: 26 us -> 18 us  [exchange(): return lax.ppermute(x, axis, [(p, p ^ j) for p in range(count)])]
    ppermute x12, starting transfers between devices: 13.4 us -> 15.5 us  [exchange(): return lax.ppermute(x, axis, [(p, p ^ j) for p in range(count)])]
    pallas_call x1 -> x2, Pallas kernels: 1.06 us -> 2.03 us  [the longest x1 1.08 us: body(): pl.pallas_call(down_share_kernel, in_specs=[SMEM, HBM], out_specs=VMEM, o...]
    pallas_call x1, Pallas kernels: 2.17 us -> 2.99 us  [body(): pl.pallas_call(functools.partial(pick_kernel, pool, local, depth), in_spe...]
  transfers between devices with their start and end apart: 12 -> 12, of which waited for: 8 -> 6; matrix products, arithmetic and copies ran while one was open for 2% -> 2% of each run, Pallas kernels for 18% -> 23%
where the time goes in v4:
time: 49.9 us; the launch traced here: 49.7 us
  waiting for transfers between devices  18 us (36%)
  starting transfers between devices  15.5 us (31%)
  Pallas kernels  14.3 us (29%)
  other arithmetic  1.08 us (2%)
  between operations  0.76 us (2%)
    ppermute x12, waiting for transfers between devices, exchange(): return lax.ppermute(x, axis, [(p, p ^ j) for p in range(count)])  18 us
    ppermute x12, starting transfers between devices, exchange(): return lax.ppermute(x, axis, [(p, p ^ j) for p in range(count)])  15.5 us
    pallas_call x1, Pallas kernels, body(): pl.pallas_call(base_kernel, in_specs=[SMEM, HBM, HBM], out_specs=[VMEM] *...  6.21 us
    pallas_call x1, Pallas kernels, body(): pl.pallas_call(functools.partial(pick_kernel, pool, local, depth), in_spe...  2.99 us
    pallas_call x1, Pallas kernels, body(): pl.pallas_call(functools.partial(finish_kernel, buffers, pool, local, dep...  1.8 us
    pallas_call x1, Pallas kernels, body(): pl.pallas_call(down_share_kernel, in_specs=[SMEM, HBM], out_specs=VMEM, o...  1.08 us
  transfers between devices with their start and end apart: 12, of which 6 were waited for; matrix products, arithmetic and copies ran while one was open for 2% of the time, Pallas kernels for 23%

profile of v4, /device:TPU:0, one launch (start us, length us, event | category | flops | bytes accessed | tf_op | source)
XLA Modules:
  0.0 49.7 jit_solution(5504893659718707167)
XLA Ops:
  0.0 0.0 copy-start
  0.0 0.0 copy-start.2
  0.0 0.0 copy-start.1
  0.0 0.0 copy-start.3
  0.0 1.1 %down_share.1 = bf16[1,1280,128]{2,1,0:T(8,128)(2,1)S(1)} custom-call(s32[1]{0:T(128)} %bitcast.2.group_ref, bf16[1,2560,128]{2,1,0:T(8,128)(2,1)} %down_ref.1), custom_call_target="tpu_custom_call" | custom-call | bytes 655360 | tf_op jit(solution)/shard_map/down_share/pallas_call | solution.py:295
  1.1 4.1 %collective-permute-start.4 = (bf16[1,1280,128]{2,1,0:T(8,128)(2,1)S(1)}, bf16[1,1280,128]{2,1,0:T(8,128)(2,1)S(1)}, u32[]{:S(2)}, u32[]{:S(2)}) collective-permute-start(bf16[1,1280,128]{2,1,0:T(8,128)(2,1)S(1)} %down_share.1), channel_id=1, source_target_pairs={{0,8},{2,10},{4,12},{6,14},{8,0},{10,2},{12,4},{14,6},{1,9},{3,11}... | collective-permute-start | bytes 983048 | tf_op jit(solution)/shard_map/ppermute | solution.py:289
  5.2 3.0 %pick.1 = (bf16[64,2560]{1,0:T(8,128)(2,1)S(1)}, bf16[64,2560]{1,0:T(8,128)(2,1)}, bf16[64,2560]{1,0:T(8,128)(2,1)S(1)}, bf16[64,2560]{1,0:T(8,128)(2,1)}) custom-call(s32[1]{0:T(128)} %bitcast.me_ref, s32[1,128]{1,0:T(1,128)} %bitcast.7, bf16[128,2560]{1,0:T(8,128)(2,1)} %tokens_hbm.2), custom_call_target="tpu_custom_call" | custom-call | flops 167772160 | bytes 1966080 | tf_op jit(solution)/shard_map/pick/pallas_call | solution.py:310
  8.2 2.6 %collective-permute-start = (bf16[64,2560]{1,0:T(8,128)(2,1)}, bf16[64,2560]{1,0:T(8,128)(2,1)S(1)}, u32[]{:S(2)}, u32[]{:S(2)}) collective-permute-start(bf16[64,2560]{1,0:T(8,128)(2,1)} %get-tuple-element.35), channel_id=1, source_target_pairs={{0,6},{2,4},{4,2},{6,0},{8,14},{10,12},{12,10},{14,8},{1,7},{3,5},... | collective-permute-start | bytes 983048 | tf_op jit(solution)/shard_map/ppermute | solution.py:289
  10.8 0.5 %collective-permute-start.1 = (bf16[64,2560]{1,0:T(8,128)(2,1)}, bf16[64,2560]{1,0:T(8,128)(2,1)S(1)}, u32[]{:S(2)}, u32[]{:S(2)}) collective-permute-start(bf16[64,2560]{1,0:T(8,128)(2,1)} %get-tuple-element.36), channel_id=1, source_target_pairs={{0,2},{2,0},{4,6},{6,4},{8,10},{10,8},{12,14},{14,12},{1,3},{3,1},... | collective-permute-start | bytes 983048 | tf_op jit(solution)/shard_map/ppermute | solution.py:289
  11.3 0.5 collective-permute-start.2
  12.4 0.9 %up_share.1 = (bf16[1,128,512]{2,1,0:T(8,128)(2,1)S(1)}, f32[1,128]{1,0:T(1,128)S(1)}) custom-call(s32[1]{0:T(128)} %bitcast.2.group_ref, s32[1]{0:T(128)} %bitcast.3.core_ref, s32[1]{0:T(128)S(6)} %copy.9.ranks_ref, bf16[1,128,2048]{2,1,0:T(8,128)(2,1)} %up_ref.1), custom_call_target="tpu_custom_call" | custom-call | flops 65536 | bytes 262144 | tf_op jit(solution)/shard_map/up_share/pallas_call | solution.py:330
  13.4 0.1 collective-permute-start.3
  13.5 0.7 %convert_element_type.4 = f32[128]{0:T(128)S(1)} convert(s32[128]{0:T(128)} %param.10) | non-fusion elementwise | flops 128 | bytes 1024 | tf_op jit(solution)/shard_map/convert_element_type | solution.py:371
  14.1 6.2 %base.1 = (f32[128,1024]{1,0:T(8,128)S(1)}, f32[128,1024]{1,0:T(8,128)S(1)}) custom-call(s32[1]{0:T(128)} %bitcast.3.core_ref, bf16[128,2560]{1,0:T(8,128)(2,1)} %tokens_hbm.2, bf16[2560,2048]{1,0:T(8,128)(2,1)} %weight_hbm.1), custom_call_target="tpu_custom_call" | custom-call | flops 1342177280 | bytes 10485760 | tf_op jit(solution)/shard_map/base/pallas_call | solution.py:348
  20.4 0.5 %collective-permute-done.4.refs_4_ = bf16[1,1280,128]{2,1,0:T(8,128)(2,1)S(1)} collective-permute-done((bf16[1,1280,128]{2,1,0:T(8,128)(2,1)S(1)}, bf16[1,1280,128]{2,1,0:T(8,128)(2,1)S(1)}, u32[]{:S(2)}, u32[]{:S(2)}) %collective-permute-start.4) | collective-permute-done | bytes 327712 | tf_op jit(solution)/shard_map/ppermute | solution.py:289
  20.9 1.8 %collective-permute-start.7 = (bf16[1,1280,128]{2,1,0:T(8,128)(2,1)S(1)}, bf16[1,1280,128]{2,1,0:T(8,128)(2,1)S(1)}, u32[]{:S(2)}, u32[]{:S(2)}) collective-permute-start(bf16[1,1280,128]{2,1,0:T(8,128)(2,1)S(1)} %collective-permute-done.4.refs_4_), channel_id=1, source_target_pairs={{0,16},{16,0},{1,17},{17,1},{2,18},{18,2},{3,19},{19,3},{4,20},{20... | collective-permute-start | bytes 983048 | tf_op jit(solution)/shard_map/ppermute | solution.py:289
  22.7 6.4 %collective-permute-done.3.refs_0_ = bf16[1,128,512]{2,1,0:T(8,128)(2,1)S(1)} collective-permute-done((bf16[1,128,512]{2,1,0:T(8,128)(2,1)S(1)}, bf16[1,128,512]{2,1,0:T(8,128)(2,1)S(1)}, u32[]{:S(2)}, u32[]{:S(2)}) %collective-permute-start.3) | collective-permute-done | bytes 131104 | tf_op jit(solution)/shard_map/ppermute | solution.py:289
  29.1 1.5 %collective-permute-start.5 = (bf16[1,128,512]{2,1,0:T(8,128)(2,1)S(1)}, bf16[1,128,512]{2,1,0:T(8,128)(2,1)S(1)}, u32[]{:S(2)}, u32[]{:S(2)}) collective-permute-start(bf16[1,128,512]{2,1,0:T(8,128)(2,1)S(1)} %collective-permute-done.3.refs_0_), channel_id=1, source_target_pairs={{0,16},{16,0},{1,17},{17,1},{2,18},{18,2},{3,19},{19,3},{4,20},{20... | collective-permute-start | bytes 393224 | tf_op jit(solution)/shard_map/ppermute | solution.py:289
  30.6 0.3 fusion
  30.9 0.1 pad_maximum_fusion
  31.0 0.0 collective-permute-done.refs_1_
  31.1 0.0 collective-permute-done.1.refs_2_
  31.1 3.2 %collective-permute-done.2.refs_3_ = bf16[64,2560]{1,0:T(8,128)(2,1)S(1)} collective-permute-done((bf16[64,2560]{1,0:T(8,128)(2,1)S(1)}, bf16[64,2560]{1,0:T(8,128)(2,1)S(1)}, u32[]{:S(2)}, u32[]{:S(2)}) %collective-permute-start.2) | collective-permute-done | bytes 327712 | tf_op jit(solution)/shard_map/ppermute | solution.py:289
  34.3 0.0 collective-permute-done.5.refs_1_
  34.3 0.0 collective-permute-start.6
  34.3 0.0 collective-permute-done.7.refs_5_
  34.3 0.0 copy-done
  34.3 0.5 %down.1.low_ref = f32[256,128]{1,0:T(8,128)S(1)} custom-call(s32[1]{0:T(128)} %bitcast.2.group_ref, bf16[1,2560,128]{2,1,0:T(8,128)(2,1)S(1)} %copy-done, bf16[64,2560]{1,0:T(8,128)(2,1)S(1)} %get-tuple-element.50.refs_0_, bf16[64,2560]{1,0:T(8,128)(2,1)S(1)} %collective-permute-done.refs_1_, bf16[64,2560]{1,0:T(8,128)(2,1)S(1)} %collective-permute-done.1.refs_2_, ...), custom_call_target="tpu_custom_call" | custom-call | flops 335544320 | bytes 1966080 | tf_op jit(solution)/shard_map/down/pallas_call | solution.py:381
  34.9 0.6 %collective-permute-start.8 = (f32[256,128]{1,0:T(8,128)S(1)}, f32[256,128]{1,0:T(8,128)S(1)}, u32[]{:S(2)}, u32[]{:S(2)}) collective-permute-start(f32[256,128]{1,0:T(8,128)S(1)} %down.1.low_ref), channel_id=1, source_target_pairs={{0,1},{1,0},{2,3},{3,2},{4,5},{5,4},{6,7},{7,6},{8,9},{9,8},{10,11... | collective-permute-start | bytes 393224 | tf_op jit(solution)/shard_map/ppermute | solution.py:289
  35.4 1.0 %collective-permute-done.8.other_ref = f32[256,128]{1,0:T(8,128)S(1)} collective-permute-done((f32[256,128]{1,0:T(8,128)S(1)}, f32[256,128]{1,0:T(8,128)S(1)}, u32[]{:S(2)}, u32[]{:S(2)}) %collective-permute-start.8) | collective-permute-done | bytes 131104 | tf_op jit(solution)/shard_map/ppermute | solution.py:289
  36.4 0.0 copy-done.1
  36.4 0.8 %up.1 = (s16[64,1152]{1,0:T(8,128)(2,1)S(1)}, s16[64,1152]{1,0:T(8,128)(2,1)S(1)}, s16[64,1152]{1,0:T(8,128)(2,1)S(1)}, s16[64,1152]{1,0:T(8,128)(2,1)S(1)}) custom-call(s32[1]{0:T(128)} %bitcast.2.group_ref, s32[1]{0:T(128)} %bitcast.3.core_ref, f32[256,128]{1,0:T(8,128)S(1)} %down.1.low_ref, f32[256,128]{1,0:T(8,128)S(1)} %collective-permute-done.8.other_ref, ...), custom_call_target="tpu_custom_call" | custom-call | flops 268435456 | bytes 524288 | tf_op jit(solution)/shard_map/up/pallas_call | solution.py:392
  37.2 3.2 %collective-permute-start.10 = (s16[64,1152]{1,0:T(8,128)(2,1)S(1)}, s16[64,1152]{1,0:T(8,128)(2,1)S(1)}, u32[]{:S(2)}, u32[]{:S(2)}) collective-permute-start(s16[64,1152]{1,0:T(8,128)(2,1)S(1)} %get-tuple-element.59), channel_id=1, source_target_pairs={{0,6},{2,4},{4,2},{6,0},{8,14},{10,12},{12,10},{14,8},{1,7},{3,5},... | collective-permute-start | bytes 442376 | tf_op jit(solution)/shard_map/ppermute | solution.py:289
  40.4 0.5 %collective-permute-start.11 = (s16[64,1152]{1,0:T(8,128)(2,1)S(1)}, s16[64,1152]{1,0:T(8,128)(2,1)S(1)}, u32[]{:S(2)}, u32[]{:S(2)}) collective-permute-start(s16[64,1152]{1,0:T(8,128)(2,1)S(1)} %get-tuple-element.60), channel_id=1, source_target_pairs={{0,2},{2,0},{4,6},{6,4},{8,10},{10,8},{12,14},{14,12},{1,3},{3,1},... | collective-permute-start | bytes 442376 | tf_op jit(solution)/shard_map/ppermute | solution.py:289
  40.9 0.1 collective-permute-start.9
  41.0 0.0 copy-done.3
  41.0 4.0 %collective-permute-done.10.refs_2_ = s16[64,1152]{1,0:T(8,128)(2,1)S(1)} collective-permute-done((s16[64,1152]{1,0:T(8,128)(2,1)S(1)}, s16[64,1152]{1,0:T(8,128)(2,1)S(1)}, u32[]{:S(2)}, u32[]{:S(2)}) %collective-permute-start.10) | collective-permute-done | bytes 147488 | tf_op jit(solution)/shard_map/ppermute | solution.py:289
  45.0 2.8 %collective-permute-done.11.refs_3_ = s16[64,1152]{1,0:T(8,128)(2,1)S(1)} collective-permute-done((s16[64,1152]{1,0:T(8,128)(2,1)S(1)}, s16[64,1152]{1,0:T(8,128)(2,1)S(1)}, u32[]{:S(2)}, u32[]{:S(2)}) %collective-permute-start.11) | collective-permute-done | bytes 147488 | tf_op jit(solution)/shard_map/ppermute | solution.py:289
  47.9 0.0 collective-permute-done.9.refs_1_
  47.9 0.0 collective-permute-done.6.other_ref
  47.9 0.0 copy-done.2
  47.9 1.8 %finish.1 = bf16[128,4,2,128]{3,2,1,0:T(2,128)(2,1)} custom-call(s32[1]{0:T(128)} %bitcast.me_ref, s32[1,128]{1,0:T(1,128)S(1)} %bitcast.8, f32[128,1024]{1,0:T(8,128)S(1)} %get-tuple-element.46.mine_ref, f32[128,1024]{1,0:T(8,128)S(1)} %collective-permute-done.6.other_ref, f32[128,128]{1,0:T(8,128)S(1)} %get-tuple-element.48.cos_ref, ...), custom_call_target="tpu_custom_call" | custom-call | flops 134217728 | bytes 524288 | tf_op jit(solution)/shard_map/finish/pallas_call | solution.py:405
  (2 shorter events, 0.0 us)
Async XLA Ops:
  0.0 34.3 %copy-start = (bf16[1,2560,128]{2,1,0:T(8,128)(2,1)S(1)}, bf16[1,2560,128]{2,1,0:T(8,128)(2,1)}, u32[]{:S(2)}) copy-start(bf16[1,2560,128]{2,1,0:T(8,128)(2,1)} %down_ref.1) | copy-start | bytes 1966084
  0.0 47.9 %copy-start.2 = (s32[128,1]{0,1:T(1,128)S(1)}, s32[128,1]{0,1:T(1,128)}, u32[]{:S(2)}) copy-start(s32[128,1]{0,1:T(1,128)} %param.9) | copy-start | bytes 1540
  0.0 36.4 %copy-start.1 = (bf16[1,128,2048]{2,1,0:T(8,128)(2,1)S(1)}, bf16[1,128,2048]{2,1,0:T(8,128)(2,1)}, u32[]{:S(2)}) copy-start(bf16[1,128,2048]{2,1,0:T(8,128)(2,1)} %up_ref.1) | copy-start | bytes 1572868
  0.0 41.0 %copy-start.3 = (bf16[128]{0:T(256)(128)(2,1)S(1)}, bf16[128]{0:T(256)(128)(2,1)}, u32[]{:S(2)}) copy-start(bf16[128]{0:T(256)(128)(2,1)} %param.15) | copy-start | bytes 772
  1.1 19.8 %collective-permute-start.4 = (bf16[1,1280,128]{2,1,0:T(8,128)(2,1)S(1)}, bf16[1,1280,128]{2,1,0:T(8,128)(2,1)S(1)}, u32[]{:S(2)}, u32[]{:S(2)}) collective-permute-start(bf16[1,1280,128]{2,1,0:T(8,128)(2,1)S(1)} %down_share.1), channel_id=1, source_target_pairs={{0,8},{2,10},{4,12},{6,14},{8,0},{10,2},{12,4},{14,6},{1,9},{3,11}... | collective-permute-start | bytes 983048 | tf_op jit(solution)/shard_map/ppermute | solution.py:289
  8.2 22.8 %collective-permute-start = (bf16[64,2560]{1,0:T(8,128)(2,1)}, bf16[64,2560]{1,0:T(8,128)(2,1)S(1)}, u32[]{:S(2)}, u32[]{:S(2)}) collective-permute-start(bf16[64,2560]{1,0:T(8,128)(2,1)} %get-tuple-element.35), channel_id=1, source_target_pairs={{0,6},{2,4},{4,2},{6,0},{8,14},{10,12},{12,10},{14,8},{1,7},{3,5},... | collective-permute-start | bytes 983048 | tf_op jit(solution)/shard_map/ppermute | solution.py:289
  10.8 20.2 %collective-permute-start.1 = (bf16[64,2560]{1,0:T(8,128)(2,1)}, bf16[64,2560]{1,0:T(8,128)(2,1)S(1)}, u32[]{:S(2)}, u32[]{:S(2)}) collective-permute-start(bf16[64,2560]{1,0:T(8,128)(2,1)} %get-tuple-element.36), channel_id=1, source_target_pairs={{0,2},{2,0},{4,6},{6,4},{8,10},{10,8},{12,14},{14,12},{1,3},{3,1},... | collective-permute-start | bytes 983048 | tf_op jit(solution)/shard_map/ppermute | solution.py:289
  11.3 23.0 %collective-permute-start.2 = (bf16[64,2560]{1,0:T(8,128)(2,1)S(1)}, bf16[64,2560]{1,0:T(8,128)(2,1)S(1)}, u32[]{:S(2)}, u32[]{:S(2)}) collective-permute-start(bf16[64,2560]{1,0:T(8,128)(2,1)S(1)} %get-tuple-element.37), channel_id=1, source_target_pairs={{0,4},{2,6},{4,0},{6,2},{8,12},{10,14},{12,8},{14,10},{1,5},{3,7},... | collective-permute-start | bytes 983048 | tf_op jit(solution)/shard_map/ppermute | solution.py:289
  13.4 15.7 %collective-permute-start.3 = (bf16[1,128,512]{2,1,0:T(8,128)(2,1)S(1)}, bf16[1,128,512]{2,1,0:T(8,128)(2,1)S(1)}, u32[]{:S(2)}, u32[]{:S(2)}) collective-permute-start(bf16[1,128,512]{2,1,0:T(8,128)(2,1)S(1)} %get-tuple-element.40), channel_id=1, source_target_pairs={{0,8},{2,10},{4,12},{6,14},{8,0},{10,2},{12,4},{14,6},{1,9},{3,11}... | collective-permute-start | bytes 393224 | tf_op jit(solution)/shard_map/ppermute | solution.py:289
  20.9 13.4 %collective-permute-start.7 = (bf16[1,1280,128]{2,1,0:T(8,128)(2,1)S(1)}, bf16[1,1280,128]{2,1,0:T(8,128)(2,1)S(1)}, u32[]{:S(2)}, u32[]{:S(2)}) collective-permute-start(bf16[1,1280,128]{2,1,0:T(8,128)(2,1)S(1)} %collective-permute-done.4.refs_4_), channel_id=1, source_target_pairs={{0,16},{16,0},{1,17},{17,1},{2,18},{18,2},{3,19},{19,3},{4,20},{20... | collective-permute-start | bytes 983048 | tf_op jit(solution)/shard_map/ppermute | solution.py:289
  29.1 5.2 %collective-permute-start.5 = (bf16[1,128,512]{2,1,0:T(8,128)(2,1)S(1)}, bf16[1,128,512]{2,1,0:T(8,128)(2,1)S(1)}, u32[]{:S(2)}, u32[]{:S(2)}) collective-permute-start(bf16[1,128,512]{2,1,0:T(8,128)(2,1)S(1)} %collective-permute-done.3.refs_0_), channel_id=1, source_target_pairs={{0,16},{16,0},{1,17},{17,1},{2,18},{18,2},{3,19},{19,3},{4,20},{20... | collective-permute-start | bytes 393224 | tf_op jit(solution)/shard_map/ppermute | solution.py:289
  34.3 13.6 %collective-permute-start.6 = (f32[128,1024]{1,0:T(8,128)S(1)}, f32[128,1024]{1,0:T(8,128)S(1)}, u32[]{:S(2)}, u32[]{:S(2)}) collective-permute-start(f32[128,1024]{1,0:T(8,128)S(1)} %get-tuple-element.47), channel_id=1, source_target_pairs={{0,1},{1,0},{2,3},{3,2},{4,5},{5,4},{6,7},{7,6},{8,9},{9,8},{10,11... | collective-permute-start | bytes 1572872 | tf_op jit(solution)/shard_map/ppermute | solution.py:289
  34.9 1.5 %collective-permute-start.8 = (f32[256,128]{1,0:T(8,128)S(1)}, f32[256,128]{1,0:T(8,128)S(1)}, u32[]{:S(2)}, u32[]{:S(2)}) collective-permute-start(f32[256,128]{1,0:T(8,128)S(1)} %down.1.low_ref), channel_id=1, source_target_pairs={{0,1},{1,0},{2,3},{3,2},{4,5},{5,4},{6,7},{7,6},{8,9},{9,8},{10,11... | collective-permute-start | bytes 393224 | tf_op jit(solution)/shard_map/ppermute | solution.py:289
  37.2 7.9 %collective-permute-start.10 = (s16[64,1152]{1,0:T(8,128)(2,1)S(1)}, s16[64,1152]{1,0:T(8,128)(2,1)S(1)}, u32[]{:S(2)}, u32[]{:S(2)}) collective-permute-start(s16[64,1152]{1,0:T(8,128)(2,1)S(1)} %get-tuple-element.59), channel_id=1, source_target_pairs={{0,6},{2,4},{4,2},{6,0},{8,14},{10,12},{12,10},{14,8},{1,7},{3,5},... | collective-permute-start | bytes 442376 | tf_op jit(solution)/shard_map/ppermute | solution.py:289
  40.4 7.5 %collective-permute-start.11 = (s16[64,1152]{1,0:T(8,128)(2,1)S(1)}, s16[64,1152]{1,0:T(8,128)(2,1)S(1)}, u32[]{:S(2)}, u32[]{:S(2)}) collective-permute-start(s16[64,1152]{1,0:T(8,128)(2,1)S(1)} %get-tuple-element.60), channel_id=1, source_target_pairs={{0,2},{2,0},{4,6},{6,4},{8,10},{10,8},{12,14},{14,12},{1,3},{3,1},... | collective-permute-start | bytes 442376 | tf_op jit(solution)/shard_map/ppermute | solution.py:289
  40.9 7.0 %collective-permute-start.9 = (s16[64,1152]{1,0:T(8,128)(2,1)S(1)}, s16[64,1152]{1,0:T(8,128)(2,1)S(1)}, u32[]{:S(2)}, u32[]{:S(2)}) collective-permute-start(s16[64,1152]{1,0:T(8,128)(2,1)S(1)} %get-tuple-element.58), channel_id=1, source_target_pairs={{0,4},{2,6},{4,0},{6,2},{8,12},{10,14},{12,8},{14,10},{1,5},{3,7},... | collective-permute-start | bytes 442376 | tf_op jit(solution)/shard_map/ppermute | solution.py:289

commit v5 on v4

--- a/solution.py
+++ b/solution.py
@@ -67,14 +67,6 @@
     return high, low
 
 
-def down_share_kernel(group_ref, down_hbm, out_ref, sem):
-    share = out_ref.shape[1]
-    at = pl.multiple_of(group_ref[0] * share, share)
-    copy = pltpu.make_async_copy(down_hbm.at[:, pl.ds(at, share), :], out_ref, sem)
-    copy.start()
-    copy.wait()
-
-
 def up_share_kernel(cores, group_ref, core_ref, ranks_ref, up_hbm, out_ref, factor_ref, own_ref, sem):
     local, rank, share = out_ref.shape
     at = core_ref[0] * (up_hbm.shape[2] // cores) + group_ref[0] * share
@@ -95,40 +87,60 @@
 
 
 def pick_kernel(
-    pool, local, depth, me_ref, adapter_hbm, tokens_hbm, *refs
+    pool, local, depth, me_ref, group_ref, adapter_hbm, tokens_hbm, down_hbm, *refs
 ):
-    outs, (adapter_ref, tokens_ref, adapter_sem, sems) = refs[:-4], refs[-4:]
+    share_ref, outs = refs[0], refs[1:-4]
+    adapter_ref, tokens_ref, share_sem, sems = refs[-4:]
     rows, width = tokens_ref.shape
-    step = width // sems.shape[0]
-    adapter_copy = pltpu.make_async_copy(adapter_hbm, adapter_ref, adapter_sem)
+    share = share_ref.shape[1]
+    parts = sems.shape[0] - 1
+    part = rows // parts
+    adapter_copy = pltpu.make_async_copy(adapter_hbm, adapter_ref, sems.at[parts])
     adapter_copy.start()
     copies = [
         pltpu.make_async_copy(
-            tokens_hbm.at[:, pl.ds(i * step, step)],
-            tokens_ref.at[:, pl.ds(i * step, step)],
+            tokens_hbm.at[pl.ds(i * part, part), :],
+            tokens_ref.at[pl.ds(i * part, part), :],
             sems.at[i],
         )
-        for i in range(sems.shape[0])
+        for i in range(parts)
     ]
     for copy in copies:
         copy.start()
+    at = pl.multiple_of(group_ref[0] * share, share)
+    share_copy = pltpu.make_async_copy(down_hbm.at[:, pl.ds(at, share), :], share_ref, share_sem)
+    share_copy.start()
     adapter_copy.wait()
     place = slot_places(adapter_ref[...], me_ref[0], pool, local, depth)
     size = outs[0].shape[0]
     slots = len(outs) * size
     picker = jnp.where(iota((slots, rows), 0) == place, 1.0, 0.0).astype(jnp.bfloat16)
-    for i, copy in enumerate(copies):
+    for copy in copies:
         copy.wait()
-        at = i * step
+    step = 512
+    for at in range(0, width, step):
         block = jnp.dot(
             picker, tokens_ref[:, at : at + step], preferred_element_type=jnp.float32
         )
         for j, out in enumerate(outs):
             out[:, at : at + step] = block[j * size : (j + 1) * size].astype(jnp.bfloat16)
+    share_copy.wait()
 
 
 def base_kernel(
-    core_ref, tokens_hbm, weight_hbm, theirs_ref, mine_ref, tokens_ref, weight_ref, tokens_sem, sems
+    core_ref,
+    tokens_hbm,
+    weight_hbm,
+    down_hbm,
+    up_hbm,
+    theirs_ref,
+    mine_ref,
+    down_ref,
+    up_ref,
+    tokens_ref,
+    weight_ref,
+    other_sems,
+    sems,
 ):
     rows, columns = mine_ref.shape
     steps = sems.shape[1]
@@ -145,9 +157,13 @@
                     sems.at[half, k],
                 )
             )
-    tokens_copy = pltpu.make_async_copy(tokens_hbm, tokens_ref, tokens_sem)
-    tokens_copy.start()
-    for copy in copies:
+    tokens_copy = pltpu.make_async_copy(tokens_hbm, tokens_ref, other_sems.at[0])
+    own = pl.multiple_of(core_ref[0] * columns, columns)
+    factor_copies = [
+        pltpu.make_async_copy(down_hbm, down_ref, other_sems.at[1]),
+        pltpu.make_async_copy(up_hbm.at[:, :, pl.ds(own, columns)], up_ref, other_sems.at[2]),
+    ]
+    for copy in [tokens_copy] + copies + factor_copies:
         copy.start()
     tokens_copy.wait()
     for half, out in enumerate((theirs_ref, mine_ref)):
@@ -162,6 +178,8 @@
                 out[...] = term
             else:
                 out[...] += term
+    for copy in factor_copies:
+        copy.wait()
 
 
 def down_kernel(buffers, groups, local, depth, group_ref, down_ref, *refs):
@@ -188,7 +206,7 @@
 
 
 def up_kernel(
-    buffers, groups, local, depth, group_ref, core_ref, low_ref, other_ref, factor_ref, up_ref, *refs
+    buffers, groups, local, depth, group_ref, low_ref, other_ref, factor_ref, up_ref, *refs
 ):
     shares, outs, term_ref = refs[:groups], refs[groups : groups + buffers], refs[-1]
     rows, rank = low_ref.shape
@@ -206,8 +224,7 @@
     )
     for k in range(groups):
         at = pl.multiple_of((group_ref[0] ^ k) * share, share)
-        own_at = pl.multiple_of(core_ref[0] * columns + at, share)
-        factors = [up_ref[a, :, pl.ds(own_at, share)] for a in range(local)]
+        factors = [up_ref[a, :, pl.ds(at, share)] for a in range(local)]
         factors += [shares[k][a] for a in range(local)]
         term = jnp.dot(
             spread, jnp.concatenate(factors, axis=0), preferred_element_type=jnp.float32
@@ -246,6 +263,7 @@
 
     scale = jnp.exp2(picked(columns, LANES)[:, :1] - 15.0)
     cosine, sine, gain = cos_ref[...], sin_ref[...], gain_ref[...]
+    entries = []
     for at in range(0, columns, 2 * head):
         projected = mine_ref[:, at : at + 2 * head] + other_ref[:, at : at + 2 * head]
         projected = projected + picked(at, 2 * head) * scale
@@ -253,8 +271,15 @@
         mean = jnp.mean(key * key, axis=1, keepdims=True)
         normed = key * lax.rsqrt(mean + NORM_EPS) * gain
         rotated = normed * cosine + pltpu.roll(normed, head // 2, 1) * sine
-        entry = jnp.stack([rotated, value], axis=1)
-        out_ref[:, at // (2 * head)] = entry.astype(jnp.bfloat16)
+        entries += [rotated.astype(jnp.bfloat16), value.astype(jnp.bfloat16)]
+    kinds, block = len(entries), 16
+    n = kinds * block
+    source = (iota((n, n), 0) % kinds) * block + iota((n, n), 0) // kinds
+    order = jnp.where(iota((n, n), 1) == source, 1.0, 0.0).astype(jnp.bfloat16)
+    for i in range(rows // block):
+        stacked = jnp.concatenate([e[i * block : (i + 1) * block] for e in entries], axis=0)
+        mixed = jnp.dot(order, stacked, preferred_element_type=jnp.float32)
+        out_ref[i * n : (i + 1) * n, :] = mixed.astype(jnp.bfloat16)
 
 
 def body(
@@ -291,37 +316,26 @@
     def hand_round(share):
         return [share] + [exchange(share, "groups", groups, k) for k in range(1, groups)]
 
+    adapter_row = row_adapters.reshape(1, rows)
     down_share = width // groups
-    down_part = pl.pallas_call(
-        down_share_kernel,
-        in_specs=[SMEM, HBM],
-        out_specs=VMEM,
-        out_shape=jax.ShapeDtypeStruct((local, down_share, rank), bf16),
-        scratch_shapes=[pltpu.SemaphoreType.DMA],
-        compiler_params=params(),
-        cost_estimate=cost(0, 4 * local * rank * down_share),
-        name="down_share",
-    )(group, in_hbm(adapter_down))
-    far_down = exchange(down_part, "pool", pool, pool // 2)
-
-    adapter_row = row_adapters.reshape(1, rows)
-    steps = 5
-    tokens_now, _ = lax.optimization_barrier((tokens, down_part))
-    picked = pl.pallas_call(
+    parts = rows // 16
+    down_part, *picked = pl.pallas_call(
         functools.partial(pick_kernel, pool, local, depth),
-        in_specs=[SMEM, HBM, HBM],
-        out_specs=[VMEM] * buffers,
-        out_shape=[jax.ShapeDtypeStruct((size, width), bf16)] * buffers,
+        in_specs=[SMEM] * 2 + [HBM] * 3,
+        out_specs=[VMEM] * (1 + buffers),
+        out_shape=[jax.ShapeDtypeStruct((local, down_share, rank), bf16)]
+        + [jax.ShapeDtypeStruct((size, width), bf16)] * buffers,
         scratch_shapes=[
             pltpu.VMEM((1, rows), jnp.int32),
             pltpu.VMEM((rows, width), bf16),
             pltpu.SemaphoreType.DMA,
-            pltpu.SemaphoreType.DMA((steps,)),
+            pltpu.SemaphoreType.DMA((parts + 1,)),
         ],
         compiler_params=params(),
         cost_estimate=cost(2 * buffers * size * rows * width, 2 * (rows + buffers * size) * width),
         name="pick",
-    )(me, in_hbm(adapter_row), in_hbm(tokens_now))
+    )(me, group, in_hbm(adapter_row), in_hbm(tokens), in_hbm(adapter_down))
+    far_down = exchange(down_part, "pool", pool, pool // 2)
     order = far_first(buffers)
     arrived = [picked[0]] + [exchange(picked[j], "pool", pool, j) for j in order]
 
@@ -345,21 +359,32 @@
     )(group, core, ranks_now, in_hbm(adapter_up_now))
     far_up = exchange(up_part, "pool", pool, pool // 2)
 
-    theirs, mine = pl.pallas_call(
+    steps = 5
+    theirs, mine, own_down, own_up = pl.pallas_call(
         base_kernel,
-        in_specs=[SMEM, HBM, HBM],
-        out_specs=[VMEM] * 2,
-        out_shape=[jax.ShapeDtypeStruct((rows, columns), f32)] * 2,
+        in_specs=[SMEM] + [HBM] * 4,
+        out_specs=[VMEM] * 4,
+        out_shape=[jax.ShapeDtypeStruct((rows, columns), f32)] * 2
+        + [
+            jax.ShapeDtypeStruct(adapter_down.shape, bf16),
+            jax.ShapeDtypeStruct((local, rank, columns), bf16),
+        ],
         scratch_shapes=[
             pltpu.VMEM((rows, width), bf16),
             pltpu.VMEM((2, width, columns), bf16),
-            pltpu.SemaphoreType.DMA,
+            pltpu.SemaphoreType.DMA((3,)),
             pltpu.SemaphoreType.DMA((2, steps)),
         ],
         compiler_params=params(),
         cost_estimate=cost(4 * rows * width * columns, 4 * width * columns),
         name="base",
-    )(core, in_hbm(tokens), in_hbm(key_value_weight))
+    )(
+        core,
+        in_hbm(tokens),
+        in_hbm(key_value_weight),
+        in_hbm(adapter_down),
+        in_hbm(adapter_up),
+    )
     far_down, theirs = lax.optimization_barrier((far_down, theirs))
     far_downs = hand_round(far_down)
     far_up, _ = lax.optimization_barrier((far_up, far_down))
@@ -373,10 +398,9 @@
     cosine = jnp.concatenate([cosine, cosine], axis=1)
     sine = jnp.concatenate([-sine, sine], axis=1)
 
-    arrived, far_ups, theirs, mine, cosine, sine = lax.optimization_barrier(
-        (arrived, far_ups, theirs, mine, cosine, sine)
-    )
-    other = exchange(theirs, "tp", cores, 1)
+    arrived, far_ups, mine, cosine, sine = lax.optimization_barrier(
+        (arrived, far_ups, mine, cosine, sine)
+    )
     slots = buffers * size
     low = pl.pallas_call(
         functools.partial(down_kernel, buffers, groups, local, depth),
@@ -386,19 +410,21 @@
         compiler_params=params(),
         cost_estimate=cost(4 * local * slots * rank * width, 2 * (slots + rank) * width),
         name="down",
-    )(group, adapter_down, *arrived, *far_downs)
+    )(group, own_down, *arrived, *far_downs)
     low_other = exchange(low, "tp", cores, 1)
 
     terms = pl.pallas_call(
         functools.partial(up_kernel, buffers, groups, local, depth),
-        in_specs=[SMEM] * 2 + [VMEM] * (4 + groups),
+        in_specs=[SMEM] + [VMEM] * (4 + groups),
         out_specs=[VMEM] * buffers,
         out_shape=[jax.ShapeDtypeStruct((size, columns + LANES), jnp.int16)] * buffers,
         scratch_shapes=[pltpu.VMEM((slots, columns), f32)],
         compiler_params=params(),
         cost_estimate=cost(8 * local * slots * rank * columns, 2 * slots * columns),
         name="up",
-    )(group, core, low, low_other, factor, adapter_up, *far_ups)
+    )(group, low, low_other, factor, own_up, *far_ups)
+    terms, theirs = lax.optimization_barrier((terms, theirs))
+    other = exchange(theirs, "tp", cores, 1)
     order = return_order(buffers)
     returned = [terms[0]] + [exchange(terms[j], "pool", pool, j) for j in order]
 
@@ -406,7 +432,7 @@
         functools.partial(finish_kernel, buffers, pool, local, depth),
         in_specs=[SMEM] + [VMEM] * (6 + buffers),
         out_specs=VMEM,
-        out_shape=jax.ShapeDtypeStruct((rows, columns // (2 * head), 2, head), bf16),
+        out_shape=jax.ShapeDtypeStruct((rows * columns // head, head), bf16),
         compiler_params=params(),
         cost_estimate=cost(4 * rows * slots * columns, 2 * slots * columns),
         name="finish",
@@ -420,7 +446,7 @@
         key_norm_gain.astype(f32)[None, :],
         *returned,
     )
-    return out
+    return out.reshape(rows, columns // (2 * head), 2, head)
 
 
 def solution(mesh):

time: 49.9 us -> 50.4 us (1.010)
  waiting for transfers between devices: 18 us -> 21.8 us
  Pallas kernels: 14.3 us -> 11.3 us
    ppermute x12, waiting for transfers between devices: 18 us -> 21.8 us  [exchange(): return lax.ppermute(x, axis, [(p, p ^ j) for p in range(count)])]
    pallas_call x2 -> x1, Pallas kernels: 7.29 us -> 5.63 us  [body(): pl.pallas_call(base_kernel, in_specs=[SMEM] + [HBM] * 4, out_specs=[VMEM]...]
    pallas_call x1, Pallas kernels: 2.99 us -> 1.78 us  [body(): pl.pallas_call(functools.partial(pick_kernel, pool, local, depth), in_spe...]
  transfers between devices with their start and end apart: 12 -> 12, of which waited for: 6 -> 6; matrix products, arithmetic and copies ran while one was open for 2% -> 2% of each run, Pallas kernels for 23% -> 13%
where the time goes in v5:
time: 50.4 us; the launch traced here: 50.3 us
  waiting for transfers between devices  21.8 us (43%)
  starting transfers between devices  15.3 us (30%)
  Pallas kernels  11.3 us (22%)
  other arithmetic  1.08 us (2%)
  between operations  0.75 us (1%)
    ppermute x12, waiting for transfers between devices, exchange(): return lax.ppermute(x, axis, [(p, p ^ j) for p in range(count)])  21.8 us
    ppermute x12, starting transfers between devices, exchange(): return lax.ppermute(x, axis, [(p, p ^ j) for p in range(count)])  15.3 us
    pallas_call x1, Pallas kernels, body(): pl.pallas_call(base_kernel, in_specs=[SMEM] + [HBM] * 4, out_specs=[VMEM]...  5.63 us
    pallas_call x1, Pallas kernels, body(): pl.pallas_call(functools.partial(pick_kernel, pool, local, depth), in_spe...  1.78 us
    pallas_call x1, Pallas kernels, body(): pl.pallas_call(functools.partial(finish_kernel, buffers, pool, local, dep...  1.7 us
  transfers between devices with their start and end apart: 12, of which 6 were waited for; matrix products, arithmetic and copies ran while one was open for 2% of the time, Pallas kernels for 13%

profile of v5, /device:TPU:0, one launch (start us, length us, event | category | flops | bytes accessed | tf_op | source)
XLA Modules:
  0.0 50.3 jit_solution(13950648403999423744)
XLA Ops:
  0.0 0.0 copy-start
  0.0 0.0 copy-start.1
  0.0 1.8 %pick.1 = (bf16[1,1280,128]{2,1,0:T(8,128)(2,1)S(1)}, bf16[64,2560]{1,0:T(8,128)(2,1)S(1)}, bf16[64,2560]{1,0:T(8,128)(2,1)S(1)}, bf16[64,2560]{1,0:T(8,128)(2,1)S(1)}, bf16[64,2560]{1,0:T(8,128)(2,1)S(1)}) custom-call(s32[1]{0:T(128)} %bitcast.me_ref, s32[1]{0:T(128)} %bitcast.2.group_ref, s32[1,128]{1,0:T(1,128)} %bitcast.8, bf16[128,2560]{1,0:T(8,128)(2,1)} %tokens_hbm.3, ...), custom_call_target="tpu_custom_call" | custom-call | flops 167772160 | bytes 1966080 | tf_op jit(solution)/shard_map/pick/pallas_call | solution.py:322
  1.8 4.1 %collective-permute-start.4 = (bf16[1,1280,128]{2,1,0:T(8,128)(2,1)S(1)}, bf16[1,1280,128]{2,1,0:T(8,128)(2,1)S(1)}, u32[]{:S(2)}, u32[]{:S(2)}) collective-permute-start(bf16[1,1280,128]{2,1,0:T(8,128)(2,1)S(1)} %get-tuple-element.46), channel_id=1, source_target_pairs={{0,8},{2,10},{4,12},{6,14},{8,0},{10,2},{12,4},{14,6},{1,9},{3,11}... | collective-permute-start | bytes 983048 | tf_op jit(solution)/shard_map/ppermute | solution.py:314
  5.9 2.5 %collective-permute-start = (bf16[64,2560]{1,0:T(8,128)(2,1)S(1)}, bf16[64,2560]{1,0:T(8,128)(2,1)S(1)}, u32[]{:S(2)}, u32[]{:S(2)}) collective-permute-start(bf16[64,2560]{1,0:T(8,128)(2,1)S(1)} %get-tuple-element.40), channel_id=1, source_target_pairs={{0,6},{2,4},{4,2},{6,0},{8,14},{10,12},{12,10},{14,8},{1,7},{3,5},... | collective-permute-start | bytes 983048 | tf_op jit(solution)/shard_map/ppermute | solution.py:314
  8.4 0.5 collective-permute-start.1
  8.9 0.5 collective-permute-start.2
  10.0 0.9 %up_share.1 = (bf16[1,128,512]{2,1,0:T(8,128)(2,1)S(1)}, f32[1,128]{1,0:T(1,128)S(1)}) custom-call(s32[1]{0:T(128)} %bitcast.2.group_ref, s32[1]{0:T(128)} %bitcast.3.core_ref, s32[1]{0:T(128)S(6)} %copy.9.ranks_ref, bf16[1,128,2048]{2,1,0:T(8,128)(2,1)} %up_hbm.2), custom_call_target="tpu_custom_call" | custom-call | flops 65536 | bytes 262144 | tf_op jit(solution)/shard_map/up_share/pallas_call | solution.py:344
  11.0 0.1 collective-permute-start.3
  11.2 0.7 %convert_element_type.4 = f32[128]{0:T(128)S(1)} convert(s32[128]{0:T(128)} %param.10) | non-fusion elementwise | flops 128 | bytes 1024 | tf_op jit(solution)/shard_map/convert_element_type | solution.py:396
  11.8 5.6 %base.1 = (f32[128,1024]{1,0:T(8,128)S(1)}, f32[128,1024]{1,0:T(8,128)S(1)}, bf16[1,2560,128]{2,1,0:T(8,128)(2,1)S(1)}, bf16[1,128,1024]{2,1,0:T(8,128)(2,1)S(1)}) custom-call(s32[1]{0:T(128)} %bitcast.3.core_ref, bf16[128,2560]{1,0:T(8,128)(2,1)} %tokens_hbm.3, bf16[2560,2048]{1,0:T(8,128)(2,1)} %weight_hbm.1, bf16[1,2560,128]{2,1,0:T(8,128)(2,1)} %down_hbm.3, ...), custom_call_target="tpu_custom_call" | custom-call | flops 1342177280 | bytes 10485760 | tf_op jit(solution)/shard_map/base/pallas_call | solution.py:363
  17.5 4.1 %collective-permute-done.4.refs_4_ = bf16[1,1280,128]{2,1,0:T(8,128)(2,1)S(1)} collective-permute-done((bf16[1,1280,128]{2,1,0:T(8,128)(2,1)S(1)}, bf16[1,1280,128]{2,1,0:T(8,128)(2,1)S(1)}, u32[]{:S(2)}, u32[]{:S(2)}) %collective-permute-start.4) | collective-permute-done | bytes 327712 | tf_op jit(solution)/shard_map/ppermute | solution.py:314
  21.6 1.8 %collective-permute-start.6 = (bf16[1,1280,128]{2,1,0:T(8,128)(2,1)S(1)}, bf16[1,1280,128]{2,1,0:T(8,128)(2,1)S(1)}, u32[]{:S(2)}, u32[]{:S(2)}) collective-permute-start(bf16[1,1280,128]{2,1,0:T(8,128)(2,1)S(1)} %collective-permute-done.4.refs_4_), channel_id=1, source_target_pairs={{0,16},{16,0},{1,17},{17,1},{2,18},{18,2},{3,19},{19,3},{4,20},{20... | collective-permute-start | bytes 983048 | tf_op jit(solution)/shard_map/ppermute | solution.py:314
  23.4 6.4 %collective-permute-done.3.refs_0_ = bf16[1,128,512]{2,1,0:T(8,128)(2,1)S(1)} collective-permute-done((bf16[1,128,512]{2,1,0:T(8,128)(2,1)S(1)}, bf16[1,128,512]{2,1,0:T(8,128)(2,1)S(1)}, u32[]{:S(2)}, u32[]{:S(2)}) %collective-permute-start.3) | collective-permute-done | bytes 131104 | tf_op jit(solution)/shard_map/ppermute | solution.py:314
  29.8 1.5 %collective-permute-start.5 = (bf16[1,128,512]{2,1,0:T(8,128)(2,1)S(1)}, bf16[1,128,512]{2,1,0:T(8,128)(2,1)S(1)}, u32[]{:S(2)}, u32[]{:S(2)}) collective-permute-start(bf16[1,128,512]{2,1,0:T(8,128)(2,1)S(1)} %collective-permute-done.3.refs_0_), channel_id=1, source_target_pairs={{0,16},{16,0},{1,17},{17,1},{2,18},{18,2},{3,19},{19,3},{4,20},{20... | collective-permute-start | bytes 393224 | tf_op jit(solution)/shard_map/ppermute | solution.py:314
  31.3 0.3 fusion
  31.6 0.1 pad_maximum_fusion
  31.7 0.0 collective-permute-done.refs_1_
  31.7 0.0 collective-permute-done.1.refs_2_
  31.7 0.0 collective-permute-done.2.refs_3_
  31.8 3.0 %collective-permute-done.5.refs_1_ = bf16[1,128,512]{2,1,0:T(8,128)(2,1)S(1)} collective-permute-done((bf16[1,128,512]{2,1,0:T(8,128)(2,1)S(1)}, bf16[1,128,512]{2,1,0:T(8,128)(2,1)S(1)}, u32[]{:S(2)}, u32[]{:S(2)}) %collective-permute-start.5) | collective-permute-done | bytes 131104 | tf_op jit(solution)/shard_map/ppermute | solution.py:314
  34.8 0.0 collective-permute-done.6.refs_5_
  34.8 0.5 %down.1.low_ref = f32[256,128]{1,0:T(8,128)S(1)} custom-call(s32[1]{0:T(128)} %bitcast.2.group_ref, bf16[1,2560,128]{2,1,0:T(8,128)(2,1)S(1)} %get-tuple-element.52.down_ref, bf16[64,2560]{1,0:T(8,128)(2,1)S(1)} %get-tuple-element.53.refs_0_, bf16[64,2560]{1,0:T(8,128)(2,1)S(1)} %collective-permute-done.refs_1_, ...), custom_call_target="tpu_custom_call" | custom-call | flops 335544320 | bytes 1966080 | tf_op jit(solution)/shard_map/down/pallas_call | solution.py:405
  35.3 0.1 collective-permute-start.7
  35.4 1.3 %collective-permute-done.7.other_ref = f32[256,128]{1,0:T(8,128)S(1)} collective-permute-done((f32[256,128]{1,0:T(8,128)S(1)}, f32[256,128]{1,0:T(8,128)S(1)}, u32[]{:S(2)}, u32[]{:S(2)}) %collective-permute-start.7) | collective-permute-done | bytes 131104 | tf_op jit(solution)/shard_map/ppermute | solution.py:314
  36.7 0.8 %up.1 = (s16[64,1152]{1,0:T(8,128)(2,1)S(1)}, s16[64,1152]{1,0:T(8,128)(2,1)S(1)}, s16[64,1152]{1,0:T(8,128)(2,1)S(1)}, s16[64,1152]{1,0:T(8,128)(2,1)S(1)}) custom-call(s32[1]{0:T(128)} %bitcast.2.group_ref, f32[256,128]{1,0:T(8,128)S(1)} %down.1.low_ref, f32[256,128]{1,0:T(8,128)S(1)} %collective-permute-done.7.other_ref, ...), custom_call_target="tpu_custom_call" | custom-call | flops 268435456 | bytes 524288 | tf_op jit(solution)/shard_map/up/pallas_call | solution.py:416
  37.5 0.2 collective-permute-start.8
  37.7 3.3 %collective-permute-start.10 = (s16[64,1152]{1,0:T(8,128)(2,1)S(1)}, s16[64,1152]{1,0:T(8,128)(2,1)S(1)}, u32[]{:S(2)}, u32[]{:S(2)}) collective-permute-start(s16[64,1152]{1,0:T(8,128)(2,1)S(1)} %get-tuple-element.71), channel_id=1, source_target_pairs={{0,6},{2,4},{4,2},{6,0},{8,14},{10,12},{12,10},{14,8},{1,7},{3,5},... | collective-permute-start | bytes 442376 | tf_op jit(solution)/shard_map/ppermute | solution.py:314
  41.0 0.5 %collective-permute-start.11 = (s16[64,1152]{1,0:T(8,128)(2,1)S(1)}, s16[64,1152]{1,0:T(8,128)(2,1)S(1)}, u32[]{:S(2)}, u32[]{:S(2)}) collective-permute-start(s16[64,1152]{1,0:T(8,128)(2,1)S(1)} %get-tuple-element.72), channel_id=1, source_target_pairs={{0,2},{2,0},{4,6},{6,4},{8,10},{10,8},{12,14},{14,12},{1,3},{3,1},... | collective-permute-start | bytes 442376 | tf_op jit(solution)/shard_map/ppermute | solution.py:314
  41.5 0.1 collective-permute-start.9
  41.6 0.0 copy-done.1
  41.6 4.1 %collective-permute-done.10.refs_2_ = s16[64,1152]{1,0:T(8,128)(2,1)S(1)} collective-permute-done((s16[64,1152]{1,0:T(8,128)(2,1)S(1)}, s16[64,1152]{1,0:T(8,128)(2,1)S(1)}, u32[]{:S(2)}, u32[]{:S(2)}) %collective-permute-start.10) | collective-permute-done | bytes 147488 | tf_op jit(solution)/shard_map/ppermute | solution.py:314
  45.7 2.8 %collective-permute-done.11.refs_3_ = s16[64,1152]{1,0:T(8,128)(2,1)S(1)} collective-permute-done((s16[64,1152]{1,0:T(8,128)(2,1)S(1)}, s16[64,1152]{1,0:T(8,128)(2,1)S(1)}, u32[]{:S(2)}, u32[]{:S(2)}) %collective-permute-start.11) | collective-permute-done | bytes 147488 | tf_op jit(solution)/shard_map/ppermute | solution.py:314
  48.6 0.0 collective-permute-done.9.refs_1_
  48.6 0.0 collective-permute-done.8.other_ref
  48.6 0.0 copy-done
  48.6 1.7 %finish.1 = bf16[1024,128]{1,0:T(8,128)(2,1)} custom-call(s32[1]{0:T(128)} %bitcast.me_ref, s32[1,128]{1,0:T(1,128)S(1)} %bitcast.9, f32[128,1024]{1,0:T(8,128)S(1)} %get-tuple-element.51.mine_ref, f32[128,1024]{1,0:T(8,128)S(1)} %collective-permute-done.8.other_ref, f32[128,128]{1,0:T(8,128)S(1)} %get-tuple-element.67.cos_ref, ...), custom_call_target="tpu_custom_call" | custom-call | flops 134217728 | bytes 524288 | tf_op jit(solution)/shard_map/finish/pallas_call | solution.py:431
  (2 shorter events, 0.0 us)
Async XLA Ops:
  0.0 48.6 %copy-start = (s32[128,1]{0,1:T(1,128)S(1)}, s32[128,1]{0,1:T(1,128)}, u32[]{:S(2)}) copy-start(s32[128,1]{0,1:T(1,128)} %param.9) | copy-start | bytes 1540
  0.0 41.6 %copy-start.1 = (bf16[128]{0:T(256)(128)(2,1)S(1)}, bf16[128]{0:T(256)(128)(2,1)}, u32[]{:S(2)}) copy-start(bf16[128]{0:T(256)(128)(2,1)} %param.15) | copy-start | bytes 772
  1.8 19.8 %collective-permute-start.4 = (bf16[1,1280,128]{2,1,0:T(8,128)(2,1)S(1)}, bf16[1,1280,128]{2,1,0:T(8,128)(2,1)S(1)}, u32[]{:S(2)}, u32[]{:S(2)}) collective-permute-start(bf16[1,1280,128]{2,1,0:T(8,128)(2,1)S(1)} %get-tuple-element.46), channel_id=1, source_target_pairs={{0,8},{2,10},{4,12},{6,14},{8,0},{10,2},{12,4},{14,6},{1,9},{3,11}... | collective-permute-start | bytes 983048 | tf_op jit(solution)/shard_map/ppermute | solution.py:314
  5.9 25.8 %collective-permute-start = (bf16[64,2560]{1,0:T(8,128)(2,1)S(1)}, bf16[64,2560]{1,0:T(8,128)(2,1)S(1)}, u32[]{:S(2)}, u32[]{:S(2)}) collective-permute-start(bf16[64,2560]{1,0:T(8,128)(2,1)S(1)} %get-tuple-element.40), channel_id=1, source_target_pairs={{0,6},{2,4},{4,2},{6,0},{8,14},{10,12},{12,10},{14,8},{1,7},{3,5},... | collective-permute-start | bytes 983048 | tf_op jit(solution)/shard_map/ppermute | solution.py:314
  8.4 23.3 %collective-permute-start.1 = (bf16[64,2560]{1,0:T(8,128)(2,1)S(1)}, bf16[64,2560]{1,0:T(8,128)(2,1)S(1)}, u32[]{:S(2)}, u32[]{:S(2)}) collective-permute-start(bf16[64,2560]{1,0:T(8,128)(2,1)S(1)} %get-tuple-element.41), channel_id=1, source_target_pairs={{0,2},{2,0},{4,6},{6,4},{8,10},{10,8},{12,14},{14,12},{1,3},{3,1},... | collective-permute-start | bytes 983048 | tf_op jit(solution)/shard_map/ppermute | solution.py:314
  8.9 22.8 %collective-permute-start.2 = (bf16[64,2560]{1,0:T(8,128)(2,1)S(1)}, bf16[64,2560]{1,0:T(8,128)(2,1)S(1)}, u32[]{:S(2)}, u32[]{:S(2)}) collective-permute-start(bf16[64,2560]{1,0:T(8,128)(2,1)S(1)} %get-tuple-element.42), channel_id=1, source_target_pairs={{0,4},{2,6},{4,0},{6,2},{8,12},{10,14},{12,8},{14,10},{1,5},{3,7},... | collective-permute-start | bytes 983048 | tf_op jit(solution)/shard_map/ppermute | solution.py:314
  11.0 18.8 %collective-permute-start.3 = (bf16[1,128,512]{2,1,0:T(8,128)(2,1)S(1)}, bf16[1,128,512]{2,1,0:T(8,128)(2,1)S(1)}, u32[]{:S(2)}, u32[]{:S(2)}) collective-permute-start(bf16[1,128,512]{2,1,0:T(8,128)(2,1)S(1)} %get-tuple-element.45), channel_id=1, source_target_pairs={{0,8},{2,10},{4,12},{6,14},{8,0},{10,2},{12,4},{14,6},{1,9},{3,11}... | collective-permute-start | bytes 393224 | tf_op jit(solution)/shard_map/ppermute | solution.py:314
  21.6 13.2 %collective-permute-start.6 = (bf16[1,1280,128]{2,1,0:T(8,128)(2,1)S(1)}, bf16[1,1280,128]{2,1,0:T(8,128)(2,1)S(1)}, u32[]{:S(2)}, u32[]{:S(2)}) collective-permute-start(bf16[1,1280,128]{2,1,0:T(8,128)(2,1)S(1)} %collective-permute-done.4.refs_4_), channel_id=1, source_target_pairs={{0,16},{16,0},{1,17},{17,1},{2,18},{18,2},{3,19},{19,3},{4,20},{20... | collective-permute-start | bytes 983048 | tf_op jit(solution)/shard_map/ppermute | solution.py:314
  29.8 5.0 %collective-permute-start.5 = (bf16[1,128,512]{2,1,0:T(8,128)(2,1)S(1)}, bf16[1,128,512]{2,1,0:T(8,128)(2,1)S(1)}, u32[]{:S(2)}, u32[]{:S(2)}) collective-permute-start(bf16[1,128,512]{2,1,0:T(8,128)(2,1)S(1)} %collective-permute-done.3.refs_0_), channel_id=1, source_target_pairs={{0,16},{16,0},{1,17},{17,1},{2,18},{18,2},{3,19},{19,3},{4,20},{20... | collective-permute-start | bytes 393224 | tf_op jit(solution)/shard_map/ppermute | solution.py:314
  35.3 1.4 %collective-permute-start.7 = (f32[256,128]{1,0:T(8,128)S(1)}, f32[256,128]{1,0:T(8,128)S(1)}, u32[]{:S(2)}, u32[]{:S(2)}) collective-permute-start(f32[256,128]{1,0:T(8,128)S(1)} %down.1.low_ref), channel_id=1, source_target_pairs={{0,1},{1,0},{2,3},{3,2},{4,5},{5,4},{6,7},{7,6},{8,9},{9,8},{10,11... | collective-permute-start | bytes 393224 | tf_op jit(solution)/shard_map/ppermute | solution.py:314
  37.5 11.1 %collective-permute-start.8 = (f32[128,1024]{1,0:T(8,128)S(1)}, f32[128,1024]{1,0:T(8,128)S(1)}, u32[]{:S(2)}, u32[]{:S(2)}) collective-permute-start(f32[128,1024]{1,0:T(8,128)S(1)} %get-tuple-element.66), channel_id=1, source_target_pairs={{0,1},{1,0},{2,3},{3,2},{4,5},{5,4},{6,7},{7,6},{8,9},{9,8},{10,11... | collective-permute-start | bytes 1572872 | tf_op jit(solution)/shard_map/ppermute | solution.py:314
  37.7 8.0 %collective-permute-start.10 = (s16[64,1152]{1,0:T(8,128)(2,1)S(1)}, s16[64,1152]{1,0:T(8,128)(2,1)S(1)}, u32[]{:S(2)}, u32[]{:S(2)}) collective-permute-start(s16[64,1152]{1,0:T(8,128)(2,1)S(1)} %get-tuple-element.71), channel_id=1, source_target_pairs={{0,6},{2,4},{4,2},{6,0},{8,14},{10,12},{12,10},{14,8},{1,7},{3,5},... | collective-permute-start | bytes 442376 | tf_op jit(solution)/shard_map/ppermute | solution.py:314
  41.0 7.5 %collective-permute-start.11 = (s16[64,1152]{1,0:T(8,128)(2,1)S(1)}, s16[64,1152]{1,0:T(8,128)(2,1)S(1)}, u32[]{:S(2)}, u32[]{:S(2)}) collective-permute-start(s16[64,1152]{1,0:T(8,128)(2,1)S(1)} %get-tuple-element.72), channel_id=1, source_target_pairs={{0,2},{2,0},{4,6},{6,4},{8,10},{10,8},{12,14},{14,12},{1,3},{3,1},... | collective-permute-start | bytes 442376 | tf_op jit(solution)/shard_map/ppermute | solution.py:314
  41.5 7.0 %collective-permute-start.9 = (s16[64,1152]{1,0:T(8,128)(2,1)S(1)}, s16[64,1152]{1,0:T(8,128)(2,1)S(1)}, u32[]{:S(2)}, u32[]{:S(2)}) collective-permute-start(s16[64,1152]{1,0:T(8,128)(2,1)S(1)} %get-tuple-element.70), channel_id=1, source_target_pairs={{0,4},{2,6},{4,0},{6,2},{8,12},{10,14},{12,8},{14,10},{1,5},{3,7},... | collective-permute-start | bytes 442376 | tf_op jit(solution)/shard_map/ppermute | solution.py:314

commit v6 on v5

--- a/solution.py
+++ b/solution.py
@@ -58,7 +58,7 @@
 
 def return_order(count):
     order = far_first(count)
-    return order[-1:] + order[:-1]
+    return order[1:] + order[:1]
 
 
 def halves(x):
@@ -67,23 +67,18 @@
     return high, low
 
 
-def up_share_kernel(cores, group_ref, core_ref, ranks_ref, up_hbm, out_ref, factor_ref, own_ref, sem):
-    local, rank, share = out_ref.shape
-    at = core_ref[0] * (up_hbm.shape[2] // cores) + group_ref[0] * share
-    copy = pltpu.make_async_copy(
-        up_hbm.at[:, :, pl.ds(pl.multiple_of(at, share), share)], own_ref, sem
-    )
+def scale_up_kernel(core_ref, ranks_ref, up_hbm, out_ref, own_ref, sem):
+    local, rank, columns = out_ref.shape
+    at = pl.multiple_of(core_ref[0] * columns, columns)
+    copy = pltpu.make_async_copy(up_hbm.at[:, :, pl.ds(at, columns)], own_ref, sem)
     copy.start()
     copy.wait()
     for a in range(local):
         used = ranks_ref[a]
 
-        def factor(shape, dim):
-            scale = jnp.float32(ALPHA) / jnp.full(shape, used, jnp.int32).astype(jnp.float32)
-            return jnp.where(iota(shape, dim) < used, scale, 0.0)
-
-        factor_ref[a : a + 1, :] = factor((1, rank), 1)
-        out_ref[a] = (own_ref[a].astype(jnp.float32) * factor((rank, 1), 0)).astype(jnp.bfloat16)
+        scale = jnp.float32(ALPHA) / jnp.full((rank, 1), used, jnp.int32).astype(jnp.float32)
+        factor = jnp.where(iota((rank, 1), 0) < used, scale, 0.0)
+        out_ref[a] = (own_ref[a].astype(jnp.float32) * factor).astype(jnp.bfloat16)
 
 
 def pick_kernel(
@@ -132,11 +127,9 @@
     tokens_hbm,
     weight_hbm,
     down_hbm,
-    up_hbm,
     theirs_ref,
     mine_ref,
     down_ref,
-    up_ref,
     tokens_ref,
     weight_ref,
     other_sems,
@@ -158,12 +151,8 @@
                 )
             )
     tokens_copy = pltpu.make_async_copy(tokens_hbm, tokens_ref, other_sems.at[0])
-    own = pl.multiple_of(core_ref[0] * columns, columns)
-    factor_copies = [
-        pltpu.make_async_copy(down_hbm, down_ref, other_sems.at[1]),
-        pltpu.make_async_copy(up_hbm.at[:, :, pl.ds(own, columns)], up_ref, other_sems.at[2]),
-    ]
-    for copy in [tokens_copy] + copies + factor_copies:
+    down_copy = pltpu.make_async_copy(down_hbm, down_ref, other_sems.at[1])
+    for copy in [tokens_copy] + copies + [down_copy]:
         copy.start()
     tokens_copy.wait()
     for half, out in enumerate((theirs_ref, mine_ref)):
@@ -178,8 +167,7 @@
                 out[...] = term
             else:
                 out[...] += term
-    for copy in factor_copies:
-        copy.wait()
+    down_copy.wait()
 
 
 def down_kernel(buffers, groups, local, depth, group_ref, down_ref, *refs):
@@ -205,48 +193,36 @@
     out[...] = low
 
 
-def up_kernel(
-    buffers, groups, local, depth, group_ref, low_ref, other_ref, factor_ref, up_ref, *refs
-):
-    shares, outs, term_ref = refs[:groups], refs[groups : groups + buffers], refs[-1]
+def up_kernel(buffers, local, depth, low_ref, other_ref, up_ref, far_ref, *outs):
     rows, rank = low_ref.shape
     size = rows // buffers
-    columns = term_ref.shape[1]
-    share = columns // groups
-    which = (iota((rows, 1), 0) // depth) % (2 * local)
-    low = low_ref[...] + other_ref[...]
-    for a in range(local):
-        low = jnp.where(which == a, low * factor_ref[a : a + 1, :], low)
-    both = jnp.concatenate(halves(low), axis=0)
-    which = jnp.concatenate([which, which], axis=0)
+    columns = up_ref.shape[2]
+    both = jnp.concatenate(halves(low_ref[...] + other_ref[...]), axis=0)
+    which = (iota((2 * rows, 1), 0) // depth) % (2 * local)
     spread = jnp.concatenate(
         [jnp.where(which == i, both, jnp.zeros_like(both)) for i in range(2 * local)], axis=1
     )
-    for k in range(groups):
-        at = pl.multiple_of((group_ref[0] ^ k) * share, share)
-        factors = [up_ref[a, :, pl.ds(at, share)] for a in range(local)]
-        factors += [shares[k][a] for a in range(local)]
-        term = jnp.dot(
-            spread, jnp.concatenate(factors, axis=0), preferred_element_type=jnp.float32
-        )
-        term_ref[:, pl.ds(at, share)] = term[:rows] + term[rows:]
+    factors = [up_ref[a] for a in range(local)] + [far_ref[a] for a in range(local)]
+    term = jnp.dot(
+        spread, jnp.concatenate(factors, axis=0), preferred_element_type=jnp.float32
+    )
+    term = term[:rows] + term[rows:]
+    top = jnp.max(jnp.abs(term), axis=1, keepdims=True)
+    exponent = jnp.ceil(jnp.log2(jnp.maximum(top, 1e-30)) + 1e-3)
+    code = jnp.clip(jnp.round(term * jnp.exp2(15.0 - exponent)), -32767.0, 32767.0)
+    code = code.astype(jnp.int32).astype(jnp.int16)
+    exponent = jnp.broadcast_to(exponent.astype(jnp.int32), (rows, LANES)).astype(jnp.int16)
     for j, out in enumerate(outs):
-        term = term_ref[j * size : (j + 1) * size, :]
-        top = jnp.max(jnp.abs(term), axis=1, keepdims=True)
-        exponent = jnp.ceil(jnp.log2(jnp.maximum(top, 1e-30)) + 1e-3)
-        code = jnp.round(term * jnp.exp2(15.0 - exponent))
-        code = jnp.clip(code, -32767.0, 32767.0)
-        out[:, :columns] = code.astype(jnp.int32).astype(jnp.int16)
-        out[:, columns:] = jnp.broadcast_to(
-            exponent.astype(jnp.int32), (size, LANES)
-        ).astype(jnp.int16)
+        out[:, :columns] = code[j * size : (j + 1) * size]
+        out[:, columns:] = exponent[j * size : (j + 1) * size]
 
 
 def finish_kernel(
     buffers, pool, local, depth, me_ref, adapter_ref, mine_ref, other_ref, cos_ref, sin_ref, gain_ref, *refs
 ):
     order = [0] + return_order(buffers)
-    ins, out_ref = [refs[order.index(j)] for j in range(buffers)], refs[-1]
+    ins = [refs[order.index(j)] for j in range(buffers)]
+    out_hbm, out_ref, sems = refs[-3:]
     rows, columns = mine_ref.shape
     head = cos_ref.shape[1]
     place = to_column(slot_places(adapter_ref[...], me_ref[0], pool, local, depth))
@@ -276,10 +252,19 @@
     n = kinds * block
     source = (iota((n, n), 0) % kinds) * block + iota((n, n), 0) // kinds
     order = jnp.where(iota((n, n), 1) == source, 1.0, 0.0).astype(jnp.bfloat16)
+    copies = []
     for i in range(rows // block):
         stacked = jnp.concatenate([e[i * block : (i + 1) * block] for e in entries], axis=0)
         mixed = jnp.dot(order, stacked, preferred_element_type=jnp.float32)
         out_ref[i * n : (i + 1) * n, :] = mixed.astype(jnp.bfloat16)
+        if i % 2:
+            done = pl.ds((i - 1) * n, 2 * n)
+            copies.append(
+                pltpu.make_async_copy(out_ref.at[done, :], out_hbm.at[done, :], sems.at[i // 2])
+            )
+            copies[-1].start()
+    for copy in copies:
+        copy.wait()
 
 
 def body(
@@ -339,56 +324,41 @@
     order = far_first(buffers)
     arrived = [picked[0]] + [exchange(picked[j], "pool", pool, j) for j in order]
 
-    up_share = columns // groups
     ranks_now, adapter_up_now, _ = lax.optimization_barrier((ranks, adapter_up, picked))
-    up_part, factor = pl.pallas_call(
-        functools.partial(up_share_kernel, cores),
-        in_specs=[SMEM] * 3 + [HBM],
-        out_specs=[VMEM] * 2,
-        out_shape=[
-            jax.ShapeDtypeStruct((local, rank, up_share), bf16),
-            jax.ShapeDtypeStruct((local, rank), f32),
-        ],
+    own_up = pl.pallas_call(
+        scale_up_kernel,
+        in_specs=[SMEM] * 2 + [HBM],
+        out_specs=VMEM,
+        out_shape=jax.ShapeDtypeStruct((local, rank, columns), bf16),
         scratch_shapes=[
-            pltpu.VMEM((local, rank, up_share), bf16),
+            pltpu.VMEM((local, rank, columns), bf16),
             pltpu.SemaphoreType.DMA,
         ],
         compiler_params=params(),
-        cost_estimate=cost(local * rank * up_share, 4 * local * rank * up_share),
-        name="up_share",
-    )(group, core, ranks_now, in_hbm(adapter_up_now))
-    far_up = exchange(up_part, "pool", pool, pool // 2)
+        cost_estimate=cost(local * rank * columns, 4 * local * rank * columns),
+        name="scale_up",
+    )(core, ranks_now, in_hbm(adapter_up_now))
+    far_up = exchange(own_up, "pool", pool, pool // 2)
 
     steps = 5
-    theirs, mine, own_down, own_up = pl.pallas_call(
+    theirs, mine, own_down = pl.pallas_call(
         base_kernel,
-        in_specs=[SMEM] + [HBM] * 4,
-        out_specs=[VMEM] * 4,
+        in_specs=[SMEM] + [HBM] * 3,
+        out_specs=[VMEM] * 3,
         out_shape=[jax.ShapeDtypeStruct((rows, columns), f32)] * 2
-        + [
-            jax.ShapeDtypeStruct(adapter_down.shape, bf16),
-            jax.ShapeDtypeStruct((local, rank, columns), bf16),
-        ],
+        + [jax.ShapeDtypeStruct(adapter_down.shape, bf16)],
         scratch_shapes=[
             pltpu.VMEM((rows, width), bf16),
             pltpu.VMEM((2, width, columns), bf16),
-            pltpu.SemaphoreType.DMA((3,)),
+            pltpu.SemaphoreType.DMA((2,)),
             pltpu.SemaphoreType.DMA((2, steps)),
         ],
         compiler_params=params(),
         cost_estimate=cost(4 * rows * width * columns, 4 * width * columns),
         name="base",
-    )(
-        core,
-        in_hbm(tokens),
-        in_hbm(key_value_weight),
-        in_hbm(adapter_down),
-        in_hbm(adapter_up),
-    )
+    )(core, in_hbm(tokens), in_hbm(key_value_weight), in_hbm(adapter_down))
     far_down, theirs = lax.optimization_barrier((far_down, theirs))
     far_downs = hand_round(far_down)
-    far_up, _ = lax.optimization_barrier((far_up, far_down))
-    far_ups = hand_round(far_up)
     half_dim = head // 2
     frequency = jnp.power(
         f32(ROPE_THETA), -jnp.arange(half_dim, dtype=f32) * (2.0 / head)
@@ -398,9 +368,7 @@
     cosine = jnp.concatenate([cosine, cosine], axis=1)
     sine = jnp.concatenate([-sine, sine], axis=1)
 
-    arrived, far_ups, mine, cosine, sine = lax.optimization_barrier(
-        (arrived, far_ups, mine, cosine, sine)
-    )
+    arrived, mine, cosine, sine = lax.optimization_barrier((arrived, mine, cosine, sine))
     slots = buffers * size
     low = pl.pallas_call(
         functools.partial(down_kernel, buffers, groups, local, depth),
@@ -414,15 +382,14 @@
     low_other = exchange(low, "tp", cores, 1)
 
     terms = pl.pallas_call(
-        functools.partial(up_kernel, buffers, groups, local, depth),
-        in_specs=[SMEM] + [VMEM] * (4 + groups),
+        functools.partial(up_kernel, buffers, local, depth),
+        in_specs=[VMEM] * 4,
         out_specs=[VMEM] * buffers,
         out_shape=[jax.ShapeDtypeStruct((size, columns + LANES), jnp.int16)] * buffers,
-        scratch_shapes=[pltpu.VMEM((slots, columns), f32)],
         compiler_params=params(),
         cost_estimate=cost(8 * local * slots * rank * columns, 2 * slots * columns),
         name="up",
-    )(group, low, low_other, factor, own_up, *far_ups)
+    )(low, low_other, own_up, far_up)
     terms, theirs = lax.optimization_barrier((terms, theirs))
     other = exchange(theirs, "tp", cores, 1)
     order = return_order(buffers)
@@ -431,8 +398,12 @@
     out = pl.pallas_call(
         functools.partial(finish_kernel, buffers, pool, local, depth),
         in_specs=[SMEM] + [VMEM] * (6 + buffers),
-        out_specs=VMEM,
+        out_specs=HBM,
         out_shape=jax.ShapeDtypeStruct((rows * columns // head, head), bf16),
+        scratch_shapes=[
+            pltpu.VMEM((rows * columns // head, head), bf16),
+            pltpu.SemaphoreType.DMA((rows // 32,)),
+        ],
         compiler_params=params(),
         cost_estimate=cost(4 * rows * slots * columns, 2 * slots * columns),
         name="finish",

time: 50.4 us -> 48.5 us (0.962)
  starting transfers between devices: 15.3 us -> 13.4 us
    ppermute x12 -> x11, starting transfers between devices: 15.3 us -> 13.4 us  [exchange(): return lax.ppermute(x, axis, [(p, p ^ j) for p in range(count)])]
    ppermute x12 -> x11, waiting for transfers between devices: 21.8 us -> 21.6 us  [exchange(): return lax.ppermute(x, axis, [(p, p ^ j) for p in range(count)])]
  transfers between devices with their start and end apart: 12 -> 11, of which waited for: 6 -> 6; matrix products, arithmetic and copies ran while one was open for 2% -> 2% of each run, Pallas kernels for 13% -> 15%
where the time goes in v6:
time: 48.5 us; the launch traced here: 48.3 us
  waiting for transfers between devices  21.6 us (45%)
  starting transfers between devices  13.4 us (28%)
  Pallas kernels  11.5 us (24%)
  other arithmetic  1.08 us (2%)
  between operations  0.74 us (2%)
    ppermute x11, waiting for transfers between devices, exchange(): return lax.ppermute(x, axis, [(p, p ^ j) for p in range(count)])  21.6 us
    ppermute x11, starting transfers between devices, exchange(): return lax.ppermute(x, axis, [(p, p ^ j) for p in range(count)])  13.4 us
    pallas_call x1, Pallas kernels, body(): pl.pallas_call(base_kernel, in_specs=[SMEM] + [HBM] * 3, out_specs=[VMEM]...  5.93 us
    pallas_call x1, Pallas kernels, body(): pl.pallas_call(functools.partial(pick_kernel, pool, local, depth), in_spe...  1.78 us
    pallas_call x1, Pallas kernels, body(): pl.pallas_call(functools.partial(finish_kernel, buffers, pool, local, dep...  1.65 us
    pallas_call x1, Pallas kernels, body(): pl.pallas_call(scale_up_kernel, in_specs=[SMEM] * 2 + [HBM], out_specs=VM...  1.01 us
  transfers between devices with their start and end apart: 11, of which 6 were waited for; matrix products, arithmetic and copies ran while one was open for 2% of the time, Pallas kernels for 15%

profile of v6, /device:TPU:0, one launch (start us, length us, event | category | flops | bytes accessed | tf_op | source)
XLA Modules:
  0.0 48.3 jit_solution(6410698305178123270)
XLA Ops:
  0.0 0.0 copy-start
  0.0 0.0 copy-start.1
  0.0 1.8 %pick.1 = (bf16[1,1280,128]{2,1,0:T(8,128)(2,1)S(1)}, bf16[64,2560]{1,0:T(8,128)(2,1)S(1)}, bf16[64,2560]{1,0:T(8,128)(2,1)S(1)}, bf16[64,2560]{1,0:T(8,128)(2,1)S(1)}, bf16[64,2560]{1,0:T(8,128)(2,1)S(1)}) custom-call(s32[1]{0:T(128)} %bitcast.me_ref, s32[1]{0:T(128)} %bitcast.2.group_ref, s32[1,128]{1,0:T(1,128)} %bitcast.8, bf16[128,2560]{1,0:T(8,128)(2,1)} %tokens_hbm.3, ...), custom_call_target="tpu_custom_call" | custom-call | flops 167772160 | bytes 1966080 | tf_op jit(solution)/shard_map/pick/pallas_call | solution.py:307
  1.8 4.1 %collective-permute-start.3 = (bf16[1,1280,128]{2,1,0:T(8,128)(2,1)S(1)}, bf16[1,1280,128]{2,1,0:T(8,128)(2,1)S(1)}, u32[]{:S(2)}, u32[]{:S(2)}) collective-permute-start(bf16[1,1280,128]{2,1,0:T(8,128)(2,1)S(1)} %get-tuple-element.44), channel_id=1, source_target_pairs={{0,8},{2,10},{4,12},{6,14},{8,0},{10,2},{12,4},{14,6},{1,9},{3,11}... | collective-permute-start | bytes 983048 | tf_op jit(solution)/shard_map/ppermute | solution.py:299
  5.9 2.5 %collective-permute-start = (bf16[64,2560]{1,0:T(8,128)(2,1)S(1)}, bf16[64,2560]{1,0:T(8,128)(2,1)S(1)}, u32[]{:S(2)}, u32[]{:S(2)}) collective-permute-start(bf16[64,2560]{1,0:T(8,128)(2,1)S(1)} %get-tuple-element.34), channel_id=1, source_target_pairs={{0,6},{2,4},{4,2},{6,0},{8,14},{10,12},{12,10},{14,8},{1,7},{3,5},... | collective-permute-start | bytes 983048 | tf_op jit(solution)/shard_map/ppermute | solution.py:299
  8.4 0.5 %collective-permute-start.1 = (bf16[64,2560]{1,0:T(8,128)(2,1)S(1)}, bf16[64,2560]{1,0:T(8,128)(2,1)S(1)}, u32[]{:S(2)}, u32[]{:S(2)}) collective-permute-start(bf16[64,2560]{1,0:T(8,128)(2,1)S(1)} %get-tuple-element.35), channel_id=1, source_target_pairs={{0,2},{2,0},{4,6},{6,4},{8,10},{10,8},{12,14},{14,12},{1,3},{3,1},... | collective-permute-start | bytes 983048 | tf_op jit(solution)/shard_map/ppermute | solution.py:299
  8.9 0.5 collective-permute-start.2
  10.0 1.0 %scale_up.1.up_ref = bf16[1,128,1024]{2,1,0:T(8,128)(2,1)S(1)} custom-call(s32[1]{0:T(128)} %bitcast.3.core_ref, s32[1]{0:T(128)S(6)} %copy.9.ranks_ref, bf16[1,128,2048]{2,1,0:T(8,128)(2,1)} %up_hbm), custom_call_target="tpu_custom_call" | custom-call | flops 131072 | bytes 524288 | tf_op jit(solution)/shard_map/scale_up/pallas_call | solution.py:328
  11.1 0.1 collective-permute-start.6
  11.2 0.7 %convert_element_type.4 = f32[128]{0:T(128)S(1)} convert(s32[128]{0:T(128)} %param.10) | non-fusion elementwise | flops 128 | bytes 1024 | tf_op jit(solution)/shard_map/convert_element_type | solution.py:366
  11.9 5.9 %base.1 = (f32[128,1024]{1,0:T(8,128)S(1)}, f32[128,1024]{1,0:T(8,128)S(1)}, bf16[1,2560,128]{2,1,0:T(8,128)(2,1)S(1)}) custom-call(s32[1]{0:T(128)} %bitcast.3.core_ref, bf16[128,2560]{1,0:T(8,128)(2,1)} %tokens_hbm.3, bf16[2560,2048]{1,0:T(8,128)(2,1)} %weight_hbm.1, bf16[1,2560,128]{2,1,0:T(8,128)(2,1)} %down_hbm.3), custom_call_target="tpu_custom_call" | custom-call | flops 1342177280 | bytes 10485760 | tf_op jit(solution)/shard_map/base/pallas_call | solution.py:344
  17.8 3.8 %collective-permute-done.3.refs_4_ = bf16[1,1280,128]{2,1,0:T(8,128)(2,1)S(1)} collective-permute-done((bf16[1,1280,128]{2,1,0:T(8,128)(2,1)S(1)}, bf16[1,1280,128]{2,1,0:T(8,128)(2,1)S(1)}, u32[]{:S(2)}, u32[]{:S(2)}) %collective-permute-start.3) | collective-permute-done | bytes 327712 | tf_op jit(solution)/shard_map/ppermute | solution.py:299
  21.6 1.8 %collective-permute-start.4 = (bf16[1,1280,128]{2,1,0:T(8,128)(2,1)S(1)}, bf16[1,1280,128]{2,1,0:T(8,128)(2,1)S(1)}, u32[]{:S(2)}, u32[]{:S(2)}) collective-permute-start(bf16[1,1280,128]{2,1,0:T(8,128)(2,1)S(1)} %collective-permute-done.3.refs_4_), channel_id=1, source_target_pairs={{0,16},{16,0},{1,17},{17,1},{2,18},{18,2},{3,19},{19,3},{4,20},{20... | collective-permute-start | bytes 983048 | tf_op jit(solution)/shard_map/ppermute | solution.py:299
  23.4 0.3 fusion
  23.7 0.1 pad_maximum_fusion
  23.8 5.2 %collective-permute-done.refs_1_ = bf16[64,2560]{1,0:T(8,128)(2,1)S(1)} collective-permute-done((bf16[64,2560]{1,0:T(8,128)(2,1)S(1)}, bf16[64,2560]{1,0:T(8,128)(2,1)S(1)}, u32[]{:S(2)}, u32[]{:S(2)}) %collective-permute-start) | collective-permute-done | bytes 327712 | tf_op jit(solution)/shard_map/ppermute | solution.py:299
  29.0 0.0 collective-permute-done.1.refs_2_
  29.0 5.6 %collective-permute-done.2.refs_3_ = bf16[64,2560]{1,0:T(8,128)(2,1)S(1)} collective-permute-done((bf16[64,2560]{1,0:T(8,128)(2,1)S(1)}, bf16[64,2560]{1,0:T(8,128)(2,1)S(1)}, u32[]{:S(2)}, u32[]{:S(2)}) %collective-permute-start.2) | collective-permute-done | bytes 327712 | tf_op jit(solution)/shard_map/ppermute | solution.py:299
  34.6 0.0 collective-permute-done.4.refs_5_
  34.6 0.5 %down.1.low_ref = f32[256,128]{1,0:T(8,128)S(1)} custom-call(s32[1]{0:T(128)} %bitcast.2.group_ref, bf16[1,2560,128]{2,1,0:T(8,128)(2,1)S(1)} %get-tuple-element.39.down_ref, bf16[64,2560]{1,0:T(8,128)(2,1)S(1)} %get-tuple-element.40.refs_0_, bf16[64,2560]{1,0:T(8,128)(2,1)S(1)} %collective-permute-done.refs_1_, ...), custom_call_target="tpu_custom_call" | custom-call | flops 335544320 | bytes 1966080 | tf_op jit(solution)/shard_map/down/pallas_call | solution.py:373
  35.1 0.1 collective-permute-start.5
  35.2 0.0 collective-permute-done.6.far_ref
  35.2 1.3 %collective-permute-done.5.other_ref = f32[256,128]{1,0:T(8,128)S(1)} collective-permute-done((f32[256,128]{1,0:T(8,128)S(1)}, f32[256,128]{1,0:T(8,128)S(1)}, u32[]{:S(2)}, u32[]{:S(2)}) %collective-permute-start.5) | collective-permute-done | bytes 131104 | tf_op jit(solution)/shard_map/ppermute | solution.py:299
  36.5 0.6 %up.1 = (s16[64,1152]{1,0:T(8,128)(2,1)S(1)}, s16[64,1152]{1,0:T(8,128)(2,1)S(1)}, s16[64,1152]{1,0:T(8,128)(2,1)S(1)}, s16[64,1152]{1,0:T(8,128)(2,1)S(1)}) custom-call(f32[256,128]{1,0:T(8,128)S(1)} %down.1.low_ref, f32[256,128]{1,0:T(8,128)S(1)} %collective-permute-done.5.other_ref, bf16[1,128,1024]{2,1,0:T(8,128)(2,1)S(1)} %scale_up.1.up_ref, ...), custom_call_target="tpu_custom_call" | custom-call | flops 268435456 | bytes 524288 | tf_op jit(solution)/shard_map/up/pallas_call | solution.py:384
  37.2 0.2 collective-permute-start.7
  37.4 0.0 collective-permute-start.10
  37.4 1.0 %collective-permute-start.8 = (s16[64,1152]{1,0:T(8,128)(2,1)S(1)}, s16[64,1152]{1,0:T(8,128)(2,1)S(1)}, u32[]{:S(2)}, u32[]{:S(2)}) collective-permute-start(s16[64,1152]{1,0:T(8,128)(2,1)S(1)} %get-tuple-element.58), channel_id=1, source_target_pairs={{0,2},{2,0},{4,6},{6,4},{8,10},{10,8},{12,14},{14,12},{1,3},{3,1},... | collective-permute-start | bytes 442376 | tf_op jit(solution)/shard_map/ppermute | solution.py:299
  38.4 2.5 %collective-permute-start.9 = (s16[64,1152]{1,0:T(8,128)(2,1)S(1)}, s16[64,1152]{1,0:T(8,128)(2,1)S(1)}, u32[]{:S(2)}, u32[]{:S(2)}) collective-permute-start(s16[64,1152]{1,0:T(8,128)(2,1)S(1)} %get-tuple-element.59), channel_id=1, source_target_pairs={{0,4},{2,6},{4,0},{6,2},{8,12},{10,14},{12,8},{14,10},{1,5},{3,7},... | collective-permute-start | bytes 442376 | tf_op jit(solution)/shard_map/ppermute | solution.py:299
  40.9 0.0 copy-done.1
  40.9 4.1 %collective-permute-done.10.refs_3_ = s16[64,1152]{1,0:T(8,128)(2,1)S(1)} collective-permute-done((s16[64,1152]{1,0:T(8,128)(2,1)S(1)}, s16[64,1152]{1,0:T(8,128)(2,1)S(1)}, u32[]{:S(2)}, u32[]{:S(2)}) %collective-permute-start.10) | collective-permute-done | bytes 147488 | tf_op jit(solution)/shard_map/ppermute | solution.py:299
  45.0 1.7 %collective-permute-done.8.refs_1_ = s16[64,1152]{1,0:T(8,128)(2,1)S(1)} collective-permute-done((s16[64,1152]{1,0:T(8,128)(2,1)S(1)}, s16[64,1152]{1,0:T(8,128)(2,1)S(1)}, u32[]{:S(2)}, u32[]{:S(2)}) %collective-permute-start.8) | collective-permute-done | bytes 147488 | tf_op jit(solution)/shard_map/ppermute | solution.py:299
  46.6 0.0 collective-permute-done.9.refs_2_
  46.7 0.0 collective-permute-done.7.other_ref
  46.7 0.0 copy-done
  46.7 1.7 %finish.1 = bf16[1024,128]{1,0:T(8,128)(2,1)} custom-call(s32[1]{0:T(128)} %bitcast.me_ref, s32[1,128]{1,0:T(1,128)S(1)} %bitcast.9, f32[128,1024]{1,0:T(8,128)S(1)} %get-tuple-element.38.mine_ref, f32[128,1024]{1,0:T(8,128)S(1)} %collective-permute-done.7.other_ref, f32[128,128]{1,0:T(8,128)S(1)} %get-tuple-element.55.cos_ref, ...), custom_call_target="tpu_custom_call" | custom-call | flops 134217728 | bytes 524288 | tf_op jit(solution)/shard_map/finish/pallas_call | solution.py:398
  (2 shorter events, 0.0 us)
Async XLA Ops:
  0.0 46.7 %copy-start = (s32[128,1]{0,1:T(1,128)S(1)}, s32[128,1]{0,1:T(1,128)}, u32[]{:S(2)}) copy-start(s32[128,1]{0,1:T(1,128)} %param.9) | copy-start | bytes 1540
  0.0 40.9 %copy-start.1 = (bf16[128]{0:T(256)(128)(2,1)S(1)}, bf16[128]{0:T(256)(128)(2,1)}, u32[]{:S(2)}) copy-start(bf16[128]{0:T(256)(128)(2,1)} %param.15) | copy-start | bytes 772
  1.8 19.8 %collective-permute-start.3 = (bf16[1,1280,128]{2,1,0:T(8,128)(2,1)S(1)}, bf16[1,1280,128]{2,1,0:T(8,128)(2,1)S(1)}, u32[]{:S(2)}, u32[]{:S(2)}) collective-permute-start(bf16[1,1280,128]{2,1,0:T(8,128)(2,1)S(1)} %get-tuple-element.44), channel_id=1, source_target_pairs={{0,8},{2,10},{4,12},{6,14},{8,0},{10,2},{12,4},{14,6},{1,9},{3,11}... | collective-permute-start | bytes 983048 | tf_op jit(solution)/shard_map/ppermute | solution.py:299
  5.9 23.1 %collective-permute-start = (bf16[64,2560]{1,0:T(8,128)(2,1)S(1)}, bf16[64,2560]{1,0:T(8,128)(2,1)S(1)}, u32[]{:S(2)}, u32[]{:S(2)}) collective-permute-start(bf16[64,2560]{1,0:T(8,128)(2,1)S(1)} %get-tuple-element.34), channel_id=1, source_target_pairs={{0,6},{2,4},{4,2},{6,0},{8,14},{10,12},{12,10},{14,8},{1,7},{3,5},... | collective-permute-start | bytes 983048 | tf_op jit(solution)/shard_map/ppermute | solution.py:299
  8.4 20.6 %collective-permute-start.1 = (bf16[64,2560]{1,0:T(8,128)(2,1)S(1)}, bf16[64,2560]{1,0:T(8,128)(2,1)S(1)}, u32[]{:S(2)}, u32[]{:S(2)}) collective-permute-start(bf16[64,2560]{1,0:T(8,128)(2,1)S(1)} %get-tuple-element.35), channel_id=1, source_target_pairs={{0,2},{2,0},{4,6},{6,4},{8,10},{10,8},{12,14},{14,12},{1,3},{3,1},... | collective-permute-start | bytes 983048 | tf_op jit(solution)/shard_map/ppermute | solution.py:299
  8.9 25.6 %collective-permute-start.2 = (bf16[64,2560]{1,0:T(8,128)(2,1)S(1)}, bf16[64,2560]{1,0:T(8,128)(2,1)S(1)}, u32[]{:S(2)}, u32[]{:S(2)}) collective-permute-start(bf16[64,2560]{1,0:T(8,128)(2,1)S(1)} %get-tuple-element.36), channel_id=1, source_target_pairs={{0,4},{2,6},{4,0},{6,2},{8,12},{10,14},{12,8},{14,10},{1,5},{3,7},... | collective-permute-start | bytes 983048 | tf_op jit(solution)/shard_map/ppermute | solution.py:299
  11.1 24.1 %collective-permute-start.6 = (bf16[1,128,1024]{2,1,0:T(8,128)(2,1)S(1)}, bf16[1,128,1024]{2,1,0:T(8,128)(2,1)S(1)}, u32[]{:S(2)}, u32[]{:S(2)}) collective-permute-start(bf16[1,128,1024]{2,1,0:T(8,128)(2,1)S(1)} %scale_up.1.up_ref), channel_id=1, source_target_pairs={{0,8},{2,10},{4,12},{6,14},{8,0},{10,2},{12,4},{14,6},{1,9},{3,11}... | collective-permute-start | bytes 786440 | tf_op jit(solution)/shard_map/ppermute | solution.py:299
  21.6 13.0 %collective-permute-start.4 = (bf16[1,1280,128]{2,1,0:T(8,128)(2,1)S(1)}, bf16[1,1280,128]{2,1,0:T(8,128)(2,1)S(1)}, u32[]{:S(2)}, u32[]{:S(2)}) collective-permute-start(bf16[1,1280,128]{2,1,0:T(8,128)(2,1)S(1)} %collective-permute-done.3.refs_4_), channel_id=1, source_target_pairs={{0,16},{16,0},{1,17},{17,1},{2,18},{18,2},{3,19},{19,3},{4,20},{20... | collective-permute-start | bytes 983048 | tf_op jit(solution)/shard_map/ppermute | solution.py:299
  35.1 1.4 %collective-permute-start.5 = (f32[256,128]{1,0:T(8,128)S(1)}, f32[256,128]{1,0:T(8,128)S(1)}, u32[]{:S(2)}, u32[]{:S(2)}) collective-permute-start(f32[256,128]{1,0:T(8,128)S(1)} %down.1.low_ref), channel_id=1, source_target_pairs={{0,1},{1,0},{2,3},{3,2},{4,5},{5,4},{6,7},{7,6},{8,9},{9,8},{10,11... | collective-permute-start | bytes 393224 | tf_op jit(solution)/shard_map/ppermute | solution.py:299
  37.2 9.5 %collective-permute-start.7 = (f32[128,1024]{1,0:T(8,128)S(1)}, f32[128,1024]{1,0:T(8,128)S(1)}, u32[]{:S(2)}, u32[]{:S(2)}) collective-permute-start(f32[128,1024]{1,0:T(8,128)S(1)} %get-tuple-element.54), channel_id=1, source_target_pairs={{0,1},{1,0},{2,3},{3,2},{4,5},{5,4},{6,7},{7,6},{8,9},{9,8},{10,11... | collective-permute-start | bytes 1572872 | tf_op jit(solution)/shard_map/ppermute | solution.py:299
  37.4 7.6 %collective-permute-start.10 = (s16[64,1152]{1,0:T(8,128)(2,1)S(1)}, s16[64,1152]{1,0:T(8,128)(2,1)S(1)}, u32[]{:S(2)}, u32[]{:S(2)}) collective-permute-start(s16[64,1152]{1,0:T(8,128)(2,1)S(1)} %get-tuple-element.60), channel_id=1, source_target_pairs={{0,6},{2,4},{4,2},{6,0},{8,14},{10,12},{12,10},{14,8},{1,7},{3,5},... | collective-permute-start | bytes 442376 | tf_op jit(solution)/shard_map/ppermute | solution.py:299
  37.4 9.3 %collective-permute-start.8 = (s16[64,1152]{1,0:T(8,128)(2,1)S(1)}, s16[64,1152]{1,0:T(8,128)(2,1)S(1)}, u32[]{:S(2)}, u32[]{:S(2)}) collective-permute-start(s16[64,1152]{1,0:T(8,128)(2,1)S(1)} %get-tuple-element.58), channel_id=1, source_target_pairs={{0,2},{2,0},{4,6},{6,4},{8,10},{10,8},{12,14},{14,12},{1,3},{3,1},... | collective-permute-start | bytes 442376 | tf_op jit(solution)/shard_map/ppermute | solution.py:299
  38.4 8.3 %collective-permute-start.9 = (s16[64,1152]{1,0:T(8,128)(2,1)S(1)}, s16[64,1152]{1,0:T(8,128)(2,1)S(1)}, u32[]{:S(2)}, u32[]{:S(2)}) collective-permute-start(s16[64,1152]{1,0:T(8,128)(2,1)S(1)} %get-tuple-element.59), channel_id=1, source_target_pairs={{0,4},{2,6},{4,0},{6,2},{8,12},{10,14},{12,8},{14,10},{1,5},{3,7},... | collective-permute-start | bytes 442376 | tf_op jit(solution)/shard_map/ppermute | solution.py:299

commit v7 on v6

--- a/solution.py
+++ b/solution.py
@@ -53,7 +53,7 @@
 
 
 def far_first(count):
-    return sorted(range(1, count), key=lambda j: (-bin(j).count("1"), j))
+    return sorted(range(1, count), key=lambda j: (-bin(j).count("1"), -j))
 
 
 def return_order(count):
@@ -368,6 +368,8 @@
     cosine = jnp.concatenate([cosine, cosine], axis=1)
     sine = jnp.concatenate([-sine, sine], axis=1)
 
+    arrived[1], theirs = lax.optimization_barrier((arrived[1], theirs))
+    other = exchange(theirs, "tp", cores, 1)
     arrived, mine, cosine, sine = lax.optimization_barrier((arrived, mine, cosine, sine))
     slots = buffers * size
     low = pl.pallas_call(
@@ -390,8 +392,6 @@
         cost_estimate=cost(8 * local * slots * rank * columns, 2 * slots * columns),
         name="up",
     )(low, low_other, own_up, far_up)
-    terms, theirs = lax.optimization_barrier((terms, theirs))
-    other = exchange(theirs, "tp", cores, 1)
     order = return_order(buffers)
     returned = [terms[0]] + [exchange(terms[j], "pool", pool, j) for j in order]
 

time: 48.5 us -> 49 us (1.010)
  waiting for transfers between devices: 21.6 us -> 22.3 us
    ppermute x11, waiting for transfers between devices: 21.6 us -> 22.3 us  [exchange(): return lax.ppermute(x, axis, [(p, p ^ j) for p in range(count)])]
  transfers between devices with their start and end apart: 11 -> 11, of which waited for: 6 -> 7; matrix products, arithmetic and copies ran while one was open for 2% -> 2% of each run, Pallas kernels for 15% -> 17%
where the time goes in v7:
time: 49 us; the launch traced here: 48.8 us
  waiting for transfers between devices  22.3 us (46%)
  starting transfers between devices  13.2 us (27%)
  Pallas kernels  11.5 us (23%)
  other arithmetic  1.08 us (2%)
  between operations  0.75 us (2%)
    ppermute x11, waiting for transfers between devices, exchange(): return lax.ppermute(x, axis, [(p, p ^ j) for p in range(count)])  22.3 us
    ppermute x11, starting transfers between devices, exchange(): return lax.ppermute(x, axis, [(p, p ^ j) for p in range(count)])  13.2 us
    pallas_call x1, Pallas kernels, body(): pl.pallas_call(base_kernel, in_specs=[SMEM] + [HBM] * 3, out_specs=[VMEM]...  5.92 us
    pallas_call x1, Pallas kernels, body(): pl.pallas_call(functools.partial(pick_kernel, pool, local, depth), in_spe...  1.78 us
    pallas_call x1, Pallas kernels, body(): pl.pallas_call(functools.partial(finish_kernel, buffers, pool, local, dep...  1.65 us
    pallas_call x1, Pallas kernels, body(): pl.pallas_call(scale_up_kernel, in_specs=[SMEM] * 2 + [HBM], out_specs=VM...  1.01 us
  transfers between devices with their start and end apart: 11, of which 7 were waited for; matrix products, arithmetic and copies ran while one was open for 2% of the time, Pallas kernels for 17%

profile of v7, /device:TPU:0, one launch (start us, length us, event | category | flops | bytes accessed | tf_op | source)
XLA Modules:
  0.0 48.8 jit_solution(8721374995922790721)
XLA Ops:
  0.0 0.0 copy-start
  0.0 0.0 copy-start.1
  0.0 1.8 %pick.1 = (bf16[1,1280,128]{2,1,0:T(8,128)(2,1)S(1)}, bf16[64,2560]{1,0:T(8,128)(2,1)S(1)}, bf16[64,2560]{1,0:T(8,128)(2,1)S(1)}, bf16[64,2560]{1,0:T(8,128)(2,1)S(1)}, bf16[64,2560]{1,0:T(8,128)(2,1)S(1)}) custom-call(s32[1]{0:T(128)} %bitcast.me_ref, s32[1]{0:T(128)} %bitcast.2.group_ref, s32[1,128]{1,0:T(1,128)} %bitcast.8, bf16[128,2560]{1,0:T(8,128)(2,1)} %tokens_hbm.3, ...), custom_call_target="tpu_custom_call" | custom-call | flops 167772160 | bytes 1966080 | tf_op jit(solution)/shard_map/pick/pallas_call | solution.py:307
  1.8 4.1 %collective-permute-start.1 = (bf16[1,1280,128]{2,1,0:T(8,128)(2,1)S(1)}, bf16[1,1280,128]{2,1,0:T(8,128)(2,1)S(1)}, u32[]{:S(2)}, u32[]{:S(2)}) collective-permute-start(bf16[1,1280,128]{2,1,0:T(8,128)(2,1)S(1)} %get-tuple-element.32), channel_id=1, source_target_pairs={{0,8},{2,10},{4,12},{6,14},{8,0},{10,2},{12,4},{14,6},{1,9},{3,11}... | collective-permute-start | bytes 983048 | tf_op jit(solution)/shard_map/ppermute | solution.py:299
  5.9 2.5 %collective-permute-start = (bf16[64,2560]{1,0:T(8,128)(2,1)S(1)}, bf16[64,2560]{1,0:T(8,128)(2,1)S(1)}, u32[]{:S(2)}, u32[]{:S(2)}) collective-permute-start(bf16[64,2560]{1,0:T(8,128)(2,1)S(1)} %get-tuple-element.31), channel_id=1, source_target_pairs={{0,6},{2,4},{4,2},{6,0},{8,14},{10,12},{12,10},{14,8},{1,7},{3,5},... | collective-permute-start | bytes 983048 | tf_op jit(solution)/shard_map/ppermute | solution.py:299
  8.4 0.5 collective-permute-start.2
  8.9 0.5 %collective-permute-start.3 = (bf16[64,2560]{1,0:T(8,128)(2,1)S(1)}, bf16[64,2560]{1,0:T(8,128)(2,1)S(1)}, u32[]{:S(2)}, u32[]{:S(2)}) collective-permute-start(bf16[64,2560]{1,0:T(8,128)(2,1)S(1)} %get-tuple-element.37), channel_id=1, source_target_pairs={{0,2},{2,0},{4,6},{6,4},{8,10},{10,8},{12,14},{14,12},{1,3},{3,1},... | collective-permute-start | bytes 983048 | tf_op jit(solution)/shard_map/ppermute | solution.py:299
  10.0 1.0 %scale_up.1.up_ref = bf16[1,128,1024]{2,1,0:T(8,128)(2,1)S(1)} custom-call(s32[1]{0:T(128)} %bitcast.3.core_ref, s32[1]{0:T(128)S(6)} %copy.9.ranks_ref, bf16[1,128,2048]{2,1,0:T(8,128)(2,1)} %up_hbm), custom_call_target="tpu_custom_call" | custom-call | flops 131072 | bytes 524288 | tf_op jit(solution)/shard_map/scale_up/pallas_call | solution.py:328
  11.1 0.1 collective-permute-start.7
  11.2 0.7 %convert_element_type.4 = f32[128]{0:T(128)S(1)} convert(s32[128]{0:T(128)} %param.10) | non-fusion elementwise | flops 128 | bytes 1024 | tf_op jit(solution)/shard_map/convert_element_type | solution.py:366
  11.9 5.9 %base.1 = (f32[128,1024]{1,0:T(8,128)S(1)}, f32[128,1024]{1,0:T(8,128)S(1)}, bf16[1,2560,128]{2,1,0:T(8,128)(2,1)S(1)}) custom-call(s32[1]{0:T(128)} %bitcast.3.core_ref, bf16[128,2560]{1,0:T(8,128)(2,1)} %tokens_hbm.3, bf16[2560,2048]{1,0:T(8,128)(2,1)} %weight_hbm.1, bf16[1,2560,128]{2,1,0:T(8,128)(2,1)} %down_hbm.3), custom_call_target="tpu_custom_call" | custom-call | flops 1342177280 | bytes 10485760 | tf_op jit(solution)/shard_map/base/pallas_call | solution.py:344
  17.8 3.8 %collective-permute-done.1.refs_4_ = bf16[1,1280,128]{2,1,0:T(8,128)(2,1)S(1)} collective-permute-done((bf16[1,1280,128]{2,1,0:T(8,128)(2,1)S(1)}, bf16[1,1280,128]{2,1,0:T(8,128)(2,1)S(1)}, u32[]{:S(2)}, u32[]{:S(2)}) %collective-permute-start.1) | collective-permute-done | bytes 327712 | tf_op jit(solution)/shard_map/ppermute | solution.py:299
  21.6 1.8 %collective-permute-start.5 = (bf16[1,1280,128]{2,1,0:T(8,128)(2,1)S(1)}, bf16[1,1280,128]{2,1,0:T(8,128)(2,1)S(1)}, u32[]{:S(2)}, u32[]{:S(2)}) collective-permute-start(bf16[1,1280,128]{2,1,0:T(8,128)(2,1)S(1)} %collective-permute-done.1.refs_4_), channel_id=1, source_target_pairs={{0,16},{16,0},{1,17},{17,1},{2,18},{18,2},{3,19},{19,3},{4,20},{20... | collective-permute-start | bytes 983048 | tf_op jit(solution)/shard_map/ppermute | solution.py:299
  23.4 0.3 fusion
  23.7 5.3 %collective-permute-done.refs_1_ = bf16[64,2560]{1,0:T(8,128)(2,1)S(1)} collective-permute-done((bf16[64,2560]{1,0:T(8,128)(2,1)S(1)}, bf16[64,2560]{1,0:T(8,128)(2,1)S(1)}, u32[]{:S(2)}, u32[]{:S(2)}) %collective-permute-start) | collective-permute-done | bytes 327712 | tf_op jit(solution)/shard_map/ppermute | solution.py:299
  29.0 0.0 collective-permute-start.4
  29.0 0.1 pad_maximum_fusion
  29.1 5.4 %collective-permute-done.2.refs_2_ = bf16[64,2560]{1,0:T(8,128)(2,1)S(1)} collective-permute-done((bf16[64,2560]{1,0:T(8,128)(2,1)S(1)}, bf16[64,2560]{1,0:T(8,128)(2,1)S(1)}, u32[]{:S(2)}, u32[]{:S(2)}) %collective-permute-start.2) | collective-permute-done | bytes 327712 | tf_op jit(solution)/shard_map/ppermute | solution.py:299
  34.6 0.0 collective-permute-done.3.refs_3_
  34.6 0.0 collective-permute-done.5.refs_5_
  34.6 0.5 %down.1.low_ref = f32[256,128]{1,0:T(8,128)S(1)} custom-call(s32[1]{0:T(128)} %bitcast.2.group_ref, bf16[1,2560,128]{2,1,0:T(8,128)(2,1)S(1)} %get-tuple-element.43.down_ref, bf16[64,2560]{1,0:T(8,128)(2,1)S(1)} %get-tuple-element.44.refs_0_, bf16[64,2560]{1,0:T(8,128)(2,1)S(1)} %collective-permute-done.refs_1_, ...), custom_call_target="tpu_custom_call" | custom-call | flops 335544320 | bytes 1966080 | tf_op jit(solution)/shard_map/down/pallas_call | solution.py:375
  35.1 0.1 collective-permute-start.6
  35.2 0.0 collective-permute-done.7.far_ref
  35.2 1.3 %collective-permute-done.6.other_ref = f32[256,128]{1,0:T(8,128)S(1)} collective-permute-done((f32[256,128]{1,0:T(8,128)S(1)}, f32[256,128]{1,0:T(8,128)S(1)}, u32[]{:S(2)}, u32[]{:S(2)}) %collective-permute-start.6) | collective-permute-done | bytes 131104 | tf_op jit(solution)/shard_map/ppermute | solution.py:299
  36.5 0.6 %up.1 = (s16[64,1152]{1,0:T(8,128)(2,1)S(1)}, s16[64,1152]{1,0:T(8,128)(2,1)S(1)}, s16[64,1152]{1,0:T(8,128)(2,1)S(1)}, s16[64,1152]{1,0:T(8,128)(2,1)S(1)}) custom-call(f32[256,128]{1,0:T(8,128)S(1)} %down.1.low_ref, f32[256,128]{1,0:T(8,128)S(1)} %collective-permute-done.6.other_ref, bf16[1,128,1024]{2,1,0:T(8,128)(2,1)S(1)} %scale_up.1.up_ref, ...), custom_call_target="tpu_custom_call" | custom-call | flops 268435456 | bytes 524288 | tf_op jit(solution)/shard_map/up/pallas_call | solution.py:386
  37.2 0.1 collective-permute-start.10
  37.2 2.0 %collective-permute-start.8 = (s16[64,1152]{1,0:T(8,128)(2,1)S(1)}, s16[64,1152]{1,0:T(8,128)(2,1)S(1)}, u32[]{:S(2)}, u32[]{:S(2)}) collective-permute-start(s16[64,1152]{1,0:T(8,128)(2,1)S(1)} %get-tuple-element.52), channel_id=1, source_target_pairs={{0,4},{2,6},{4,0},{6,2},{8,12},{10,14},{12,8},{14,10},{1,5},{3,7},... | collective-permute-start | bytes 442376 | tf_op jit(solution)/shard_map/ppermute | solution.py:299
  39.2 1.5 %collective-permute-start.9 = (s16[64,1152]{1,0:T(8,128)(2,1)S(1)}, s16[64,1152]{1,0:T(8,128)(2,1)S(1)}, u32[]{:S(2)}, u32[]{:S(2)}) collective-permute-start(s16[64,1152]{1,0:T(8,128)(2,1)S(1)} %get-tuple-element.53), channel_id=1, source_target_pairs={{0,2},{2,0},{4,6},{6,4},{8,10},{10,8},{12,14},{14,12},{1,3},{3,1},... | collective-permute-start | bytes 442376 | tf_op jit(solution)/shard_map/ppermute | solution.py:299
  40.7 0.0 copy-done.1
  40.7 0.0 collective-permute-done.4.other_ref
  40.7 4.1 %collective-permute-done.10.refs_3_ = s16[64,1152]{1,0:T(8,128)(2,1)S(1)} collective-permute-done((s16[64,1152]{1,0:T(8,128)(2,1)S(1)}, s16[64,1152]{1,0:T(8,128)(2,1)S(1)}, u32[]{:S(2)}, u32[]{:S(2)}) %collective-permute-start.10) | collective-permute-done | bytes 147488 | tf_op jit(solution)/shard_map/ppermute | solution.py:299
  44.9 1.4 %collective-permute-done.8.refs_1_ = s16[64,1152]{1,0:T(8,128)(2,1)S(1)} collective-permute-done((s16[64,1152]{1,0:T(8,128)(2,1)S(1)}, s16[64,1152]{1,0:T(8,128)(2,1)S(1)}, u32[]{:S(2)}, u32[]{:S(2)}) %collective-permute-start.8) | collective-permute-done | bytes 147488 | tf_op jit(solution)/shard_map/ppermute | solution.py:299
  46.3 0.9 %collective-permute-done.9.refs_2_ = s16[64,1152]{1,0:T(8,128)(2,1)S(1)} collective-permute-done((s16[64,1152]{1,0:T(8,128)(2,1)S(1)}, s16[64,1152]{1,0:T(8,128)(2,1)S(1)}, u32[]{:S(2)}, u32[]{:S(2)}) %collective-permute-start.9) | collective-permute-done | bytes 147488 | tf_op jit(solution)/shard_map/ppermute | solution.py:299
  47.2 0.0 copy-done
  47.2 1.6 %finish.1 = bf16[1024,128]{1,0:T(8,128)(2,1)} custom-call(s32[1]{0:T(128)} %bitcast.me_ref, s32[1,128]{1,0:T(1,128)S(1)} %bitcast.9, f32[128,1024]{1,0:T(8,128)S(1)} %get-tuple-element.39.mine_ref, f32[128,1024]{1,0:T(8,128)S(1)} %collective-permute-done.4.other_ref, f32[128,128]{1,0:T(8,128)S(1)} %get-tuple-element.41.cos_ref, ...), custom_call_target="tpu_custom_call" | custom-call | flops 134217728 | bytes 524288 | tf_op jit(solution)/shard_map/finish/pallas_call | solution.py:398
  (2 shorter events, 0.0 us)
Async XLA Ops:
  0.0 47.2 %copy-start = (s32[128,1]{0,1:T(1,128)S(1)}, s32[128,1]{0,1:T(1,128)}, u32[]{:S(2)}) copy-start(s32[128,1]{0,1:T(1,128)} %param.9) | copy-start | bytes 1540
  0.0 40.7 %copy-start.1 = (bf16[128]{0:T(256)(128)(2,1)S(1)}, bf16[128]{0:T(256)(128)(2,1)}, u32[]{:S(2)}) copy-start(bf16[128]{0:T(256)(128)(2,1)} %param.15) | copy-start | bytes 772
  1.8 19.8 %collective-permute-start.1 = (bf16[1,1280,128]{2,1,0:T(8,128)(2,1)S(1)}, bf16[1,1280,128]{2,1,0:T(8,128)(2,1)S(1)}, u32[]{:S(2)}, u32[]{:S(2)}) collective-permute-start(bf16[1,1280,128]{2,1,0:T(8,128)(2,1)S(1)} %get-tuple-element.32), channel_id=1, source_target_pairs={{0,8},{2,10},{4,12},{6,14},{8,0},{10,2},{12,4},{14,6},{1,9},{3,11}... | collective-permute-start | bytes 983048 | tf_op jit(solution)/shard_map/ppermute | solution.py:299
  5.9 23.1 %collective-permute-start = (bf16[64,2560]{1,0:T(8,128)(2,1)S(1)}, bf16[64,2560]{1,0:T(8,128)(2,1)S(1)}, u32[]{:S(2)}, u32[]{:S(2)}) collective-permute-start(bf16[64,2560]{1,0:T(8,128)(2,1)S(1)} %get-tuple-element.31), channel_id=1, source_target_pairs={{0,6},{2,4},{4,2},{6,0},{8,14},{10,12},{12,10},{14,8},{1,7},{3,5},... | collective-permute-start | bytes 983048 | tf_op jit(solution)/shard_map/ppermute | solution.py:299
  8.4 26.1 %collective-permute-start.2 = (bf16[64,2560]{1,0:T(8,128)(2,1)S(1)}, bf16[64,2560]{1,0:T(8,128)(2,1)S(1)}, u32[]{:S(2)}, u32[]{:S(2)}) collective-permute-start(bf16[64,2560]{1,0:T(8,128)(2,1)S(1)} %get-tuple-element.36), channel_id=1, source_target_pairs={{0,4},{2,6},{4,0},{6,2},{8,12},{10,14},{12,8},{14,10},{1,5},{3,7},... | collective-permute-start | bytes 983048 | tf_op jit(solution)/shard_map/ppermute | solution.py:299
  8.9 25.7 %collective-permute-start.3 = (bf16[64,2560]{1,0:T(8,128)(2,1)S(1)}, bf16[64,2560]{1,0:T(8,128)(2,1)S(1)}, u32[]{:S(2)}, u32[]{:S(2)}) collective-permute-start(bf16[64,2560]{1,0:T(8,128)(2,1)S(1)} %get-tuple-element.37), channel_id=1, source_target_pairs={{0,2},{2,0},{4,6},{6,4},{8,10},{10,8},{12,14},{14,12},{1,3},{3,1},... | collective-permute-start | bytes 983048 | tf_op jit(solution)/shard_map/ppermute | solution.py:299
  11.1 24.1 %collective-permute-start.7 = (bf16[1,128,1024]{2,1,0:T(8,128)(2,1)S(1)}, bf16[1,128,1024]{2,1,0:T(8,128)(2,1)S(1)}, u32[]{:S(2)}, u32[]{:S(2)}) collective-permute-start(bf16[1,128,1024]{2,1,0:T(8,128)(2,1)S(1)} %scale_up.1.up_ref), channel_id=1, source_target_pairs={{0,8},{2,10},{4,12},{6,14},{8,0},{10,2},{12,4},{14,6},{1,9},{3,11}... | collective-permute-start | bytes 786440 | tf_op jit(solution)/shard_map/ppermute | solution.py:299
  21.6 13.0 %collective-permute-start.5 = (bf16[1,1280,128]{2,1,0:T(8,128)(2,1)S(1)}, bf16[1,1280,128]{2,1,0:T(8,128)(2,1)S(1)}, u32[]{:S(2)}, u32[]{:S(2)}) collective-permute-start(bf16[1,1280,128]{2,1,0:T(8,128)(2,1)S(1)} %collective-permute-done.1.refs_4_), channel_id=1, source_target_pairs={{0,16},{16,0},{1,17},{17,1},{2,18},{18,2},{3,19},{19,3},{4,20},{20... | collective-permute-start | bytes 983048 | tf_op jit(solution)/shard_map/ppermute | solution.py:299
  29.0 11.7 %collective-permute-start.4 = (f32[128,1024]{1,0:T(8,128)S(1)}, f32[128,1024]{1,0:T(8,128)S(1)}, u32[]{:S(2)}, u32[]{:S(2)}) collective-permute-start(f32[128,1024]{1,0:T(8,128)S(1)} %get-tuple-element.40), channel_id=1, source_target_pairs={{0,1},{1,0},{2,3},{3,2},{4,5},{5,4},{6,7},{7,6},{8,9},{9,8},{10,11... | collective-permute-start | bytes 1572872 | tf_op jit(solution)/shard_map/ppermute | solution.py:299
  35.1 1.4 %collective-permute-start.6 = (f32[256,128]{1,0:T(8,128)S(1)}, f32[256,128]{1,0:T(8,128)S(1)}, u32[]{:S(2)}, u32[]{:S(2)}) collective-permute-start(f32[256,128]{1,0:T(8,128)S(1)} %down.1.low_ref), channel_id=1, source_target_pairs={{0,1},{1,0},{2,3},{3,2},{4,5},{5,4},{6,7},{7,6},{8,9},{9,8},{10,11... | collective-permute-start | bytes 393224 | tf_op jit(solution)/shard_map/ppermute | solution.py:299
  37.2 7.7 %collective-permute-start.10 = (s16[64,1152]{1,0:T(8,128)(2,1)S(1)}, s16[64,1152]{1,0:T(8,128)(2,1)S(1)}, u32[]{:S(2)}, u32[]{:S(2)}) collective-permute-start(s16[64,1152]{1,0:T(8,128)(2,1)S(1)} %get-tuple-element.54), channel_id=1, source_target_pairs={{0,6},{2,4},{4,2},{6,0},{8,14},{10,12},{12,10},{14,8},{1,7},{3,5},... | collective-permute-start | bytes 442376 | tf_op jit(solution)/shard_map/ppermute | solution.py:299
  37.2 9.0 %collective-permute-start.8 = (s16[64,1152]{1,0:T(8,128)(2,1)S(1)}, s16[64,1152]{1,0:T(8,128)(2,1)S(1)}, u32[]{:S(2)}, u32[]{:S(2)}) collective-permute-start(s16[64,1152]{1,0:T(8,128)(2,1)S(1)} %get-tuple-element.52), channel_id=1, source_target_pairs={{0,4},{2,6},{4,0},{6,2},{8,12},{10,14},{12,8},{14,10},{1,5},{3,7},... | collective-permute-start | bytes 442376 | tf_op jit(solution)/shard_map/ppermute | solution.py:299
  39.2 7.9 %collective-permute-start.9 = (s16[64,1152]{1,0:T(8,128)(2,1)S(1)}, s16[64,1152]{1,0:T(8,128)(2,1)S(1)}, u32[]{:S(2)}, u32[]{:S(2)}) collective-permute-start(s16[64,1152]{1,0:T(8,128)(2,1)S(1)} %get-tuple-element.53), channel_id=1, source_target_pairs={{0,2},{2,0},{4,6},{6,4},{8,10},{10,8},{12,14},{14,12},{1,3},{3,1},... | collective-permute-start | bytes 442376 | tf_op jit(solution)/shard_map/ppermute | solution.py:299

commit v8 on v5

--- a/solution.py
+++ b/solution.py
@@ -12,6 +12,8 @@
 NORM_EPS = 1e-06
 VMEM_LIMIT = 48 * 1024 * 1024
 LANES = 128
+EXPONENT_BITS = 8
+EXPONENT_BIAS = 128
 
 VMEM = pl.BlockSpec(memory_space=pltpu.VMEM)
 HBM = pl.BlockSpec(memory_space=pltpu.HBM)
@@ -53,12 +55,12 @@
 
 
 def far_first(count):
-    return sorted(range(1, count), key=lambda j: (-bin(j).count("1"), j))
+    return sorted(range(1, count), key=lambda j: (-bin(j).count("1"), -j))
 
 
 def return_order(count):
     order = far_first(count)
-    return order[-1:] + order[:-1]
+    return order
 
 
 def halves(x):
@@ -67,32 +69,13 @@
     return high, low
 
 
-def up_share_kernel(cores, group_ref, core_ref, ranks_ref, up_hbm, out_ref, factor_ref, own_ref, sem):
-    local, rank, share = out_ref.shape
-    at = core_ref[0] * (up_hbm.shape[2] // cores) + group_ref[0] * share
-    copy = pltpu.make_async_copy(
-        up_hbm.at[:, :, pl.ds(pl.multiple_of(at, share), share)], own_ref, sem
-    )
-    copy.start()
-    copy.wait()
-    for a in range(local):
-        used = ranks_ref[a]
-
-        def factor(shape, dim):
-            scale = jnp.float32(ALPHA) / jnp.full(shape, used, jnp.int32).astype(jnp.float32)
-            return jnp.where(iota(shape, dim) < used, scale, 0.0)
-
-        factor_ref[a : a + 1, :] = factor((1, rank), 1)
-        out_ref[a] = (own_ref[a].astype(jnp.float32) * factor((rank, 1), 0)).astype(jnp.bfloat16)
-
-
 def pick_kernel(
-    pool, local, depth, me_ref, group_ref, adapter_hbm, tokens_hbm, down_hbm, *refs
+    pool, local, depth, columns, me_ref, group_ref, core_ref, adapter_hbm, tokens_hbm, down_hbm, up_hbm, *refs
 ):
-    share_ref, outs = refs[0], refs[1:-4]
-    adapter_ref, tokens_ref, share_sem, sems = refs[-4:]
+    down_ref, up_ref, outs = refs[0], refs[1], refs[2:-4]
+    adapter_ref, tokens_ref, share_sems, sems = refs[-4:]
     rows, width = tokens_ref.shape
-    share = share_ref.shape[1]
+    down_share, up_share = down_ref.shape[1], up_ref.shape[2]
     parts = sems.shape[0] - 1
     part = rows // parts
     adapter_copy = pltpu.make_async_copy(adapter_hbm, adapter_ref, sems.at[parts])
@@ -107,9 +90,18 @@
     ]
     for copy in copies:
         copy.start()
-    at = pl.multiple_of(group_ref[0] * share, share)
-    share_copy = pltpu.make_async_copy(down_hbm.at[:, pl.ds(at, share), :], share_ref, share_sem)
-    share_copy.start()
+    at = pl.multiple_of(group_ref[0] * down_share, down_share)
+    up_at = pl.multiple_of(core_ref[0] * columns + group_ref[0] * up_share, up_share)
+    share_copies = [
+        pltpu.make_async_copy(
+            down_hbm.at[:, pl.ds(at, down_share), :], down_ref, share_sems.at[0]
+        ),
+        pltpu.make_async_copy(
+            up_hbm.at[:, :, pl.ds(up_at, up_share)], up_ref, share_sems.at[1]
+        ),
+    ]
+    for copy in share_copies:
+        copy.start()
     adapter_copy.wait()
     place = slot_places(adapter_ref[...], me_ref[0], pool, local, depth)
     size = outs[0].shape[0]
@@ -124,7 +116,8 @@
         )
         for j, out in enumerate(outs):
             out[:, at : at + step] = block[j * size : (j + 1) * size].astype(jnp.bfloat16)
-    share_copy.wait()
+    for copy in share_copies:
+        copy.wait()
 
 
 def base_kernel(
@@ -206,47 +199,54 @@
 
 
 def up_kernel(
-    buffers, groups, local, depth, group_ref, low_ref, other_ref, factor_ref, up_ref, *refs
+    buffers, groups, local, depth, group_ref, low_ref, other_ref, factor_ref, far_factor_ref, up_ref, *refs
 ):
     shares, outs, term_ref = refs[:groups], refs[groups : groups + buffers], refs[-1]
     rows, rank = low_ref.shape
     size = rows // buffers
-    columns = term_ref.shape[1]
+    columns = up_ref.shape[2]
     share = columns // groups
     which = (iota((rows, 1), 0) // depth) % (2 * local)
     low = low_ref[...] + other_ref[...]
-    for a in range(local):
-        low = jnp.where(which == a, low * factor_ref[a : a + 1, :], low)
-    both = jnp.concatenate(halves(low), axis=0)
+    factors = [factor_ref[a : a + 1, :] for a in range(local)]
+    factors += [far_factor_ref[a : a + 1, :] for a in range(local)]
+    scale = factors[0]
+    for i in range(1, 2 * local):
+        scale = jnp.where(which == i, factors[i], scale)
+    both = jnp.concatenate(halves(low * scale), axis=0)
     which = jnp.concatenate([which, which], axis=0)
     spread = jnp.concatenate(
         [jnp.where(which == i, both, jnp.zeros_like(both)) for i in range(2 * local)], axis=1
     )
     for k in range(groups):
         at = pl.multiple_of((group_ref[0] ^ k) * share, share)
-        factors = [up_ref[a, :, pl.ds(at, share)] for a in range(local)]
-        factors += [shares[k][a] for a in range(local)]
+        up = [up_ref[a, :, pl.ds(at, share)] for a in range(local)]
+        up += [shares[k][a] for a in range(local)]
         term = jnp.dot(
-            spread, jnp.concatenate(factors, axis=0), preferred_element_type=jnp.float32
+            spread, jnp.concatenate(up, axis=0), preferred_element_type=jnp.float32
         )
         term_ref[:, pl.ds(at, share)] = term[:rows] + term[rows:]
+    lane = iota((1, LANES), 1)
     for j, out in enumerate(outs):
         term = term_ref[j * size : (j + 1) * size, :]
         top = jnp.max(jnp.abs(term), axis=1, keepdims=True)
         exponent = jnp.ceil(jnp.log2(jnp.maximum(top, 1e-30)) + 1e-3)
-        code = jnp.round(term * jnp.exp2(15.0 - exponent))
-        code = jnp.clip(code, -32767.0, 32767.0)
-        out[:, :columns] = code.astype(jnp.int32).astype(jnp.int16)
-        out[:, columns:] = jnp.broadcast_to(
-            exponent.astype(jnp.int32), (size, LANES)
-        ).astype(jnp.int16)
+        code = jnp.clip(jnp.round(term * jnp.exp2(15.0 - exponent)), -32767.0, 32767.0)
+        code = code.astype(jnp.int32)
+        biased = exponent.astype(jnp.int32) + EXPONENT_BIAS
+        first = code[:, :LANES]
+        marked = (first & -2) | ((biased >> jnp.minimum(lane, EXPONENT_BITS - 1)) & 1)
+        first = jnp.where(lane < EXPONENT_BITS, marked, first)
+        out[:, :LANES] = first.astype(jnp.int16)
+        out[:, LANES:] = code[:, LANES:].astype(jnp.int16)
 
 
 def finish_kernel(
     buffers, pool, local, depth, me_ref, adapter_ref, mine_ref, other_ref, cos_ref, sin_ref, gain_ref, *refs
 ):
     order = [0] + return_order(buffers)
-    ins, out_ref = [refs[order.index(j)] for j in range(buffers)], refs[-1]
+    ins = [refs[order.index(j)] for j in range(buffers)]
+    out_hbm, out_ref, sems = refs[-3:]
     rows, columns = mine_ref.shape
     head = cos_ref.shape[1]
     place = to_column(slot_places(adapter_ref[...], me_ref[0], pool, local, depth))
@@ -261,7 +261,11 @@
         low = jnp.dot(picker, low, preferred_element_type=jnp.float32)
         return high * 256.0 + low
 
-    scale = jnp.exp2(picked(columns, LANES)[:, :1] - 15.0)
+    lane = iota((1, LANES), 1)
+    bits = picked(0, LANES).astype(jnp.int32) & 1
+    bits = jnp.where(lane < EXPONENT_BITS, bits << jnp.minimum(lane, EXPONENT_BITS - 1), 0)
+    exponent = jnp.sum(bits.astype(jnp.float32), axis=1, keepdims=True) - EXPONENT_BIAS
+    scale = jnp.exp2(exponent - 15.0)
     cosine, sine, gain = cos_ref[...], sin_ref[...], gain_ref[...]
     entries = []
     for at in range(0, columns, 2 * head):
@@ -276,10 +280,19 @@
     n = kinds * block
     source = (iota((n, n), 0) % kinds) * block + iota((n, n), 0) // kinds
     order = jnp.where(iota((n, n), 1) == source, 1.0, 0.0).astype(jnp.bfloat16)
+    copies = []
     for i in range(rows // block):
         stacked = jnp.concatenate([e[i * block : (i + 1) * block] for e in entries], axis=0)
         mixed = jnp.dot(order, stacked, preferred_element_type=jnp.float32)
         out_ref[i * n : (i + 1) * n, :] = mixed.astype(jnp.bfloat16)
+        if i % 2:
+            done = pl.ds((i - 1) * n, 2 * n)
+            copies.append(
+                pltpu.make_async_copy(out_ref.at[done, :], out_hbm.at[done, :], sems.at[i // 2])
+            )
+            copies[-1].start()
+    for copy in copies:
+        copy.wait()
 
 
 def body(
@@ -319,45 +332,38 @@
     adapter_row = row_adapters.reshape(1, rows)
     down_share = width // groups
     parts = rows // 16
-    down_part, *picked = pl.pallas_call(
-        functools.partial(pick_kernel, pool, local, depth),
-        in_specs=[SMEM] * 2 + [HBM] * 3,
-        out_specs=[VMEM] * (1 + buffers),
-        out_shape=[jax.ShapeDtypeStruct((local, down_share, rank), bf16)]
+    up_share = columns // groups
+    down_part, up_part, *picked = pl.pallas_call(
+        functools.partial(pick_kernel, pool, local, depth, columns),
+        in_specs=[SMEM] * 3 + [HBM] * 4,
+        out_specs=[VMEM] * (2 + buffers),
+        out_shape=[
+            jax.ShapeDtypeStruct((local, down_share, rank), bf16),
+            jax.ShapeDtypeStruct((local, rank, up_share), bf16),
+        ]
         + [jax.ShapeDtypeStruct((size, width), bf16)] * buffers,
         scratch_shapes=[
             pltpu.VMEM((1, rows), jnp.int32),
             pltpu.VMEM((rows, width), bf16),
-            pltpu.SemaphoreType.DMA,
+            pltpu.SemaphoreType.DMA((2,)),
             pltpu.SemaphoreType.DMA((parts + 1,)),
         ],
         compiler_params=params(),
         cost_estimate=cost(2 * buffers * size * rows * width, 2 * (rows + buffers * size) * width),
         name="pick",
-    )(me, group, in_hbm(adapter_row), in_hbm(tokens), in_hbm(adapter_down))
+    )(
+        me,
+        group,
+        core,
+        in_hbm(adapter_row),
+        in_hbm(tokens),
+        in_hbm(adapter_down),
+        in_hbm(adapter_up),
+    )
     far_down = exchange(down_part, "pool", pool, pool // 2)
+    far_up = exchange(up_part, "pool", pool, pool // 2)
     order = far_first(buffers)
     arrived = [picked[0]] + [exchange(picked[j], "pool", pool, j) for j in order]
-
-    up_share = columns // groups
-    ranks_now, adapter_up_now, _ = lax.optimization_barrier((ranks, adapter_up, picked))
-    up_part, factor = pl.pallas_call(
-        functools.partial(up_share_kernel, cores),
-        in_specs=[SMEM] * 3 + [HBM],
-        out_specs=[VMEM] * 2,
-        out_shape=[
-            jax.ShapeDtypeStruct((local, rank, up_share), bf16),
-            jax.ShapeDtypeStruct((local, rank), f32),
-        ],
-        scratch_shapes=[
-            pltpu.VMEM((local, rank, up_share), bf16),
-            pltpu.SemaphoreType.DMA,
-        ],
-        compiler_params=params(),
-        cost_estimate=cost(local * rank * up_share, 4 * local * rank * up_share),
-        name="up_share",
-    )(group, core, ranks_now, in_hbm(adapter_up_now))
-    far_up = exchange(up_part, "pool", pool, pool // 2)
 
     steps = 5
     theirs, mine, own_down, own_up = pl.pallas_call(
@@ -389,6 +395,11 @@
     far_downs = hand_round(far_down)
     far_up, _ = lax.optimization_barrier((far_up, far_down))
     far_ups = hand_round(far_up)
+    mask = (jnp.arange(rank, dtype=jnp.int32)[None, :] < ranks[:, None]).astype(f32)
+    factor = mask * (f32(ALPHA) / ranks.astype(f32))[:, None]
+    factor, _ = lax.optimization_barrier((factor, arrived[1]))
+    far_factor = exchange(factor, "pool", pool, pool // 2)
+
     half_dim = head // 2
     frequency = jnp.power(
         f32(ROPE_THETA), -jnp.arange(half_dim, dtype=f32) * (2.0 / head)
@@ -398,8 +409,10 @@
     cosine = jnp.concatenate([cosine, cosine], axis=1)
     sine = jnp.concatenate([-sine, sine], axis=1)
 
-    arrived, far_ups, mine, cosine, sine = lax.optimization_barrier(
-        (arrived, far_ups, mine, cosine, sine)
+    arrived[-1], theirs = lax.optimization_barrier((arrived[-1], theirs))
+    other = exchange(theirs, "tp", cores, 1)
+    arrived, far_ups, far_factor, mine, cosine, sine = lax.optimization_barrier(
+        (arrived, far_ups, far_factor, mine, cosine, sine)
     )
     slots = buffers * size
     low = pl.pallas_call(
@@ -415,24 +428,26 @@
 
     terms = pl.pallas_call(
         functools.partial(up_kernel, buffers, groups, local, depth),
-        in_specs=[SMEM] + [VMEM] * (4 + groups),
+        in_specs=[SMEM] + [VMEM] * (5 + groups),
         out_specs=[VMEM] * buffers,
-        out_shape=[jax.ShapeDtypeStruct((size, columns + LANES), jnp.int16)] * buffers,
+        out_shape=[jax.ShapeDtypeStruct((size, columns), jnp.int16)] * buffers,
         scratch_shapes=[pltpu.VMEM((slots, columns), f32)],
         compiler_params=params(),
         cost_estimate=cost(8 * local * slots * rank * columns, 2 * slots * columns),
         name="up",
-    )(group, low, low_other, factor, own_up, *far_ups)
-    terms, theirs = lax.optimization_barrier((terms, theirs))
-    other = exchange(theirs, "tp", cores, 1)
+    )(group, low, low_other, factor, far_factor, own_up, *far_ups)
     order = return_order(buffers)
     returned = [terms[0]] + [exchange(terms[j], "pool", pool, j) for j in order]
 
     out = pl.pallas_call(
         functools.partial(finish_kernel, buffers, pool, local, depth),
         in_specs=[SMEM] + [VMEM] * (6 + buffers),
-        out_specs=VMEM,
+        out_specs=HBM,
         out_shape=jax.ShapeDtypeStruct((rows * columns // head, head), bf16),
+        scratch_shapes=[
+            pltpu.VMEM((rows * columns // head, head), bf16),
+            pltpu.SemaphoreType.DMA((rows // 32,)),
+        ],
         compiler_params=params(),
         cost_estimate=cost(4 * rows * slots * columns, 2 * slots * columns),
         name="finish",

time: 50.4 us -> 49.2 us (0.976)
  Pallas kernels: 11.3 us -> 10.5 us
  waiting for transfers between devices: 21.8 us -> 21.1 us
    pallas_call x2 -> x1, Pallas kernels: 2.73 us -> 1.89 us  [body(): pl.pallas_call(functools.partial(pick_kernel, pool, local, depth, columns...]
    ppermute x12 -> x13, waiting for transfers between devices: 21.8 us -> 21.1 us  [exchange(): return lax.ppermute(x, axis, [(p, p ^ j) for p in range(count)])]
    ppermute x12 -> x13, starting transfers between devices: 15.3 us -> 15.5 us  [exchange(): return lax.ppermute(x, axis, [(p, p ^ j) for p in range(count)])]
  transfers between devices with their start and end apart: 12 -> 13, of which waited for: 6 -> 9; matrix products, arithmetic and copies ran while one was open for 2% -> 2% of each run, Pallas kernels for 13% -> 14%
where the time goes in v8:
time: 49.2 us; the launch traced here: 49 us
  waiting for transfers between devices  21.1 us (43%)
  starting transfers between devices  15.5 us (32%)
  Pallas kernels  10.5 us (21%)
  other arithmetic  1.08 us (2%)
  between operations  0.78 us (2%)
    ppermute x13, waiting for transfers between devices, exchange(): return lax.ppermute(x, axis, [(p, p ^ j) for p in range(count)])  21.1 us
    ppermute x13, starting transfers between devices, exchange(): return lax.ppermute(x, axis, [(p, p ^ j) for p in range(count)])  15.5 us
    pallas_call x1, Pallas kernels, body(): pl.pallas_call(base_kernel, in_specs=[SMEM] + [HBM] * 4, out_specs=[VMEM]...  5.62 us
    pallas_call x1, Pallas kernels, body(): pl.pallas_call(functools.partial(pick_kernel, pool, local, depth, columns...  1.89 us
    pallas_call x1, Pallas kernels, body(): pl.pallas_call(functools.partial(finish_kernel, buffers, pool, local, dep...  1.66 us
  transfers between devices with their start and end apart: 13, of which 9 were waited for; matrix products, arithmetic and copies ran while one was open for 2% of the time, Pallas kernels for 14%

profile of v8, /device:TPU:0, one launch (start us, length us, event | category | flops | bytes accessed | tf_op | source)
XLA Modules:
  0.0 49.0 jit_solution(17997206497883013710)
XLA Ops:
  0.0 0.0 copy-start
  0.0 0.0 copy-start.1
  0.0 1.9 %pick.1 = (bf16[1,1280,128]{2,1,0:T(8,128)(2,1)S(1)}, bf16[1,128,512]{2,1,0:T(8,128)(2,1)S(1)}, bf16[64,2560]{1,0:T(8,128)(2,1)S(1)}, bf16[64,2560]{1,0:T(8,128)...) custom-call(s32[1]{0:T(128)} %bitcast.me_ref, s32[1]{0:T(128)} %bitcast.2.group_ref, ...), custom_call_target="tpu_custom_call" | custom-call | flops 167772160 | bytes 1966080 | tf_op jit(solution)/shard_map/pick/pallas_call | solution.py:336
  1.9 4.1 %collective-permute-start.3 = (bf16[1,1280,128]{2,1,0:T(8,128)(2,1)S(1)}, bf16[1,1280,128]{2,1,0:T(8,128)(2,1)S(1)}, u32[]{:S(2)}, u32[]{:S(2)}) collective-permute-start(bf16[1,1280,128]{2,1,0:T(8,128)(2,1)S(1)} %get-tuple-element.39), channel_id=1, source_target_pairs={{0,8},{2,10},{4,12},{6,14},{8,0},{10,2},{12,4},{14,6},{1,9},{3,11}... | collective-permute-start | bytes 983048 | tf_op jit(solution)/shard_map/ppermute | solution.py:327
  6.0 0.1 collective-permute-start.4
  6.1 1.8 %collective-permute-start.2 = (bf16[64,2560]{1,0:T(8,128)(2,1)S(1)}, bf16[64,2560]{1,0:T(8,128)(2,1)S(1)}, u32[]{:S(2)}, u32[]{:S(2)}) collective-permute-start(bf16[64,2560]{1,0:T(8,128)(2,1)S(1)} %get-tuple-element.38), channel_id=1, source_target_pairs={{0,2},{2,0},{4,6},{6,4},{8,10},{10,8},{12,14},{14,12},{1,3},{3,1},... | collective-permute-start | bytes 983048 | tf_op jit(solution)/shard_map/ppermute | solution.py:327
  7.9 1.5 %collective-permute-start = (bf16[64,2560]{1,0:T(8,128)(2,1)S(1)}, bf16[64,2560]{1,0:T(8,128)(2,1)S(1)}, u32[]{:S(2)}, u32[]{:S(2)}) collective-permute-start(bf16[64,2560]{1,0:T(8,128)(2,1)S(1)} %get-tuple-element.36), channel_id=1, source_target_pairs={{0,6},{2,4},{4,2},{6,0},{8,14},{10,12},{12,10},{14,8},{1,7},{3,5},... | collective-permute-start | bytes 983048 | tf_op jit(solution)/shard_map/ppermute | solution.py:327
  9.4 0.2 collective-permute-start.1
  9.6 0.7 %convert_element_type.9 = f32[128]{0:T(128)S(1)} convert(s32[128]{0:T(128)} %param.10) | non-fusion elementwise | flops 128 | bytes 1024 | tf_op jit(solution)/shard_map/convert_element_type | solution.py:407
  10.2 5.6 %base.1 = (f32[128,1024]{1,0:T(8,128)S(1)}, f32[128,1024]{1,0:T(8,128)S(1)}, bf16[1,2560,128]{2,1,0:T(8,128)(2,1)S(1)}, bf16[1,128,1024]{2,1,0:T(8,128)(2,1)S(1)}) custom-call(s32[1]{0:T(128)} %bitcast.3.core_ref, bf16[128,2560]{1,0:T(8,128)(2,1)} %tokens_hbm.3, bf16[2560,2048]{1,0:T(8,128)(2,1)} %weight_hbm.1, bf16[1,2560,128]{2,1,0:T(8,128)(2,1)} %down_hbm.3, ...), custom_call_target="tpu_custom_call" | custom-call | flops 1342177280 | bytes 10485760 | tf_op jit(solution)/shard_map/base/pallas_call | solution.py:369
  15.9 8.6 %collective-permute-done.3.refs_4_ = bf16[1,1280,128]{2,1,0:T(8,128)(2,1)S(1)} collective-permute-done((bf16[1,1280,128]{2,1,0:T(8,128)(2,1)S(1)}, bf16[1,1280,128]{2,1,0:T(8,128)(2,1)S(1)}, u32[]{:S(2)}, u32[]{:S(2)}) %collective-permute-start.3) | collective-permute-done | bytes 327712 | tf_op jit(solution)/shard_map/ppermute | solution.py:327
  24.5 1.8 %collective-permute-start.8 = (bf16[1,1280,128]{2,1,0:T(8,128)(2,1)S(1)}, bf16[1,1280,128]{2,1,0:T(8,128)(2,1)S(1)}, u32[]{:S(2)}, u32[]{:S(2)}) collective-permute-start(bf16[1,1280,128]{2,1,0:T(8,128)(2,1)S(1)} %collective-permute-done.3.refs_4_), channel_id=1, source_target_pairs={{0,16},{16,0},{1,17},{17,1},{2,18},{18,2},{3,19},{19,3},{4,20},{20... | collective-permute-start | bytes 983048 | tf_op jit(solution)/shard_map/ppermute | solution.py:327
  26.3 0.3 fusion
  27.3 0.0 collective-permute-done.4.refs_0_
  27.3 0.7 %collective-permute-start.5 = (bf16[1,128,512]{2,1,0:T(8,128)(2,1)S(1)}, bf16[1,128,512]{2,1,0:T(8,128)(2,1)S(1)}, u32[]{:S(2)}, u32[]{:S(2)}) collective-permute-start(bf16[1,128,512]{2,1,0:T(8,128)(2,1)S(1)} %collective-permute-done.4.refs_0_), channel_id=1, source_target_pairs={{0,16},{16,0},{1,17},{17,1},{2,18},{18,2},{3,19},{19,3},{4,20},{20... | collective-permute-start | bytes 393224 | tf_op jit(solution)/shard_map/ppermute | solution.py:327
  28.0 0.0 collective-permute-done.2.refs_3_
  28.0 0.1 collective-permute-done.refs_1_
  28.1 1.7 %collective-permute-start.6 = (f32[1,128]{1,0:T(1,128)S(1)}, f32[1,128]{1,0:T(1,128)S(1)}, u32[]{:S(2)}, u32[]{:S(2)}) collective-permute-start(f32[1,128]{1,0:T(1,128)S(1)} %compare_select_fusion.factor_ref), channel_id=1, source_target_pairs={{0,8},{2,10},{4,12},{6,14},{8,0},{10,2},{12,4},{14,6},{1,9},{3,11}... | collective-permute-start | bytes 1544 | tf_op jit(solution)/shard_map/ppermute | solution.py:327
  29.9 0.0 collective-permute-start.7
  29.9 0.1 pad_maximum_fusion
  30.0 2.2 %collective-permute-done.1.refs_2_ = bf16[64,2560]{1,0:T(8,128)(2,1)S(1)} collective-permute-done((bf16[64,2560]{1,0:T(8,128)(2,1)S(1)}, bf16[64,2560]{1,0:T(8,128)(2,1)S(1)}, u32[]{:S(2)}, u32[]{:S(2)}) %collective-permute-start.1) | collective-permute-done | bytes 327712 | tf_op jit(solution)/shard_map/ppermute | solution.py:327
  32.2 0.4 collective-permute-done.6.far_factor_ref
  32.6 2.7 %collective-permute-done.5.refs_1_ = bf16[1,128,512]{2,1,0:T(8,128)(2,1)S(1)} collective-permute-done((bf16[1,128,512]{2,1,0:T(8,128)(2,1)S(1)}, bf16[1,128,512]{2,1,0:T(8,128)(2,1)S(1)}, u32[]{:S(2)}, u32[]{:S(2)}) %collective-permute-start.5) | collective-permute-done | bytes 131104 | tf_op jit(solution)/shard_map/ppermute | solution.py:327
  35.3 0.0 collective-permute-done.8.refs_5_
  35.3 0.5 %down.1.low_ref = f32[256,128]{1,0:T(8,128)S(1)} custom-call(s32[1]{0:T(128)} %bitcast.2.group_ref, bf16[1,2560,128]{2,1,0:T(8,128)(2,1)S(1)} %get-tuple-element.52.down_ref, bf16[64,2560]{1,0:T(8,128)(2,1)S(1)} %get-tuple-element.53.refs_0_, bf16[64,2560]{1,0:T(8,128)(2,1)S(1)} %collective-permute-done.refs_1_, ...), custom_call_target="tpu_custom_call" | custom-call | flops 335544320 | bytes 1966080 | tf_op jit(solution)/shard_map/down/pallas_call | solution.py:418
  35.8 0.1 collective-permute-start.9
  35.9 1.3 %collective-permute-done.9.other_ref = f32[256,128]{1,0:T(8,128)S(1)} collective-permute-done((f32[256,128]{1,0:T(8,128)S(1)}, f32[256,128]{1,0:T(8,128)S(1)}, u32[]{:S(2)}, u32[]{:S(2)}) %collective-permute-start.9) | collective-permute-done | bytes 131104 | tf_op jit(solution)/shard_map/ppermute | solution.py:327
  37.2 0.8 %up.1 = (s16[64,1024]{1,0:T(8,128)(2,1)S(1)}, s16[64,1024]{1,0:T(8,128)(2,1)S(1)}, s16[64,1024]{1,0:T(8,128)(2,1)S(1)}, s16[64,1024]{1,0:T(8,128)(2,1)S(1)}) custom-call(s32[1]{0:T(128)} %bitcast.2.group_ref, f32[256,128]{1,0:T(8,128)S(1)} %down.1.low_ref, f32[256,128]{1,0:T(8,128)S(1)} %collective-permute-done.9.other_ref, ...), custom_call_target="tpu_custom_call" | custom-call | flops 268435456 | bytes 524288 | tf_op jit(solution)/shard_map/up/pallas_call | solution.py:429
  38.0 2.5 %collective-permute-start.10 = (s16[64,1024]{1,0:T(8,128)(2,1)S(1)}, s16[64,1024]{1,0:T(8,128)(2,1)S(1)}, u32[]{:S(2)}, u32[]{:S(2)}) collective-permute-start(s16[64,1024]{1,0:T(8,128)(2,1)S(1)} %get-tuple-element.62), channel_id=1, source_target_pairs={{0,6},{2,4},{4,2},{6,0},{8,14},{10,12},{12,10},{14,8},{1,7},{3,5},... | collective-permute-start | bytes 393224 | tf_op jit(solution)/shard_map/ppermute | solution.py:327
  40.5 0.3 collective-permute-start.11
  40.8 0.8 %collective-permute-start.12 = (s16[64,1024]{1,0:T(8,128)(2,1)S(1)}, s16[64,1024]{1,0:T(8,128)(2,1)S(1)}, u32[]{:S(2)}, u32[]{:S(2)}) collective-permute-start(s16[64,1024]{1,0:T(8,128)(2,1)S(1)} %get-tuple-element.64), channel_id=1, source_target_pairs={{0,2},{2,0},{4,6},{6,4},{8,10},{10,8},{12,14},{14,12},{1,3},{3,1},... | collective-permute-start | bytes 393224 | tf_op jit(solution)/shard_map/ppermute | solution.py:327
  41.6 0.0 copy-done.1
  41.6 0.0 collective-permute-done.7.other_ref
  41.6 3.7 %collective-permute-done.10.refs_1_ = s16[64,1024]{1,0:T(8,128)(2,1)S(1)} collective-permute-done((s16[64,1024]{1,0:T(8,128)(2,1)S(1)}, s16[64,1024]{1,0:T(8,128)(2,1)S(1)}, u32[]{:S(2)}, u32[]{:S(2)}) %collective-permute-start.10) | collective-permute-done | bytes 131104 | tf_op jit(solution)/shard_map/ppermute | solution.py:327
  45.3 1.8 %collective-permute-done.11.refs_2_ = s16[64,1024]{1,0:T(8,128)(2,1)S(1)} collective-permute-done((s16[64,1024]{1,0:T(8,128)(2,1)S(1)}, s16[64,1024]{1,0:T(8,128)(2,1)S(1)}, u32[]{:S(2)}, u32[]{:S(2)}) %collective-permute-start.11) | collective-permute-done | bytes 131104 | tf_op jit(solution)/shard_map/ppermute | solution.py:327
  47.2 0.2 collective-permute-done.12.refs_3_
  47.3 0.0 copy-done
  47.3 1.7 %finish.1 = bf16[1024,128]{1,0:T(8,128)(2,1)} custom-call(s32[1]{0:T(128)} %bitcast.me_ref, s32[1,128]{1,0:T(1,128)S(1)} %bitcast.12, f32[128,1024]{1,0:T(8,128)S(1)} %get-tuple-element.48.mine_ref, f32[128,1024]{1,0:T(8,128)S(1)} %collective-permute-done.7.other_ref, f32[128,128]{1,0:T(8,128)S(1)} %get-tuple-element.50.cos_ref, ...), custom_call_target="tpu_custom_call" | custom-call | flops 134217728 | bytes 524288 | tf_op jit(solution)/shard_map/finish/pallas_call | solution.py:442
  (3 shorter events, 0.0 us)
Async XLA Ops:
  0.0 47.3 %copy-start = (s32[128,1]{0,1:T(1,128)S(1)}, s32[128,1]{0,1:T(1,128)}, u32[]{:S(2)}) copy-start(s32[128,1]{0,1:T(1,128)} %param.9) | copy-start | bytes 1540
  0.0 41.6 %copy-start.1 = (bf16[128]{0:T(256)(128)(2,1)S(1)}, bf16[128]{0:T(256)(128)(2,1)}, u32[]{:S(2)}) copy-start(bf16[128]{0:T(256)(128)(2,1)} %param.15) | copy-start | bytes 772
  1.9 22.6 %collective-permute-start.3 = (bf16[1,1280,128]{2,1,0:T(8,128)(2,1)S(1)}, bf16[1,1280,128]{2,1,0:T(8,128)(2,1)S(1)}, u32[]{:S(2)}, u32[]{:S(2)}) collective-permute-start(bf16[1,1280,128]{2,1,0:T(8,128)(2,1)S(1)} %get-tuple-element.39), channel_id=1, source_target_pairs={{0,8},{2,10},{4,12},{6,14},{8,0},{10,2},{12,4},{14,6},{1,9},{3,11}... | collective-permute-start | bytes 983048 | tf_op jit(solution)/shard_map/ppermute | solution.py:327
  6.0 21.3 %collective-permute-start.4 = (bf16[1,128,512]{2,1,0:T(8,128)(2,1)S(1)}, bf16[1,128,512]{2,1,0:T(8,128)(2,1)S(1)}, u32[]{:S(2)}, u32[]{:S(2)}) collective-permute-start(bf16[1,128,512]{2,1,0:T(8,128)(2,1)S(1)} %get-tuple-element.43), channel_id=1, source_target_pairs={{0,8},{2,10},{4,12},{6,14},{8,0},{10,2},{12,4},{14,6},{1,9},{3,11}... | collective-permute-start | bytes 393224 | tf_op jit(solution)/shard_map/ppermute | solution.py:327
  6.1 21.9 %collective-permute-start.2 = (bf16[64,2560]{1,0:T(8,128)(2,1)S(1)}, bf16[64,2560]{1,0:T(8,128)(2,1)S(1)}, u32[]{:S(2)}, u32[]{:S(2)}) collective-permute-start(bf16[64,2560]{1,0:T(8,128)(2,1)S(1)} %get-tuple-element.38), channel_id=1, source_target_pairs={{0,2},{2,0},{4,6},{6,4},{8,10},{10,8},{12,14},{14,12},{1,3},{3,1},... | collective-permute-start | bytes 983048 | tf_op jit(solution)/shard_map/ppermute | solution.py:327
  7.9 20.3 %collective-permute-start = (bf16[64,2560]{1,0:T(8,128)(2,1)S(1)}, bf16[64,2560]{1,0:T(8,128)(2,1)S(1)}, u32[]{:S(2)}, u32[]{:S(2)}) collective-permute-start(bf16[64,2560]{1,0:T(8,128)(2,1)S(1)} %get-tuple-element.36), channel_id=1, source_target_pairs={{0,6},{2,4},{4,2},{6,0},{8,14},{10,12},{12,10},{14,8},{1,7},{3,5},... | collective-permute-start | bytes 983048 | tf_op jit(solution)/shard_map/ppermute | solution.py:327
  9.4 22.8 %collective-permute-start.1 = (bf16[64,2560]{1,0:T(8,128)(2,1)S(1)}, bf16[64,2560]{1,0:T(8,128)(2,1)S(1)}, u32[]{:S(2)}, u32[]{:S(2)}) collective-permute-start(bf16[64,2560]{1,0:T(8,128)(2,1)S(1)} %get-tuple-element.37), channel_id=1, source_target_pairs={{0,4},{2,6},{4,0},{6,2},{8,12},{10,14},{12,8},{14,10},{1,5},{3,7},... | collective-permute-start | bytes 983048 | tf_op jit(solution)/shard_map/ppermute | solution.py:327
  24.5 10.8 %collective-permute-start.8 = (bf16[1,1280,128]{2,1,0:T(8,128)(2,1)S(1)}, bf16[1,1280,128]{2,1,0:T(8,128)(2,1)S(1)}, u32[]{:S(2)}, u32[]{:S(2)}) collective-permute-start(bf16[1,1280,128]{2,1,0:T(8,128)(2,1)S(1)} %collective-permute-done.3.refs_4_), channel_id=1, source_target_pairs={{0,16},{16,0},{1,17},{17,1},{2,18},{18,2},{3,19},{19,3},{4,20},{20... | collective-permute-start | bytes 983048 | tf_op jit(solution)/shard_map/ppermute | solution.py:327
  27.3 8.0 %collective-permute-start.5 = (bf16[1,128,512]{2,1,0:T(8,128)(2,1)S(1)}, bf16[1,128,512]{2,1,0:T(8,128)(2,1)S(1)}, u32[]{:S(2)}, u32[]{:S(2)}) collective-permute-start(bf16[1,128,512]{2,1,0:T(8,128)(2,1)S(1)} %collective-permute-done.4.refs_0_), channel_id=1, source_target_pairs={{0,16},{16,0},{1,17},{17,1},{2,18},{18,2},{3,19},{19,3},{4,20},{20... | collective-permute-start | bytes 393224 | tf_op jit(solution)/shard_map/ppermute | solution.py:327
  28.1 4.4 %collective-permute-start.6 = (f32[1,128]{1,0:T(1,128)S(1)}, f32[1,128]{1,0:T(1,128)S(1)}, u32[]{:S(2)}, u32[]{:S(2)}) collective-permute-start(f32[1,128]{1,0:T(1,128)S(1)} %compare_select_fusion.factor_ref), channel_id=1, source_target_pairs={{0,8},{2,10},{4,12},{6,14},{8,0},{10,2},{12,4},{14,6},{1,9},{3,11}... | collective-permute-start | bytes 1544 | tf_op jit(solution)/shard_map/ppermute | solution.py:327
  29.9 11.7 %collective-permute-start.7 = (f32[128,1024]{1,0:T(8,128)S(1)}, f32[128,1024]{1,0:T(8,128)S(1)}, u32[]{:S(2)}, u32[]{:S(2)}) collective-permute-start(f32[128,1024]{1,0:T(8,128)S(1)} %get-tuple-element.49), channel_id=1, source_target_pairs={{0,1},{1,0},{2,3},{3,2},{4,5},{5,4},{6,7},{7,6},{8,9},{9,8},{10,11... | collective-permute-start | bytes 1572872 | tf_op jit(solution)/shard_map/ppermute | solution.py:327
  35.8 1.4 %collective-permute-start.9 = (f32[256,128]{1,0:T(8,128)S(1)}, f32[256,128]{1,0:T(8,128)S(1)}, u32[]{:S(2)}, u32[]{:S(2)}) collective-permute-start(f32[256,128]{1,0:T(8,128)S(1)} %down.1.low_ref), channel_id=1, source_target_pairs={{0,1},{1,0},{2,3},{3,2},{4,5},{5,4},{6,7},{7,6},{8,9},{9,8},{10,11... | collective-permute-start | bytes 393224 | tf_op jit(solution)/shard_map/ppermute | solution.py:327
  38.0 7.3 %collective-permute-start.10 = (s16[64,1024]{1,0:T(8,128)(2,1)S(1)}, s16[64,1024]{1,0:T(8,128)(2,1)S(1)}, u32[]{:S(2)}, u32[]{:S(2)}) collective-permute-start(s16[64,1024]{1,0:T(8,128)(2,1)S(1)} %get-tuple-element.62), channel_id=1, source_target_pairs={{0,6},{2,4},{4,2},{6,0},{8,14},{10,12},{12,10},{14,8},{1,7},{3,5},... | collective-permute-start | bytes 393224 | tf_op jit(solution)/shard_map/ppermute | solution.py:327
  40.5 6.7 %collective-permute-start.11 = (s16[64,1024]{1,0:T(8,128)(2,1)S(1)}, s16[64,1024]{1,0:T(8,128)(2,1)S(1)}, u32[]{:S(2)}, u32[]{:S(2)}) collective-permute-start(s16[64,1024]{1,0:T(8,128)(2,1)S(1)} %get-tuple-element.63), channel_id=1, source_target_pairs={{0,4},{2,6},{4,0},{6,2},{8,12},{10,14},{12,8},{14,10},{1,5},{3,7},... | collective-permute-start | bytes 393224 | tf_op jit(solution)/shard_map/ppermute | solution.py:327
  40.8 6.5 %collective-permute-start.12 = (s16[64,1024]{1,0:T(8,128)(2,1)S(1)}, s16[64,1024]{1,0:T(8,128)(2,1)S(1)}, u32[]{:S(2)}, u32[]{:S(2)}) collective-permute-start(s16[64,1024]{1,0:T(8,128)(2,1)S(1)} %get-tuple-element.64), channel_id=1, source_target_pairs={{0,2},{2,0},{4,6},{6,4},{8,10},{10,8},{12,14},{14,12},{1,3},{3,1},... | collective-permute-start | bytes 393224 | tf_op jit(solution)/shard_map/ppermute | solution.py:327

commit v9 on v8

--- a/solution.py
+++ b/solution.py
@@ -12,6 +12,7 @@
 NORM_EPS = 1e-06
 VMEM_LIMIT = 48 * 1024 * 1024
 LANES = 128
+CHUNKS = 2
 EXPONENT_BITS = 8
 EXPONENT_BIAS = 128
 
@@ -54,6 +55,11 @@
     return ((buffer * 2 + far) * local + (row - holder * local)) * depth + slot
 
 
+def chunk_places(share):
+    first = (share // LANES + 1) // 2 * LANES
+    return [(0, first), (first, share - first)]
+
+
 def far_first(count):
     return sorted(range(1, count), key=lambda j: (-bin(j).count("1"), -j))
 
@@ -72,10 +78,10 @@
 def pick_kernel(
     pool, local, depth, columns, me_ref, group_ref, core_ref, adapter_hbm, tokens_hbm, down_hbm, up_hbm, *refs
 ):
-    down_ref, up_ref, outs = refs[0], refs[1], refs[2:-4]
+    up_ref, down_refs, outs = refs[0], refs[1 : 1 + CHUNKS], refs[1 + CHUNKS : -4]
     adapter_ref, tokens_ref, share_sems, sems = refs[-4:]
     rows, width = tokens_ref.shape
-    down_share, up_share = down_ref.shape[1], up_ref.shape[2]
+    up_share = up_ref.shape[2]
     parts = sems.shape[0] - 1
     part = rows // parts
     adapter_copy = pltpu.make_async_copy(adapter_hbm, adapter_ref, sems.at[parts])
@@ -90,16 +96,20 @@
     ]
     for copy in copies:
         copy.start()
-    at = pl.multiple_of(group_ref[0] * down_share, down_share)
     up_at = pl.multiple_of(core_ref[0] * columns + group_ref[0] * up_share, up_share)
     share_copies = [
         pltpu.make_async_copy(
-            down_hbm.at[:, pl.ds(at, down_share), :], down_ref, share_sems.at[0]
-        ),
-        pltpu.make_async_copy(
-            up_hbm.at[:, :, pl.ds(up_at, up_share)], up_ref, share_sems.at[1]
+            up_hbm.at[:, :, pl.ds(up_at, up_share)], up_ref, share_sems.at[0]
         ),
     ]
+    share = sum(ref.shape[1] for ref in down_refs)
+    for c, (offset, chunk) in enumerate(chunk_places(share)):
+        at = pl.multiple_of(group_ref[0] * share + offset, LANES)
+        share_copies.append(
+            pltpu.make_async_copy(
+                down_hbm.at[:, pl.ds(at, chunk), :], down_refs[c], share_sems.at[1 + c]
+            )
+        )
     for copy in share_copies:
         copy.start()
     adapter_copy.wait()
@@ -178,14 +188,15 @@
 def down_kernel(buffers, groups, local, depth, group_ref, down_ref, *refs):
     order = [0] + far_first(buffers)
     ins = [refs[order.index(j)] for j in range(buffers)]
-    shares, out = refs[buffers : buffers + groups], refs[-1]
+    shares, out = refs[buffers:-1], refs[-1]
     rank = out.shape[1]
-    share = shares[0].shape[1]
+    share = ins[0].shape[1] // groups
     total = None
-    for k in range(groups):
-        at = pl.multiple_of((group_ref[0] ^ k) * share, share)
-        rows = jnp.concatenate([x[:, pl.ds(at, share)] for x in ins], axis=0)
-        factors = [down_ref[a, pl.ds(at, share), :] for a in range(local)]
+    for k in range(groups * CHUNKS):
+        offset, chunk = chunk_places(share)[k // groups]
+        at = pl.multiple_of((group_ref[0] ^ (k % groups)) * share + offset, LANES)
+        rows = jnp.concatenate([x[:, pl.ds(at, chunk)] for x in ins], axis=0)
+        factors = [down_ref[a, pl.ds(at, chunk), :] for a in range(local)]
         factors += [shares[k][a] for a in range(local)]
         term = jnp.dot(
             rows, jnp.concatenate(factors, axis=1), preferred_element_type=jnp.float32
@@ -330,22 +341,20 @@
         return [share] + [exchange(share, "groups", groups, k) for k in range(1, groups)]
 
     adapter_row = row_adapters.reshape(1, rows)
-    down_share = width // groups
+    chunks = [size for _, size in chunk_places(width // groups)]
     parts = rows // 16
     up_share = columns // groups
-    down_part, up_part, *picked = pl.pallas_call(
+    up_part, *parts_picked = pl.pallas_call(
         functools.partial(pick_kernel, pool, local, depth, columns),
         in_specs=[SMEM] * 3 + [HBM] * 4,
-        out_specs=[VMEM] * (2 + buffers),
-        out_shape=[
-            jax.ShapeDtypeStruct((local, down_share, rank), bf16),
-            jax.ShapeDtypeStruct((local, rank, up_share), bf16),
-        ]
+        out_specs=[VMEM] * (1 + CHUNKS + buffers),
+        out_shape=[jax.ShapeDtypeStruct((local, rank, up_share), bf16)]
+        + [jax.ShapeDtypeStruct((local, chunk, rank), bf16) for chunk in chunks]
         + [jax.ShapeDtypeStruct((size, width), bf16)] * buffers,
         scratch_shapes=[
             pltpu.VMEM((1, rows), jnp.int32),
             pltpu.VMEM((rows, width), bf16),
-            pltpu.SemaphoreType.DMA((2,)),
+            pltpu.SemaphoreType.DMA((1 + CHUNKS,)),
             pltpu.SemaphoreType.DMA((parts + 1,)),
         ],
         compiler_params=params(),
@@ -360,8 +369,9 @@
         in_hbm(adapter_down),
         in_hbm(adapter_up),
     )
-    far_down = exchange(down_part, "pool", pool, pool // 2)
+    down_parts, picked = parts_picked[:CHUNKS], parts_picked[CHUNKS:]
     far_up = exchange(up_part, "pool", pool, pool // 2)
+    far_down = exchange(down_parts[0], "pool", pool, pool // 2)
     order = far_first(buffers)
     arrived = [picked[0]] + [exchange(picked[j], "pool", pool, j) for j in order]
 
@@ -391,10 +401,13 @@
         in_hbm(adapter_down),
         in_hbm(adapter_up),
     )
-    far_down, theirs = lax.optimization_barrier((far_down, theirs))
+    far_up, far_down, theirs = lax.optimization_barrier((far_up, far_down, theirs))
+    far_ups = hand_round(far_up)
     far_downs = hand_round(far_down)
-    far_up, _ = lax.optimization_barrier((far_up, far_down))
-    far_ups = hand_round(far_up)
+    for part in down_parts[1:]:
+        part, _ = lax.optimization_barrier((part, far_down))
+        far_down = exchange(part, "pool", pool, pool // 2)
+        far_downs += hand_round(far_down)
     mask = (jnp.arange(rank, dtype=jnp.int32)[None, :] < ranks[:, None]).astype(f32)
     factor = mask * (f32(ALPHA) / ranks.astype(f32))[:, None]
     factor, _ = lax.optimization_barrier((factor, arrived[1]))
@@ -417,7 +430,7 @@
     slots = buffers * size
     low = pl.pallas_call(
         functools.partial(down_kernel, buffers, groups, local, depth),
-        in_specs=[SMEM] + [VMEM] * (1 + buffers + groups),
+        in_specs=[SMEM] + [VMEM] * (1 + buffers + groups * CHUNKS),
         out_specs=VMEM,
         out_shape=jax.ShapeDtypeStruct((slots, rank), f32),
         compiler_params=params(),

time: 49.2 us -> 50.5 us (1.026)
  starting transfers between devices: 15.5 us -> 18.2 us
  waiting for transfers between devices: 21.1 us -> 20.3 us
  other arithmetic: 1.08 us -> 0.43 us
    ppermute x13 -> x15, starting transfers between devices: 15.5 us -> 18.2 us  [exchange(): return lax.ppermute(x, axis, [(p, p ^ j) for p in range(count)])]
    ppermute x13 -> x15, waiting for transfers between devices: 21.1 us -> 20.3 us  [exchange(): return lax.ppermute(x, axis, [(p, p ^ j) for p in range(count)])]
    convert_element_type x1, other arithmetic: 0.66 us -> 0.01 us  [body(): angles = positions.astype(f32)[:, None] * frequency[None, :]]
  transfers between devices with their start and end apart: 13 -> 15, of which waited for: 9 -> 7; matrix products, arithmetic and copies ran while one was open for 2% -> 1% of each run, Pallas kernels for 14% -> 14%
where the time goes in v9:
time: 50.5 us; the launch traced here: 50.3 us
  waiting for transfers between devices  20.3 us (40%)
  starting transfers between devices  18.2 us (36%)
  Pallas kernels  10.5 us (21%)
  between operations  0.8 us (2%)
    ppermute x15, waiting for transfers between devices, exchange(): return lax.ppermute(x, axis, [(p, p ^ j) for p in range(count)])  20.3 us
    ppermute x15, starting transfers between devices, exchange(): return lax.ppermute(x, axis, [(p, p ^ j) for p in range(count)])  18.2 us
    pallas_call x1, Pallas kernels, body(): pl.pallas_call(base_kernel, in_specs=[SMEM] + [HBM] * 4, out_specs=[VMEM]...  5.64 us
    pallas_call x1, Pallas kernels, body(): pl.pallas_call(functools.partial(pick_kernel, pool, local, depth, columns...  1.91 us
    pallas_call x1, Pallas kernels, body(): pl.pallas_call(functools.partial(finish_kernel, buffers, pool, local, dep...  1.66 us
  transfers between devices with their start and end apart: 15, of which 7 were waited for; matrix products, arithmetic and copies ran while one was open for 1% of the time, Pallas kernels for 14%

profile of v9, /device:TPU:0, one launch (start us, length us, event | category | flops | bytes accessed | tf_op | source)
XLA Modules:
  0.0 50.3 jit_solution(5691111703552683655)
XLA Ops:
  0.0 0.0 copy-start
  0.0 0.0 copy-start.1
  0.0 0.0 copy-start.2
  0.0 1.9 %pick.1 = (bf16[1,128,512]{2,1,0:T(8,128)(2,1)S(1)}, bf16[1,640,128]{2,1,0:T(8,128)(2,1)S(1)}, bf16[1,640,128]{2,1,0:T(8,128)(2,1)S(1)}, bf16[64,2560]{1,0:T(8,1...) custom-call(s32[1]{0:T(128)} %bitcast.me_ref, ...), custom_call_target="tpu_custom_call" | custom-call | flops 167772160 | bytes 1966080 | tf_op jit(solution)/shard_map/pick/pallas_call | solution.py:347
  1.9 4.1 %collective-permute-start.4 = (bf16[1,640,128]{2,1,0:T(8,128)(2,1)S(1)}, bf16[1,640,128]{2,1,0:T(8,128)(2,1)S(1)}, u32[]{:S(2)}, u32[]{:S(2)}) collective-permute-start(bf16[1,640,128]{2,1,0:T(8,128)(2,1)S(1)} %get-tuple-element.42), channel_id=1, source_target_pairs={{0,8},{2,10},{4,12},{6,14},{8,0},{10,2},{12,4},{14,6},{1,9},{3,11}... | collective-permute-start | bytes 491528 | tf_op jit(solution)/shard_map/ppermute | solution.py:338
  6.0 0.1 collective-permute-start.3
  6.1 1.8 %collective-permute-start.2 = (bf16[64,2560]{1,0:T(8,128)(2,1)S(1)}, bf16[64,2560]{1,0:T(8,128)(2,1)S(1)}, u32[]{:S(2)}, u32[]{:S(2)}) collective-permute-start(bf16[64,2560]{1,0:T(8,128)(2,1)S(1)} %get-tuple-element.40), channel_id=1, source_target_pairs={{0,2},{2,0},{4,6},{6,4},{8,10},{10,8},{12,14},{14,12},{1,3},{3,1},... | collective-permute-start | bytes 983048 | tf_op jit(solution)/shard_map/ppermute | solution.py:338
  7.9 1.5 %collective-permute-start = (bf16[64,2560]{1,0:T(8,128)(2,1)S(1)}, bf16[64,2560]{1,0:T(8,128)(2,1)S(1)}, u32[]{:S(2)}, u32[]{:S(2)}) collective-permute-start(bf16[64,2560]{1,0:T(8,128)(2,1)S(1)} %get-tuple-element.38), channel_id=1, source_target_pairs={{0,6},{2,4},{4,2},{6,0},{8,14},{10,12},{12,10},{14,8},{1,7},{3,5},... | collective-permute-start | bytes 983048 | tf_op jit(solution)/shard_map/ppermute | solution.py:338
  9.4 0.2 collective-permute-start.1
  9.6 5.6 %base.1 = (f32[128,1024]{1,0:T(8,128)S(1)}, f32[128,1024]{1,0:T(8,128)S(1)}, bf16[1,2560,128]{2,1,0:T(8,128)(2,1)S(1)}, bf16[1,128,1024]{2,1,0:T(8,128)(2,1)S(1)}) custom-call(s32[1]{0:T(128)} %bitcast.3.core_ref, bf16[128,2560]{1,0:T(8,128)(2,1)} %tokens_hbm.3, bf16[2560,2048]{1,0:T(8,128)(2,1)} %weight_hbm.1, bf16[1,2560,128]{2,1,0:T(8,128)(2,1)} %down_hbm.3, ...), custom_call_target="tpu_custom_call" | custom-call | flops 1342177280 | bytes 10485760 | tf_op jit(solution)/shard_map/base/pallas_call | solution.py:379
  15.2 0.0 copy-done.1
  15.3 4.2 %collective-permute-done.3.refs_0_ = bf16[1,128,512]{2,1,0:T(8,128)(2,1)S(1)} collective-permute-done((bf16[1,128,512]{2,1,0:T(8,128)(2,1)S(1)}, bf16[1,128,512]{2,1,0:T(8,128)(2,1)S(1)}, u32[]{:S(2)}, u32[]{:S(2)}) %collective-permute-start.3) | collective-permute-done | bytes 131104 | tf_op jit(solution)/shard_map/ppermute | solution.py:338
  19.5 0.0 collective-permute-done.4.refs_4_
  19.5 1.5 %collective-permute-start.5 = (bf16[1,128,512]{2,1,0:T(8,128)(2,1)S(1)}, bf16[1,128,512]{2,1,0:T(8,128)(2,1)S(1)}, u32[]{:S(2)}, u32[]{:S(2)}) collective-permute-start(bf16[1,128,512]{2,1,0:T(8,128)(2,1)S(1)} %collective-permute-done.3.refs_0_), channel_id=1, source_target_pairs={{0,16},{16,0},{1,17},{17,1},{2,18},{18,2},{3,19},{19,3},{4,20},{20... | collective-permute-start | bytes 393224 | tf_op jit(solution)/shard_map/ppermute | solution.py:338
  21.0 0.0 collective-permute-start.9
  21.0 0.3 fusion
  22.0 0.0 collective-permute-done.2.refs_3_
  22.0 0.6 %collective-permute-start.8 = (bf16[1,640,128]{2,1,0:T(8,128)(2,1)S(1)}, bf16[1,640,128]{2,1,0:T(8,128)(2,1)S(1)}, u32[]{:S(2)}, u32[]{:S(2)}) collective-permute-start(bf16[1,640,128]{2,1,0:T(8,128)(2,1)S(1)} %collective-permute-done.4.refs_4_), channel_id=1, source_target_pairs={{0,16},{16,0},{1,17},{17,1},{2,18},{18,2},{3,19},{19,3},{4,20},{20... | collective-permute-start | bytes 491528 | tf_op jit(solution)/shard_map/ppermute | solution.py:338
  22.6 7.4 %collective-permute-done.9.refs_6_ = bf16[1,640,128]{2,1,0:T(8,128)(2,1)S(1)} collective-permute-done((bf16[1,640,128]{2,1,0:T(8,128)(2,1)S(1)}, bf16[1,640,128]{2,1,0:T(8,128)(2,1)S(1)}, u32[]{:S(2)}, u32[]{:S(2)}) %collective-permute-start.9) | collective-permute-done | bytes 163872 | tf_op jit(solution)/shard_map/ppermute | solution.py:338
  30.0 1.4 %collective-permute-start.10 = (bf16[1,640,128]{2,1,0:T(8,128)(2,1)S(1)}, bf16[1,640,128]{2,1,0:T(8,128)(2,1)S(1)}, u32[]{:S(2)}, u32[]{:S(2)}) collective-permute-start(bf16[1,640,128]{2,1,0:T(8,128)(2,1)S(1)} %collective-permute-done.9.refs_6_), channel_id=1, source_target_pairs={{0,16},{16,0},{1,17},{17,1},{2,18},{18,2},{3,19},{19,3},{4,20},{20... | collective-permute-start | bytes 491528 | tf_op jit(solution)/shard_map/ppermute | solution.py:338
  31.4 0.0 collective-permute-done.refs_1_
  31.4 3.4 %collective-permute-start.6 = (f32[1,128]{1,0:T(1,128)S(1)}, f32[1,128]{1,0:T(1,128)S(1)}, u32[]{:S(2)}, u32[]{:S(2)}) collective-permute-start(f32[1,128]{1,0:T(1,128)S(1)} %compare_select_fusion.factor_ref), channel_id=1, source_target_pairs={{0,8},{2,10},{4,12},{6,14},{8,0},{10,2},{12,4},{14,6},{1,9},{3,11}... | collective-permute-start | bytes 1544 | tf_op jit(solution)/shard_map/ppermute | solution.py:338
  34.8 0.0 collective-permute-done.5.refs_1_
  34.8 0.0 collective-permute-start.7
  34.8 0.1 pad_maximum_fusion
  34.9 0.0 collective-permute-done.1.refs_2_
  34.9 1.4 %collective-permute-done.6.far_factor_ref = f32[1,128]{1,0:T(1,128)S(1)} collective-permute-done((f32[1,128]{1,0:T(1,128)S(1)}, f32[1,128]{1,0:T(1,128)S(1)}, u32[]{:S(2)}, u32[]{:S(2)}) %collective-permute-start.6) | collective-permute-done | bytes 544 | tf_op jit(solution)/shard_map/ppermute | solution.py:338
  36.3 0.0 collective-permute-done.8.refs_5_
  36.3 0.0 collective-permute-done.10.refs_7_
  36.3 0.6 %down.1.low_ref = f32[256,128]{1,0:T(8,128)S(1)} custom-call(s32[1]{0:T(128)} %bitcast.2.group_ref, bf16[1,2560,128]{2,1,0:T(8,128)(2,1)S(1)} %get-tuple-element.53.down_ref, bf16[64,2560]{1,0:T(8,128)(2,1)S(1)} %get-tuple-element.54.refs_0_, bf16[64,2560]{1,0:T(8,128)(2,1)S(1)} %collective-permute-done.refs_1_, ...), custom_call_target="tpu_custom_call" | custom-call | flops 335544320 | bytes 1966080 | tf_op jit(solution)/shard_map/down/pallas_call | solution.py:431
  36.9 0.1 collective-permute-start.11
  37.0 1.3 %collective-permute-done.11.other_ref = f32[256,128]{1,0:T(8,128)S(1)} collective-permute-done((f32[256,128]{1,0:T(8,128)S(1)}, f32[256,128]{1,0:T(8,128)S(1)}, u32[]{:S(2)}, u32[]{:S(2)}) %collective-permute-start.11) | collective-permute-done | bytes 131104 | tf_op jit(solution)/shard_map/ppermute | solution.py:338
  38.3 0.8 %up.1 = (s16[64,1024]{1,0:T(8,128)(2,1)S(1)}, s16[64,1024]{1,0:T(8,128)(2,1)S(1)}, s16[64,1024]{1,0:T(8,128)(2,1)S(1)}, s16[64,1024]{1,0:T(8,128)(2,1)S(1)}) custom-call(s32[1]{0:T(128)} %bitcast.2.group_ref, f32[256,128]{1,0:T(8,128)S(1)} %down.1.low_ref, f32[256,128]{1,0:T(8,128)S(1)} %collective-permute-done.11.other_ref, ...), custom_call_target="tpu_custom_call" | custom-call | flops 268435456 | bytes 524288 | tf_op jit(solution)/shard_map/up/pallas_call | solution.py:442
  39.1 2.9 %collective-permute-start.12 = (s16[64,1024]{1,0:T(8,128)(2,1)S(1)}, s16[64,1024]{1,0:T(8,128)(2,1)S(1)}, u32[]{:S(2)}, u32[]{:S(2)}) collective-permute-start(s16[64,1024]{1,0:T(8,128)(2,1)S(1)} %get-tuple-element.66), channel_id=1, source_target_pairs={{0,6},{2,4},{4,2},{6,0},{8,14},{10,12},{12,10},{14,8},{1,7},{3,5},... | collective-permute-start | bytes 393224 | tf_op jit(solution)/shard_map/ppermute | solution.py:338
  42.0 0.1 collective-permute-start.13
  42.2 0.5 %collective-permute-start.14 = (s16[64,1024]{1,0:T(8,128)(2,1)S(1)}, s16[64,1024]{1,0:T(8,128)(2,1)S(1)}, u32[]{:S(2)}, u32[]{:S(2)}) collective-permute-start(s16[64,1024]{1,0:T(8,128)(2,1)S(1)} %get-tuple-element.68), channel_id=1, source_target_pairs={{0,2},{2,0},{4,6},{6,4},{8,10},{10,8},{12,14},{14,12},{1,3},{3,1},... | collective-permute-start | bytes 393224 | tf_op jit(solution)/shard_map/ppermute | solution.py:338
  42.7 0.0 copy-done.2
  42.7 3.7 %collective-permute-done.12.refs_1_ = s16[64,1024]{1,0:T(8,128)(2,1)S(1)} collective-permute-done((s16[64,1024]{1,0:T(8,128)(2,1)S(1)}, s16[64,1024]{1,0:T(8,128)(2,1)S(1)}, u32[]{:S(2)}, u32[]{:S(2)}) %collective-permute-start.12) | collective-permute-done | bytes 131104 | tf_op jit(solution)/shard_map/ppermute | solution.py:338
  46.4 2.1 %collective-permute-done.13.refs_2_ = s16[64,1024]{1,0:T(8,128)(2,1)S(1)} collective-permute-done((s16[64,1024]{1,0:T(8,128)(2,1)S(1)}, s16[64,1024]{1,0:T(8,128)(2,1)S(1)}, u32[]{:S(2)}, u32[]{:S(2)}) %collective-permute-start.13) | collective-permute-done | bytes 131104 | tf_op jit(solution)/shard_map/ppermute | solution.py:338
  48.5 0.2 collective-permute-done.14.refs_3_
  48.7 0.0 collective-permute-done.7.other_ref
  48.7 0.0 copy-done
  48.7 1.7 %finish.1 = bf16[1024,128]{1,0:T(8,128)(2,1)} custom-call(s32[1]{0:T(128)} %bitcast.me_ref, s32[1,128]{1,0:T(1,128)S(1)} %bitcast.12, f32[128,1024]{1,0:T(8,128)S(1)} %get-tuple-element.49.mine_ref, f32[128,1024]{1,0:T(8,128)S(1)} %collective-permute-done.7.other_ref, f32[128,128]{1,0:T(8,128)S(1)} %get-tuple-element.51.cos_ref, ...), custom_call_target="tpu_custom_call" | custom-call | flops 134217728 | bytes 524288 | tf_op jit(solution)/shard_map/finish/pallas_call | solution.py:455
  (4 shorter events, 0.0 us)
Async XLA Ops:
  0.0 48.7 %copy-start = (s32[128,1]{0,1:T(1,128)S(1)}, s32[128,1]{0,1:T(1,128)}, u32[]{:S(2)}) copy-start(s32[128,1]{0,1:T(1,128)} %param.9) | copy-start | bytes 1540
  0.0 15.2 %copy-start.1 = (s32[128]{0:T(128)S(1)}, s32[128]{0:T(128)}, u32[]{:S(2)}) copy-start(s32[128]{0:T(128)} %param.10) | copy-start | bytes 1540
  0.0 42.7 %copy-start.2 = (bf16[128]{0:T(256)(128)(2,1)S(1)}, bf16[128]{0:T(256)(128)(2,1)}, u32[]{:S(2)}) copy-start(bf16[128]{0:T(256)(128)(2,1)} %param.15) | copy-start | bytes 772
  1.9 17.5 %collective-permute-start.4 = (bf16[1,640,128]{2,1,0:T(8,128)(2,1)S(1)}, bf16[1,640,128]{2,1,0:T(8,128)(2,1)S(1)}, u32[]{:S(2)}, u32[]{:S(2)}) collective-permute-start(bf16[1,640,128]{2,1,0:T(8,128)(2,1)S(1)} %get-tuple-element.42), channel_id=1, source_target_pairs={{0,8},{2,10},{4,12},{6,14},{8,0},{10,2},{12,4},{14,6},{1,9},{3,11}... | collective-permute-start | bytes 491528 | tf_op jit(solution)/shard_map/ppermute | solution.py:338
  6.0 13.4 %collective-permute-start.3 = (bf16[1,128,512]{2,1,0:T(8,128)(2,1)S(1)}, bf16[1,128,512]{2,1,0:T(8,128)(2,1)S(1)}, u32[]{:S(2)}, u32[]{:S(2)}) collective-permute-start(bf16[1,128,512]{2,1,0:T(8,128)(2,1)S(1)} %get-tuple-element.41), channel_id=1, source_target_pairs={{0,8},{2,10},{4,12},{6,14},{8,0},{10,2},{12,4},{14,6},{1,9},{3,11}... | collective-permute-start | bytes 393224 | tf_op jit(solution)/shard_map/ppermute | solution.py:338
  6.1 15.9 %collective-permute-start.2 = (bf16[64,2560]{1,0:T(8,128)(2,1)S(1)}, bf16[64,2560]{1,0:T(8,128)(2,1)S(1)}, u32[]{:S(2)}, u32[]{:S(2)}) collective-permute-start(bf16[64,2560]{1,0:T(8,128)(2,1)S(1)} %get-tuple-element.40), channel_id=1, source_target_pairs={{0,2},{2,0},{4,6},{6,4},{8,10},{10,8},{12,14},{14,12},{1,3},{3,1},... | collective-permute-start | bytes 983048 | tf_op jit(solution)/shard_map/ppermute | solution.py:338
  7.9 23.6 %collective-permute-start = (bf16[64,2560]{1,0:T(8,128)(2,1)S(1)}, bf16[64,2560]{1,0:T(8,128)(2,1)S(1)}, u32[]{:S(2)}, u32[]{:S(2)}) collective-permute-start(bf16[64,2560]{1,0:T(8,128)(2,1)S(1)} %get-tuple-element.38), channel_id=1, source_target_pairs={{0,6},{2,4},{4,2},{6,0},{8,14},{10,12},{12,10},{14,8},{1,7},{3,5},... | collective-permute-start | bytes 983048 | tf_op jit(solution)/shard_map/ppermute | solution.py:338
  9.4 25.5 %collective-permute-start.1 = (bf16[64,2560]{1,0:T(8,128)(2,1)S(1)}, bf16[64,2560]{1,0:T(8,128)(2,1)S(1)}, u32[]{:S(2)}, u32[]{:S(2)}) collective-permute-start(bf16[64,2560]{1,0:T(8,128)(2,1)S(1)} %get-tuple-element.39), channel_id=1, source_target_pairs={{0,4},{2,6},{4,0},{6,2},{8,12},{10,14},{12,8},{14,10},{1,5},{3,7},... | collective-permute-start | bytes 983048 | tf_op jit(solution)/shard_map/ppermute | solution.py:338
  19.5 15.4 %collective-permute-start.5 = (bf16[1,128,512]{2,1,0:T(8,128)(2,1)S(1)}, bf16[1,128,512]{2,1,0:T(8,128)(2,1)S(1)}, u32[]{:S(2)}, u32[]{:S(2)}) collective-permute-start(bf16[1,128,512]{2,1,0:T(8,128)(2,1)S(1)} %collective-permute-done.3.refs_0_), channel_id=1, source_target_pairs={{0,16},{16,0},{1,17},{17,1},{2,18},{18,2},{3,19},{19,3},{4,20},{20... | collective-permute-start | bytes 393224 | tf_op jit(solution)/shard_map/ppermute | solution.py:338
  21.0 9.0 %collective-permute-start.9 = (bf16[1,640,128]{2,1,0:T(8,128)(2,1)S(1)}, bf16[1,640,128]{2,1,0:T(8,128)(2,1)S(1)}, u32[]{:S(2)}, u32[]{:S(2)}) collective-permute-start(bf16[1,640,128]{2,1,0:T(8,128)(2,1)S(1)} %get-tuple-element.60), channel_id=1, source_target_pairs={{0,8},{2,10},{4,12},{6,14},{8,0},{10,2},{12,4},{14,6},{1,9},{3,11}... | collective-permute-start | bytes 491528 | tf_op jit(solution)/shard_map/ppermute | solution.py:338
  22.0 14.3 %collective-permute-start.8 = (bf16[1,640,128]{2,1,0:T(8,128)(2,1)S(1)}, bf16[1,640,128]{2,1,0:T(8,128)(2,1)S(1)}, u32[]{:S(2)}, u32[]{:S(2)}) collective-permute-start(bf16[1,640,128]{2,1,0:T(8,128)(2,1)S(1)} %collective-permute-done.4.refs_4_), channel_id=1, source_target_pairs={{0,16},{16,0},{1,17},{17,1},{2,18},{18,2},{3,19},{19,3},{4,20},{20... | collective-permute-start | bytes 491528 | tf_op jit(solution)/shard_map/ppermute | solution.py:338
  30.0 6.4 %collective-permute-start.10 = (bf16[1,640,128]{2,1,0:T(8,128)(2,1)S(1)}, bf16[1,640,128]{2,1,0:T(8,128)(2,1)S(1)}, u32[]{:S(2)}, u32[]{:S(2)}) collective-permute-start(bf16[1,640,128]{2,1,0:T(8,128)(2,1)S(1)} %collective-permute-done.9.refs_6_), channel_id=1, source_target_pairs={{0,16},{16,0},{1,17},{17,1},{2,18},{18,2},{3,19},{19,3},{4,20},{20... | collective-permute-start | bytes 491528 | tf_op jit(solution)/shard_map/ppermute | solution.py:338
  31.4 4.9 %collective-permute-start.6 = (f32[1,128]{1,0:T(1,128)S(1)}, f32[1,128]{1,0:T(1,128)S(1)}, u32[]{:S(2)}, u32[]{:S(2)}) collective-permute-start(f32[1,128]{1,0:T(1,128)S(1)} %compare_select_fusion.factor_ref), channel_id=1, source_target_pairs={{0,8},{2,10},{4,12},{6,14},{8,0},{10,2},{12,4},{14,6},{1,9},{3,11}... | collective-permute-start | bytes 1544 | tf_op jit(solution)/shard_map/ppermute | solution.py:338
  34.8 13.8 %collective-permute-start.7 = (f32[128,1024]{1,0:T(8,128)S(1)}, f32[128,1024]{1,0:T(8,128)S(1)}, u32[]{:S(2)}, u32[]{:S(2)}) collective-permute-start(f32[128,1024]{1,0:T(8,128)S(1)} %get-tuple-element.50), channel_id=1, source_target_pairs={{0,1},{1,0},{2,3},{3,2},{4,5},{5,4},{6,7},{7,6},{8,9},{9,8},{10,11... | collective-permute-start | bytes 1572872 | tf_op jit(solution)/shard_map/ppermute | solution.py:338
  36.9 1.4 %collective-permute-start.11 = (f32[256,128]{1,0:T(8,128)S(1)}, f32[256,128]{1,0:T(8,128)S(1)}, u32[]{:S(2)}, u32[]{:S(2)}) collective-permute-start(f32[256,128]{1,0:T(8,128)S(1)} %down.1.low_ref), channel_id=1, source_target_pairs={{0,1},{1,0},{2,3},{3,2},{4,5},{5,4},{6,7},{7,6},{8,9},{9,8},{10,11... | collective-permute-start | bytes 393224 | tf_op jit(solution)/shard_map/ppermute | solution.py:338
  39.1 7.3 %collective-permute-start.12 = (s16[64,1024]{1,0:T(8,128)(2,1)S(1)}, s16[64,1024]{1,0:T(8,128)(2,1)S(1)}, u32[]{:S(2)}, u32[]{:S(2)}) collective-permute-start(s16[64,1024]{1,0:T(8,128)(2,1)S(1)} %get-tuple-element.66), channel_id=1, source_target_pairs={{0,6},{2,4},{4,2},{6,0},{8,14},{10,12},{12,10},{14,8},{1,7},{3,5},... | collective-permute-start | bytes 393224 | tf_op jit(solution)/shard_map/ppermute | solution.py:338
  42.0 6.4 %collective-permute-start.13 = (s16[64,1024]{1,0:T(8,128)(2,1)S(1)}, s16[64,1024]{1,0:T(8,128)(2,1)S(1)}, u32[]{:S(2)}, u32[]{:S(2)}) collective-permute-start(s16[64,1024]{1,0:T(8,128)(2,1)S(1)} %get-tuple-element.67), channel_id=1, source_target_pairs={{0,4},{2,6},{4,0},{6,2},{8,12},{10,14},{12,8},{14,10},{1,5},{3,7},... | collective-permute-start | bytes 393224 | tf_op jit(solution)/shard_map/ppermute | solution.py:338
  42.2 6.5 %collective-permute-start.14 = (s16[64,1024]{1,0:T(8,128)(2,1)S(1)}, s16[64,1024]{1,0:T(8,128)(2,1)S(1)}, u32[]{:S(2)}, u32[]{:S(2)}) collective-permute-start(s16[64,1024]{1,0:T(8,128)(2,1)S(1)} %get-tuple-element.68), channel_id=1, source_target_pairs={{0,2},{2,0},{4,6},{6,4},{8,10},{10,8},{12,14},{14,12},{1,3},{3,1},... | collective-permute-start | bytes 393224 | tf_op jit(solution)/shard_map/ppermute | solution.py:338

commit v10 on v5

--- a/solution.py
+++ b/solution.py
@@ -12,6 +12,8 @@
 NORM_EPS = 1e-06
 VMEM_LIMIT = 48 * 1024 * 1024
 LANES = 128
+EXPONENT_BITS = 8
+EXPONENT_BIAS = 128
 
 VMEM = pl.BlockSpec(memory_space=pltpu.VMEM)
 HBM = pl.BlockSpec(memory_space=pltpu.HBM)
@@ -53,7 +55,7 @@
 
 
 def far_first(count):
-    return sorted(range(1, count), key=lambda j: (-bin(j).count("1"), j))
+    return sorted(range(1, count), key=lambda j: (-bin(j).count("1"), -j))
 
 
 def return_order(count):
@@ -211,7 +213,7 @@
     shares, outs, term_ref = refs[:groups], refs[groups : groups + buffers], refs[-1]
     rows, rank = low_ref.shape
     size = rows // buffers
-    columns = term_ref.shape[1]
+    columns = up_ref.shape[2]
     share = columns // groups
     which = (iota((rows, 1), 0) // depth) % (2 * local)
     low = low_ref[...] + other_ref[...]
@@ -224,29 +226,33 @@
     )
     for k in range(groups):
         at = pl.multiple_of((group_ref[0] ^ k) * share, share)
-        factors = [up_ref[a, :, pl.ds(at, share)] for a in range(local)]
-        factors += [shares[k][a] for a in range(local)]
+        up = [up_ref[a, :, pl.ds(at, share)] for a in range(local)]
+        up += [shares[k][a] for a in range(local)]
         term = jnp.dot(
-            spread, jnp.concatenate(factors, axis=0), preferred_element_type=jnp.float32
+            spread, jnp.concatenate(up, axis=0), preferred_element_type=jnp.float32
         )
         term_ref[:, pl.ds(at, share)] = term[:rows] + term[rows:]
+    lane = iota((1, LANES), 1)
     for j, out in enumerate(outs):
         term = term_ref[j * size : (j + 1) * size, :]
         top = jnp.max(jnp.abs(term), axis=1, keepdims=True)
         exponent = jnp.ceil(jnp.log2(jnp.maximum(top, 1e-30)) + 1e-3)
-        code = jnp.round(term * jnp.exp2(15.0 - exponent))
-        code = jnp.clip(code, -32767.0, 32767.0)
-        out[:, :columns] = code.astype(jnp.int32).astype(jnp.int16)
-        out[:, columns:] = jnp.broadcast_to(
-            exponent.astype(jnp.int32), (size, LANES)
-        ).astype(jnp.int16)
+        code = jnp.clip(jnp.round(term * jnp.exp2(15.0 - exponent)), -32767.0, 32767.0)
+        code = code.astype(jnp.int32)
+        biased = exponent.astype(jnp.int32) + EXPONENT_BIAS
+        first = code[:, :LANES]
+        marked = (first & -2) | ((biased >> jnp.minimum(lane, EXPONENT_BITS - 1)) & 1)
+        first = jnp.where(lane < EXPONENT_BITS, marked, first)
+        out[:, :LANES] = first.astype(jnp.int16)
+        out[:, LANES:] = code[:, LANES:].astype(jnp.int16)
 
 
 def finish_kernel(
     buffers, pool, local, depth, me_ref, adapter_ref, mine_ref, other_ref, cos_ref, sin_ref, gain_ref, *refs
 ):
     order = [0] + return_order(buffers)
-    ins, out_ref = [refs[order.index(j)] for j in range(buffers)], refs[-1]
+    ins = [refs[order.index(j)] for j in range(buffers)]
+    out_hbm, out_ref, sems = refs[-3:]
     rows, columns = mine_ref.shape
     head = cos_ref.shape[1]
     place = to_column(slot_places(adapter_ref[...], me_ref[0], pool, local, depth))
@@ -261,7 +267,11 @@
         low = jnp.dot(picker, low, preferred_element_type=jnp.float32)
         return high * 256.0 + low
 
-    scale = jnp.exp2(picked(columns, LANES)[:, :1] - 15.0)
+    lane = iota((1, LANES), 1)
+    bits = picked(0, LANES).astype(jnp.int32) & 1
+    bits = jnp.where(lane < EXPONENT_BITS, bits << jnp.minimum(lane, EXPONENT_BITS - 1), 0)
+    exponent = jnp.sum(bits.astype(jnp.float32), axis=1, keepdims=True) - EXPONENT_BIAS
+    scale = jnp.exp2(exponent - 15.0)
     cosine, sine, gain = cos_ref[...], sin_ref[...], gain_ref[...]
     entries = []
     for at in range(0, columns, 2 * head):
@@ -276,10 +286,19 @@
     n = kinds * block
     source = (iota((n, n), 0) % kinds) * block + iota((n, n), 0) // kinds
     order = jnp.where(iota((n, n), 1) == source, 1.0, 0.0).astype(jnp.bfloat16)
+    copies = []
     for i in range(rows // block):
         stacked = jnp.concatenate([e[i * block : (i + 1) * block] for e in entries], axis=0)
         mixed = jnp.dot(order, stacked, preferred_element_type=jnp.float32)
         out_ref[i * n : (i + 1) * n, :] = mixed.astype(jnp.bfloat16)
+        if i % 2:
+            done = pl.ds((i - 1) * n, 2 * n)
+            copies.append(
+                pltpu.make_async_copy(out_ref.at[done, :], out_hbm.at[done, :], sems.at[i // 2])
+            )
+            copies[-1].start()
+    for copy in copies:
+        copy.wait()
 
 
 def body(
@@ -398,9 +417,9 @@
     cosine = jnp.concatenate([cosine, cosine], axis=1)
     sine = jnp.concatenate([-sine, sine], axis=1)
 
-    arrived, far_ups, mine, cosine, sine = lax.optimization_barrier(
-        (arrived, far_ups, mine, cosine, sine)
-    )
+    arrived[1], theirs = lax.optimization_barrier((arrived[1], theirs))
+    other = exchange(theirs, "tp", cores, 1)
+    arrived, mine, cosine, sine = lax.optimization_barrier((arrived, mine, cosine, sine))
     slots = buffers * size
     low = pl.pallas_call(
         functools.partial(down_kernel, buffers, groups, local, depth),
@@ -417,22 +436,24 @@
         functools.partial(up_kernel, buffers, groups, local, depth),
         in_specs=[SMEM] + [VMEM] * (4 + groups),
         out_specs=[VMEM] * buffers,
-        out_shape=[jax.ShapeDtypeStruct((size, columns + LANES), jnp.int16)] * buffers,
+        out_shape=[jax.ShapeDtypeStruct((size, columns), jnp.int16)] * buffers,
         scratch_shapes=[pltpu.VMEM((slots, columns), f32)],
         compiler_params=params(),
         cost_estimate=cost(8 * local * slots * rank * columns, 2 * slots * columns),
         name="up",
     )(group, low, low_other, factor, own_up, *far_ups)
-    terms, theirs = lax.optimization_barrier((terms, theirs))
-    other = exchange(theirs, "tp", cores, 1)
     order = return_order(buffers)
     returned = [terms[0]] + [exchange(terms[j], "pool", pool, j) for j in order]
 
     out = pl.pallas_call(
         functools.partial(finish_kernel, buffers, pool, local, depth),
         in_specs=[SMEM] + [VMEM] * (6 + buffers),
-        out_specs=VMEM,
+        out_specs=HBM,
         out_shape=jax.ShapeDtypeStruct((rows * columns // head, head), bf16),
+        scratch_shapes=[
+            pltpu.VMEM((rows * columns // head, head), bf16),
+            pltpu.SemaphoreType.DMA((rows // 32,)),
+        ],
         compiler_params=params(),
         cost_estimate=cost(4 * rows * slots * columns, 2 * slots * columns),
         name="finish",

time: 50.4 us -> 47.2 us (0.937)
  waiting for transfers between devices: 21.8 us -> 19.1 us
  starting transfers between devices: 15.3 us -> 14.7 us
    ppermute x12, waiting for transfers between devices: 21.8 us -> 19.1 us  [exchange(): return lax.ppermute(x, axis, [(p, p ^ j) for p in range(count)])]
    ppermute x12, starting transfers between devices: 15.3 us -> 14.7 us  [exchange(): return lax.ppermute(x, axis, [(p, p ^ j) for p in range(count)])]
  transfers between devices with their start and end apart: 12 -> 12, of which waited for: 6 -> 7; matrix products, arithmetic and copies ran while one was open for 2% -> 2% of each run, Pallas kernels for 13% -> 17%
where the time goes in v10:
time: 47.2 us; the launch traced here: 47 us
  waiting for transfers between devices  19.1 us (40%)
  starting transfers between devices  14.7 us (31%)
  Pallas kernels  11.3 us (24%)
  other arithmetic  1.08 us (2%)
  between operations  0.74 us (2%)
    ppermute x12, waiting for transfers between devices, exchange(): return lax.ppermute(x, axis, [(p, p ^ j) for p in range(count)])  19.1 us
    ppermute x12, starting transfers between devices, exchange(): return lax.ppermute(x, axis, [(p, p ^ j) for p in range(count)])  14.7 us
    pallas_call x1, Pallas kernels, body(): pl.pallas_call(base_kernel, in_specs=[SMEM] + [HBM] * 4, out_specs=[VMEM]...  5.63 us
    pallas_call x1, Pallas kernels, body(): pl.pallas_call(functools.partial(pick_kernel, pool, local, depth), in_spe...  1.78 us
    pallas_call x1, Pallas kernels, body(): pl.pallas_call(functools.partial(finish_kernel, buffers, pool, local, dep...  1.66 us
    pallas_call x1, Pallas kernels, body(): pl.pallas_call(functools.partial(up_share_kernel, cores), in_specs=[SMEM]...  0.95 us
  transfers between devices with their start and end apart: 12, of which 7 were waited for; matrix products, arithmetic and copies ran while one was open for 2% of the time, Pallas kernels for 17%

profile of v10, /device:TPU:0, one launch (start us, length us, event | category | flops | bytes accessed | tf_op | source)
XLA Modules:
  0.0 47.0 jit_solution(38308555308621888)
XLA Ops:
  0.0 0.0 copy-start
  0.0 0.0 copy-start.1
  0.0 1.8 %pick.1 = (bf16[1,1280,128]{2,1,0:T(8,128)(2,1)S(1)}, bf16[64,2560]{1,0:T(8,128)(2,1)S(1)}, bf16[64,2560]{1,0:T(8,128)(2,1)S(1)}, bf16[64,2560]{1,0:T(8,128)(2,1)S(1)}, bf16[64,2560]{1,0:T(8,128)(2,1)S(1)}) custom-call(s32[1]{0:T(128)} %bitcast.me_ref, s32[1]{0:T(128)} %bitcast.2.group_ref, s32[1,128]{1,0:T(1,128)} %bitcast.8, bf16[128,2560]{1,0:T(8,128)(2,1)} %tokens_hbm.3, ...), custom_call_target="tpu_custom_call" | custom-call | flops 167772160 | bytes 1966080 | tf_op jit(solution)/shard_map/pick/pallas_call | solution.py:341
  1.8 4.1 %collective-permute-start.1 = (bf16[1,1280,128]{2,1,0:T(8,128)(2,1)S(1)}, bf16[1,1280,128]{2,1,0:T(8,128)(2,1)S(1)}, u32[]{:S(2)}, u32[]{:S(2)}) collective-permute-start(bf16[1,1280,128]{2,1,0:T(8,128)(2,1)S(1)} %get-tuple-element.36), channel_id=1, source_target_pairs={{0,8},{2,10},{4,12},{6,14},{8,0},{10,2},{12,4},{14,6},{1,9},{3,11}... | collective-permute-start | bytes 983048 | tf_op jit(solution)/shard_map/ppermute | solution.py:333
  5.9 2.5 %collective-permute-start = (bf16[64,2560]{1,0:T(8,128)(2,1)S(1)}, bf16[64,2560]{1,0:T(8,128)(2,1)S(1)}, u32[]{:S(2)}, u32[]{:S(2)}) collective-permute-start(bf16[64,2560]{1,0:T(8,128)(2,1)S(1)} %get-tuple-element.35), channel_id=1, source_target_pairs={{0,6},{2,4},{4,2},{6,0},{8,14},{10,12},{12,10},{14,8},{1,7},{3,5},... | collective-permute-start | bytes 983048 | tf_op jit(solution)/shard_map/ppermute | solution.py:333
  8.4 0.5 collective-permute-start.2
  8.9 0.5 %collective-permute-start.3 = (bf16[64,2560]{1,0:T(8,128)(2,1)S(1)}, bf16[64,2560]{1,0:T(8,128)(2,1)S(1)}, u32[]{:S(2)}, u32[]{:S(2)}) collective-permute-start(bf16[64,2560]{1,0:T(8,128)(2,1)S(1)} %get-tuple-element.41), channel_id=1, source_target_pairs={{0,2},{2,0},{4,6},{6,4},{8,10},{10,8},{12,14},{14,12},{1,3},{3,1},... | collective-permute-start | bytes 983048 | tf_op jit(solution)/shard_map/ppermute | solution.py:333
  10.0 0.9 %up_share.1 = (bf16[1,128,512]{2,1,0:T(8,128)(2,1)S(1)}, f32[1,128]{1,0:T(1,128)S(1)}) custom-call(s32[1]{0:T(128)} %bitcast.2.group_ref, s32[1]{0:T(128)} %bitcast.3.core_ref, s32[1]{0:T(128)S(6)} %copy.9.ranks_ref, bf16[1,128,2048]{2,1,0:T(8,128)(2,1)} %up_hbm.2), custom_call_target="tpu_custom_call" | custom-call | flops 65536 | bytes 262144 | tf_op jit(solution)/shard_map/up_share/pallas_call | solution.py:363
  11.0 0.1 collective-permute-start.7
  11.1 0.7 %convert_element_type.4 = f32[128]{0:T(128)S(1)} convert(s32[128]{0:T(128)} %param.10) | non-fusion elementwise | flops 128 | bytes 1024 | tf_op jit(solution)/shard_map/convert_element_type | solution.py:415
  11.8 5.6 %base.1 = (f32[128,1024]{1,0:T(8,128)S(1)}, f32[128,1024]{1,0:T(8,128)S(1)}, bf16[1,2560,128]{2,1,0:T(8,128)(2,1)S(1)}, bf16[1,128,1024]{2,1,0:T(8,128)(2,1)S(1)}) custom-call(s32[1]{0:T(128)} %bitcast.3.core_ref, bf16[128,2560]{1,0:T(8,128)(2,1)} %tokens_hbm.3, bf16[2560,2048]{1,0:T(8,128)(2,1)} %weight_hbm.1, bf16[1,2560,128]{2,1,0:T(8,128)(2,1)} %down_hbm.3, ...), custom_call_target="tpu_custom_call" | custom-call | flops 1342177280 | bytes 10485760 | tf_op jit(solution)/shard_map/base/pallas_call | solution.py:382
  17.5 4.1 %collective-permute-done.1.refs_4_ = bf16[1,1280,128]{2,1,0:T(8,128)(2,1)S(1)} collective-permute-done((bf16[1,1280,128]{2,1,0:T(8,128)(2,1)S(1)}, bf16[1,1280,128]{2,1,0:T(8,128)(2,1)S(1)}, u32[]{:S(2)}, u32[]{:S(2)}) %collective-permute-start.1) | collective-permute-done | bytes 327712 | tf_op jit(solution)/shard_map/ppermute | solution.py:333
  21.6 1.8 %collective-permute-start.5 = (bf16[1,1280,128]{2,1,0:T(8,128)(2,1)S(1)}, bf16[1,1280,128]{2,1,0:T(8,128)(2,1)S(1)}, u32[]{:S(2)}, u32[]{:S(2)}) collective-permute-start(bf16[1,1280,128]{2,1,0:T(8,128)(2,1)S(1)} %collective-permute-done.1.refs_4_), channel_id=1, source_target_pairs={{0,16},{16,0},{1,17},{17,1},{2,18},{18,2},{3,19},{19,3},{4,20},{20... | collective-permute-start | bytes 983048 | tf_op jit(solution)/shard_map/ppermute | solution.py:333
  23.4 0.3 fusion
  23.7 2.5 %collective-permute-done.refs_1_ = bf16[64,2560]{1,0:T(8,128)(2,1)S(1)} collective-permute-done((bf16[64,2560]{1,0:T(8,128)(2,1)S(1)}, bf16[64,2560]{1,0:T(8,128)(2,1)S(1)}, u32[]{:S(2)}, u32[]{:S(2)}) %collective-permute-start) | collective-permute-done | bytes 327712 | tf_op jit(solution)/shard_map/ppermute | solution.py:333
  26.2 0.0 collective-permute-start.4
  26.2 0.1 pad_maximum_fusion
  26.3 5.4 %collective-permute-done.2.refs_2_ = bf16[64,2560]{1,0:T(8,128)(2,1)S(1)} collective-permute-done((bf16[64,2560]{1,0:T(8,128)(2,1)S(1)}, bf16[64,2560]{1,0:T(8,128)(2,1)S(1)}, u32[]{:S(2)}, u32[]{:S(2)}) %collective-permute-start.2) | collective-permute-done | bytes 327712 | tf_op jit(solution)/shard_map/ppermute | solution.py:333
  31.8 0.0 collective-permute-done.3.refs_3_
  31.8 0.0 collective-permute-done.7.refs_0_
  31.8 1.5 %collective-permute-start.8 = (bf16[1,128,512]{2,1,0:T(8,128)(2,1)S(1)}, bf16[1,128,512]{2,1,0:T(8,128)(2,1)S(1)}, u32[]{:S(2)}, u32[]{:S(2)}) collective-permute-start(bf16[1,128,512]{2,1,0:T(8,128)(2,1)S(1)} %collective-permute-done.7.refs_0_), channel_id=1, source_target_pairs={{0,16},{16,0},{1,17},{17,1},{2,18},{18,2},{3,19},{19,3},{4,20},{20... | collective-permute-start | bytes 393224 | tf_op jit(solution)/shard_map/ppermute | solution.py:333
  33.3 0.0 collective-permute-done.5.refs_5_
  33.3 0.5 %down.1.low_ref = f32[256,128]{1,0:T(8,128)S(1)} custom-call(s32[1]{0:T(128)} %bitcast.2.group_ref, bf16[1,2560,128]{2,1,0:T(8,128)(2,1)S(1)} %get-tuple-element.47.down_ref, bf16[64,2560]{1,0:T(8,128)(2,1)S(1)} %get-tuple-element.48.refs_0_, bf16[64,2560]{1,0:T(8,128)(2,1)S(1)} %collective-permute-done.refs_1_, ...), custom_call_target="tpu_custom_call" | custom-call | flops 335544320 | bytes 1966080 | tf_op jit(solution)/shard_map/down/pallas_call | solution.py:424
  33.8 0.1 collective-permute-start.6
  33.9 2.8 %collective-permute-done.8.refs_1_ = bf16[1,128,512]{2,1,0:T(8,128)(2,1)S(1)} collective-permute-done((bf16[1,128,512]{2,1,0:T(8,128)(2,1)S(1)}, bf16[1,128,512]{2,1,0:T(8,128)(2,1)S(1)}, u32[]{:S(2)}, u32[]{:S(2)}) %collective-permute-start.8) | collective-permute-done | bytes 131104 | tf_op jit(solution)/shard_map/ppermute | solution.py:333
  36.7 0.0 collective-permute-done.6.other_ref
  36.7 0.8 %up.1 = (s16[64,1024]{1,0:T(8,128)(2,1)S(1)}, s16[64,1024]{1,0:T(8,128)(2,1)S(1)}, s16[64,1024]{1,0:T(8,128)(2,1)S(1)}, s16[64,1024]{1,0:T(8,128)(2,1)S(1)}) custom-call(s32[1]{0:T(128)} %bitcast.2.group_ref, f32[256,128]{1,0:T(8,128)S(1)} %down.1.low_ref, f32[256,128]{1,0:T(8,128)S(1)} %collective-permute-done.6.other_ref, ...), custom_call_target="tpu_custom_call" | custom-call | flops 268435456 | bytes 524288 | tf_op jit(solution)/shard_map/up/pallas_call | solution.py:435
  37.5 1.4 %collective-permute-start.10 = (s16[64,1024]{1,0:T(8,128)(2,1)S(1)}, s16[64,1024]{1,0:T(8,128)(2,1)S(1)}, u32[]{:S(2)}, u32[]{:S(2)}) collective-permute-start(s16[64,1024]{1,0:T(8,128)(2,1)S(1)} %get-tuple-element.61), channel_id=1, source_target_pairs={{0,6},{2,4},{4,2},{6,0},{8,14},{10,12},{12,10},{14,8},{1,7},{3,5},... | collective-permute-start | bytes 393224 | tf_op jit(solution)/shard_map/ppermute | solution.py:333
  39.0 0.6 %collective-permute-start.11 = (s16[64,1024]{1,0:T(8,128)(2,1)S(1)}, s16[64,1024]{1,0:T(8,128)(2,1)S(1)}, u32[]{:S(2)}, u32[]{:S(2)}) collective-permute-start(s16[64,1024]{1,0:T(8,128)(2,1)S(1)} %get-tuple-element.62), channel_id=1, source_target_pairs={{0,4},{2,6},{4,0},{6,2},{8,12},{10,14},{12,8},{14,10},{1,5},{3,7},... | collective-permute-start | bytes 393224 | tf_op jit(solution)/shard_map/ppermute | solution.py:333
  39.6 1.5 %collective-permute-start.9 = (s16[64,1024]{1,0:T(8,128)(2,1)S(1)}, s16[64,1024]{1,0:T(8,128)(2,1)S(1)}, u32[]{:S(2)}, u32[]{:S(2)}) collective-permute-start(s16[64,1024]{1,0:T(8,128)(2,1)S(1)} %get-tuple-element.60), channel_id=1, source_target_pairs={{0,2},{2,0},{4,6},{6,4},{8,10},{10,8},{12,14},{14,12},{1,3},{3,1},... | collective-permute-start | bytes 393224 | tf_op jit(solution)/shard_map/ppermute | solution.py:333
  41.1 0.0 copy-done.1
  41.1 0.0 collective-permute-done.4.other_ref
  41.1 3.0 %collective-permute-done.10.refs_2_ = s16[64,1024]{1,0:T(8,128)(2,1)S(1)} collective-permute-done((s16[64,1024]{1,0:T(8,128)(2,1)S(1)}, s16[64,1024]{1,0:T(8,128)(2,1)S(1)}, u32[]{:S(2)}, u32[]{:S(2)}) %collective-permute-start.10) | collective-permute-done | bytes 131104 | tf_op jit(solution)/shard_map/ppermute | solution.py:333
  44.0 0.4 collective-permute-done.11.refs_3_
  44.5 0.9 %collective-permute-done.9.refs_1_ = s16[64,1024]{1,0:T(8,128)(2,1)S(1)} collective-permute-done((s16[64,1024]{1,0:T(8,128)(2,1)S(1)}, s16[64,1024]{1,0:T(8,128)(2,1)S(1)}, u32[]{:S(2)}, u32[]{:S(2)}) %collective-permute-start.9) | collective-permute-done | bytes 131104 | tf_op jit(solution)/shard_map/ppermute | solution.py:333
  45.4 0.0 copy-done
  45.4 1.7 %finish.1 = bf16[1024,128]{1,0:T(8,128)(2,1)} custom-call(s32[1]{0:T(128)} %bitcast.me_ref, s32[1,128]{1,0:T(1,128)S(1)} %bitcast.9, f32[128,1024]{1,0:T(8,128)S(1)} %get-tuple-element.43.mine_ref, f32[128,1024]{1,0:T(8,128)S(1)} %collective-permute-done.4.other_ref, f32[128,128]{1,0:T(8,128)S(1)} %get-tuple-element.45.cos_ref, ...), custom_call_target="tpu_custom_call" | custom-call | flops 134217728 | bytes 524288 | tf_op jit(solution)/shard_map/finish/pallas_call | solution.py:448
  (2 shorter events, 0.0 us)
Async XLA Ops:
  0.0 45.4 %copy-start = (s32[128,1]{0,1:T(1,128)S(1)}, s32[128,1]{0,1:T(1,128)}, u32[]{:S(2)}) copy-start(s32[128,1]{0,1:T(1,128)} %param.9) | copy-start | bytes 1540
  0.0 41.1 %copy-start.1 = (bf16[128]{0:T(256)(128)(2,1)S(1)}, bf16[128]{0:T(256)(128)(2,1)}, u32[]{:S(2)}) copy-start(bf16[128]{0:T(256)(128)(2,1)} %param.15) | copy-start | bytes 772
  1.8 19.8 %collective-permute-start.1 = (bf16[1,1280,128]{2,1,0:T(8,128)(2,1)S(1)}, bf16[1,1280,128]{2,1,0:T(8,128)(2,1)S(1)}, u32[]{:S(2)}, u32[]{:S(2)}) collective-permute-start(bf16[1,1280,128]{2,1,0:T(8,128)(2,1)S(1)} %get-tuple-element.36), channel_id=1, source_target_pairs={{0,8},{2,10},{4,12},{6,14},{8,0},{10,2},{12,4},{14,6},{1,9},{3,11}... | collective-permute-start | bytes 983048 | tf_op jit(solution)/shard_map/ppermute | solution.py:333
  5.9 20.3 %collective-permute-start = (bf16[64,2560]{1,0:T(8,128)(2,1)S(1)}, bf16[64,2560]{1,0:T(8,128)(2,1)S(1)}, u32[]{:S(2)}, u32[]{:S(2)}) collective-permute-start(bf16[64,2560]{1,0:T(8,128)(2,1)S(1)} %get-tuple-element.35), channel_id=1, source_target_pairs={{0,6},{2,4},{4,2},{6,0},{8,14},{10,12},{12,10},{14,8},{1,7},{3,5},... | collective-permute-start | bytes 983048 | tf_op jit(solution)/shard_map/ppermute | solution.py:333
  8.4 23.3 %collective-permute-start.2 = (bf16[64,2560]{1,0:T(8,128)(2,1)S(1)}, bf16[64,2560]{1,0:T(8,128)(2,1)S(1)}, u32[]{:S(2)}, u32[]{:S(2)}) collective-permute-start(bf16[64,2560]{1,0:T(8,128)(2,1)S(1)} %get-tuple-element.40), channel_id=1, source_target_pairs={{0,4},{2,6},{4,0},{6,2},{8,12},{10,14},{12,8},{14,10},{1,5},{3,7},... | collective-permute-start | bytes 983048 | tf_op jit(solution)/shard_map/ppermute | solution.py:333
  8.9 22.9 %collective-permute-start.3 = (bf16[64,2560]{1,0:T(8,128)(2,1)S(1)}, bf16[64,2560]{1,0:T(8,128)(2,1)S(1)}, u32[]{:S(2)}, u32[]{:S(2)}) collective-permute-start(bf16[64,2560]{1,0:T(8,128)(2,1)S(1)} %get-tuple-element.41), channel_id=1, source_target_pairs={{0,2},{2,0},{4,6},{6,4},{8,10},{10,8},{12,14},{14,12},{1,3},{3,1},... | collective-permute-start | bytes 983048 | tf_op jit(solution)/shard_map/ppermute | solution.py:333
  11.0 20.8 %collective-permute-start.7 = (bf16[1,128,512]{2,1,0:T(8,128)(2,1)S(1)}, bf16[1,128,512]{2,1,0:T(8,128)(2,1)S(1)}, u32[]{:S(2)}, u32[]{:S(2)}) collective-permute-start(bf16[1,128,512]{2,1,0:T(8,128)(2,1)S(1)} %get-tuple-element.57), channel_id=1, source_target_pairs={{0,8},{2,10},{4,12},{6,14},{8,0},{10,2},{12,4},{14,6},{1,9},{3,11}... | collective-permute-start | bytes 393224 | tf_op jit(solution)/shard_map/ppermute | solution.py:333
  21.6 11.7 %collective-permute-start.5 = (bf16[1,1280,128]{2,1,0:T(8,128)(2,1)S(1)}, bf16[1,1280,128]{2,1,0:T(8,128)(2,1)S(1)}, u32[]{:S(2)}, u32[]{:S(2)}) collective-permute-start(bf16[1,1280,128]{2,1,0:T(8,128)(2,1)S(1)} %collective-permute-done.1.refs_4_), channel_id=1, source_target_pairs={{0,16},{16,0},{1,17},{17,1},{2,18},{18,2},{3,19},{19,3},{4,20},{20... | collective-permute-start | bytes 983048 | tf_op jit(solution)/shard_map/ppermute | solution.py:333
  26.2 14.9 %collective-permute-start.4 = (f32[128,1024]{1,0:T(8,128)S(1)}, f32[128,1024]{1,0:T(8,128)S(1)}, u32[]{:S(2)}, u32[]{:S(2)}) collective-permute-start(f32[128,1024]{1,0:T(8,128)S(1)} %get-tuple-element.44), channel_id=1, source_target_pairs={{0,1},{1,0},{2,3},{3,2},{4,5},{5,4},{6,7},{7,6},{8,9},{9,8},{10,11... | collective-permute-start | bytes 1572872 | tf_op jit(solution)/shard_map/ppermute | solution.py:333
  31.8 5.0 %collective-permute-start.8 = (bf16[1,128,512]{2,1,0:T(8,128)(2,1)S(1)}, bf16[1,128,512]{2,1,0:T(8,128)(2,1)S(1)}, u32[]{:S(2)}, u32[]{:S(2)}) collective-permute-start(bf16[1,128,512]{2,1,0:T(8,128)(2,1)S(1)} %collective-permute-done.7.refs_0_), channel_id=1, source_target_pairs={{0,16},{16,0},{1,17},{17,1},{2,18},{18,2},{3,19},{19,3},{4,20},{20... | collective-permute-start | bytes 393224 | tf_op jit(solution)/shard_map/ppermute | solution.py:333
  33.8 2.9 %collective-permute-start.6 = (f32[256,128]{1,0:T(8,128)S(1)}, f32[256,128]{1,0:T(8,128)S(1)}, u32[]{:S(2)}, u32[]{:S(2)}) collective-permute-start(f32[256,128]{1,0:T(8,128)S(1)} %down.1.low_ref), channel_id=1, source_target_pairs={{0,1},{1,0},{2,3},{3,2},{4,5},{5,4},{6,7},{7,6},{8,9},{9,8},{10,11... | collective-permute-start | bytes 393224 | tf_op jit(solution)/shard_map/ppermute | solution.py:333
  37.5 6.5 %collective-permute-start.10 = (s16[64,1024]{1,0:T(8,128)(2,1)S(1)}, s16[64,1024]{1,0:T(8,128)(2,1)S(1)}, u32[]{:S(2)}, u32[]{:S(2)}) collective-permute-start(s16[64,1024]{1,0:T(8,128)(2,1)S(1)} %get-tuple-element.61), channel_id=1, source_target_pairs={{0,6},{2,4},{4,2},{6,0},{8,14},{10,12},{12,10},{14,8},{1,7},{3,5},... | collective-permute-start | bytes 393224 | tf_op jit(solution)/shard_map/ppermute | solution.py:333
  39.0 5.5 %collective-permute-start.11 = (s16[64,1024]{1,0:T(8,128)(2,1)S(1)}, s16[64,1024]{1,0:T(8,128)(2,1)S(1)}, u32[]{:S(2)}, u32[]{:S(2)}) collective-permute-start(s16[64,1024]{1,0:T(8,128)(2,1)S(1)} %get-tuple-element.62), channel_id=1, source_target_pairs={{0,4},{2,6},{4,0},{6,2},{8,12},{10,14},{12,8},{14,10},{1,5},{3,7},... | collective-permute-start | bytes 393224 | tf_op jit(solution)/shard_map/ppermute | solution.py:333
  39.6 5.8 %collective-permute-start.9 = (s16[64,1024]{1,0:T(8,128)(2,1)S(1)}, s16[64,1024]{1,0:T(8,128)(2,1)S(1)}, u32[]{:S(2)}, u32[]{:S(2)}) collective-permute-start(s16[64,1024]{1,0:T(8,128)(2,1)S(1)} %get-tuple-element.60), channel_id=1, source_target_pairs={{0,2},{2,0},{4,6},{6,4},{8,10},{10,8},{12,14},{14,12},{1,3},{3,1},... | collective-permute-start | bytes 393224 | tf_op jit(solution)/shard_map/ppermute | solution.py:333

commit v11 on v10

--- a/solution.py
+++ b/solution.py
@@ -417,7 +417,7 @@
     cosine = jnp.concatenate([cosine, cosine], axis=1)
     sine = jnp.concatenate([-sine, sine], axis=1)
 
-    arrived[1], theirs = lax.optimization_barrier((arrived[1], theirs))
+    far_up, theirs = lax.optimization_barrier((far_up, theirs))
     other = exchange(theirs, "tp", cores, 1)
     arrived, mine, cosine, sine = lax.optimization_barrier((arrived, mine, cosine, sine))
     slots = buffers * size

time: 47.2 us -> 48.1 us (1.019)
  starting transfers between devices: 14.7 us -> 15.2 us
    ppermute x12, starting transfers between devices: 14.7 us -> 15.2 us  [exchange(): return lax.ppermute(x, axis, [(p, p ^ j) for p in range(count)])]
  transfers between devices with their start and end apart: 12 -> 12, of which waited for: 7 -> 7; matrix products, arithmetic and copies ran while one was open for 2% -> 2% of each run, Pallas kernels for 17% -> 16%
where the time goes in v11:
time: 48.1 us; the launch traced here: 47.9 us
  waiting for transfers between devices  19.5 us (41%)
  starting transfers between devices  15.2 us (32%)
  Pallas kernels  11.3 us (23%)
  other arithmetic  1.08 us (2%)
  between operations  0.74 us (2%)
    ppermute x12, waiting for transfers between devices, exchange(): return lax.ppermute(x, axis, [(p, p ^ j) for p in range(count)])  19.5 us
    ppermute x12, starting transfers between devices, exchange(): return lax.ppermute(x, axis, [(p, p ^ j) for p in range(count)])  15.2 us
    pallas_call x1, Pallas kernels, body(): pl.pallas_call(base_kernel, in_specs=[SMEM] + [HBM] * 4, out_specs=[VMEM]...  5.64 us
    pallas_call x1, Pallas kernels, body(): pl.pallas_call(functools.partial(pick_kernel, pool, local, depth), in_spe...  1.78 us
    pallas_call x1, Pallas kernels, body(): pl.pallas_call(functools.partial(finish_kernel, buffers, pool, local, dep...  1.66 us
  transfers between devices with their start and end apart: 12, of which 7 were waited for; matrix products, arithmetic and copies ran while one was open for 2% of the time, Pallas kernels for 16%

profile of v11, /device:TPU:0, one launch (start us, length us, event | category | flops | bytes accessed | tf_op | source)
XLA Modules:
  0.0 47.9 jit_solution(5662264300684971446)
XLA Ops:
  0.0 0.0 copy-start
  0.0 0.0 copy-start.1
  0.0 1.8 %pick.1 = (bf16[1,1280,128]{2,1,0:T(8,128)(2,1)S(1)}, bf16[64,2560]{1,0:T(8,128)(2,1)S(1)}, bf16[64,2560]{1,0:T(8,128)(2,1)S(1)}, bf16[64,2560]{1,0:T(8,128)(2,1)S(1)}, bf16[64,2560]{1,0:T(8,128)(2,1)S(1)}) custom-call(s32[1]{0:T(128)} %bitcast.me_ref, s32[1]{0:T(128)} %bitcast.2.group_ref, s32[1,128]{1,0:T(1,128)} %bitcast.8, bf16[128,2560]{1,0:T(8,128)(2,1)} %tokens_hbm.3, ...), custom_call_target="tpu_custom_call" | custom-call | flops 167772160 | bytes 1966080 | tf_op jit(solution)/shard_map/pick/pallas_call | solution.py:341
  1.8 4.1 %collective-permute-start.4 = (bf16[1,1280,128]{2,1,0:T(8,128)(2,1)S(1)}, bf16[1,1280,128]{2,1,0:T(8,128)(2,1)S(1)}, u32[]{:S(2)}, u32[]{:S(2)}) collective-permute-start(bf16[1,1280,128]{2,1,0:T(8,128)(2,1)S(1)} %get-tuple-element.42), channel_id=1, source_target_pairs={{0,8},{2,10},{4,12},{6,14},{8,0},{10,2},{12,4},{14,6},{1,9},{3,11}... | collective-permute-start | bytes 983048 | tf_op jit(solution)/shard_map/ppermute | solution.py:333
  5.9 2.5 %collective-permute-start = (bf16[64,2560]{1,0:T(8,128)(2,1)S(1)}, bf16[64,2560]{1,0:T(8,128)(2,1)S(1)}, u32[]{:S(2)}, u32[]{:S(2)}) collective-permute-start(bf16[64,2560]{1,0:T(8,128)(2,1)S(1)} %get-tuple-element.34), channel_id=1, source_target_pairs={{0,6},{2,4},{4,2},{6,0},{8,14},{10,12},{12,10},{14,8},{1,7},{3,5},... | collective-permute-start | bytes 983048 | tf_op jit(solution)/shard_map/ppermute | solution.py:333
  8.4 0.5 collective-permute-start.1
  8.9 0.5 %collective-permute-start.2 = (bf16[64,2560]{1,0:T(8,128)(2,1)S(1)}, bf16[64,2560]{1,0:T(8,128)(2,1)S(1)}, u32[]{:S(2)}, u32[]{:S(2)}) collective-permute-start(bf16[64,2560]{1,0:T(8,128)(2,1)S(1)} %get-tuple-element.36), channel_id=1, source_target_pairs={{0,2},{2,0},{4,6},{6,4},{8,10},{10,8},{12,14},{14,12},{1,3},{3,1},... | collective-permute-start | bytes 983048 | tf_op jit(solution)/shard_map/ppermute | solution.py:333
  10.0 0.9 %up_share.1 = (bf16[1,128,512]{2,1,0:T(8,128)(2,1)S(1)}, f32[1,128]{1,0:T(1,128)S(1)}) custom-call(s32[1]{0:T(128)} %bitcast.2.group_ref, s32[1]{0:T(128)} %bitcast.3.core_ref, s32[1]{0:T(128)S(6)} %copy.9.ranks_ref, bf16[1,128,2048]{2,1,0:T(8,128)(2,1)} %up_hbm.2), custom_call_target="tpu_custom_call" | custom-call | flops 65536 | bytes 262144 | tf_op jit(solution)/shard_map/up_share/pallas_call | solution.py:363
  11.0 0.1 collective-permute-start.3
  11.1 0.7 %convert_element_type.4 = f32[128]{0:T(128)S(1)} convert(s32[128]{0:T(128)} %param.10) | non-fusion elementwise | flops 128 | bytes 1024 | tf_op jit(solution)/shard_map/convert_element_type | solution.py:415
  11.8 5.6 %base.1 = (f32[128,1024]{1,0:T(8,128)S(1)}, f32[128,1024]{1,0:T(8,128)S(1)}, bf16[1,2560,128]{2,1,0:T(8,128)(2,1)S(1)}, bf16[1,128,1024]{2,1,0:T(8,128)(2,1)S(1)}) custom-call(s32[1]{0:T(128)} %bitcast.3.core_ref, bf16[128,2560]{1,0:T(8,128)(2,1)} %tokens_hbm.3, bf16[2560,2048]{1,0:T(8,128)(2,1)} %weight_hbm.1, bf16[1,2560,128]{2,1,0:T(8,128)(2,1)} %down_hbm.3, ...), custom_call_target="tpu_custom_call" | custom-call | flops 1342177280 | bytes 10485760 | tf_op jit(solution)/shard_map/base/pallas_call | solution.py:382
  17.5 4.1 %collective-permute-done.4.refs_4_ = bf16[1,1280,128]{2,1,0:T(8,128)(2,1)S(1)} collective-permute-done((bf16[1,1280,128]{2,1,0:T(8,128)(2,1)S(1)}, bf16[1,1280,128]{2,1,0:T(8,128)(2,1)S(1)}, u32[]{:S(2)}, u32[]{:S(2)}) %collective-permute-start.4) | collective-permute-done | bytes 327712 | tf_op jit(solution)/shard_map/ppermute | solution.py:333
  21.6 1.8 %collective-permute-start.6 = (bf16[1,1280,128]{2,1,0:T(8,128)(2,1)S(1)}, bf16[1,1280,128]{2,1,0:T(8,128)(2,1)S(1)}, u32[]{:S(2)}, u32[]{:S(2)}) collective-permute-start(bf16[1,1280,128]{2,1,0:T(8,128)(2,1)S(1)} %collective-permute-done.4.refs_4_), channel_id=1, source_target_pairs={{0,16},{16,0},{1,17},{17,1},{2,18},{18,2},{3,19},{19,3},{4,20},{20... | collective-permute-start | bytes 983048 | tf_op jit(solution)/shard_map/ppermute | solution.py:333
  23.4 0.3 fusion
  23.7 6.1 %collective-permute-done.3.refs_0_ = bf16[1,128,512]{2,1,0:T(8,128)(2,1)S(1)} collective-permute-done((bf16[1,128,512]{2,1,0:T(8,128)(2,1)S(1)}, bf16[1,128,512]{2,1,0:T(8,128)(2,1)S(1)}, u32[]{:S(2)}, u32[]{:S(2)}) %collective-permute-start.3) | collective-permute-done | bytes 131104 | tf_op jit(solution)/shard_map/ppermute | solution.py:333
  29.8 0.0 collective-permute-start.5
  29.8 0.1 pad_maximum_fusion
  29.9 0.0 collective-permute-done.refs_1_
  29.9 1.6 %collective-permute-start.8 = (bf16[1,128,512]{2,1,0:T(8,128)(2,1)S(1)}, bf16[1,128,512]{2,1,0:T(8,128)(2,1)S(1)}, u32[]{:S(2)}, u32[]{:S(2)}) collective-permute-start(bf16[1,128,512]{2,1,0:T(8,128)(2,1)S(1)} %collective-permute-done.3.refs_0_), channel_id=1, source_target_pairs={{0,16},{16,0},{1,17},{17,1},{2,18},{18,2},{3,19},{19,3},{4,20},{20... | collective-permute-start | bytes 393224 | tf_op jit(solution)/shard_map/ppermute | solution.py:333
  31.5 0.3 collective-permute-done.1.refs_2_
  31.8 0.0 collective-permute-done.2.refs_3_
  31.8 0.0 collective-permute-done.6.refs_5_
  31.8 0.5 %down.1.low_ref = f32[256,128]{1,0:T(8,128)S(1)} custom-call(s32[1]{0:T(128)} %bitcast.2.group_ref, bf16[1,2560,128]{2,1,0:T(8,128)(2,1)S(1)} %get-tuple-element.50.down_ref, bf16[64,2560]{1,0:T(8,128)(2,1)S(1)} %get-tuple-element.51.refs_0_, bf16[64,2560]{1,0:T(8,128)(2,1)S(1)} %collective-permute-done.refs_1_, ...), custom_call_target="tpu_custom_call" | custom-call | flops 335544320 | bytes 1966080 | tf_op jit(solution)/shard_map/down/pallas_call | solution.py:424
  32.3 0.1 collective-permute-start.7
  32.4 3.5 %collective-permute-done.8.refs_1_ = bf16[1,128,512]{2,1,0:T(8,128)(2,1)S(1)} collective-permute-done((bf16[1,128,512]{2,1,0:T(8,128)(2,1)S(1)}, bf16[1,128,512]{2,1,0:T(8,128)(2,1)S(1)}, u32[]{:S(2)}, u32[]{:S(2)}) %collective-permute-start.8) | collective-permute-done | bytes 131104 | tf_op jit(solution)/shard_map/ppermute | solution.py:333
  35.9 0.0 collective-permute-done.7.other_ref
  35.9 0.8 %up.1 = (s16[64,1024]{1,0:T(8,128)(2,1)S(1)}, s16[64,1024]{1,0:T(8,128)(2,1)S(1)}, s16[64,1024]{1,0:T(8,128)(2,1)S(1)}, s16[64,1024]{1,0:T(8,128)(2,1)S(1)}) custom-call(s32[1]{0:T(128)} %bitcast.2.group_ref, f32[256,128]{1,0:T(8,128)S(1)} %down.1.low_ref, f32[256,128]{1,0:T(8,128)S(1)} %collective-permute-done.7.other_ref, ...), custom_call_target="tpu_custom_call" | custom-call | flops 268435456 | bytes 524288 | tf_op jit(solution)/shard_map/up/pallas_call | solution.py:435
  36.7 3.4 %collective-permute-start.10 = (s16[64,1024]{1,0:T(8,128)(2,1)S(1)}, s16[64,1024]{1,0:T(8,128)(2,1)S(1)}, u32[]{:S(2)}, u32[]{:S(2)}) collective-permute-start(s16[64,1024]{1,0:T(8,128)(2,1)S(1)} %get-tuple-element.59), channel_id=1, source_target_pairs={{0,6},{2,4},{4,2},{6,0},{8,14},{10,12},{12,10},{14,8},{1,7},{3,5},... | collective-permute-start | bytes 393224 | tf_op jit(solution)/shard_map/ppermute | solution.py:333
  40.1 0.0 collective-permute-start.11
  40.1 0.6 %collective-permute-start.9 = (s16[64,1024]{1,0:T(8,128)(2,1)S(1)}, s16[64,1024]{1,0:T(8,128)(2,1)S(1)}, u32[]{:S(2)}, u32[]{:S(2)}) collective-permute-start(s16[64,1024]{1,0:T(8,128)(2,1)S(1)} %get-tuple-element.58), channel_id=1, source_target_pairs={{0,2},{2,0},{4,6},{6,4},{8,10},{10,8},{12,14},{14,12},{1,3},{3,1},... | collective-permute-start | bytes 393224 | tf_op jit(solution)/shard_map/ppermute | solution.py:333
  40.7 0.0 copy-done.1
  40.7 0.0 collective-permute-done.5.other_ref
  40.7 3.7 %collective-permute-done.10.refs_2_ = s16[64,1024]{1,0:T(8,128)(2,1)S(1)} collective-permute-done((s16[64,1024]{1,0:T(8,128)(2,1)S(1)}, s16[64,1024]{1,0:T(8,128)(2,1)S(1)}, u32[]{:S(2)}, u32[]{:S(2)}) %collective-permute-start.10) | collective-permute-done | bytes 131104 | tf_op jit(solution)/shard_map/ppermute | solution.py:333
  44.4 1.2 %collective-permute-done.11.refs_3_ = s16[64,1024]{1,0:T(8,128)(2,1)S(1)} collective-permute-done((s16[64,1024]{1,0:T(8,128)(2,1)S(1)}, s16[64,1024]{1,0:T(8,128)(2,1)S(1)}, u32[]{:S(2)}, u32[]{:S(2)}) %collective-permute-start.11) | collective-permute-done | bytes 131104 | tf_op jit(solution)/shard_map/ppermute | solution.py:333
  45.6 0.6 %collective-permute-done.9.refs_1_ = s16[64,1024]{1,0:T(8,128)(2,1)S(1)} collective-permute-done((s16[64,1024]{1,0:T(8,128)(2,1)S(1)}, s16[64,1024]{1,0:T(8,128)(2,1)S(1)}, u32[]{:S(2)}, u32[]{:S(2)}) %collective-permute-start.9) | collective-permute-done | bytes 131104 | tf_op jit(solution)/shard_map/ppermute | solution.py:333
  46.3 0.0 copy-done
  46.3 1.7 %finish.1 = bf16[1024,128]{1,0:T(8,128)(2,1)} custom-call(s32[1]{0:T(128)} %bitcast.me_ref, s32[1,128]{1,0:T(1,128)S(1)} %bitcast.9, f32[128,1024]{1,0:T(8,128)S(1)} %get-tuple-element.38.mine_ref, f32[128,1024]{1,0:T(8,128)S(1)} %collective-permute-done.5.other_ref, f32[128,128]{1,0:T(8,128)S(1)} %get-tuple-element.48.cos_ref, ...), custom_call_target="tpu_custom_call" | custom-call | flops 134217728 | bytes 524288 | tf_op jit(solution)/shard_map/finish/pallas_call | solution.py:448
  (2 shorter events, 0.0 us)
Async XLA Ops:
  0.0 46.3 %copy-start = (s32[128,1]{0,1:T(1,128)S(1)}, s32[128,1]{0,1:T(1,128)}, u32[]{:S(2)}) copy-start(s32[128,1]{0,1:T(1,128)} %param.9) | copy-start | bytes 1540
  0.0 40.7 %copy-start.1 = (bf16[128]{0:T(256)(128)(2,1)S(1)}, bf16[128]{0:T(256)(128)(2,1)}, u32[]{:S(2)}) copy-start(bf16[128]{0:T(256)(128)(2,1)} %param.15) | copy-start | bytes 772
  1.8 19.8 %collective-permute-start.4 = (bf16[1,1280,128]{2,1,0:T(8,128)(2,1)S(1)}, bf16[1,1280,128]{2,1,0:T(8,128)(2,1)S(1)}, u32[]{:S(2)}, u32[]{:S(2)}) collective-permute-start(bf16[1,1280,128]{2,1,0:T(8,128)(2,1)S(1)} %get-tuple-element.42), channel_id=1, source_target_pairs={{0,8},{2,10},{4,12},{6,14},{8,0},{10,2},{12,4},{14,6},{1,9},{3,11}... | collective-permute-start | bytes 983048 | tf_op jit(solution)/shard_map/ppermute | solution.py:333
  5.9 24.0 %collective-permute-start = (bf16[64,2560]{1,0:T(8,128)(2,1)S(1)}, bf16[64,2560]{1,0:T(8,128)(2,1)S(1)}, u32[]{:S(2)}, u32[]{:S(2)}) collective-permute-start(bf16[64,2560]{1,0:T(8,128)(2,1)S(1)} %get-tuple-element.34), channel_id=1, source_target_pairs={{0,6},{2,4},{4,2},{6,0},{8,14},{10,12},{12,10},{14,8},{1,7},{3,5},... | collective-permute-start | bytes 983048 | tf_op jit(solution)/shard_map/ppermute | solution.py:333
  8.4 23.3 %collective-permute-start.1 = (bf16[64,2560]{1,0:T(8,128)(2,1)S(1)}, bf16[64,2560]{1,0:T(8,128)(2,1)S(1)}, u32[]{:S(2)}, u32[]{:S(2)}) collective-permute-start(bf16[64,2560]{1,0:T(8,128)(2,1)S(1)} %get-tuple-element.35), channel_id=1, source_target_pairs={{0,4},{2,6},{4,0},{6,2},{8,12},{10,14},{12,8},{14,10},{1,5},{3,7},... | collective-permute-start | bytes 983048 | tf_op jit(solution)/shard_map/ppermute | solution.py:333
  8.9 22.9 %collective-permute-start.2 = (bf16[64,2560]{1,0:T(8,128)(2,1)S(1)}, bf16[64,2560]{1,0:T(8,128)(2,1)S(1)}, u32[]{:S(2)}, u32[]{:S(2)}) collective-permute-start(bf16[64,2560]{1,0:T(8,128)(2,1)S(1)} %get-tuple-element.36), channel_id=1, source_target_pairs={{0,2},{2,0},{4,6},{6,4},{8,10},{10,8},{12,14},{14,12},{1,3},{3,1},... | collective-permute-start | bytes 983048 | tf_op jit(solution)/shard_map/ppermute | solution.py:333
  11.0 18.8 %collective-permute-start.3 = (bf16[1,128,512]{2,1,0:T(8,128)(2,1)S(1)}, bf16[1,128,512]{2,1,0:T(8,128)(2,1)S(1)}, u32[]{:S(2)}, u32[]{:S(2)}) collective-permute-start(bf16[1,128,512]{2,1,0:T(8,128)(2,1)S(1)} %get-tuple-element.41), channel_id=1, source_target_pairs={{0,8},{2,10},{4,12},{6,14},{8,0},{10,2},{12,4},{14,6},{1,9},{3,11}... | collective-permute-start | bytes 393224 | tf_op jit(solution)/shard_map/ppermute | solution.py:333
  21.6 10.2 %collective-permute-start.6 = (bf16[1,1280,128]{2,1,0:T(8,128)(2,1)S(1)}, bf16[1,1280,128]{2,1,0:T(8,128)(2,1)S(1)}, u32[]{:S(2)}, u32[]{:S(2)}) collective-permute-start(bf16[1,1280,128]{2,1,0:T(8,128)(2,1)S(1)} %collective-permute-done.4.refs_4_), channel_id=1, source_target_pairs={{0,16},{16,0},{1,17},{17,1},{2,18},{18,2},{3,19},{19,3},{4,20},{20... | collective-permute-start | bytes 983048 | tf_op jit(solution)/shard_map/ppermute | solution.py:333
  29.8 10.9 %collective-permute-start.5 = (f32[128,1024]{1,0:T(8,128)S(1)}, f32[128,1024]{1,0:T(8,128)S(1)}, u32[]{:S(2)}, u32[]{:S(2)}) collective-permute-start(f32[128,1024]{1,0:T(8,128)S(1)} %get-tuple-element.47), channel_id=1, source_target_pairs={{0,1},{1,0},{2,3},{3,2},{4,5},{5,4},{6,7},{7,6},{8,9},{9,8},{10,11... | collective-permute-start | bytes 1572872 | tf_op jit(solution)/shard_map/ppermute | solution.py:333
  29.9 6.0 %collective-permute-start.8 = (bf16[1,128,512]{2,1,0:T(8,128)(2,1)S(1)}, bf16[1,128,512]{2,1,0:T(8,128)(2,1)S(1)}, u32[]{:S(2)}, u32[]{:S(2)}) collective-permute-start(bf16[1,128,512]{2,1,0:T(8,128)(2,1)S(1)} %collective-permute-done.3.refs_0_), channel_id=1, source_target_pairs={{0,16},{16,0},{1,17},{17,1},{2,18},{18,2},{3,19},{19,3},{4,20},{20... | collective-permute-start | bytes 393224 | tf_op jit(solution)/shard_map/ppermute | solution.py:333
  32.3 3.6 %collective-permute-start.7 = (f32[256,128]{1,0:T(8,128)S(1)}, f32[256,128]{1,0:T(8,128)S(1)}, u32[]{:S(2)}, u32[]{:S(2)}) collective-permute-start(f32[256,128]{1,0:T(8,128)S(1)} %down.1.low_ref), channel_id=1, source_target_pairs={{0,1},{1,0},{2,3},{3,2},{4,5},{5,4},{6,7},{7,6},{8,9},{9,8},{10,11... | collective-permute-start | bytes 393224 | tf_op jit(solution)/shard_map/ppermute | solution.py:333
  36.7 7.7 %collective-permute-start.10 = (s16[64,1024]{1,0:T(8,128)(2,1)S(1)}, s16[64,1024]{1,0:T(8,128)(2,1)S(1)}, u32[]{:S(2)}, u32[]{:S(2)}) collective-permute-start(s16[64,1024]{1,0:T(8,128)(2,1)S(1)} %get-tuple-element.59), channel_id=1, source_target_pairs={{0,6},{2,4},{4,2},{6,0},{8,14},{10,12},{12,10},{14,8},{1,7},{3,5},... | collective-permute-start | bytes 393224 | tf_op jit(solution)/shard_map/ppermute | solution.py:333
  40.1 5.6 %collective-permute-start.11 = (s16[64,1024]{1,0:T(8,128)(2,1)S(1)}, s16[64,1024]{1,0:T(8,128)(2,1)S(1)}, u32[]{:S(2)}, u32[]{:S(2)}) collective-permute-start(s16[64,1024]{1,0:T(8,128)(2,1)S(1)} %get-tuple-element.60), channel_id=1, source_target_pairs={{0,4},{2,6},{4,0},{6,2},{8,12},{10,14},{12,8},{14,10},{1,5},{3,7},... | collective-permute-start | bytes 393224 | tf_op jit(solution)/shard_map/ppermute | solution.py:333
  40.1 6.2 %collective-permute-start.9 = (s16[64,1024]{1,0:T(8,128)(2,1)S(1)}, s16[64,1024]{1,0:T(8,128)(2,1)S(1)}, u32[]{:S(2)}, u32[]{:S(2)}) collective-permute-start(s16[64,1024]{1,0:T(8,128)(2,1)S(1)} %get-tuple-element.58), channel_id=1, source_target_pairs={{0,2},{2,0},{4,6},{6,4},{8,10},{10,8},{12,14},{14,12},{1,3},{3,1},... | collective-permute-start | bytes 393224 | tf_op jit(solution)/shard_map/ppermute | solution.py:333

commit v12 on v11

--- a/solution.py
+++ b/solution.py
@@ -355,9 +355,6 @@
         name="pick",
     )(me, group, in_hbm(adapter_row), in_hbm(tokens), in_hbm(adapter_down))
     far_down = exchange(down_part, "pool", pool, pool // 2)
-    order = far_first(buffers)
-    arrived = [picked[0]] + [exchange(picked[j], "pool", pool, j) for j in order]
-
     up_share = columns // groups
     ranks_now, adapter_up_now, _ = lax.optimization_barrier((ranks, adapter_up, picked))
     up_part, factor = pl.pallas_call(
@@ -378,6 +375,12 @@
     )(group, core, ranks_now, in_hbm(adapter_up_now))
     far_up = exchange(up_part, "pool", pool, pool // 2)
 
+    order = far_first(buffers)
+    early, late = order[:1], order[1:]
+    late_rows, _ = lax.optimization_barrier(([picked[j] for j in late], up_part))
+    leaving = [picked[j] for j in early] + late_rows
+    arrived = [picked[0]] + [exchange(x, "pool", pool, j) for x, j in zip(leaving, order)]
+
     steps = 5
     theirs, mine, own_down, own_up = pl.pallas_call(
         base_kernel,
@@ -417,7 +420,7 @@
     cosine = jnp.concatenate([cosine, cosine], axis=1)
     sine = jnp.concatenate([-sine, sine], axis=1)
 
-    far_up, theirs = lax.optimization_barrier((far_up, theirs))
+    far_ups, theirs = lax.optimization_barrier((far_ups, theirs))
     other = exchange(theirs, "tp", cores, 1)
     arrived, mine, cosine, sine = lax.optimization_barrier((arrived, mine, cosine, sine))
     slots = buffers * size

time: 48.1 us -> 47.4 us (0.985)
  waiting for transfers between devices: 19.5 us -> 18.4 us
    ppermute x12, waiting for transfers between devices: 19.5 us -> 18.4 us  [exchange(): return lax.ppermute(x, axis, [(p, p ^ j) for p in range(count)])]
  transfers between devices with their start and end apart: 12 -> 12, of which waited for: 7 -> 6; matrix products, arithmetic and copies ran while one was open for 2% -> 2% of each run, Pallas kernels for 16% -> 17%
where the time goes in v12:
time: 47.4 us; the launch traced here: 47.2 us
  waiting for transfers between devices  18.4 us (39%)
  starting transfers between devices  15.6 us (33%)
  Pallas kernels  11.3 us (24%)
  other arithmetic  1.08 us (2%)
  between operations  0.75 us (2%)
    ppermute x12, waiting for transfers between devices, exchange(): return lax.ppermute(x, axis, [(p, p ^ j) for p in range(count)])  18.4 us
    ppermute x12, starting transfers between devices, exchange(): return lax.ppermute(x, axis, [(p, p ^ j) for p in range(count)])  15.6 us
    pallas_call x1, Pallas kernels, body(): pl.pallas_call(base_kernel, in_specs=[SMEM] + [HBM] * 4, out_specs=[VMEM]...  5.63 us
    pallas_call x1, Pallas kernels, body(): pl.pallas_call(functools.partial(pick_kernel, pool, local, depth), in_spe...  1.78 us
    pallas_call x1, Pallas kernels, body(): pl.pallas_call(functools.partial(finish_kernel, buffers, pool, local, dep...  1.67 us
    pallas_call x1, Pallas kernels, body(): pl.pallas_call(functools.partial(up_share_kernel, cores), in_specs=[SMEM]...  0.95 us
  transfers between devices with their start and end apart: 12, of which 6 were waited for; matrix products, arithmetic and copies ran while one was open for 2% of the time, Pallas kernels for 17%

profile of v12, /device:TPU:0, one launch (start us, length us, event | category | flops | bytes accessed | tf_op | source)
XLA Modules:
  0.0 47.2 jit_solution(9066267367898844969)
XLA Ops:
  0.0 0.0 copy-start
  0.0 0.0 copy-start.1
  0.0 1.8 %pick.1 = (bf16[1,1280,128]{2,1,0:T(8,128)(2,1)S(1)}, bf16[64,2560]{1,0:T(8,128)(2,1)S(1)}, bf16[64,2560]{1,0:T(8,128)(2,1)S(1)}, bf16[64,2560]{1,0:T(8,128)(2,1)S(1)}, bf16[64,2560]{1,0:T(8,128)(2,1)S(1)}) custom-call(s32[1]{0:T(128)} %bitcast.me_ref, s32[1]{0:T(128)} %bitcast.2.group_ref, s32[1,128]{1,0:T(1,128)} %bitcast.8, bf16[128,2560]{1,0:T(8,128)(2,1)} %tokens_hbm.3, ...), custom_call_target="tpu_custom_call" | custom-call | flops 167772160 | bytes 1966080 | tf_op jit(solution)/shard_map/pick/pallas_call | solution.py:341
  1.8 4.1 %collective-permute-start.4 = (bf16[1,1280,128]{2,1,0:T(8,128)(2,1)S(1)}, bf16[1,1280,128]{2,1,0:T(8,128)(2,1)S(1)}, u32[]{:S(2)}, u32[]{:S(2)}) collective-permute-start(bf16[1,1280,128]{2,1,0:T(8,128)(2,1)S(1)} %get-tuple-element.48), channel_id=1, source_target_pairs={{0,8},{2,10},{4,12},{6,14},{8,0},{10,2},{12,4},{14,6},{1,9},{3,11}... | collective-permute-start | bytes 983048 | tf_op jit(solution)/shard_map/ppermute | solution.py:333
  5.9 2.5 %collective-permute-start = (bf16[64,2560]{1,0:T(8,128)(2,1)S(1)}, bf16[64,2560]{1,0:T(8,128)(2,1)S(1)}, u32[]{:S(2)}, u32[]{:S(2)}) collective-permute-start(bf16[64,2560]{1,0:T(8,128)(2,1)S(1)} %get-tuple-element.38), channel_id=1, source_target_pairs={{0,6},{2,4},{4,2},{6,0},{8,14},{10,12},{12,10},{14,8},{1,7},{3,5},... | collective-permute-start | bytes 983048 | tf_op jit(solution)/shard_map/ppermute | solution.py:333
  9.1 0.9 %up_share.1 = (bf16[1,128,512]{2,1,0:T(8,128)(2,1)S(1)}, f32[1,128]{1,0:T(1,128)S(1)}) custom-call(s32[1]{0:T(128)} %bitcast.2.group_ref, s32[1]{0:T(128)} %bitcast.3.core_ref, s32[1]{0:T(128)S(6)} %copy.9.ranks_ref, bf16[1,128,2048]{2,1,0:T(8,128)(2,1)} %up_hbm.2), custom_call_target="tpu_custom_call" | custom-call | flops 65536 | bytes 262144 | tf_op jit(solution)/shard_map/up_share/pallas_call | solution.py:360
  10.0 0.4 collective-permute-start.3
  10.4 0.4 collective-permute-start.1
  10.9 0.3 collective-permute-start.2
  11.2 0.7 %convert_element_type.4 = f32[128]{0:T(128)S(1)} convert(s32[128]{0:T(128)} %param.10) | non-fusion elementwise | flops 128 | bytes 1024 | tf_op jit(solution)/shard_map/convert_element_type | solution.py:418
  11.8 5.6 %base.1 = (f32[128,1024]{1,0:T(8,128)S(1)}, f32[128,1024]{1,0:T(8,128)S(1)}, bf16[1,2560,128]{2,1,0:T(8,128)(2,1)S(1)}, bf16[1,128,1024]{2,1,0:T(8,128)(2,1)S(1)}) custom-call(s32[1]{0:T(128)} %bitcast.3.core_ref, bf16[128,2560]{1,0:T(8,128)(2,1)} %tokens_hbm.3, bf16[2560,2048]{1,0:T(8,128)(2,1)} %weight_hbm.1, bf16[1,2560,128]{2,1,0:T(8,128)(2,1)} %down_hbm.3, ...), custom_call_target="tpu_custom_call" | custom-call | flops 1342177280 | bytes 10485760 | tf_op jit(solution)/shard_map/base/pallas_call | solution.py:385
  17.5 4.9 %collective-permute-done.4.refs_4_ = bf16[1,1280,128]{2,1,0:T(8,128)(2,1)S(1)} collective-permute-done((bf16[1,1280,128]{2,1,0:T(8,128)(2,1)S(1)}, bf16[1,1280,128]{2,1,0:T(8,128)(2,1)S(1)}, u32[]{:S(2)}, u32[]{:S(2)}) %collective-permute-start.4) | collective-permute-done | bytes 327712 | tf_op jit(solution)/shard_map/ppermute | solution.py:333
  22.3 2.1 %collective-permute-start.7 = (bf16[1,1280,128]{2,1,0:T(8,128)(2,1)S(1)}, bf16[1,1280,128]{2,1,0:T(8,128)(2,1)S(1)}, u32[]{:S(2)}, u32[]{:S(2)}) collective-permute-start(bf16[1,1280,128]{2,1,0:T(8,128)(2,1)S(1)} %collective-permute-done.4.refs_4_), channel_id=1, source_target_pairs={{0,16},{16,0},{1,17},{17,1},{2,18},{18,2},{3,19},{19,3},{4,20},{20... | collective-permute-start | bytes 983048 | tf_op jit(solution)/shard_map/ppermute | solution.py:333
  24.5 1.9 %collective-permute-done.3.refs_0_ = bf16[1,128,512]{2,1,0:T(8,128)(2,1)S(1)} collective-permute-done((bf16[1,128,512]{2,1,0:T(8,128)(2,1)S(1)}, bf16[1,128,512]{2,1,0:T(8,128)(2,1)S(1)}, u32[]{:S(2)}, u32[]{:S(2)}) %collective-permute-start.3) | collective-permute-done | bytes 131104 | tf_op jit(solution)/shard_map/ppermute | solution.py:333
  26.4 1.5 %collective-permute-start.5 = (bf16[1,128,512]{2,1,0:T(8,128)(2,1)S(1)}, bf16[1,128,512]{2,1,0:T(8,128)(2,1)S(1)}, u32[]{:S(2)}, u32[]{:S(2)}) collective-permute-start(bf16[1,128,512]{2,1,0:T(8,128)(2,1)S(1)} %collective-permute-done.3.refs_0_), channel_id=1, source_target_pairs={{0,16},{16,0},{1,17},{17,1},{2,18},{18,2},{3,19},{19,3},{4,20},{20... | collective-permute-start | bytes 393224 | tf_op jit(solution)/shard_map/ppermute | solution.py:333
  27.9 0.3 fusion
  28.3 4.1 %collective-permute-done.5.refs_1_ = bf16[1,128,512]{2,1,0:T(8,128)(2,1)S(1)} collective-permute-done((bf16[1,128,512]{2,1,0:T(8,128)(2,1)S(1)}, bf16[1,128,512]{2,1,0:T(8,128)(2,1)S(1)}, u32[]{:S(2)}, u32[]{:S(2)}) %collective-permute-start.5) | collective-permute-done | bytes 131104 | tf_op jit(solution)/shard_map/ppermute | solution.py:333
  32.4 0.0 collective-permute-start.6
  32.4 0.1 pad_maximum_fusion
  32.5 0.0 collective-permute-done.1.refs_2_
  32.5 0.0 collective-permute-done.2.refs_3_
  32.5 0.0 collective-permute-done.refs_1_
  32.5 0.0 collective-permute-done.7.refs_5_
  32.5 0.5 %down.1.low_ref = f32[256,128]{1,0:T(8,128)S(1)} custom-call(s32[1]{0:T(128)} %bitcast.2.group_ref, bf16[1,2560,128]{2,1,0:T(8,128)(2,1)S(1)} %get-tuple-element.56.down_ref, bf16[64,2560]{1,0:T(8,128)(2,1)S(1)} %get-tuple-element.57.refs_0_, bf16[64,2560]{1,0:T(8,128)(2,1)S(1)} %collective-permute-done.refs_1_, ...), custom_call_target="tpu_custom_call" | custom-call | flops 335544320 | bytes 1966080 | tf_op jit(solution)/shard_map/down/pallas_call | solution.py:427
  33.1 0.6 %collective-permute-start.8 = (f32[256,128]{1,0:T(8,128)S(1)}, f32[256,128]{1,0:T(8,128)S(1)}, u32[]{:S(2)}, u32[]{:S(2)}) collective-permute-start(f32[256,128]{1,0:T(8,128)S(1)} %down.1.low_ref), channel_id=1, source_target_pairs={{0,1},{1,0},{2,3},{3,2},{4,5},{5,4},{6,7},{7,6},{8,9},{9,8},{10,11... | collective-permute-start | bytes 393224 | tf_op jit(solution)/shard_map/ppermute | solution.py:333
  33.6 1.0 %collective-permute-done.8.other_ref = f32[256,128]{1,0:T(8,128)S(1)} collective-permute-done((f32[256,128]{1,0:T(8,128)S(1)}, f32[256,128]{1,0:T(8,128)S(1)}, u32[]{:S(2)}, u32[]{:S(2)}) %collective-permute-start.8) | collective-permute-done | bytes 131104 | tf_op jit(solution)/shard_map/ppermute | solution.py:333
  34.6 0.8 %up.1 = (s16[64,1024]{1,0:T(8,128)(2,1)S(1)}, s16[64,1024]{1,0:T(8,128)(2,1)S(1)}, s16[64,1024]{1,0:T(8,128)(2,1)S(1)}, s16[64,1024]{1,0:T(8,128)(2,1)S(1)}) custom-call(s32[1]{0:T(128)} %bitcast.2.group_ref, f32[256,128]{1,0:T(8,128)S(1)} %down.1.low_ref, f32[256,128]{1,0:T(8,128)S(1)} %collective-permute-done.8.other_ref, ...), custom_call_target="tpu_custom_call" | custom-call | flops 268435456 | bytes 524288 | tf_op jit(solution)/shard_map/up/pallas_call | solution.py:438
  35.4 3.0 %collective-permute-start.10 = (s16[64,1024]{1,0:T(8,128)(2,1)S(1)}, s16[64,1024]{1,0:T(8,128)(2,1)S(1)}, u32[]{:S(2)}, u32[]{:S(2)}) collective-permute-start(s16[64,1024]{1,0:T(8,128)(2,1)S(1)} %get-tuple-element.67), channel_id=1, source_target_pairs={{0,6},{2,4},{4,2},{6,0},{8,14},{10,12},{12,10},{14,8},{1,7},{3,5},... | collective-permute-start | bytes 393224 | tf_op jit(solution)/shard_map/ppermute | solution.py:333
  38.4 0.5 %collective-permute-start.11 = (s16[64,1024]{1,0:T(8,128)(2,1)S(1)}, s16[64,1024]{1,0:T(8,128)(2,1)S(1)}, u32[]{:S(2)}, u32[]{:S(2)}) collective-permute-start(s16[64,1024]{1,0:T(8,128)(2,1)S(1)} %get-tuple-element.68), channel_id=1, source_target_pairs={{0,4},{2,6},{4,0},{6,2},{8,12},{10,14},{12,8},{14,10},{1,5},{3,7},... | collective-permute-start | bytes 393224 | tf_op jit(solution)/shard_map/ppermute | solution.py:333
  39.0 0.1 collective-permute-start.9
  39.1 0.0 copy-done.1
  39.1 3.7 %collective-permute-done.10.refs_2_ = s16[64,1024]{1,0:T(8,128)(2,1)S(1)} collective-permute-done((s16[64,1024]{1,0:T(8,128)(2,1)S(1)}, s16[64,1024]{1,0:T(8,128)(2,1)S(1)}, u32[]{:S(2)}, u32[]{:S(2)}) %collective-permute-start.10) | collective-permute-done | bytes 131104 | tf_op jit(solution)/shard_map/ppermute | solution.py:333
  42.8 2.8 %collective-permute-done.11.refs_3_ = s16[64,1024]{1,0:T(8,128)(2,1)S(1)} collective-permute-done((s16[64,1024]{1,0:T(8,128)(2,1)S(1)}, s16[64,1024]{1,0:T(8,128)(2,1)S(1)}, u32[]{:S(2)}, u32[]{:S(2)}) %collective-permute-start.11) | collective-permute-done | bytes 131104 | tf_op jit(solution)/shard_map/ppermute | solution.py:333
  45.5 0.0 collective-permute-done.9.refs_1_
  45.5 0.0 collective-permute-done.6.other_ref
  45.5 0.0 copy-done
  45.5 1.7 %finish.1 = bf16[1024,128]{1,0:T(8,128)(2,1)} custom-call(s32[1]{0:T(128)} %bitcast.me_ref, s32[1,128]{1,0:T(1,128)S(1)} %bitcast.9, f32[128,1024]{1,0:T(8,128)S(1)} %get-tuple-element.47.mine_ref, f32[128,1024]{1,0:T(8,128)S(1)} %collective-permute-done.6.other_ref, f32[128,128]{1,0:T(8,128)S(1)} %get-tuple-element.54.cos_ref, ...), custom_call_target="tpu_custom_call" | custom-call | flops 134217728 | bytes 524288 | tf_op jit(solution)/shard_map/finish/pallas_call | solution.py:451
  (2 shorter events, 0.0 us)
Async XLA Ops:
  0.0 45.5 %copy-start = (s32[128,1]{0,1:T(1,128)S(1)}, s32[128,1]{0,1:T(1,128)}, u32[]{:S(2)}) copy-start(s32[128,1]{0,1:T(1,128)} %param.9) | copy-start | bytes 1540
  0.0 39.1 %copy-start.1 = (bf16[128]{0:T(256)(128)(2,1)S(1)}, bf16[128]{0:T(256)(128)(2,1)}, u32[]{:S(2)}) copy-start(bf16[128]{0:T(256)(128)(2,1)} %param.15) | copy-start | bytes 772
  1.8 20.5 %collective-permute-start.4 = (bf16[1,1280,128]{2,1,0:T(8,128)(2,1)S(1)}, bf16[1,1280,128]{2,1,0:T(8,128)(2,1)S(1)}, u32[]{:S(2)}, u32[]{:S(2)}) collective-permute-start(bf16[1,1280,128]{2,1,0:T(8,128)(2,1)S(1)} %get-tuple-element.48), channel_id=1, source_target_pairs={{0,8},{2,10},{4,12},{6,14},{8,0},{10,2},{12,4},{14,6},{1,9},{3,11}... | collective-permute-start | bytes 983048 | tf_op jit(solution)/shard_map/ppermute | solution.py:333
  5.9 26.6 %collective-permute-start = (bf16[64,2560]{1,0:T(8,128)(2,1)S(1)}, bf16[64,2560]{1,0:T(8,128)(2,1)S(1)}, u32[]{:S(2)}, u32[]{:S(2)}) collective-permute-start(bf16[64,2560]{1,0:T(8,128)(2,1)S(1)} %get-tuple-element.38), channel_id=1, source_target_pairs={{0,6},{2,4},{4,2},{6,0},{8,14},{10,12},{12,10},{14,8},{1,7},{3,5},... | collective-permute-start | bytes 983048 | tf_op jit(solution)/shard_map/ppermute | solution.py:333
  10.0 16.4 %collective-permute-start.3 = (bf16[1,128,512]{2,1,0:T(8,128)(2,1)S(1)}, bf16[1,128,512]{2,1,0:T(8,128)(2,1)S(1)}, u32[]{:S(2)}, u32[]{:S(2)}) collective-permute-start(bf16[1,128,512]{2,1,0:T(8,128)(2,1)S(1)} %get-tuple-element.43), channel_id=1, source_target_pairs={{0,8},{2,10},{4,12},{6,14},{8,0},{10,2},{12,4},{14,6},{1,9},{3,11}... | collective-permute-start | bytes 393224 | tf_op jit(solution)/shard_map/ppermute | solution.py:333
  10.4 22.0 %collective-permute-start.1 = (bf16[64,2560]{1,0:T(8,128)(2,1)S(1)}, bf16[64,2560]{1,0:T(8,128)(2,1)S(1)}, u32[]{:S(2)}, u32[]{:S(2)}) collective-permute-start(bf16[64,2560]{1,0:T(8,128)(2,1)S(1)} %get-tuple-element.44), channel_id=1, source_target_pairs={{0,4},{2,6},{4,0},{6,2},{8,12},{10,14},{12,8},{14,10},{1,5},{3,7},... | collective-permute-start | bytes 983048 | tf_op jit(solution)/shard_map/ppermute | solution.py:333
  10.9 21.6 %collective-permute-start.2 = (bf16[64,2560]{1,0:T(8,128)(2,1)S(1)}, bf16[64,2560]{1,0:T(8,128)(2,1)S(1)}, u32[]{:S(2)}, u32[]{:S(2)}) collective-permute-start(bf16[64,2560]{1,0:T(8,128)(2,1)S(1)} %get-tuple-element.45), channel_id=1, source_target_pairs={{0,2},{2,0},{4,6},{6,4},{8,10},{10,8},{12,14},{14,12},{1,3},{3,1},... | collective-permute-start | bytes 983048 | tf_op jit(solution)/shard_map/ppermute | solution.py:333
  22.3 10.2 %collective-permute-start.7 = (bf16[1,1280,128]{2,1,0:T(8,128)(2,1)S(1)}, bf16[1,1280,128]{2,1,0:T(8,128)(2,1)S(1)}, u32[]{:S(2)}, u32[]{:S(2)}) collective-permute-start(bf16[1,1280,128]{2,1,0:T(8,128)(2,1)S(1)} %collective-permute-done.4.refs_4_), channel_id=1, source_target_pairs={{0,16},{16,0},{1,17},{17,1},{2,18},{18,2},{3,19},{19,3},{4,20},{20... | collective-permute-start | bytes 983048 | tf_op jit(solution)/shard_map/ppermute | solution.py:333
  26.4 6.0 %collective-permute-start.5 = (bf16[1,128,512]{2,1,0:T(8,128)(2,1)S(1)}, bf16[1,128,512]{2,1,0:T(8,128)(2,1)S(1)}, u32[]{:S(2)}, u32[]{:S(2)}) collective-permute-start(bf16[1,128,512]{2,1,0:T(8,128)(2,1)S(1)} %collective-permute-done.3.refs_0_), channel_id=1, source_target_pairs={{0,16},{16,0},{1,17},{17,1},{2,18},{18,2},{3,19},{19,3},{4,20},{20... | collective-permute-start | bytes 393224 | tf_op jit(solution)/shard_map/ppermute | solution.py:333
  32.4 13.2 %collective-permute-start.6 = (f32[128,1024]{1,0:T(8,128)S(1)}, f32[128,1024]{1,0:T(8,128)S(1)}, u32[]{:S(2)}, u32[]{:S(2)}) collective-permute-start(f32[128,1024]{1,0:T(8,128)S(1)} %get-tuple-element.53), channel_id=1, source_target_pairs={{0,1},{1,0},{2,3},{3,2},{4,5},{5,4},{6,7},{7,6},{8,9},{9,8},{10,11... | collective-permute-start | bytes 1572872 | tf_op jit(solution)/shard_map/ppermute | solution.py:333
  33.1 1.6 %collective-permute-start.8 = (f32[256,128]{1,0:T(8,128)S(1)}, f32[256,128]{1,0:T(8,128)S(1)}, u32[]{:S(2)}, u32[]{:S(2)}) collective-permute-start(f32[256,128]{1,0:T(8,128)S(1)} %down.1.low_ref), channel_id=1, source_target_pairs={{0,1},{1,0},{2,3},{3,2},{4,5},{5,4},{6,7},{7,6},{8,9},{9,8},{10,11... | collective-permute-start | bytes 393224 | tf_op jit(solution)/shard_map/ppermute | solution.py:333
  35.4 7.3 %collective-permute-start.10 = (s16[64,1024]{1,0:T(8,128)(2,1)S(1)}, s16[64,1024]{1,0:T(8,128)(2,1)S(1)}, u32[]{:S(2)}, u32[]{:S(2)}) collective-permute-start(s16[64,1024]{1,0:T(8,128)(2,1)S(1)} %get-tuple-element.67), channel_id=1, source_target_pairs={{0,6},{2,4},{4,2},{6,0},{8,14},{10,12},{12,10},{14,8},{1,7},{3,5},... | collective-permute-start | bytes 393224 | tf_op jit(solution)/shard_map/ppermute | solution.py:333
  38.4 7.1 %collective-permute-start.11 = (s16[64,1024]{1,0:T(8,128)(2,1)S(1)}, s16[64,1024]{1,0:T(8,128)(2,1)S(1)}, u32[]{:S(2)}, u32[]{:S(2)}) collective-permute-start(s16[64,1024]{1,0:T(8,128)(2,1)S(1)} %get-tuple-element.68), channel_id=1, source_target_pairs={{0,4},{2,6},{4,0},{6,2},{8,12},{10,14},{12,8},{14,10},{1,5},{3,7},... | collective-permute-start | bytes 393224 | tf_op jit(solution)/shard_map/ppermute | solution.py:333
  39.0 6.6 %collective-permute-start.9 = (s16[64,1024]{1,0:T(8,128)(2,1)S(1)}, s16[64,1024]{1,0:T(8,128)(2,1)S(1)}, u32[]{:S(2)}, u32[]{:S(2)}) collective-permute-start(s16[64,1024]{1,0:T(8,128)(2,1)S(1)} %get-tuple-element.66), channel_id=1, source_target_pairs={{0,2},{2,0},{4,6},{6,4},{8,10},{10,8},{12,14},{14,12},{1,3},{3,1},... | collective-permute-start | bytes 393224 | tf_op jit(solution)/shard_map/ppermute | solution.py:333

commit v13 on v10

--- a/solution.py
+++ b/solution.py
@@ -43,7 +43,7 @@
     )
 
 
-def slot_places(row, me, pool, local, depth):
+def slot_places(row, me, pool, local, depth, far_outer):
     n = row.shape[1]
     column = to_column(row)
     earlier = (column == row) & (iota((n, n), 0) < iota((n, n), 1))
@@ -51,7 +51,8 @@
     holder = row // local
     apart = holder ^ me
     buffer, far = apart % (pool // 2), apart // (pool // 2)
-    return ((buffer * 2 + far) * local + (row - holder * local)) * depth + slot
+    block = far * (pool // 2) + buffer if far_outer else buffer * 2 + far
+    return (block * local + (row - holder * local)) * depth + slot
 
 
 def far_first(count):
@@ -113,7 +114,7 @@
     share_copy = pltpu.make_async_copy(down_hbm.at[:, pl.ds(at, share), :], share_ref, share_sem)
     share_copy.start()
     adapter_copy.wait()
-    place = slot_places(adapter_ref[...], me_ref[0], pool, local, depth)
+    place = slot_places(adapter_ref[...], me_ref[0], pool, local, depth, False)
     size = outs[0].shape[0]
     slots = len(outs) * size
     picker = jnp.where(iota((slots, rows), 0) == place, 1.0, 0.0).astype(jnp.bfloat16)
@@ -200,63 +201,73 @@
             rows, jnp.concatenate(factors, axis=1), preferred_element_type=jnp.float32
         )
         total = term if total is None else total + term
-    which = (iota((total.shape[0], 1), 0) // depth) % (2 * local)
-    low = total[:, :rank]
-    for i in range(1, 2 * local):
-        low = jnp.where(which == i, total[:, i * rank : (i + 1) * rank], low)
-    out[...] = low
-
-
-def up_kernel(
-    buffers, groups, local, depth, group_ref, low_ref, other_ref, factor_ref, up_ref, *refs
-):
-    shares, outs, term_ref = refs[:groups], refs[groups : groups + buffers], refs[-1]
-    rows, rank = low_ref.shape
-    size = rows // buffers
-    columns = up_ref.shape[2]
-    share = columns // groups
-    which = (iota((rows, 1), 0) // depth) % (2 * local)
-    low = low_ref[...] + other_ref[...]
-    for a in range(local):
-        low = jnp.where(which == a, low * factor_ref[a : a + 1, :], low)
+    for j in range(buffers):
+        for i in range(2 * local):
+            far, a = i // local, i % local
+            source, target = (j * 2 * local + i) * depth, ((far * buffers + j) * local + a) * depth
+            out[target : target + depth, :] = total[
+                source : source + depth, i * rank : (i + 1) * rank
+            ]
+
+
+def code_terms(low, up, local, depth, outs, columns, scale=None):
+    rows = low.shape[0]
+    size = rows // len(outs)
+    which = (iota((rows, 1), 0) // depth) % local
+    if scale is not None:
+        for a in range(local):
+            low = jnp.where(which == a, low * scale[a : a + 1, :], low)
     both = jnp.concatenate(halves(low), axis=0)
     which = jnp.concatenate([which, which], axis=0)
     spread = jnp.concatenate(
-        [jnp.where(which == i, both, jnp.zeros_like(both)) for i in range(2 * local)], axis=1
-    )
+        [jnp.where(which == a, both, jnp.zeros_like(both)) for a in range(local)], axis=1
+    )
+    term = jnp.dot(spread, jnp.concatenate(up, axis=0), preferred_element_type=jnp.float32)
+    term = term[:rows] + term[rows:]
+    top = jnp.max(jnp.abs(term), axis=1, keepdims=True)
+    exponent = jnp.ceil(jnp.log2(jnp.maximum(top, 1e-30)) + 1e-3)
+    code = jnp.clip(jnp.round(term * jnp.exp2(15.0 - exponent)), -32767.0, 32767.0)
+    code = code.astype(jnp.int32)
+    lane = iota((1, LANES), 1)
+    biased = exponent.astype(jnp.int32) + EXPONENT_BIAS
+    first = code[:, :LANES]
+    marked = (first & -2) | ((biased >> jnp.minimum(lane, EXPONENT_BITS - 1)) & 1)
+    first = jnp.where(lane < EXPONENT_BITS, marked, first).astype(jnp.int16)
+    rest = code[:, LANES:].astype(jnp.int16)
+    for j, out in enumerate(outs):
+        out[:, :LANES] = first[j * size : (j + 1) * size]
+        out[:, LANES:] = rest[j * size : (j + 1) * size]
+
+
+def near_kernel(local, depth, low_ref, other_ref, factor_ref, up_ref, *outs):
+    rows = low_ref.shape[0] // 2
+    low = low_ref[:rows, :] + other_ref[:rows, :]
+    up = [up_ref[a] for a in range(local)]
+    code_terms(low, up, local, depth, outs, up_ref.shape[2], factor_ref[...])
+
+
+def far_kernel(groups, local, depth, group_ref, low_ref, other_ref, *refs):
+    shares, outs, up_ref = refs[:groups], refs[groups:-1], refs[-1]
+    rows = low_ref.shape[0] // 2
+    low = low_ref[rows:, :] + other_ref[rows:, :]
+    share = shares[0].shape[2]
     for k in range(groups):
         at = pl.multiple_of((group_ref[0] ^ k) * share, share)
-        up = [up_ref[a, :, pl.ds(at, share)] for a in range(local)]
-        up += [shares[k][a] for a in range(local)]
-        term = jnp.dot(
-            spread, jnp.concatenate(up, axis=0), preferred_element_type=jnp.float32
-        )
-        term_ref[:, pl.ds(at, share)] = term[:rows] + term[rows:]
-    lane = iota((1, LANES), 1)
-    for j, out in enumerate(outs):
-        term = term_ref[j * size : (j + 1) * size, :]
-        top = jnp.max(jnp.abs(term), axis=1, keepdims=True)
-        exponent = jnp.ceil(jnp.log2(jnp.maximum(top, 1e-30)) + 1e-3)
-        code = jnp.clip(jnp.round(term * jnp.exp2(15.0 - exponent)), -32767.0, 32767.0)
-        code = code.astype(jnp.int32)
-        biased = exponent.astype(jnp.int32) + EXPONENT_BIAS
-        first = code[:, :LANES]
-        marked = (first & -2) | ((biased >> jnp.minimum(lane, EXPONENT_BITS - 1)) & 1)
-        first = jnp.where(lane < EXPONENT_BITS, marked, first)
-        out[:, :LANES] = first.astype(jnp.int16)
-        out[:, LANES:] = code[:, LANES:].astype(jnp.int16)
+        up_ref[:, :, pl.ds(at, share)] = shares[k][...]
+    up = [up_ref[a] for a in range(local)]
+    code_terms(low, up, local, depth, outs, up_ref.shape[2])
 
 
 def finish_kernel(
     buffers, pool, local, depth, me_ref, adapter_ref, mine_ref, other_ref, cos_ref, sin_ref, gain_ref, *refs
 ):
     order = [0] + return_order(buffers)
-    ins = [refs[order.index(j)] for j in range(buffers)]
+    ins = [refs[(1 - f) * buffers + order.index(j)] for f in range(2) for j in range(buffers)]
     out_hbm, out_ref, sems = refs[-3:]
     rows, columns = mine_ref.shape
     head = cos_ref.shape[1]
-    place = to_column(slot_places(adapter_ref[...], me_ref[0], pool, local, depth))
-    slots = buffers * ins[0].shape[0]
+    place = to_column(slot_places(adapter_ref[...], me_ref[0], pool, local, depth, True))
+    slots = len(ins) * ins[0].shape[0]
     picker = jnp.where(iota((rows, slots), 1) == place, 1.0, 0.0).astype(jnp.bfloat16)
 
     def picked(at, size):
@@ -432,22 +443,40 @@
     )(group, own_down, *arrived, *far_downs)
     low_other = exchange(low, "tp", cores, 1)
 
-    terms = pl.pallas_call(
-        functools.partial(up_kernel, buffers, groups, local, depth),
-        in_specs=[SMEM] + [VMEM] * (4 + groups),
+    half = local * depth
+    coded = [jax.ShapeDtypeStruct((half, columns), jnp.int16)] * buffers
+    order = return_order(buffers)
+
+    def come_back(terms):
+        return [terms[0]] + [exchange(terms[j], "pool", pool, j) for j in order]
+
+    near = pl.pallas_call(
+        functools.partial(near_kernel, local, depth),
+        in_specs=[VMEM] * 4,
         out_specs=[VMEM] * buffers,
-        out_shape=[jax.ShapeDtypeStruct((size, columns), jnp.int16)] * buffers,
-        scratch_shapes=[pltpu.VMEM((slots, columns), f32)],
-        compiler_params=params(),
-        cost_estimate=cost(8 * local * slots * rank * columns, 2 * slots * columns),
-        name="up",
-    )(group, low, low_other, factor, own_up, *far_ups)
-    order = return_order(buffers)
-    returned = [terms[0]] + [exchange(terms[j], "pool", pool, j) for j in order]
+        out_shape=coded,
+        compiler_params=params(),
+        cost_estimate=cost(4 * local * slots * rank * columns, slots * columns),
+        name="near_terms",
+    )(low, low_other, factor, own_up)
+    near, low, low_other = lax.optimization_barrier((near, low, low_other))
+    returned = come_back(near)
+    far = pl.pallas_call(
+        functools.partial(far_kernel, groups, local, depth),
+        in_specs=[SMEM] + [VMEM] * (2 + groups),
+        out_specs=[VMEM] * buffers,
+        out_shape=coded,
+        scratch_shapes=[pltpu.VMEM((local, rank, columns), bf16)],
+        compiler_params=params(),
+        cost_estimate=cost(4 * local * slots * rank * columns, slots * columns),
+        name="far_terms",
+    )(group, low, low_other, *far_ups)
+    far, returned[1] = lax.optimization_barrier((far, returned[1]))
+    returned = come_back(far) + returned
 
     out = pl.pallas_call(
         functools.partial(finish_kernel, buffers, pool, local, depth),
-        in_specs=[SMEM] + [VMEM] * (6 + buffers),
+        in_specs=[SMEM] + [VMEM] * (6 + 2 * buffers),
         out_specs=HBM,
         out_shape=jax.ShapeDtypeStruct((rows * columns // head, head), bf16),
         scratch_shapes=[

time: 47.2 us -> 47.7 us (1.011)
  starting transfers between devices: 14.7 us -> 17.9 us
  waiting for transfers between devices: 19.1 us -> 16.4 us
    ppermute x12 -> x15, starting transfers between devices: 14.7 us -> 17.9 us  [exchange(): return lax.ppermute(x, axis, [(p, p ^ j) for p in range(count)])]
    ppermute x12 -> x15, waiting for transfers between devices: 19.1 us -> 16.4 us  [exchange(): return lax.ppermute(x, axis, [(p, p ^ j) for p in range(count)])]
  transfers between devices with their start and end apart: 12 -> 15, of which waited for: 7 -> 9; matrix products, arithmetic and copies ran while one was open for 2% -> 2% of each run, Pallas kernels for 17% -> 17%
where the time goes in v13:
time: 47.7 us; the launch traced here: 47.6 us
  starting transfers between devices  17.9 us (38%)
  waiting for transfers between devices  16.4 us (34%)
  Pallas kernels  11.4 us (24%)
  other arithmetic  1.08 us (2%)
  between operations  0.76 us (2%)
    ppermute x15, starting transfers between devices, exchange(): return lax.ppermute(x, axis, [(p, p ^ j) for p in range(count)])  17.9 us
    ppermute x15, waiting for transfers between devices, exchange(): return lax.ppermute(x, axis, [(p, p ^ j) for p in range(count)])  16.4 us
    pallas_call x1, Pallas kernels, body(): pl.pallas_call(base_kernel, in_specs=[SMEM] + [HBM] * 4, out_specs=[VMEM]...  5.63 us
    pallas_call x1, Pallas kernels, body(): pl.pallas_call(functools.partial(pick_kernel, pool, local, depth), in_spe...  1.78 us
    pallas_call x1, Pallas kernels, body(): pl.pallas_call(functools.partial(finish_kernel, buffers, pool, local, dep...  1.66 us
  transfers between devices with their start and end apart: 15, of which 9 were waited for; matrix products, arithmetic and copies ran while one was open for 2% of the time, Pallas kernels for 17%

profile of v13, /device:TPU:0, one launch (start us, length us, event | category | flops | bytes accessed | tf_op | source)
XLA Modules:
  0.0 47.6 jit_solution(14410407749461703055)
XLA Ops:
  0.0 0.0 copy-start
  0.0 0.0 copy-start.1
  0.0 1.8 %pick.1 = (bf16[1,1280,128]{2,1,0:T(8,128)(2,1)S(1)}, bf16[64,2560]{1,0:T(8,128)(2,1)S(1)}, bf16[64,2560]{1,0:T(8,128)(2,1)S(1)}, bf16[64,2560]{1,0:T(8,128)(2,1)S(1)}, bf16[64,2560]{1,0:T(8,128)(2,1)S(1)}) custom-call(s32[1]{0:T(128)} %bitcast.me_ref, s32[1]{0:T(128)} %bitcast.2.group_ref, s32[1,128]{1,0:T(1,128)} %bitcast.8, bf16[128,2560]{1,0:T(8,128)(2,1)} %tokens_hbm.3, ...), custom_call_target="tpu_custom_call" | custom-call | flops 167772160 | bytes 1966080 | tf_op jit(solution)/shard_map/pick/pallas_call | solution.py:352
  1.8 4.1 %collective-permute-start.1 = (bf16[1,1280,128]{2,1,0:T(8,128)(2,1)S(1)}, bf16[1,1280,128]{2,1,0:T(8,128)(2,1)S(1)}, u32[]{:S(2)}, u32[]{:S(2)}) collective-permute-start(bf16[1,1280,128]{2,1,0:T(8,128)(2,1)S(1)} %get-tuple-element.51), channel_id=1, source_target_pairs={{0,8},{2,10},{4,12},{6,14},{8,0},{10,2},{12,4},{14,6},{1,9},{3,11}... | collective-permute-start | bytes 983048 | tf_op jit(solution)/shard_map/ppermute | solution.py:344
  5.9 2.5 %collective-permute-start = (bf16[64,2560]{1,0:T(8,128)(2,1)S(1)}, bf16[64,2560]{1,0:T(8,128)(2,1)S(1)}, u32[]{:S(2)}, u32[]{:S(2)}) collective-permute-start(bf16[64,2560]{1,0:T(8,128)(2,1)S(1)} %get-tuple-element.50), channel_id=1, source_target_pairs={{0,6},{2,4},{4,2},{6,0},{8,14},{10,12},{12,10},{14,8},{1,7},{3,5},... | collective-permute-start | bytes 983048 | tf_op jit(solution)/shard_map/ppermute | solution.py:344
  8.4 0.5 collective-permute-start.2
  8.9 0.5 %collective-permute-start.3 = (bf16[64,2560]{1,0:T(8,128)(2,1)S(1)}, bf16[64,2560]{1,0:T(8,128)(2,1)S(1)}, u32[]{:S(2)}, u32[]{:S(2)}) collective-permute-start(bf16[64,2560]{1,0:T(8,128)(2,1)S(1)} %get-tuple-element.56), channel_id=1, source_target_pairs={{0,2},{2,0},{4,6},{6,4},{8,10},{10,8},{12,14},{14,12},{1,3},{3,1},... | collective-permute-start | bytes 983048 | tf_op jit(solution)/shard_map/ppermute | solution.py:344
  10.0 0.9 %up_share.1 = (bf16[1,128,512]{2,1,0:T(8,128)(2,1)S(1)}, f32[1,128]{1,0:T(1,128)S(1)}) custom-call(s32[1]{0:T(128)} %bitcast.2.group_ref, s32[1]{0:T(128)} %bitcast.3.core_ref, s32[1]{0:T(128)S(6)} %copy.9.ranks_ref, bf16[1,128,2048]{2,1,0:T(8,128)(2,1)} %up_hbm.2), custom_call_target="tpu_custom_call" | custom-call | flops 65536 | bytes 262144 | tf_op jit(solution)/shard_map/up_share/pallas_call | solution.py:374
  11.0 0.1 collective-permute-start.7
  11.1 0.7 %convert_element_type.4 = f32[128]{0:T(128)S(1)} convert(s32[128]{0:T(128)} %param.10) | non-fusion elementwise | flops 128 | bytes 1024 | tf_op jit(solution)/shard_map/convert_element_type | solution.py:426
  11.8 5.6 %base.1 = (f32[128,1024]{1,0:T(8,128)S(1)}, f32[128,1024]{1,0:T(8,128)S(1)}, bf16[1,2560,128]{2,1,0:T(8,128)(2,1)S(1)}, bf16[1,128,1024]{2,1,0:T(8,128)(2,1)S(1)}) custom-call(s32[1]{0:T(128)} %bitcast.3.core_ref, bf16[128,2560]{1,0:T(8,128)(2,1)} %tokens_hbm.3, bf16[2560,2048]{1,0:T(8,128)(2,1)} %weight_hbm.1, bf16[1,2560,128]{2,1,0:T(8,128)(2,1)} %down_hbm.3, ...), custom_call_target="tpu_custom_call" | custom-call | flops 1342177280 | bytes 10485760 | tf_op jit(solution)/shard_map/base/pallas_call | solution.py:393
  17.5 4.1 %collective-permute-done.1.refs_4_ = bf16[1,1280,128]{2,1,0:T(8,128)(2,1)S(1)} collective-permute-done((bf16[1,1280,128]{2,1,0:T(8,128)(2,1)S(1)}, bf16[1,1280,128]{2,1,0:T(8,128)(2,1)S(1)}, u32[]{:S(2)}, u32[]{:S(2)}) %collective-permute-start.1) | collective-permute-done | bytes 327712 | tf_op jit(solution)/shard_map/ppermute | solution.py:344
  21.6 1.8 %collective-permute-start.5 = (bf16[1,1280,128]{2,1,0:T(8,128)(2,1)S(1)}, bf16[1,1280,128]{2,1,0:T(8,128)(2,1)S(1)}, u32[]{:S(2)}, u32[]{:S(2)}) collective-permute-start(bf16[1,1280,128]{2,1,0:T(8,128)(2,1)S(1)} %collective-permute-done.1.refs_4_), channel_id=1, source_target_pairs={{0,16},{16,0},{1,17},{17,1},{2,18},{18,2},{3,19},{19,3},{4,20},{20... | collective-permute-start | bytes 983048 | tf_op jit(solution)/shard_map/ppermute | solution.py:344
  23.4 0.3 fusion
  23.7 2.5 %collective-permute-done.refs_1_ = bf16[64,2560]{1,0:T(8,128)(2,1)S(1)} collective-permute-done((bf16[64,2560]{1,0:T(8,128)(2,1)S(1)}, bf16[64,2560]{1,0:T(8,128)(2,1)S(1)}, u32[]{:S(2)}, u32[]{:S(2)}) %collective-permute-start) | collective-permute-done | bytes 327712 | tf_op jit(solution)/shard_map/ppermute | solution.py:344
  26.2 0.0 collective-permute-start.4
  26.2 0.1 pad_maximum_fusion
  26.3 5.4 %collective-permute-done.2.refs_2_ = bf16[64,2560]{1,0:T(8,128)(2,1)S(1)} collective-permute-done((bf16[64,2560]{1,0:T(8,128)(2,1)S(1)}, bf16[64,2560]{1,0:T(8,128)(2,1)S(1)}, u32[]{:S(2)}, u32[]{:S(2)}) %collective-permute-start.2) | collective-permute-done | bytes 327712 | tf_op jit(solution)/shard_map/ppermute | solution.py:344
  31.8 0.0 collective-permute-done.3.refs_3_
  31.8 0.0 collective-permute-done.5.refs_5_
  31.8 0.5 %down.1.low_ref = f32[256,128]{1,0:T(8,128)S(1)} custom-call(s32[1]{0:T(128)} %bitcast.2.group_ref, bf16[1,2560,128]{2,1,0:T(8,128)(2,1)S(1)} %get-tuple-element.62.down_ref, bf16[64,2560]{1,0:T(8,128)(2,1)S(1)} %get-tuple-element.63.refs_0_, bf16[64,2560]{1,0:T(8,128)(2,1)S(1)} %collective-permute-done.refs_1_, ...), custom_call_target="tpu_custom_call" | custom-call | flops 335544320 | bytes 1966080 | tf_op jit(solution)/shard_map/down/pallas_call | solution.py:435
  32.3 0.1 collective-permute-start.6
  32.4 0.0 collective-permute-done.7.refs_0_
  32.4 1.6 %collective-permute-start.8 = (bf16[1,128,512]{2,1,0:T(8,128)(2,1)S(1)}, bf16[1,128,512]{2,1,0:T(8,128)(2,1)S(1)}, u32[]{:S(2)}, u32[]{:S(2)}) collective-permute-start(bf16[1,128,512]{2,1,0:T(8,128)(2,1)S(1)} %collective-permute-done.7.refs_0_), channel_id=1, source_target_pairs={{0,16},{16,0},{1,17},{17,1},{2,18},{18,2},{3,19},{19,3},{4,20},{20... | collective-permute-start | bytes 393224 | tf_op jit(solution)/shard_map/ppermute | solution.py:344
  34.0 0.0 collective-permute-done.6.other_ref
  34.0 0.4 near_terms.1
  34.4 0.6 %collective-permute-start.9 = (s16[32,1024]{1,0:T(8,128)(2,1)S(1)}, s16[32,1024]{1,0:T(8,128)(2,1)S(1)}, u32[]{:S(2)}, u32[]{:S(2)}) collective-permute-start(s16[32,1024]{1,0:T(8,128)(2,1)S(1)} %get-tuple-element.84), channel_id=1, source_target_pairs={{0,2},{2,0},{4,6},{6,4},{8,10},{10,8},{12,14},{14,12},{1,3},{3,1},... | collective-permute-start | bytes 196616 | tf_op jit(solution)/shard_map/ppermute | solution.py:344
  35.0 0.6 %collective-permute-start.13 = (s16[32,1024]{1,0:T(8,128)(2,1)S(1)}, s16[32,1024]{1,0:T(8,128)(2,1)S(1)}, u32[]{:S(2)}, u32[]{:S(2)}) collective-permute-start(s16[32,1024]{1,0:T(8,128)(2,1)S(1)} %get-tuple-element.91), channel_id=1, source_target_pairs={{0,6},{2,4},{4,2},{6,0},{8,14},{10,12},{12,10},{14,8},{1,7},{3,5},... | collective-permute-start | bytes 196616 | tf_op jit(solution)/shard_map/ppermute | solution.py:344
  35.6 2.3 %collective-permute-start.14 = (s16[32,1024]{1,0:T(8,128)(2,1)S(1)}, s16[32,1024]{1,0:T(8,128)(2,1)S(1)}, u32[]{:S(2)}, u32[]{:S(2)}) collective-permute-start(s16[32,1024]{1,0:T(8,128)(2,1)S(1)} %get-tuple-element.92), channel_id=1, source_target_pairs={{0,4},{2,6},{4,0},{6,2},{8,12},{10,14},{12,8},{14,10},{1,5},{3,7},... | collective-permute-start | bytes 196616 | tf_op jit(solution)/shard_map/ppermute | solution.py:344
  38.0 0.3 collective-permute-done.8.refs_1_
  38.3 0.5 far_terms.1
  38.8 0.7 %collective-permute-done.9.refs_5_ = s16[32,1024]{1,0:T(8,128)(2,1)S(1)} collective-permute-done((s16[32,1024]{1,0:T(8,128)(2,1)S(1)}, s16[32,1024]{1,0:T(8,128)(2,1)S(1)}, u32[]{:S(2)}, u32[]{:S(2)}) %collective-permute-start.9) | collective-permute-done | bytes 65568 | tf_op jit(solution)/shard_map/ppermute | solution.py:344
  39.5 0.0 collective-permute-start.10
  39.5 0.6 %collective-permute-start.11 = (s16[32,1024]{1,0:T(8,128)(2,1)S(1)}, s16[32,1024]{1,0:T(8,128)(2,1)S(1)}, u32[]{:S(2)}, u32[]{:S(2)}) collective-permute-start(s16[32,1024]{1,0:T(8,128)(2,1)S(1)} %get-tuple-element.87), channel_id=1, source_target_pairs={{0,6},{2,4},{4,2},{6,0},{8,14},{10,12},{12,10},{14,8},{1,7},{3,5},... | collective-permute-start | bytes 196616 | tf_op jit(solution)/shard_map/ppermute | solution.py:344
  40.1 0.4 collective-permute-done.13.refs_6_
  40.5 2.5 %collective-permute-start.12 = (s16[32,1024]{1,0:T(8,128)(2,1)S(1)}, s16[32,1024]{1,0:T(8,128)(2,1)S(1)}, u32[]{:S(2)}, u32[]{:S(2)}) collective-permute-start(s16[32,1024]{1,0:T(8,128)(2,1)S(1)} %get-tuple-element.88), channel_id=1, source_target_pairs={{0,4},{2,6},{4,0},{6,2},{8,12},{10,14},{12,8},{14,10},{1,5},{3,7},... | collective-permute-start | bytes 196616 | tf_op jit(solution)/shard_map/ppermute | solution.py:344
  43.0 0.0 copy-done.1
  43.0 0.0 collective-permute-done.14.refs_7_
  43.0 0.0 collective-permute-done.4.other_ref
  43.0 0.8 %collective-permute-done.10.refs_1_ = s16[32,1024]{1,0:T(8,128)(2,1)S(1)} collective-permute-done((s16[32,1024]{1,0:T(8,128)(2,1)S(1)}, s16[32,1024]{1,0:T(8,128)(2,1)S(1)}, u32[]{:S(2)}, u32[]{:S(2)}) %collective-permute-start.10) | collective-permute-done | bytes 65568 | tf_op jit(solution)/shard_map/ppermute | solution.py:344
  43.7 0.9 %collective-permute-done.11.refs_2_ = s16[32,1024]{1,0:T(8,128)(2,1)S(1)} collective-permute-done((s16[32,1024]{1,0:T(8,128)(2,1)S(1)}, s16[32,1024]{1,0:T(8,128)(2,1)S(1)}, u32[]{:S(2)}, u32[]{:S(2)}) %collective-permute-start.11) | collective-permute-done | bytes 65568 | tf_op jit(solution)/shard_map/ppermute | solution.py:344
  44.6 1.3 %collective-permute-done.12.refs_3_ = s16[32,1024]{1,0:T(8,128)(2,1)S(1)} collective-permute-done((s16[32,1024]{1,0:T(8,128)(2,1)S(1)}, s16[32,1024]{1,0:T(8,128)(2,1)S(1)}, u32[]{:S(2)}, u32[]{:S(2)}) %collective-permute-start.12) | collective-permute-done | bytes 65568 | tf_op jit(solution)/shard_map/ppermute | solution.py:344
  45.9 0.0 copy-done
  45.9 1.7 %finish.1 = bf16[1024,128]{1,0:T(8,128)(2,1)} custom-call(s32[1]{0:T(128)} %bitcast.me_ref, s32[1,128]{1,0:T(1,128)S(1)} %bitcast.9, f32[128,1024]{1,0:T(8,128)S(1)} %get-tuple-element.58.mine_ref, f32[128,1024]{1,0:T(8,128)S(1)} %collective-permute-done.4.other_ref, f32[128,128]{1,0:T(8,128)S(1)} %get-tuple-element.60.cos_ref, ...), custom_call_target="tpu_custom_call" | custom-call | flops 134217728 | bytes 524288 | tf_op jit(solution)/shard_map/finish/pallas_call | solution.py:477
  (2 shorter events, 0.0 us)
Async XLA Ops:
  0.0 45.9 %copy-start = (s32[128,1]{0,1:T(1,128)S(1)}, s32[128,1]{0,1:T(1,128)}, u32[]{:S(2)}) copy-start(s32[128,1]{0,1:T(1,128)} %param.9) | copy-start | bytes 1540
  0.0 43.0 %copy-start.1 = (bf16[128]{0:T(256)(128)(2,1)S(1)}, bf16[128]{0:T(256)(128)(2,1)}, u32[]{:S(2)}) copy-start(bf16[128]{0:T(256)(128)(2,1)} %param.15) | copy-start | bytes 772
  1.8 19.8 %collective-permute-start.1 = (bf16[1,1280,128]{2,1,0:T(8,128)(2,1)S(1)}, bf16[1,1280,128]{2,1,0:T(8,128)(2,1)S(1)}, u32[]{:S(2)}, u32[]{:S(2)}) collective-permute-start(bf16[1,1280,128]{2,1,0:T(8,128)(2,1)S(1)} %get-tuple-element.51), channel_id=1, source_target_pairs={{0,8},{2,10},{4,12},{6,14},{8,0},{10,2},{12,4},{14,6},{1,9},{3,11}... | collective-permute-start | bytes 983048 | tf_op jit(solution)/shard_map/ppermute | solution.py:344
  5.9 20.3 %collective-permute-start = (bf16[64,2560]{1,0:T(8,128)(2,1)S(1)}, bf16[64,2560]{1,0:T(8,128)(2,1)S(1)}, u32[]{:S(2)}, u32[]{:S(2)}) collective-permute-start(bf16[64,2560]{1,0:T(8,128)(2,1)S(1)} %get-tuple-element.50), channel_id=1, source_target_pairs={{0,6},{2,4},{4,2},{6,0},{8,14},{10,12},{12,10},{14,8},{1,7},{3,5},... | collective-permute-start | bytes 983048 | tf_op jit(solution)/shard_map/ppermute | solution.py:344
  8.4 23.3 %collective-permute-start.2 = (bf16[64,2560]{1,0:T(8,128)(2,1)S(1)}, bf16[64,2560]{1,0:T(8,128)(2,1)S(1)}, u32[]{:S(2)}, u32[]{:S(2)}) collective-permute-start(bf16[64,2560]{1,0:T(8,128)(2,1)S(1)} %get-tuple-element.55), channel_id=1, source_target_pairs={{0,4},{2,6},{4,0},{6,2},{8,12},{10,14},{12,8},{14,10},{1,5},{3,7},... | collective-permute-start | bytes 983048 | tf_op jit(solution)/shard_map/ppermute | solution.py:344
  8.9 22.9 %collective-permute-start.3 = (bf16[64,2560]{1,0:T(8,128)(2,1)S(1)}, bf16[64,2560]{1,0:T(8,128)(2,1)S(1)}, u32[]{:S(2)}, u32[]{:S(2)}) collective-permute-start(bf16[64,2560]{1,0:T(8,128)(2,1)S(1)} %get-tuple-element.56), channel_id=1, source_target_pairs={{0,2},{2,0},{4,6},{6,4},{8,10},{10,8},{12,14},{14,12},{1,3},{3,1},... | collective-permute-start | bytes 983048 | tf_op jit(solution)/shard_map/ppermute | solution.py:344
  11.0 21.4 %collective-permute-start.7 = (bf16[1,128,512]{2,1,0:T(8,128)(2,1)S(1)}, bf16[1,128,512]{2,1,0:T(8,128)(2,1)S(1)}, u32[]{:S(2)}, u32[]{:S(2)}) collective-permute-start(bf16[1,128,512]{2,1,0:T(8,128)(2,1)S(1)} %get-tuple-element.78), channel_id=1, source_target_pairs={{0,8},{2,10},{4,12},{6,14},{8,0},{10,2},{12,4},{14,6},{1,9},{3,11}... | collective-permute-start | bytes 393224 | tf_op jit(solution)/shard_map/ppermute | solution.py:344
  21.6 10.2 %collective-permute-start.5 = (bf16[1,1280,128]{2,1,0:T(8,128)(2,1)S(1)}, bf16[1,1280,128]{2,1,0:T(8,128)(2,1)S(1)}, u32[]{:S(2)}, u32[]{:S(2)}) collective-permute-start(bf16[1,1280,128]{2,1,0:T(8,128)(2,1)S(1)} %collective-permute-done.1.refs_4_), channel_id=1, source_target_pairs={{0,16},{16,0},{1,17},{17,1},{2,18},{18,2},{3,19},{19,3},{4,20},{20... | collective-permute-start | bytes 983048 | tf_op jit(solution)/shard_map/ppermute | solution.py:344
  26.2 16.8 %collective-permute-start.4 = (f32[128,1024]{1,0:T(8,128)S(1)}, f32[128,1024]{1,0:T(8,128)S(1)}, u32[]{:S(2)}, u32[]{:S(2)}) collective-permute-start(f32[128,1024]{1,0:T(8,128)S(1)} %get-tuple-element.59), channel_id=1, source_target_pairs={{0,1},{1,0},{2,3},{3,2},{4,5},{5,4},{6,7},{7,6},{8,9},{9,8},{10,11... | collective-permute-start | bytes 1572872 | tf_op jit(solution)/shard_map/ppermute | solution.py:344
  32.3 1.7 %collective-permute-start.6 = (f32[256,128]{1,0:T(8,128)S(1)}, f32[256,128]{1,0:T(8,128)S(1)}, u32[]{:S(2)}, u32[]{:S(2)}) collective-permute-start(f32[256,128]{1,0:T(8,128)S(1)} %down.1.low_ref), channel_id=1, source_target_pairs={{0,1},{1,0},{2,3},{3,2},{4,5},{5,4},{6,7},{7,6},{8,9},{9,8},{10,11... | collective-permute-start | bytes 393224 | tf_op jit(solution)/shard_map/ppermute | solution.py:344
  32.4 5.9 %collective-permute-start.8 = (bf16[1,128,512]{2,1,0:T(8,128)(2,1)S(1)}, bf16[1,128,512]{2,1,0:T(8,128)(2,1)S(1)}, u32[]{:S(2)}, u32[]{:S(2)}) collective-permute-start(bf16[1,128,512]{2,1,0:T(8,128)(2,1)S(1)} %collective-permute-done.7.refs_0_), channel_id=1, source_target_pairs={{0,16},{16,0},{1,17},{17,1},{2,18},{18,2},{3,19},{19,3},{4,20},{20... | collective-permute-start | bytes 393224 | tf_op jit(solution)/shard_map/ppermute | solution.py:344
  34.4 5.0 %collective-permute-start.9 = (s16[32,1024]{1,0:T(8,128)(2,1)S(1)}, s16[32,1024]{1,0:T(8,128)(2,1)S(1)}, u32[]{:S(2)}, u32[]{:S(2)}) collective-permute-start(s16[32,1024]{1,0:T(8,128)(2,1)S(1)} %get-tuple-element.84), channel_id=1, source_target_pairs={{0,2},{2,0},{4,6},{6,4},{8,10},{10,8},{12,14},{14,12},{1,3},{3,1},... | collective-permute-start | bytes 196616 | tf_op jit(solution)/shard_map/ppermute | solution.py:344
  35.0 5.5 %collective-permute-start.13 = (s16[32,1024]{1,0:T(8,128)(2,1)S(1)}, s16[32,1024]{1,0:T(8,128)(2,1)S(1)}, u32[]{:S(2)}, u32[]{:S(2)}) collective-permute-start(s16[32,1024]{1,0:T(8,128)(2,1)S(1)} %get-tuple-element.91), channel_id=1, source_target_pairs={{0,6},{2,4},{4,2},{6,0},{8,14},{10,12},{12,10},{14,8},{1,7},{3,5},... | collective-permute-start | bytes 196616 | tf_op jit(solution)/shard_map/ppermute | solution.py:344
  35.6 7.3 %collective-permute-start.14 = (s16[32,1024]{1,0:T(8,128)(2,1)S(1)}, s16[32,1024]{1,0:T(8,128)(2,1)S(1)}, u32[]{:S(2)}, u32[]{:S(2)}) collective-permute-start(s16[32,1024]{1,0:T(8,128)(2,1)S(1)} %get-tuple-element.92), channel_id=1, source_target_pairs={{0,4},{2,6},{4,0},{6,2},{8,12},{10,14},{12,8},{14,10},{1,5},{3,7},... | collective-permute-start | bytes 196616 | tf_op jit(solution)/shard_map/ppermute | solution.py:344
  39.5 4.3 %collective-permute-start.10 = (s16[32,1024]{1,0:T(8,128)(2,1)S(1)}, s16[32,1024]{1,0:T(8,128)(2,1)S(1)}, u32[]{:S(2)}, u32[]{:S(2)}) collective-permute-start(s16[32,1024]{1,0:T(8,128)(2,1)S(1)} %get-tuple-element.86), channel_id=1, source_target_pairs={{0,2},{2,0},{4,6},{6,4},{8,10},{10,8},{12,14},{14,12},{1,3},{3,1},... | collective-permute-start | bytes 196616 | tf_op jit(solution)/shard_map/ppermute | solution.py:344
  39.5 5.2 %collective-permute-start.11 = (s16[32,1024]{1,0:T(8,128)(2,1)S(1)}, s16[32,1024]{1,0:T(8,128)(2,1)S(1)}, u32[]{:S(2)}, u32[]{:S(2)}) collective-permute-start(s16[32,1024]{1,0:T(8,128)(2,1)S(1)} %get-tuple-element.87), channel_id=1, source_target_pairs={{0,6},{2,4},{4,2},{6,0},{8,14},{10,12},{12,10},{14,8},{1,7},{3,5},... | collective-permute-start | bytes 196616 | tf_op jit(solution)/shard_map/ppermute | solution.py:344
  40.5 5.4 %collective-permute-start.12 = (s16[32,1024]{1,0:T(8,128)(2,1)S(1)}, s16[32,1024]{1,0:T(8,128)(2,1)S(1)}, u32[]{:S(2)}, u32[]{:S(2)}) collective-permute-start(s16[32,1024]{1,0:T(8,128)(2,1)S(1)} %get-tuple-element.88), channel_id=1, source_target_pairs={{0,4},{2,6},{4,0},{6,2},{8,12},{10,14},{12,8},{14,10},{1,5},{3,7},... | collective-permute-start | bytes 196616 | tf_op jit(solution)/shard_map/ppermute | solution.py:344

commit v14 on v12

--- a/solution.py
+++ b/solution.py
@@ -420,7 +420,7 @@
     cosine = jnp.concatenate([cosine, cosine], axis=1)
     sine = jnp.concatenate([-sine, sine], axis=1)
 
-    far_ups, theirs = lax.optimization_barrier((far_ups, theirs))
+    far_up, arrived[1], theirs = lax.optimization_barrier((far_up, arrived[1], theirs))
     other = exchange(theirs, "tp", cores, 1)
     arrived, mine, cosine, sine = lax.optimization_barrier((arrived, mine, cosine, sine))
     slots = buffers * size

time: 47.4 us -> 45.6 us (0.962)
  waiting for transfers between devices: 18.4 us -> 17.2 us
  starting transfers between devices: 15.6 us -> 15.1 us
    ppermute x12, waiting for transfers between devices: 18.4 us -> 17.2 us  [exchange(): return lax.ppermute(x, axis, [(p, p ^ j) for p in range(count)])]
    ppermute x12, starting transfers between devices: 15.6 us -> 15.1 us  [exchange(): return lax.ppermute(x, axis, [(p, p ^ j) for p in range(count)])]
  transfers between devices with their start and end apart: 12 -> 12, of which waited for: 6 -> 8; matrix products, arithmetic and copies ran while one was open for 2% -> 2% of each run, Pallas kernels for 17% -> 17%
where the time goes in v14:
time: 45.6 us; the launch traced here: 45.5 us
  waiting for transfers between devices  17.2 us (38%)
  starting transfers between devices  15.1 us (33%)
  Pallas kernels  11.3 us (25%)
  other arithmetic  1.08 us (2%)
  between operations  0.74 us (2%)
    ppermute x12, waiting for transfers between devices, exchange(): return lax.ppermute(x, axis, [(p, p ^ j) for p in range(count)])  17.2 us
    ppermute x12, starting transfers between devices, exchange(): return lax.ppermute(x, axis, [(p, p ^ j) for p in range(count)])  15.1 us
    pallas_call x1, Pallas kernels, body(): pl.pallas_call(base_kernel, in_specs=[SMEM] + [HBM] * 4, out_specs=[VMEM]...  5.63 us
    pallas_call x1, Pallas kernels, body(): pl.pallas_call(functools.partial(pick_kernel, pool, local, depth), in_spe...  1.78 us
    pallas_call x1, Pallas kernels, body(): pl.pallas_call(functools.partial(finish_kernel, buffers, pool, local, dep...  1.66 us
    pallas_call x1, Pallas kernels, body(): pl.pallas_call(functools.partial(up_share_kernel, cores), in_specs=[SMEM]...  0.95 us
  transfers between devices with their start and end apart: 12, of which 8 were waited for; matrix products, arithmetic and copies ran while one was open for 2% of the time, Pallas kernels for 17%

profile of v14, /device:TPU:0, one launch (start us, length us, event | category | flops | bytes accessed | tf_op | source)
XLA Modules:
  0.0 45.5 jit_solution(7026128824719205780)
XLA Ops:
  0.0 0.0 copy-start
  0.0 0.0 copy-start.1
  0.0 1.8 %pick.1 = (bf16[1,1280,128]{2,1,0:T(8,128)(2,1)S(1)}, bf16[64,2560]{1,0:T(8,128)(2,1)S(1)}, bf16[64,2560]{1,0:T(8,128)(2,1)S(1)}, bf16[64,2560]{1,0:T(8,128)(2,1)S(1)}, bf16[64,2560]{1,0:T(8,128)(2,1)S(1)}) custom-call(s32[1]{0:T(128)} %bitcast.me_ref, s32[1]{0:T(128)} %bitcast.2.group_ref, s32[1,128]{1,0:T(1,128)} %bitcast.8, bf16[128,2560]{1,0:T(8,128)(2,1)} %tokens_hbm.3, ...), custom_call_target="tpu_custom_call" | custom-call | flops 167772160 | bytes 1966080 | tf_op jit(solution)/shard_map/pick/pallas_call | solution.py:341
  1.8 4.1 %collective-permute-start.1 = (bf16[1,1280,128]{2,1,0:T(8,128)(2,1)S(1)}, bf16[1,1280,128]{2,1,0:T(8,128)(2,1)S(1)}, u32[]{:S(2)}, u32[]{:S(2)}) collective-permute-start(bf16[1,1280,128]{2,1,0:T(8,128)(2,1)S(1)} %get-tuple-element.43), channel_id=1, source_target_pairs={{0,8},{2,10},{4,12},{6,14},{8,0},{10,2},{12,4},{14,6},{1,9},{3,11}... | collective-permute-start | bytes 983048 | tf_op jit(solution)/shard_map/ppermute | solution.py:333
  5.9 2.5 %collective-permute-start.2 = (bf16[64,2560]{1,0:T(8,128)(2,1)S(1)}, bf16[64,2560]{1,0:T(8,128)(2,1)S(1)}, u32[]{:S(2)}, u32[]{:S(2)}) collective-permute-start(bf16[64,2560]{1,0:T(8,128)(2,1)S(1)} %get-tuple-element.39), channel_id=1, source_target_pairs={{0,6},{2,4},{4,2},{6,0},{8,14},{10,12},{12,10},{14,8},{1,7},{3,5},... | collective-permute-start | bytes 983048 | tf_op jit(solution)/shard_map/ppermute | solution.py:333
  9.1 0.9 %up_share.1 = (bf16[1,128,512]{2,1,0:T(8,128)(2,1)S(1)}, f32[1,128]{1,0:T(1,128)S(1)}) custom-call(s32[1]{0:T(128)} %bitcast.2.group_ref, s32[1]{0:T(128)} %bitcast.3.core_ref, s32[1]{0:T(128)S(6)} %copy.9.ranks_ref, bf16[1,128,2048]{2,1,0:T(8,128)(2,1)} %up_hbm.2), custom_call_target="tpu_custom_call" | custom-call | flops 65536 | bytes 262144 | tf_op jit(solution)/shard_map/up_share/pallas_call | solution.py:360
  10.0 0.4 collective-permute-start
  10.4 0.4 collective-permute-start.3
  10.9 0.3 collective-permute-start.4
  11.1 0.7 %convert_element_type.4 = f32[128]{0:T(128)S(1)} convert(s32[128]{0:T(128)} %param.10) | non-fusion elementwise | flops 128 | bytes 1024 | tf_op jit(solution)/shard_map/convert_element_type | solution.py:418
  11.8 5.6 %base.1 = (f32[128,1024]{1,0:T(8,128)S(1)}, f32[128,1024]{1,0:T(8,128)S(1)}, bf16[1,2560,128]{2,1,0:T(8,128)(2,1)S(1)}, bf16[1,128,1024]{2,1,0:T(8,128)(2,1)S(1)}) custom-call(s32[1]{0:T(128)} %bitcast.3.core_ref, bf16[128,2560]{1,0:T(8,128)(2,1)} %tokens_hbm.3, bf16[2560,2048]{1,0:T(8,128)(2,1)} %weight_hbm.1, bf16[1,2560,128]{2,1,0:T(8,128)(2,1)} %down_hbm.3, ...), custom_call_target="tpu_custom_call" | custom-call | flops 1342177280 | bytes 10485760 | tf_op jit(solution)/shard_map/base/pallas_call | solution.py:385
  17.5 4.9 %collective-permute-done.1.refs_4_ = bf16[1,1280,128]{2,1,0:T(8,128)(2,1)S(1)} collective-permute-done((bf16[1,1280,128]{2,1,0:T(8,128)(2,1)S(1)}, bf16[1,1280,128]{2,1,0:T(8,128)(2,1)S(1)}, u32[]{:S(2)}, u32[]{:S(2)}) %collective-permute-start.1) | collective-permute-done | bytes 327712 | tf_op jit(solution)/shard_map/ppermute | solution.py:333
  22.3 2.1 %collective-permute-start.6 = (bf16[1,1280,128]{2,1,0:T(8,128)(2,1)S(1)}, bf16[1,1280,128]{2,1,0:T(8,128)(2,1)S(1)}, u32[]{:S(2)}, u32[]{:S(2)}) collective-permute-start(bf16[1,1280,128]{2,1,0:T(8,128)(2,1)S(1)} %collective-permute-done.1.refs_4_), channel_id=1, source_target_pairs={{0,16},{16,0},{1,17},{17,1},{2,18},{18,2},{3,19},{19,3},{4,20},{20... | collective-permute-start | bytes 983048 | tf_op jit(solution)/shard_map/ppermute | solution.py:333
  24.5 0.3 fusion
  24.8 1.6 %collective-permute-done.refs_0_ = bf16[1,128,512]{2,1,0:T(8,128)(2,1)S(1)} collective-permute-done((bf16[1,128,512]{2,1,0:T(8,128)(2,1)S(1)}, bf16[1,128,512]{2,1,0:T(8,128)(2,1)S(1)}, u32[]{:S(2)}, u32[]{:S(2)}) %collective-permute-start) | collective-permute-done | bytes 131104 | tf_op jit(solution)/shard_map/ppermute | solution.py:333
  26.4 0.0 collective-permute-done.2.refs_1_
  26.4 0.0 collective-permute-start.5
  26.4 0.1 pad_maximum_fusion
  26.5 1.6 %collective-permute-start.8 = (bf16[1,128,512]{2,1,0:T(8,128)(2,1)S(1)}, bf16[1,128,512]{2,1,0:T(8,128)(2,1)S(1)}, u32[]{:S(2)}, u32[]{:S(2)}) collective-permute-start(bf16[1,128,512]{2,1,0:T(8,128)(2,1)S(1)} %collective-permute-done.refs_0_), channel_id=1, source_target_pairs={{0,16},{16,0},{1,17},{17,1},{2,18},{18,2},{3,19},{19,3},{4,20},{20... | collective-permute-start | bytes 393224 | tf_op jit(solution)/shard_map/ppermute | solution.py:333
  28.1 3.6 %collective-permute-done.3.refs_2_ = bf16[64,2560]{1,0:T(8,128)(2,1)S(1)} collective-permute-done((bf16[64,2560]{1,0:T(8,128)(2,1)S(1)}, bf16[64,2560]{1,0:T(8,128)(2,1)S(1)}, u32[]{:S(2)}, u32[]{:S(2)}) %collective-permute-start.3) | collective-permute-done | bytes 327712 | tf_op jit(solution)/shard_map/ppermute | solution.py:333
  31.8 0.0 collective-permute-done.4.refs_3_
  31.8 0.0 collective-permute-done.6.refs_5_
  31.8 0.5 %down.1.low_ref = f32[256,128]{1,0:T(8,128)S(1)} custom-call(s32[1]{0:T(128)} %bitcast.2.group_ref, bf16[1,2560,128]{2,1,0:T(8,128)(2,1)S(1)} %get-tuple-element.56.down_ref, bf16[64,2560]{1,0:T(8,128)(2,1)S(1)} %get-tuple-element.57.refs_0_, bf16[64,2560]{1,0:T(8,128)(2,1)S(1)} %collective-permute-done.2.refs_1_, ...), custom_call_target="tpu_custom_call" | custom-call | flops 335544320 | bytes 1966080 | tf_op jit(solution)/shard_map/down/pallas_call | solution.py:427
  32.3 0.1 collective-permute-start.7
  32.4 0.1 collective-permute-done.8.refs_1_
  32.5 1.2 %collective-permute-done.7.other_ref = f32[256,128]{1,0:T(8,128)S(1)} collective-permute-done((f32[256,128]{1,0:T(8,128)S(1)}, f32[256,128]{1,0:T(8,128)S(1)}, u32[]{:S(2)}, u32[]{:S(2)}) %collective-permute-start.7) | collective-permute-done | bytes 131104 | tf_op jit(solution)/shard_map/ppermute | solution.py:333
  33.7 0.8 %up.1 = (s16[64,1024]{1,0:T(8,128)(2,1)S(1)}, s16[64,1024]{1,0:T(8,128)(2,1)S(1)}, s16[64,1024]{1,0:T(8,128)(2,1)S(1)}, s16[64,1024]{1,0:T(8,128)(2,1)S(1)}) custom-call(s32[1]{0:T(128)} %bitcast.2.group_ref, f32[256,128]{1,0:T(8,128)S(1)} %down.1.low_ref, f32[256,128]{1,0:T(8,128)S(1)} %collective-permute-done.7.other_ref, ...), custom_call_target="tpu_custom_call" | custom-call | flops 268435456 | bytes 524288 | tf_op jit(solution)/shard_map/up/pallas_call | solution.py:438
  34.5 1.9 %collective-permute-start.10 = (s16[64,1024]{1,0:T(8,128)(2,1)S(1)}, s16[64,1024]{1,0:T(8,128)(2,1)S(1)}, u32[]{:S(2)}, u32[]{:S(2)}) collective-permute-start(s16[64,1024]{1,0:T(8,128)(2,1)S(1)} %get-tuple-element.65), channel_id=1, source_target_pairs={{0,6},{2,4},{4,2},{6,0},{8,14},{10,12},{12,10},{14,8},{1,7},{3,5},... | collective-permute-start | bytes 393224 | tf_op jit(solution)/shard_map/ppermute | solution.py:333
  36.4 0.2 collective-permute-start.11
  36.7 1.4 %collective-permute-start.9 = (s16[64,1024]{1,0:T(8,128)(2,1)S(1)}, s16[64,1024]{1,0:T(8,128)(2,1)S(1)}, u32[]{:S(2)}, u32[]{:S(2)}) collective-permute-start(s16[64,1024]{1,0:T(8,128)(2,1)S(1)} %get-tuple-element.64), channel_id=1, source_target_pairs={{0,2},{2,0},{4,6},{6,4},{8,10},{10,8},{12,14},{14,12},{1,3},{3,1},... | collective-permute-start | bytes 393224 | tf_op jit(solution)/shard_map/ppermute | solution.py:333
  38.0 0.0 copy-done.1
  38.1 0.0 collective-permute-done.5.other_ref
  38.1 3.7 %collective-permute-done.10.refs_2_ = s16[64,1024]{1,0:T(8,128)(2,1)S(1)} collective-permute-done((s16[64,1024]{1,0:T(8,128)(2,1)S(1)}, s16[64,1024]{1,0:T(8,128)(2,1)S(1)}, u32[]{:S(2)}, u32[]{:S(2)}) %collective-permute-start.10) | collective-permute-done | bytes 131104 | tf_op jit(solution)/shard_map/ppermute | solution.py:333
  41.8 1.1 %collective-permute-done.11.refs_3_ = s16[64,1024]{1,0:T(8,128)(2,1)S(1)} collective-permute-done((s16[64,1024]{1,0:T(8,128)(2,1)S(1)}, s16[64,1024]{1,0:T(8,128)(2,1)S(1)}, u32[]{:S(2)}, u32[]{:S(2)}) %collective-permute-start.11) | collective-permute-done | bytes 131104 | tf_op jit(solution)/shard_map/ppermute | solution.py:333
  42.9 0.9 %collective-permute-done.9.refs_1_ = s16[64,1024]{1,0:T(8,128)(2,1)S(1)} collective-permute-done((s16[64,1024]{1,0:T(8,128)(2,1)S(1)}, s16[64,1024]{1,0:T(8,128)(2,1)S(1)}, u32[]{:S(2)}, u32[]{:S(2)}) %collective-permute-start.9) | collective-permute-done | bytes 131104 | tf_op jit(solution)/shard_map/ppermute | solution.py:333
  43.8 0.0 copy-done
  43.8 1.7 %finish.1 = bf16[1024,128]{1,0:T(8,128)(2,1)} custom-call(s32[1]{0:T(128)} %bitcast.me_ref, s32[1,128]{1,0:T(1,128)S(1)} %bitcast.9, f32[128,1024]{1,0:T(8,128)S(1)} %get-tuple-element.52.mine_ref, f32[128,1024]{1,0:T(8,128)S(1)} %collective-permute-done.5.other_ref, f32[128,128]{1,0:T(8,128)S(1)} %get-tuple-element.54.cos_ref, ...), custom_call_target="tpu_custom_call" | custom-call | flops 134217728 | bytes 524288 | tf_op jit(solution)/shard_map/finish/pallas_call | solution.py:451
  (2 shorter events, 0.0 us)
Async XLA Ops:
  0.0 43.8 %copy-start = (s32[128,1]{0,1:T(1,128)S(1)}, s32[128,1]{0,1:T(1,128)}, u32[]{:S(2)}) copy-start(s32[128,1]{0,1:T(1,128)} %param.9) | copy-start | bytes 1540
  0.0 38.0 %copy-start.1 = (bf16[128]{0:T(256)(128)(2,1)S(1)}, bf16[128]{0:T(256)(128)(2,1)}, u32[]{:S(2)}) copy-start(bf16[128]{0:T(256)(128)(2,1)} %param.15) | copy-start | bytes 772
  1.8 20.5 %collective-permute-start.1 = (bf16[1,1280,128]{2,1,0:T(8,128)(2,1)S(1)}, bf16[1,1280,128]{2,1,0:T(8,128)(2,1)S(1)}, u32[]{:S(2)}, u32[]{:S(2)}) collective-permute-start(bf16[1,1280,128]{2,1,0:T(8,128)(2,1)S(1)} %get-tuple-element.43), channel_id=1, source_target_pairs={{0,8},{2,10},{4,12},{6,14},{8,0},{10,2},{12,4},{14,6},{1,9},{3,11}... | collective-permute-start | bytes 983048 | tf_op jit(solution)/shard_map/ppermute | solution.py:333
  5.9 20.5 %collective-permute-start.2 = (bf16[64,2560]{1,0:T(8,128)(2,1)S(1)}, bf16[64,2560]{1,0:T(8,128)(2,1)S(1)}, u32[]{:S(2)}, u32[]{:S(2)}) collective-permute-start(bf16[64,2560]{1,0:T(8,128)(2,1)S(1)} %get-tuple-element.39), channel_id=1, source_target_pairs={{0,6},{2,4},{4,2},{6,0},{8,14},{10,12},{12,10},{14,8},{1,7},{3,5},... | collective-permute-start | bytes 983048 | tf_op jit(solution)/shard_map/ppermute | solution.py:333
  10.0 16.4 %collective-permute-start = (bf16[1,128,512]{2,1,0:T(8,128)(2,1)S(1)}, bf16[1,128,512]{2,1,0:T(8,128)(2,1)S(1)}, u32[]{:S(2)}, u32[]{:S(2)}) collective-permute-start(bf16[1,128,512]{2,1,0:T(8,128)(2,1)S(1)} %get-tuple-element.42), channel_id=1, source_target_pairs={{0,8},{2,10},{4,12},{6,14},{8,0},{10,2},{12,4},{14,6},{1,9},{3,11}... | collective-permute-start | bytes 393224 | tf_op jit(solution)/shard_map/ppermute | solution.py:333
  10.4 21.3 %collective-permute-start.3 = (bf16[64,2560]{1,0:T(8,128)(2,1)S(1)}, bf16[64,2560]{1,0:T(8,128)(2,1)S(1)}, u32[]{:S(2)}, u32[]{:S(2)}) collective-permute-start(bf16[64,2560]{1,0:T(8,128)(2,1)S(1)} %get-tuple-element.49), channel_id=1, source_target_pairs={{0,4},{2,6},{4,0},{6,2},{8,12},{10,14},{12,8},{14,10},{1,5},{3,7},... | collective-permute-start | bytes 983048 | tf_op jit(solution)/shard_map/ppermute | solution.py:333
  10.9 20.9 %collective-permute-start.4 = (bf16[64,2560]{1,0:T(8,128)(2,1)S(1)}, bf16[64,2560]{1,0:T(8,128)(2,1)S(1)}, u32[]{:S(2)}, u32[]{:S(2)}) collective-permute-start(bf16[64,2560]{1,0:T(8,128)(2,1)S(1)} %get-tuple-element.50), channel_id=1, source_target_pairs={{0,2},{2,0},{4,6},{6,4},{8,10},{10,8},{12,14},{14,12},{1,3},{3,1},... | collective-permute-start | bytes 983048 | tf_op jit(solution)/shard_map/ppermute | solution.py:333
  22.3 9.4 %collective-permute-start.6 = (bf16[1,1280,128]{2,1,0:T(8,128)(2,1)S(1)}, bf16[1,1280,128]{2,1,0:T(8,128)(2,1)S(1)}, u32[]{:S(2)}, u32[]{:S(2)}) collective-permute-start(bf16[1,1280,128]{2,1,0:T(8,128)(2,1)S(1)} %collective-permute-done.1.refs_4_), channel_id=1, source_target_pairs={{0,16},{16,0},{1,17},{17,1},{2,18},{18,2},{3,19},{19,3},{4,20},{20... | collective-permute-start | bytes 983048 | tf_op jit(solution)/shard_map/ppermute | solution.py:333
  26.4 11.7 %collective-permute-start.5 = (f32[128,1024]{1,0:T(8,128)S(1)}, f32[128,1024]{1,0:T(8,128)S(1)}, u32[]{:S(2)}, u32[]{:S(2)}) collective-permute-start(f32[128,1024]{1,0:T(8,128)S(1)} %get-tuple-element.53), channel_id=1, source_target_pairs={{0,1},{1,0},{2,3},{3,2},{4,5},{5,4},{6,7},{7,6},{8,9},{9,8},{10,11... | collective-permute-start | bytes 1572872 | tf_op jit(solution)/shard_map/ppermute | solution.py:333
  26.5 6.0 %collective-permute-start.8 = (bf16[1,128,512]{2,1,0:T(8,128)(2,1)S(1)}, bf16[1,128,512]{2,1,0:T(8,128)(2,1)S(1)}, u32[]{:S(2)}, u32[]{:S(2)}) collective-permute-start(bf16[1,128,512]{2,1,0:T(8,128)(2,1)S(1)} %collective-permute-done.refs_0_), channel_id=1, source_target_pairs={{0,16},{16,0},{1,17},{17,1},{2,18},{18,2},{3,19},{19,3},{4,20},{20... | collective-permute-start | bytes 393224 | tf_op jit(solution)/shard_map/ppermute | solution.py:333
  32.3 1.4 %collective-permute-start.7 = (f32[256,128]{1,0:T(8,128)S(1)}, f32[256,128]{1,0:T(8,128)S(1)}, u32[]{:S(2)}, u32[]{:S(2)}) collective-permute-start(f32[256,128]{1,0:T(8,128)S(1)} %down.1.low_ref), channel_id=1, source_target_pairs={{0,1},{1,0},{2,3},{3,2},{4,5},{5,4},{6,7},{7,6},{8,9},{9,8},{10,11... | collective-permute-start | bytes 393224 | tf_op jit(solution)/shard_map/ppermute | solution.py:333
  34.5 7.3 %collective-permute-start.10 = (s16[64,1024]{1,0:T(8,128)(2,1)S(1)}, s16[64,1024]{1,0:T(8,128)(2,1)S(1)}, u32[]{:S(2)}, u32[]{:S(2)}) collective-permute-start(s16[64,1024]{1,0:T(8,128)(2,1)S(1)} %get-tuple-element.65), channel_id=1, source_target_pairs={{0,6},{2,4},{4,2},{6,0},{8,14},{10,12},{12,10},{14,8},{1,7},{3,5},... | collective-permute-start | bytes 393224 | tf_op jit(solution)/shard_map/ppermute | solution.py:333
  36.4 6.5 %collective-permute-start.11 = (s16[64,1024]{1,0:T(8,128)(2,1)S(1)}, s16[64,1024]{1,0:T(8,128)(2,1)S(1)}, u32[]{:S(2)}, u32[]{:S(2)}) collective-permute-start(s16[64,1024]{1,0:T(8,128)(2,1)S(1)} %get-tuple-element.66), channel_id=1, source_target_pairs={{0,4},{2,6},{4,0},{6,2},{8,12},{10,14},{12,8},{14,10},{1,5},{3,7},... | collective-permute-start | bytes 393224 | tf_op jit(solution)/shard_map/ppermute | solution.py:333
  36.7 7.1 %collective-permute-start.9 = (s16[64,1024]{1,0:T(8,128)(2,1)S(1)}, s16[64,1024]{1,0:T(8,128)(2,1)S(1)}, u32[]{:S(2)}, u32[]{:S(2)}) collective-permute-start(s16[64,1024]{1,0:T(8,128)(2,1)S(1)} %get-tuple-element.64), channel_id=1, source_target_pairs={{0,2},{2,0},{4,6},{6,4},{8,10},{10,8},{12,14},{14,12},{1,3},{3,1},... | collective-permute-start | bytes 393224 | tf_op jit(solution)/shard_map/ppermute | solution.py:333

commit v15 on v14

--- a/solution.py
+++ b/solution.py
@@ -54,6 +54,11 @@
     return ((buffer * 2 + far) * local + (row - holder * local)) * depth + slot
 
 
+def chunk_places(share):
+    first = (share // LANES) * 4 // 5 * LANES
+    return [(0, first), (first, share - first)]
+
+
 def far_first(count):
     return sorted(range(1, count), key=lambda j: (-bin(j).count("1"), -j))
 
@@ -69,13 +74,23 @@
     return high, low
 
 
-def up_share_kernel(cores, group_ref, core_ref, ranks_ref, up_hbm, out_ref, factor_ref, own_ref, sem):
-    local, rank, share = out_ref.shape
-    at = core_ref[0] * (up_hbm.shape[2] // cores) + group_ref[0] * share
+def second_kernel(
+    group_ref, core_ref, ranks_ref, down_hbm, up_hbm, out_ref, factor_ref, own_ref, sems
+):
+    local, rank, share = own_ref.shape
+    rows = out_ref.shape[1] - share // LANES * rank
+    columns = up_hbm.shape[2] // lax.axis_size("tp")
+    at = core_ref[0] * columns + group_ref[0] * share
     copy = pltpu.make_async_copy(
-        up_hbm.at[:, :, pl.ds(pl.multiple_of(at, share), share)], own_ref, sem
+        up_hbm.at[:, :, pl.ds(pl.multiple_of(at, share), share)], own_ref, sems.at[0]
     )
     copy.start()
+    width = down_hbm.shape[1] // lax.axis_size("groups")
+    start = pl.multiple_of((group_ref[0] + 1) * width - rows, LANES)
+    down_copy = pltpu.make_async_copy(
+        down_hbm.at[:, pl.ds(start, rows), :], out_ref.at[:, pl.ds(0, rows), :], sems.at[1]
+    )
+    down_copy.start()
     copy.wait()
     for a in range(local):
         used = ranks_ref[a]
@@ -85,7 +100,11 @@
             return jnp.where(iota(shape, dim) < used, scale, 0.0)
 
         factor_ref[a : a + 1, :] = factor((1, rank), 1)
-        out_ref[a] = (own_ref[a].astype(jnp.float32) * factor((rank, 1), 0)).astype(jnp.bfloat16)
+        scaled = (own_ref[a].astype(jnp.float32) * factor((rank, 1), 0)).astype(jnp.bfloat16)
+        for i in range(share // LANES):
+            top = rows + i * rank
+            out_ref[a, top : top + rank, :] = scaled[:, i * LANES : (i + 1) * LANES]
+    down_copy.wait()
 
 
 def pick_kernel(
@@ -94,7 +113,7 @@
     share_ref, outs = refs[0], refs[1:-4]
     adapter_ref, tokens_ref, share_sem, sems = refs[-4:]
     rows, width = tokens_ref.shape
-    share = share_ref.shape[1]
+    chunk = share_ref.shape[1]
     parts = sems.shape[0] - 1
     part = rows // parts
     adapter_copy = pltpu.make_async_copy(adapter_hbm, adapter_ref, sems.at[parts])
@@ -109,8 +128,8 @@
     ]
     for copy in copies:
         copy.start()
-    at = pl.multiple_of(group_ref[0] * share, share)
-    share_copy = pltpu.make_async_copy(down_hbm.at[:, pl.ds(at, share), :], share_ref, share_sem)
+    at = pl.multiple_of(group_ref[0] * (down_hbm.shape[1] // lax.axis_size("groups")), LANES)
+    share_copy = pltpu.make_async_copy(down_hbm.at[:, pl.ds(at, chunk), :], share_ref, share_sem)
     share_copy.start()
     adapter_copy.wait()
     place = slot_places(adapter_ref[...], me_ref[0], pool, local, depth)
@@ -187,15 +206,16 @@
 def down_kernel(buffers, groups, local, depth, group_ref, down_ref, *refs):
     order = [0] + far_first(buffers)
     ins = [refs[order.index(j)] for j in range(buffers)]
-    shares, out = refs[buffers : buffers + groups], refs[-1]
+    shares, out = refs[buffers:-1], refs[-1]
     rank = out.shape[1]
-    share = shares[0].shape[1]
+    share = ins[0].shape[1] // groups
     total = None
-    for k in range(groups):
-        at = pl.multiple_of((group_ref[0] ^ k) * share, share)
-        rows = jnp.concatenate([x[:, pl.ds(at, share)] for x in ins], axis=0)
-        factors = [down_ref[a, pl.ds(at, share), :] for a in range(local)]
-        factors += [shares[k][a] for a in range(local)]
+    for k in range(2 * groups):
+        offset, chunk = chunk_places(share)[k // groups]
+        at = pl.multiple_of((group_ref[0] ^ (k % groups)) * share + offset, LANES)
+        rows = jnp.concatenate([x[:, pl.ds(at, chunk)] for x in ins], axis=0)
+        factors = [down_ref[a, pl.ds(at, chunk), :] for a in range(local)]
+        factors += [shares[k][a, :chunk, :] for a in range(local)]
         term = jnp.dot(
             rows, jnp.concatenate(factors, axis=1), preferred_element_type=jnp.float32
         )
@@ -227,7 +247,17 @@
     for k in range(groups):
         at = pl.multiple_of((group_ref[0] ^ k) * share, share)
         up = [up_ref[a, :, pl.ds(at, share)] for a in range(local)]
-        up += [shares[k][a] for a in range(local)]
+        top = shares[k].shape[1] - share // LANES * rank
+        up += [
+            jnp.concatenate(
+                [
+                    shares[k][a, top + i * rank : top + (i + 1) * rank, :]
+                    for i in range(share // LANES)
+                ],
+                axis=1,
+            )
+            for a in range(local)
+        ]
         term = jnp.dot(
             spread, jnp.concatenate(up, axis=0), preferred_element_type=jnp.float32
         )
@@ -336,13 +366,13 @@
         return [share] + [exchange(share, "groups", groups, k) for k in range(1, groups)]
 
     adapter_row = row_adapters.reshape(1, rows)
-    down_share = width // groups
+    (_, first_rows), (_, second_rows) = chunk_places(width // groups)
     parts = rows // 16
-    down_part, *picked = pl.pallas_call(
+    first, *picked = pl.pallas_call(
         functools.partial(pick_kernel, pool, local, depth),
         in_specs=[SMEM] * 2 + [HBM] * 3,
         out_specs=[VMEM] * (1 + buffers),
-        out_shape=[jax.ShapeDtypeStruct((local, down_share, rank), bf16)]
+        out_shape=[jax.ShapeDtypeStruct((local, first_rows, rank), bf16)]
         + [jax.ShapeDtypeStruct((size, width), bf16)] * buffers,
         scratch_shapes=[
             pltpu.VMEM((1, rows), jnp.int32),
@@ -354,30 +384,30 @@
         cost_estimate=cost(2 * buffers * size * rows * width, 2 * (rows + buffers * size) * width),
         name="pick",
     )(me, group, in_hbm(adapter_row), in_hbm(tokens), in_hbm(adapter_down))
-    far_down = exchange(down_part, "pool", pool, pool // 2)
+    far_first_part = exchange(first, "pool", pool, pool // 2)
     up_share = columns // groups
     ranks_now, adapter_up_now, _ = lax.optimization_barrier((ranks, adapter_up, picked))
-    up_part, factor = pl.pallas_call(
-        functools.partial(up_share_kernel, cores),
-        in_specs=[SMEM] * 3 + [HBM],
+    second, factor = pl.pallas_call(
+        second_kernel,
+        in_specs=[SMEM] * 3 + [HBM] * 2,
         out_specs=[VMEM] * 2,
         out_shape=[
-            jax.ShapeDtypeStruct((local, rank, up_share), bf16),
+            jax.ShapeDtypeStruct((local, second_rows + up_share // LANES * rank, rank), bf16),
             jax.ShapeDtypeStruct((local, rank), f32),
         ],
         scratch_shapes=[
             pltpu.VMEM((local, rank, up_share), bf16),
-            pltpu.SemaphoreType.DMA,
+            pltpu.SemaphoreType.DMA((2,)),
         ],
         compiler_params=params(),
-        cost_estimate=cost(local * rank * up_share, 4 * local * rank * up_share),
-        name="up_share",
-    )(group, core, ranks_now, in_hbm(adapter_up_now))
-    far_up = exchange(up_part, "pool", pool, pool // 2)
+        cost_estimate=cost(local * rank * up_share, 4 * local * rank * (second_rows + up_share)),
+        name="second_part",
+    )(group, core, ranks_now, in_hbm(adapter_down), in_hbm(adapter_up_now))
+    far_second_part = exchange(second, "pool", pool, pool // 2)
 
     order = far_first(buffers)
     early, late = order[:1], order[1:]
-    late_rows, _ = lax.optimization_barrier(([picked[j] for j in late], up_part))
+    late_rows, _ = lax.optimization_barrier(([picked[j] for j in late], second))
     leaving = [picked[j] for j in early] + late_rows
     arrived = [picked[0]] + [exchange(x, "pool", pool, j) for x, j in zip(leaving, order)]
 
@@ -407,10 +437,11 @@
         in_hbm(adapter_down),
         in_hbm(adapter_up),
     )
-    far_down, theirs = lax.optimization_barrier((far_down, theirs))
-    far_downs = hand_round(far_down)
-    far_up, _ = lax.optimization_barrier((far_up, far_down))
-    far_ups = hand_round(far_up)
+    far_first_part, theirs = lax.optimization_barrier((far_first_part, theirs))
+    firsts = hand_round(far_first_part)
+    far_second_part, _ = lax.optimization_barrier((far_second_part, far_first_part))
+    seconds = hand_round(far_second_part)
+
     half_dim = head // 2
     frequency = jnp.power(
         f32(ROPE_THETA), -jnp.arange(half_dim, dtype=f32) * (2.0 / head)
@@ -420,19 +451,19 @@
     cosine = jnp.concatenate([cosine, cosine], axis=1)
     sine = jnp.concatenate([-sine, sine], axis=1)
 
-    far_up, arrived[1], theirs = lax.optimization_barrier((far_up, arrived[1], theirs))
+    arrived[1], theirs = lax.optimization_barrier((arrived[1], theirs))
     other = exchange(theirs, "tp", cores, 1)
     arrived, mine, cosine, sine = lax.optimization_barrier((arrived, mine, cosine, sine))
     slots = buffers * size
     low = pl.pallas_call(
         functools.partial(down_kernel, buffers, groups, local, depth),
-        in_specs=[SMEM] + [VMEM] * (1 + buffers + groups),
+        in_specs=[SMEM] + [VMEM] * (1 + buffers + 2 * groups),
         out_specs=VMEM,
         out_shape=jax.ShapeDtypeStruct((slots, rank), f32),
         compiler_params=params(),
         cost_estimate=cost(4 * local * slots * rank * width, 2 * (slots + rank) * width),
         name="down",
-    )(group, own_down, *arrived, *far_downs)
+    )(group, own_down, *arrived, *firsts, *seconds)
     low_other = exchange(low, "tp", cores, 1)
 
     terms = pl.pallas_call(
@@ -444,7 +475,7 @@
         compiler_params=params(),
         cost_estimate=cost(8 * local * slots * rank * columns, 2 * slots * columns),
         name="up",
-    )(group, low, low_other, factor, own_up, *far_ups)
+    )(group, low, low_other, factor, own_up, *seconds)
     order = return_order(buffers)
     returned = [terms[0]] + [exchange(terms[j], "pool", pool, j) for j in order]
 

time: 45.6 us -> 46.1 us (1.011)
  waiting for transfers between devices: 17.2 us -> 17.9 us
    ppermute x12, waiting for transfers between devices: 17.2 us -> 17.9 us  [exchange(): return lax.ppermute(x, axis, [(p, p ^ j) for p in range(count)])]
  transfers between devices with their start and end apart: 12 -> 12, of which waited for: 8 -> 7; matrix products, arithmetic and copies ran while one was open for 2% -> 2% of each run, Pallas kernels for 17% -> 17%
where the time goes in v15:
time: 46.1 us; the launch traced here: 45.9 us
  waiting for transfers between devices  17.9 us (39%)
  starting transfers between devices  14.8 us (32%)
  Pallas kernels  11.3 us (25%)
  other arithmetic  1.08 us (2%)
  between operations  0.75 us (2%)
    ppermute x12, waiting for transfers between devices, exchange(): return lax.ppermute(x, axis, [(p, p ^ j) for p in range(count)])  17.9 us
    ppermute x12, starting transfers between devices, exchange(): return lax.ppermute(x, axis, [(p, p ^ j) for p in range(count)])  14.8 us
    pallas_call x1, Pallas kernels, body(): pl.pallas_call(base_kernel, in_specs=[SMEM] + [HBM] * 4, out_specs=[VMEM]...  5.63 us
    pallas_call x1, Pallas kernels, body(): pl.pallas_call(functools.partial(pick_kernel, pool, local, depth), in_spe...  1.78 us
    pallas_call x1, Pallas kernels, body(): pl.pallas_call(functools.partial(finish_kernel, buffers, pool, local, dep...  1.67 us
    pallas_call x1, Pallas kernels, body(): pl.pallas_call(second_kernel, in_specs=[SMEM] * 3 + [HBM] * 2, out_specs=...  0.96 us
  transfers between devices with their start and end apart: 12, of which 7 were waited for; matrix products, arithmetic and copies ran while one was open for 2% of the time, Pallas kernels for 17%

profile of v15, /device:TPU:0, one launch (start us, length us, event | category | flops | bytes accessed | tf_op | source)
XLA Modules:
  0.0 45.9 jit_solution(6644713999678382979)
XLA Ops:
  0.0 0.0 copy-start
  0.0 0.0 copy-start.1
  0.0 1.8 %pick.1 = (bf16[1,1024,128]{2,1,0:T(8,128)(2,1)S(1)}, bf16[64,2560]{1,0:T(8,128)(2,1)S(1)}, bf16[64,2560]{1,0:T(8,128)(2,1)S(1)}, bf16[64,2560]{1,0:T(8,128)(2,1)S(1)}, bf16[64,2560]{1,0:T(8,128)(2,1)S(1)}) custom-call(s32[1]{0:T(128)} %bitcast.me_ref, s32[1]{0:T(128)} %bitcast.2.group_ref, s32[1,128]{1,0:T(1,128)} %bitcast.8, bf16[128,2560]{1,0:T(8,128)(2,1)} %tokens_hbm.3, ...), custom_call_target="tpu_custom_call" | custom-call | flops 167772160 | bytes 1966080 | tf_op jit(solution)/shard_map/pick/pallas_call | solution.py:371
  1.8 4.1 %collective-permute-start.1 = (bf16[1,1024,128]{2,1,0:T(8,128)(2,1)S(1)}, bf16[1,1024,128]{2,1,0:T(8,128)(2,1)S(1)}, u32[]{:S(2)}, u32[]{:S(2)}) collective-permute-start(bf16[1,1024,128]{2,1,0:T(8,128)(2,1)S(1)} %get-tuple-element.38), channel_id=1, source_target_pairs={{0,8},{2,10},{4,12},{6,14},{8,0},{10,2},{12,4},{14,6},{1,9},{3,11}... | collective-permute-start | bytes 786440 | tf_op jit(solution)/shard_map/ppermute | solution.py:363
  5.9 2.5 %collective-permute-start = (bf16[64,2560]{1,0:T(8,128)(2,1)S(1)}, bf16[64,2560]{1,0:T(8,128)(2,1)S(1)}, u32[]{:S(2)}, u32[]{:S(2)}) collective-permute-start(bf16[64,2560]{1,0:T(8,128)(2,1)S(1)} %get-tuple-element.37), channel_id=1, source_target_pairs={{0,6},{2,4},{4,2},{6,0},{8,14},{10,12},{12,10},{14,8},{1,7},{3,5},... | collective-permute-start | bytes 983048 | tf_op jit(solution)/shard_map/ppermute | solution.py:363
  9.1 1.0 %second_part.1 = (bf16[1,768,128]{2,1,0:T(8,128)(2,1)S(1)}, f32[1,128]{1,0:T(1,128)S(1)}) custom-call(s32[1]{0:T(128)} %bitcast.2.group_ref, s32[1]{0:T(128)} %bitcast.3.core_ref, s32[1]{0:T(128)S(6)} %copy.9.ranks_ref, bf16[1,2560,128]{2,1,0:T(8,128)(2,1)} %down_hbm.5, bf16[1,128,2048]{2,1,0:T(8,128)(2,1)} %up_hbm.2), custom_call_target="tpu_custom_call" | custom-call | flops 65536 | bytes 393216 | tf_op jit(solution)/shard_map/second_part/pallas_call | solution.py:390
  10.0 0.4 collective-permute-start.6
  10.4 0.4 collective-permute-start.2
  10.9 0.3 collective-permute-start.3
  11.2 0.7 %convert_element_type.4 = f32[128]{0:T(128)S(1)} convert(s32[128]{0:T(128)} %param.10) | non-fusion elementwise | flops 128 | bytes 1024 | tf_op jit(solution)/shard_map/convert_element_type | solution.py:449
  11.8 5.6 %base.1 = (f32[128,1024]{1,0:T(8,128)S(1)}, f32[128,1024]{1,0:T(8,128)S(1)}, bf16[1,2560,128]{2,1,0:T(8,128)(2,1)S(1)}, bf16[1,128,1024]{2,1,0:T(8,128)(2,1)S(1)}) custom-call(s32[1]{0:T(128)} %bitcast.3.core_ref, bf16[128,2560]{1,0:T(8,128)(2,1)} %tokens_hbm.3, bf16[2560,2048]{1,0:T(8,128)(2,1)} %weight_hbm.1, bf16[1,2560,128]{2,1,0:T(8,128)(2,1)} %down_hbm.5, ...), custom_call_target="tpu_custom_call" | custom-call | flops 1342177280 | bytes 10485760 | tf_op jit(solution)/shard_map/base/pallas_call | solution.py:415
  17.5 1.3 %collective-permute-done.1.refs_4_ = bf16[1,1024,128]{2,1,0:T(8,128)(2,1)S(1)} collective-permute-done((bf16[1,1024,128]{2,1,0:T(8,128)(2,1)S(1)}, bf16[1,1024,128]{2,1,0:T(8,128)(2,1)S(1)}, u32[]{:S(2)}, u32[]{:S(2)}) %collective-permute-start.1) | collective-permute-done | bytes 262176 | tf_op jit(solution)/shard_map/ppermute | solution.py:363
  18.8 1.8 %collective-permute-start.5 = (bf16[1,1024,128]{2,1,0:T(8,128)(2,1)S(1)}, bf16[1,1024,128]{2,1,0:T(8,128)(2,1)S(1)}, u32[]{:S(2)}, u32[]{:S(2)}) collective-permute-start(bf16[1,1024,128]{2,1,0:T(8,128)(2,1)S(1)} %collective-permute-done.1.refs_4_), channel_id=1, source_target_pairs={{0,16},{16,0},{1,17},{17,1},{2,18},{18,2},{3,19},{19,3},{4,20},{20... | collective-permute-start | bytes 786440 | tf_op jit(solution)/shard_map/ppermute | solution.py:363
  20.6 5.8 %collective-permute-done.6.refs_6_.refs_0_ = bf16[1,768,128]{2,1,0:T(8,128)(2,1)S(1)} collective-permute-done((bf16[1,768,128]{2,1,0:T(8,128)(2,1)S(1)}, bf16[1,768,128]{2,1,0:T(8,128)(2,1)S(1)}, u32[]{:S(2)}, u32[]{:S(2)}) %collective-permute-start.6) | collective-permute-done | bytes 196640 | tf_op jit(solution)/shard_map/ppermute | solution.py:363
  26.4 1.5 %collective-permute-start.7 = (bf16[1,768,128]{2,1,0:T(8,128)(2,1)S(1)}, bf16[1,768,128]{2,1,0:T(8,128)(2,1)S(1)}, u32[]{:S(2)}, u32[]{:S(2)}) collective-permute-start(bf16[1,768,128]{2,1,0:T(8,128)(2,1)S(1)} %collective-permute-done.6.refs_6_.refs_0_), channel_id=1, source_target_pairs={{0,16},{16,0},{1,17},{17,1},{2,18},{18,2},{3,19},{19,3},{4,20},{20... | collective-permute-start | bytes 589832 | tf_op jit(solution)/shard_map/ppermute | solution.py:363
  27.9 0.3 fusion
  28.2 0.0 collective-permute-done.refs_1_
  28.3 0.1 collective-permute-start.4
  28.3 0.1 pad_maximum_fusion
  28.4 3.3 %collective-permute-done.2.refs_2_ = bf16[64,2560]{1,0:T(8,128)(2,1)S(1)} collective-permute-done((bf16[64,2560]{1,0:T(8,128)(2,1)S(1)}, bf16[64,2560]{1,0:T(8,128)(2,1)S(1)}, u32[]{:S(2)}, u32[]{:S(2)}) %collective-permute-start.2) | collective-permute-done | bytes 327712 | tf_op jit(solution)/shard_map/ppermute | solution.py:363
  31.7 0.0 collective-permute-done.3.refs_3_
  31.7 0.4 collective-permute-done.7.refs_7_.refs_1_
  32.1 0.0 collective-permute-done.5.refs_5_
  32.1 0.5 %down.1.low_ref = f32[256,128]{1,0:T(8,128)S(1)} custom-call(s32[1]{0:T(128)} %bitcast.2.group_ref, bf16[1,2560,128]{2,1,0:T(8,128)(2,1)S(1)} %get-tuple-element.54.down_ref, bf16[64,2560]{1,0:T(8,128)(2,1)S(1)} %get-tuple-element.55.refs_0_, bf16[64,2560]{1,0:T(8,128)(2,1)S(1)} %collective-permute-done.refs_1_, ...), custom_call_target="tpu_custom_call" | custom-call | flops 335544320 | bytes 1966080 | tf_op jit(solution)/shard_map/down/pallas_call | solution.py:458
  32.6 0.1 collective-permute-start.8
  32.7 1.3 %collective-permute-done.8.other_ref = f32[256,128]{1,0:T(8,128)S(1)} collective-permute-done((f32[256,128]{1,0:T(8,128)S(1)}, f32[256,128]{1,0:T(8,128)S(1)}, u32[]{:S(2)}, u32[]{:S(2)}) %collective-permute-start.8) | collective-permute-done | bytes 131104 | tf_op jit(solution)/shard_map/ppermute | solution.py:363
  34.0 0.8 %up.1 = (s16[64,1024]{1,0:T(8,128)(2,1)S(1)}, s16[64,1024]{1,0:T(8,128)(2,1)S(1)}, s16[64,1024]{1,0:T(8,128)(2,1)S(1)}, s16[64,1024]{1,0:T(8,128)(2,1)S(1)}) custom-call(s32[1]{0:T(128)} %bitcast.2.group_ref, f32[256,128]{1,0:T(8,128)S(1)} %down.1.low_ref, f32[256,128]{1,0:T(8,128)S(1)} %collective-permute-done.8.other_ref, ...), custom_call_target="tpu_custom_call" | custom-call | flops 268435456 | bytes 524288 | tf_op jit(solution)/shard_map/up/pallas_call | solution.py:469
  34.8 2.8 %collective-permute-start.10 = (s16[64,1024]{1,0:T(8,128)(2,1)S(1)}, s16[64,1024]{1,0:T(8,128)(2,1)S(1)}, u32[]{:S(2)}, u32[]{:S(2)}) collective-permute-start(s16[64,1024]{1,0:T(8,128)(2,1)S(1)} %get-tuple-element.65), channel_id=1, source_target_pairs={{0,6},{2,4},{4,2},{6,0},{8,14},{10,12},{12,10},{14,8},{1,7},{3,5},... | collective-permute-start | bytes 393224 | tf_op jit(solution)/shard_map/ppermute | solution.py:363
  37.6 0.3 collective-permute-start.11
  37.9 0.5 %collective-permute-start.9 = (s16[64,1024]{1,0:T(8,128)(2,1)S(1)}, s16[64,1024]{1,0:T(8,128)(2,1)S(1)}, u32[]{:S(2)}, u32[]{:S(2)}) collective-permute-start(s16[64,1024]{1,0:T(8,128)(2,1)S(1)} %get-tuple-element.64), channel_id=1, source_target_pairs={{0,2},{2,0},{4,6},{6,4},{8,10},{10,8},{12,14},{14,12},{1,3},{3,1},... | collective-permute-start | bytes 393224 | tf_op jit(solution)/shard_map/ppermute | solution.py:363
  38.4 0.0 copy-done.1
  38.4 3.7 %collective-permute-done.10.refs_2_ = s16[64,1024]{1,0:T(8,128)(2,1)S(1)} collective-permute-done((s16[64,1024]{1,0:T(8,128)(2,1)S(1)}, s16[64,1024]{1,0:T(8,128)(2,1)S(1)}, u32[]{:S(2)}, u32[]{:S(2)}) %collective-permute-start.10) | collective-permute-done | bytes 131104 | tf_op jit(solution)/shard_map/ppermute | solution.py:363
  42.1 2.1 %collective-permute-done.11.refs_3_ = s16[64,1024]{1,0:T(8,128)(2,1)S(1)} collective-permute-done((s16[64,1024]{1,0:T(8,128)(2,1)S(1)}, s16[64,1024]{1,0:T(8,128)(2,1)S(1)}, u32[]{:S(2)}, u32[]{:S(2)}) %collective-permute-start.11) | collective-permute-done | bytes 131104 | tf_op jit(solution)/shard_map/ppermute | solution.py:363
  44.2 0.0 collective-permute-done.9.refs_1_
  44.3 0.0 collective-permute-done.4.other_ref
  44.3 0.0 copy-done
  44.3 1.7 %finish.1 = bf16[1024,128]{1,0:T(8,128)(2,1)} custom-call(s32[1]{0:T(128)} %bitcast.me_ref, s32[1,128]{1,0:T(1,128)S(1)} %bitcast.9, f32[128,1024]{1,0:T(8,128)S(1)} %get-tuple-element.50.mine_ref, f32[128,1024]{1,0:T(8,128)S(1)} %collective-permute-done.4.other_ref, f32[128,128]{1,0:T(8,128)S(1)} %get-tuple-element.52.cos_ref, ...), custom_call_target="tpu_custom_call" | custom-call | flops 134217728 | bytes 524288 | tf_op jit(solution)/shard_map/finish/pallas_call | solution.py:482
  (2 shorter events, 0.0 us)
Async XLA Ops:
  0.0 44.3 %copy-start = (s32[128,1]{0,1:T(1,128)S(1)}, s32[128,1]{0,1:T(1,128)}, u32[]{:S(2)}) copy-start(s32[128,1]{0,1:T(1,128)} %param.9) | copy-start | bytes 1540
  0.0 38.4 %copy-start.1 = (bf16[128]{0:T(256)(128)(2,1)S(1)}, bf16[128]{0:T(256)(128)(2,1)}, u32[]{:S(2)}) copy-start(bf16[128]{0:T(256)(128)(2,1)} %param.15) | copy-start | bytes 772
  1.8 17.0 %collective-permute-start.1 = (bf16[1,1024,128]{2,1,0:T(8,128)(2,1)S(1)}, bf16[1,1024,128]{2,1,0:T(8,128)(2,1)S(1)}, u32[]{:S(2)}, u32[]{:S(2)}) collective-permute-start(bf16[1,1024,128]{2,1,0:T(8,128)(2,1)S(1)} %get-tuple-element.38), channel_id=1, source_target_pairs={{0,8},{2,10},{4,12},{6,14},{8,0},{10,2},{12,4},{14,6},{1,9},{3,11}... | collective-permute-start | bytes 786440 | tf_op jit(solution)/shard_map/ppermute | solution.py:363
  5.9 22.4 %collective-permute-start = (bf16[64,2560]{1,0:T(8,128)(2,1)S(1)}, bf16[64,2560]{1,0:T(8,128)(2,1)S(1)}, u32[]{:S(2)}, u32[]{:S(2)}) collective-permute-start(bf16[64,2560]{1,0:T(8,128)(2,1)S(1)} %get-tuple-element.37), channel_id=1, source_target_pairs={{0,6},{2,4},{4,2},{6,0},{8,14},{10,12},{12,10},{14,8},{1,7},{3,5},... | collective-permute-start | bytes 983048 | tf_op jit(solution)/shard_map/ppermute | solution.py:363
  10.0 16.3 %collective-permute-start.6 = (bf16[1,768,128]{2,1,0:T(8,128)(2,1)S(1)}, bf16[1,768,128]{2,1,0:T(8,128)(2,1)S(1)}, u32[]{:S(2)}, u32[]{:S(2)}) collective-permute-start(bf16[1,768,128]{2,1,0:T(8,128)(2,1)S(1)} %get-tuple-element.46), channel_id=1, source_target_pairs={{0,8},{2,10},{4,12},{6,14},{8,0},{10,2},{12,4},{14,6},{1,9},{3,11}... | collective-permute-start | bytes 589832 | tf_op jit(solution)/shard_map/ppermute | solution.py:363
  10.4 21.3 %collective-permute-start.2 = (bf16[64,2560]{1,0:T(8,128)(2,1)S(1)}, bf16[64,2560]{1,0:T(8,128)(2,1)S(1)}, u32[]{:S(2)}, u32[]{:S(2)}) collective-permute-start(bf16[64,2560]{1,0:T(8,128)(2,1)S(1)} %get-tuple-element.47), channel_id=1, source_target_pairs={{0,4},{2,6},{4,0},{6,2},{8,12},{10,14},{12,8},{14,10},{1,5},{3,7},... | collective-permute-start | bytes 983048 | tf_op jit(solution)/shard_map/ppermute | solution.py:363
  10.9 20.8 %collective-permute-start.3 = (bf16[64,2560]{1,0:T(8,128)(2,1)S(1)}, bf16[64,2560]{1,0:T(8,128)(2,1)S(1)}, u32[]{:S(2)}, u32[]{:S(2)}) collective-permute-start(bf16[64,2560]{1,0:T(8,128)(2,1)S(1)} %get-tuple-element.48), channel_id=1, source_target_pairs={{0,2},{2,0},{4,6},{6,4},{8,10},{10,8},{12,14},{14,12},{1,3},{3,1},... | collective-permute-start | bytes 983048 | tf_op jit(solution)/shard_map/ppermute | solution.py:363
  18.8 13.3 %collective-permute-start.5 = (bf16[1,1024,128]{2,1,0:T(8,128)(2,1)S(1)}, bf16[1,1024,128]{2,1,0:T(8,128)(2,1)S(1)}, u32[]{:S(2)}, u32[]{:S(2)}) collective-permute-start(bf16[1,1024,128]{2,1,0:T(8,128)(2,1)S(1)} %collective-permute-done.1.refs_4_), channel_id=1, source_target_pairs={{0,16},{16,0},{1,17},{17,1},{2,18},{18,2},{3,19},{19,3},{4,20},{20... | collective-permute-start | bytes 786440 | tf_op jit(solution)/shard_map/ppermute | solution.py:363
  26.4 5.7 %collective-permute-start.7 = (bf16[1,768,128]{2,1,0:T(8,128)(2,1)S(1)}, bf16[1,768,128]{2,1,0:T(8,128)(2,1)S(1)}, u32[]{:S(2)}, u32[]{:S(2)}) collective-permute-start(bf16[1,768,128]{2,1,0:T(8,128)(2,1)S(1)} %collective-permute-done.6.refs_6_.refs_0_), channel_id=1, source_target_pairs={{0,16},{16,0},{1,17},{17,1},{2,18},{18,2},{3,19},{19,3},{4,20},{20... | collective-permute-start | bytes 589832 | tf_op jit(solution)/shard_map/ppermute | solution.py:363
  28.3 16.0 %collective-permute-start.4 = (f32[128,1024]{1,0:T(8,128)S(1)}, f32[128,1024]{1,0:T(8,128)S(1)}, u32[]{:S(2)}, u32[]{:S(2)}) collective-permute-start(f32[128,1024]{1,0:T(8,128)S(1)} %get-tuple-element.51), channel_id=1, source_target_pairs={{0,1},{1,0},{2,3},{3,2},{4,5},{5,4},{6,7},{7,6},{8,9},{9,8},{10,11... | collective-permute-start | bytes 1572872 | tf_op jit(solution)/shard_map/ppermute | solution.py:363
  32.6 1.4 %collective-permute-start.8 = (f32[256,128]{1,0:T(8,128)S(1)}, f32[256,128]{1,0:T(8,128)S(1)}, u32[]{:S(2)}, u32[]{:S(2)}) collective-permute-start(f32[256,128]{1,0:T(8,128)S(1)} %down.1.low_ref), channel_id=1, source_target_pairs={{0,1},{1,0},{2,3},{3,2},{4,5},{5,4},{6,7},{7,6},{8,9},{9,8},{10,11... | collective-permute-start | bytes 393224 | tf_op jit(solution)/shard_map/ppermute | solution.py:363
  34.8 7.3 %collective-permute-start.10 = (s16[64,1024]{1,0:T(8,128)(2,1)S(1)}, s16[64,1024]{1,0:T(8,128)(2,1)S(1)}, u32[]{:S(2)}, u32[]{:S(2)}) collective-permute-start(s16[64,1024]{1,0:T(8,128)(2,1)S(1)} %get-tuple-element.65), channel_id=1, source_target_pairs={{0,6},{2,4},{4,2},{6,0},{8,14},{10,12},{12,10},{14,8},{1,7},{3,5},... | collective-permute-start | bytes 393224 | tf_op jit(solution)/shard_map/ppermute | solution.py:363
  37.6 6.6 %collective-permute-start.11 = (s16[64,1024]{1,0:T(8,128)(2,1)S(1)}, s16[64,1024]{1,0:T(8,128)(2,1)S(1)}, u32[]{:S(2)}, u32[]{:S(2)}) collective-permute-start(s16[64,1024]{1,0:T(8,128)(2,1)S(1)} %get-tuple-element.66), channel_id=1, source_target_pairs={{0,4},{2,6},{4,0},{6,2},{8,12},{10,14},{12,8},{14,10},{1,5},{3,7},... | collective-permute-start | bytes 393224 | tf_op jit(solution)/shard_map/ppermute | solution.py:363
  37.9 6.4 %collective-permute-start.9 = (s16[64,1024]{1,0:T(8,128)(2,1)S(1)}, s16[64,1024]{1,0:T(8,128)(2,1)S(1)}, u32[]{:S(2)}, u32[]{:S(2)}) collective-permute-start(s16[64,1024]{1,0:T(8,128)(2,1)S(1)} %get-tuple-element.64), channel_id=1, source_target_pairs={{0,2},{2,0},{4,6},{6,4},{8,10},{10,8},{12,14},{14,12},{1,3},{3,1},... | collective-permute-start | bytes 393224 | tf_op jit(solution)/shard_map/ppermute | solution.py:363

commit v16 on v14

--- a/solution.py
+++ b/solution.py
@@ -59,8 +59,8 @@
 
 
 def return_order(count):
-    order = far_first(count)
-    return order[-1:] + order[:-1]
+    near_first = far_first(count)[::-1]
+    return near_first[1:2] + near_first[:1] + near_first[2:]
 
 
 def halves(x):

time: 45.6 us -> 46 us (level)
  transfers between devices with their start and end apart: 12 -> 12, of which waited for: 8 -> 7; matrix products, arithmetic and copies ran while one was open for 2% -> 2% of each run, Pallas kernels for 17% -> 17%
where the time goes in v16:
time: 46 us; the launch traced here: 45.8 us
  waiting for transfers between devices  17.6 us (38%)
  starting transfers between devices  15.1 us (33%)
  Pallas kernels  11.3 us (25%)
  other arithmetic  1.08 us (2%)
  between operations  0.74 us (2%)
    ppermute x12, waiting for transfers between devices, exchange(): return lax.ppermute(x, axis, [(p, p ^ j) for p in range(count)])  17.6 us
    ppermute x12, starting transfers between devices, exchange(): return lax.ppermute(x, axis, [(p, p ^ j) for p in range(count)])  15.1 us
    pallas_call x1, Pallas kernels, body(): pl.pallas_call(base_kernel, in_specs=[SMEM] + [HBM] * 4, out_specs=[VMEM]...  5.63 us
    pallas_call x1, Pallas kernels, body(): pl.pallas_call(functools.partial(pick_kernel, pool, local, depth), in_spe...  1.78 us
    pallas_call x1, Pallas kernels, body(): pl.pallas_call(functools.partial(finish_kernel, buffers, pool, local, dep...  1.66 us
    pallas_call x1, Pallas kernels, body(): pl.pallas_call(functools.partial(up_share_kernel, cores), in_specs=[SMEM]...  0.95 us
  transfers between devices with their start and end apart: 12, of which 7 were waited for; matrix products, arithmetic and copies ran while one was open for 2% of the time, Pallas kernels for 17%

profile of v16, /device:TPU:0, one launch (start us, length us, event | category | flops | bytes accessed | tf_op | source)
XLA Modules:
  0.0 45.8 jit_solution(4842794028675890349)
XLA Ops:
  0.0 0.0 copy-start
  0.0 0.0 copy-start.1
  0.0 1.8 %pick.1 = (bf16[1,1280,128]{2,1,0:T(8,128)(2,1)S(1)}, bf16[64,2560]{1,0:T(8,128)(2,1)S(1)}, bf16[64,2560]{1,0:T(8,128)(2,1)S(1)}, bf16[64,2560]{1,0:T(8,128)(2,1)S(1)}, bf16[64,2560]{1,0:T(8,128)(2,1)S(1)}) custom-call(s32[1]{0:T(128)} %bitcast.me_ref, s32[1]{0:T(128)} %bitcast.2.group_ref, s32[1,128]{1,0:T(1,128)} %bitcast.8, bf16[128,2560]{1,0:T(8,128)(2,1)} %tokens_hbm.3, ...), custom_call_target="tpu_custom_call" | custom-call | flops 167772160 | bytes 1966080 | tf_op jit(solution)/shard_map/pick/pallas_call | solution.py:341
  1.8 4.1 %collective-permute-start.1 = (bf16[1,1280,128]{2,1,0:T(8,128)(2,1)S(1)}, bf16[1,1280,128]{2,1,0:T(8,128)(2,1)S(1)}, u32[]{:S(2)}, u32[]{:S(2)}) collective-permute-start(bf16[1,1280,128]{2,1,0:T(8,128)(2,1)S(1)} %get-tuple-element.43), channel_id=1, source_target_pairs={{0,8},{2,10},{4,12},{6,14},{8,0},{10,2},{12,4},{14,6},{1,9},{3,11}... | collective-permute-start | bytes 983048 | tf_op jit(solution)/shard_map/ppermute | solution.py:333
  5.9 2.5 %collective-permute-start.2 = (bf16[64,2560]{1,0:T(8,128)(2,1)S(1)}, bf16[64,2560]{1,0:T(8,128)(2,1)S(1)}, u32[]{:S(2)}, u32[]{:S(2)}) collective-permute-start(bf16[64,2560]{1,0:T(8,128)(2,1)S(1)} %get-tuple-element.39), channel_id=1, source_target_pairs={{0,6},{2,4},{4,2},{6,0},{8,14},{10,12},{12,10},{14,8},{1,7},{3,5},... | collective-permute-start | bytes 983048 | tf_op jit(solution)/shard_map/ppermute | solution.py:333
  9.1 0.9 %up_share.1 = (bf16[1,128,512]{2,1,0:T(8,128)(2,1)S(1)}, f32[1,128]{1,0:T(1,128)S(1)}) custom-call(s32[1]{0:T(128)} %bitcast.2.group_ref, s32[1]{0:T(128)} %bitcast.3.core_ref, s32[1]{0:T(128)S(6)} %copy.9.ranks_ref, bf16[1,128,2048]{2,1,0:T(8,128)(2,1)} %up_hbm.2), custom_call_target="tpu_custom_call" | custom-call | flops 65536 | bytes 262144 | tf_op jit(solution)/shard_map/up_share/pallas_call | solution.py:360
  10.0 0.4 collective-permute-start
  10.4 0.4 collective-permute-start.3
  10.9 0.3 collective-permute-start.4
  11.1 0.7 %convert_element_type.4 = f32[128]{0:T(128)S(1)} convert(s32[128]{0:T(128)} %param.10) | non-fusion elementwise | flops 128 | bytes 1024 | tf_op jit(solution)/shard_map/convert_element_type | solution.py:418
  11.8 5.6 %base.1 = (f32[128,1024]{1,0:T(8,128)S(1)}, f32[128,1024]{1,0:T(8,128)S(1)}, bf16[1,2560,128]{2,1,0:T(8,128)(2,1)S(1)}, bf16[1,128,1024]{2,1,0:T(8,128)(2,1)S(1)}) custom-call(s32[1]{0:T(128)} %bitcast.3.core_ref, bf16[128,2560]{1,0:T(8,128)(2,1)} %tokens_hbm.3, bf16[2560,2048]{1,0:T(8,128)(2,1)} %weight_hbm.1, bf16[1,2560,128]{2,1,0:T(8,128)(2,1)} %down_hbm.3, ...), custom_call_target="tpu_custom_call" | custom-call | flops 1342177280 | bytes 10485760 | tf_op jit(solution)/shard_map/base/pallas_call | solution.py:385
  17.5 4.9 %collective-permute-done.1.refs_4_ = bf16[1,1280,128]{2,1,0:T(8,128)(2,1)S(1)} collective-permute-done((bf16[1,1280,128]{2,1,0:T(8,128)(2,1)S(1)}, bf16[1,1280,128]{2,1,0:T(8,128)(2,1)S(1)}, u32[]{:S(2)}, u32[]{:S(2)}) %collective-permute-start.1) | collective-permute-done | bytes 327712 | tf_op jit(solution)/shard_map/ppermute | solution.py:333
  22.3 2.1 %collective-permute-start.6 = (bf16[1,1280,128]{2,1,0:T(8,128)(2,1)S(1)}, bf16[1,1280,128]{2,1,0:T(8,128)(2,1)S(1)}, u32[]{:S(2)}, u32[]{:S(2)}) collective-permute-start(bf16[1,1280,128]{2,1,0:T(8,128)(2,1)S(1)} %collective-permute-done.1.refs_4_), channel_id=1, source_target_pairs={{0,16},{16,0},{1,17},{17,1},{2,18},{18,2},{3,19},{19,3},{4,20},{20... | collective-permute-start | bytes 983048 | tf_op jit(solution)/shard_map/ppermute | solution.py:333
  24.5 0.3 fusion
  24.8 1.6 %collective-permute-done.refs_0_ = bf16[1,128,512]{2,1,0:T(8,128)(2,1)S(1)} collective-permute-done((bf16[1,128,512]{2,1,0:T(8,128)(2,1)S(1)}, bf16[1,128,512]{2,1,0:T(8,128)(2,1)S(1)}, u32[]{:S(2)}, u32[]{:S(2)}) %collective-permute-start) | collective-permute-done | bytes 131104 | tf_op jit(solution)/shard_map/ppermute | solution.py:333
  26.4 0.0 collective-permute-done.2.refs_1_
  26.4 0.0 collective-permute-start.5
  26.4 0.1 pad_maximum_fusion
  26.5 1.6 %collective-permute-start.8 = (bf16[1,128,512]{2,1,0:T(8,128)(2,1)S(1)}, bf16[1,128,512]{2,1,0:T(8,128)(2,1)S(1)}, u32[]{:S(2)}, u32[]{:S(2)}) collective-permute-start(bf16[1,128,512]{2,1,0:T(8,128)(2,1)S(1)} %collective-permute-done.refs_0_), channel_id=1, source_target_pairs={{0,16},{16,0},{1,17},{17,1},{2,18},{18,2},{3,19},{19,3},{4,20},{20... | collective-permute-start | bytes 393224 | tf_op jit(solution)/shard_map/ppermute | solution.py:333
  28.1 3.6 %collective-permute-done.3.refs_2_ = bf16[64,2560]{1,0:T(8,128)(2,1)S(1)} collective-permute-done((bf16[64,2560]{1,0:T(8,128)(2,1)S(1)}, bf16[64,2560]{1,0:T(8,128)(2,1)S(1)}, u32[]{:S(2)}, u32[]{:S(2)}) %collective-permute-start.3) | collective-permute-done | bytes 327712 | tf_op jit(solution)/shard_map/ppermute | solution.py:333
  31.8 0.0 collective-permute-done.4.refs_3_
  31.8 0.0 collective-permute-done.6.refs_5_
  31.8 0.5 %down.1.low_ref = f32[256,128]{1,0:T(8,128)S(1)} custom-call(s32[1]{0:T(128)} %bitcast.2.group_ref, bf16[1,2560,128]{2,1,0:T(8,128)(2,1)S(1)} %get-tuple-element.56.down_ref, bf16[64,2560]{1,0:T(8,128)(2,1)S(1)} %get-tuple-element.57.refs_0_, bf16[64,2560]{1,0:T(8,128)(2,1)S(1)} %collective-permute-done.2.refs_1_, ...), custom_call_target="tpu_custom_call" | custom-call | flops 335544320 | bytes 1966080 | tf_op jit(solution)/shard_map/down/pallas_call | solution.py:427
  32.3 0.1 collective-permute-start.7
  32.4 0.1 collective-permute-done.8.refs_1_
  32.5 1.2 %collective-permute-done.7.other_ref = f32[256,128]{1,0:T(8,128)S(1)} collective-permute-done((f32[256,128]{1,0:T(8,128)S(1)}, f32[256,128]{1,0:T(8,128)S(1)}, u32[]{:S(2)}, u32[]{:S(2)}) %collective-permute-start.7) | collective-permute-done | bytes 131104 | tf_op jit(solution)/shard_map/ppermute | solution.py:333
  33.7 0.8 %up.1 = (s16[64,1024]{1,0:T(8,128)(2,1)S(1)}, s16[64,1024]{1,0:T(8,128)(2,1)S(1)}, s16[64,1024]{1,0:T(8,128)(2,1)S(1)}, s16[64,1024]{1,0:T(8,128)(2,1)S(1)}) custom-call(s32[1]{0:T(128)} %bitcast.2.group_ref, f32[256,128]{1,0:T(8,128)S(1)} %down.1.low_ref, f32[256,128]{1,0:T(8,128)S(1)} %collective-permute-done.7.other_ref, ...), custom_call_target="tpu_custom_call" | custom-call | flops 268435456 | bytes 524288 | tf_op jit(solution)/shard_map/up/pallas_call | solution.py:438
  34.5 0.7 %collective-permute-start.10 = (s16[64,1024]{1,0:T(8,128)(2,1)S(1)}, s16[64,1024]{1,0:T(8,128)(2,1)S(1)}, u32[]{:S(2)}, u32[]{:S(2)}) collective-permute-start(s16[64,1024]{1,0:T(8,128)(2,1)S(1)} %get-tuple-element.65), channel_id=1, source_target_pairs={{0,2},{2,0},{4,6},{6,4},{8,10},{10,8},{12,14},{14,12},{1,3},{3,1},... | collective-permute-start | bytes 393224 | tf_op jit(solution)/shard_map/ppermute | solution.py:333
  35.2 1.7 %collective-permute-start.11 = (s16[64,1024]{1,0:T(8,128)(2,1)S(1)}, s16[64,1024]{1,0:T(8,128)(2,1)S(1)}, u32[]{:S(2)}, u32[]{:S(2)}) collective-permute-start(s16[64,1024]{1,0:T(8,128)(2,1)S(1)} %get-tuple-element.66), channel_id=1, source_target_pairs={{0,6},{2,4},{4,2},{6,0},{8,14},{10,12},{12,10},{14,8},{1,7},{3,5},... | collective-permute-start | bytes 393224 | tf_op jit(solution)/shard_map/ppermute | solution.py:333
  36.9 1.1 %collective-permute-start.9 = (s16[64,1024]{1,0:T(8,128)(2,1)S(1)}, s16[64,1024]{1,0:T(8,128)(2,1)S(1)}, u32[]{:S(2)}, u32[]{:S(2)}) collective-permute-start(s16[64,1024]{1,0:T(8,128)(2,1)S(1)} %get-tuple-element.64), channel_id=1, source_target_pairs={{0,4},{2,6},{4,0},{6,2},{8,12},{10,14},{12,8},{14,10},{1,5},{3,7},... | collective-permute-start | bytes 393224 | tf_op jit(solution)/shard_map/ppermute | solution.py:333
  38.0 0.0 copy-done.1
  38.1 0.0 collective-permute-done.5.other_ref
  38.1 4.9 %collective-permute-done.10.refs_2_ = s16[64,1024]{1,0:T(8,128)(2,1)S(1)} collective-permute-done((s16[64,1024]{1,0:T(8,128)(2,1)S(1)}, s16[64,1024]{1,0:T(8,128)(2,1)S(1)}, u32[]{:S(2)}, u32[]{:S(2)}) %collective-permute-start.10) | collective-permute-done | bytes 131104 | tf_op jit(solution)/shard_map/ppermute | solution.py:333
  42.9 0.0 collective-permute-done.11.refs_3_
  42.9 1.2 %collective-permute-done.9.refs_1_ = s16[64,1024]{1,0:T(8,128)(2,1)S(1)} collective-permute-done((s16[64,1024]{1,0:T(8,128)(2,1)S(1)}, s16[64,1024]{1,0:T(8,128)(2,1)S(1)}, u32[]{:S(2)}, u32[]{:S(2)}) %collective-permute-start.9) | collective-permute-done | bytes 131104 | tf_op jit(solution)/shard_map/ppermute | solution.py:333
  44.1 0.0 copy-done
  44.1 1.7 %finish.1 = bf16[1024,128]{1,0:T(8,128)(2,1)} custom-call(s32[1]{0:T(128)} %bitcast.me_ref, s32[1,128]{1,0:T(1,128)S(1)} %bitcast.9, f32[128,1024]{1,0:T(8,128)S(1)} %get-tuple-element.52.mine_ref, f32[128,1024]{1,0:T(8,128)S(1)} %collective-permute-done.5.other_ref, f32[128,128]{1,0:T(8,128)S(1)} %get-tuple-element.54.cos_ref, ...), custom_call_target="tpu_custom_call" | custom-call | flops 134217728 | bytes 524288 | tf_op jit(solution)/shard_map/finish/pallas_call | solution.py:451
  (2 shorter events, 0.0 us)
Async XLA Ops:
  0.0 44.1 %copy-start = (s32[128,1]{0,1:T(1,128)S(1)}, s32[128,1]{0,1:T(1,128)}, u32[]{:S(2)}) copy-start(s32[128,1]{0,1:T(1,128)} %param.9) | copy-start | bytes 1540
  0.0 38.0 %copy-start.1 = (bf16[128]{0:T(256)(128)(2,1)S(1)}, bf16[128]{0:T(256)(128)(2,1)}, u32[]{:S(2)}) copy-start(bf16[128]{0:T(256)(128)(2,1)} %param.15) | copy-start | bytes 772
  1.8 20.5 %collective-permute-start.1 = (bf16[1,1280,128]{2,1,0:T(8,128)(2,1)S(1)}, bf16[1,1280,128]{2,1,0:T(8,128)(2,1)S(1)}, u32[]{:S(2)}, u32[]{:S(2)}) collective-permute-start(bf16[1,1280,128]{2,1,0:T(8,128)(2,1)S(1)} %get-tuple-element.43), channel_id=1, source_target_pairs={{0,8},{2,10},{4,12},{6,14},{8,0},{10,2},{12,4},{14,6},{1,9},{3,11}... | collective-permute-start | bytes 983048 | tf_op jit(solution)/shard_map/ppermute | solution.py:333
  5.9 20.5 %collective-permute-start.2 = (bf16[64,2560]{1,0:T(8,128)(2,1)S(1)}, bf16[64,2560]{1,0:T(8,128)(2,1)S(1)}, u32[]{:S(2)}, u32[]{:S(2)}) collective-permute-start(bf16[64,2560]{1,0:T(8,128)(2,1)S(1)} %get-tuple-element.39), channel_id=1, source_target_pairs={{0,6},{2,4},{4,2},{6,0},{8,14},{10,12},{12,10},{14,8},{1,7},{3,5},... | collective-permute-start | bytes 983048 | tf_op jit(solution)/shard_map/ppermute | solution.py:333
  10.0 16.4 %collective-permute-start = (bf16[1,128,512]{2,1,0:T(8,128)(2,1)S(1)}, bf16[1,128,512]{2,1,0:T(8,128)(2,1)S(1)}, u32[]{:S(2)}, u32[]{:S(2)}) collective-permute-start(bf16[1,128,512]{2,1,0:T(8,128)(2,1)S(1)} %get-tuple-element.42), channel_id=1, source_target_pairs={{0,8},{2,10},{4,12},{6,14},{8,0},{10,2},{12,4},{14,6},{1,9},{3,11}... | collective-permute-start | bytes 393224 | tf_op jit(solution)/shard_map/ppermute | solution.py:333
  10.4 21.3 %collective-permute-start.3 = (bf16[64,2560]{1,0:T(8,128)(2,1)S(1)}, bf16[64,2560]{1,0:T(8,128)(2,1)S(1)}, u32[]{:S(2)}, u32[]{:S(2)}) collective-permute-start(bf16[64,2560]{1,0:T(8,128)(2,1)S(1)} %get-tuple-element.49), channel_id=1, source_target_pairs={{0,4},{2,6},{4,0},{6,2},{8,12},{10,14},{12,8},{14,10},{1,5},{3,7},... | collective-permute-start | bytes 983048 | tf_op jit(solution)/shard_map/ppermute | solution.py:333
  10.9 20.9 %collective-permute-start.4 = (bf16[64,2560]{1,0:T(8,128)(2,1)S(1)}, bf16[64,2560]{1,0:T(8,128)(2,1)S(1)}, u32[]{:S(2)}, u32[]{:S(2)}) collective-permute-start(bf16[64,2560]{1,0:T(8,128)(2,1)S(1)} %get-tuple-element.50), channel_id=1, source_target_pairs={{0,2},{2,0},{4,6},{6,4},{8,10},{10,8},{12,14},{14,12},{1,3},{3,1},... | collective-permute-start | bytes 983048 | tf_op jit(solution)/shard_map/ppermute | solution.py:333
  22.3 9.4 %collective-permute-start.6 = (bf16[1,1280,128]{2,1,0:T(8,128)(2,1)S(1)}, bf16[1,1280,128]{2,1,0:T(8,128)(2,1)S(1)}, u32[]{:S(2)}, u32[]{:S(2)}) collective-permute-start(bf16[1,1280,128]{2,1,0:T(8,128)(2,1)S(1)} %collective-permute-done.1.refs_4_), channel_id=1, source_target_pairs={{0,16},{16,0},{1,17},{17,1},{2,18},{18,2},{3,19},{19,3},{4,20},{20... | collective-permute-start | bytes 983048 | tf_op jit(solution)/shard_map/ppermute | solution.py:333
  26.4 11.7 %collective-permute-start.5 = (f32[128,1024]{1,0:T(8,128)S(1)}, f32[128,1024]{1,0:T(8,128)S(1)}, u32[]{:S(2)}, u32[]{:S(2)}) collective-permute-start(f32[128,1024]{1,0:T(8,128)S(1)} %get-tuple-element.53), channel_id=1, source_target_pairs={{0,1},{1,0},{2,3},{3,2},{4,5},{5,4},{6,7},{7,6},{8,9},{9,8},{10,11... | collective-permute-start | bytes 1572872 | tf_op jit(solution)/shard_map/ppermute | solution.py:333
  26.5 6.0 %collective-permute-start.8 = (bf16[1,128,512]{2,1,0:T(8,128)(2,1)S(1)}, bf16[1,128,512]{2,1,0:T(8,128)(2,1)S(1)}, u32[]{:S(2)}, u32[]{:S(2)}) collective-permute-start(bf16[1,128,512]{2,1,0:T(8,128)(2,1)S(1)} %collective-permute-done.refs_0_), channel_id=1, source_target_pairs={{0,16},{16,0},{1,17},{17,1},{2,18},{18,2},{3,19},{19,3},{4,20},{20... | collective-permute-start | bytes 393224 | tf_op jit(solution)/shard_map/ppermute | solution.py:333
  32.3 1.4 %collective-permute-start.7 = (f32[256,128]{1,0:T(8,128)S(1)}, f32[256,128]{1,0:T(8,128)S(1)}, u32[]{:S(2)}, u32[]{:S(2)}) collective-permute-start(f32[256,128]{1,0:T(8,128)S(1)} %down.1.low_ref), channel_id=1, source_target_pairs={{0,1},{1,0},{2,3},{3,2},{4,5},{5,4},{6,7},{7,6},{8,9},{9,8},{10,11... | collective-permute-start | bytes 393224 | tf_op jit(solution)/shard_map/ppermute | solution.py:333
  34.5 8.4 %collective-permute-start.10 = (s16[64,1024]{1,0:T(8,128)(2,1)S(1)}, s16[64,1024]{1,0:T(8,128)(2,1)S(1)}, u32[]{:S(2)}, u32[]{:S(2)}) collective-permute-start(s16[64,1024]{1,0:T(8,128)(2,1)S(1)} %get-tuple-element.65), channel_id=1, source_target_pairs={{0,2},{2,0},{4,6},{6,4},{8,10},{10,8},{12,14},{14,12},{1,3},{3,1},... | collective-permute-start | bytes 393224 | tf_op jit(solution)/shard_map/ppermute | solution.py:333
  35.2 7.7 %collective-permute-start.11 = (s16[64,1024]{1,0:T(8,128)(2,1)S(1)}, s16[64,1024]{1,0:T(8,128)(2,1)S(1)}, u32[]{:S(2)}, u32[]{:S(2)}) collective-permute-start(s16[64,1024]{1,0:T(8,128)(2,1)S(1)} %get-tuple-element.66), channel_id=1, source_target_pairs={{0,6},{2,4},{4,2},{6,0},{8,14},{10,12},{12,10},{14,8},{1,7},{3,5},... | collective-permute-start | bytes 393224 | tf_op jit(solution)/shard_map/ppermute | solution.py:333
  36.9 7.2 %collective-permute-start.9 = (s16[64,1024]{1,0:T(8,128)(2,1)S(1)}, s16[64,1024]{1,0:T(8,128)(2,1)S(1)}, u32[]{:S(2)}, u32[]{:S(2)}) collective-permute-start(s16[64,1024]{1,0:T(8,128)(2,1)S(1)} %get-tuple-element.64), channel_id=1, source_target_pairs={{0,4},{2,6},{4,0},{6,2},{8,12},{10,14},{12,8},{14,10},{1,5},{3,7},... | collective-permute-start | bytes 393224 | tf_op jit(solution)/shard_map/ppermute | solution.py:333

commit v17 on v14

--- a/solution.py
+++ b/solution.py
@@ -247,56 +247,87 @@
         out[:, LANES:] = code[:, LANES:].astype(jnp.int16)
 
 
-def finish_kernel(
-    buffers, pool, local, depth, me_ref, adapter_ref, mine_ref, other_ref, cos_ref, sin_ref, gain_ref, *refs
-):
-    order = [0] + return_order(buffers)
-    ins = [refs[order.index(j)] for j in range(buffers)]
-    out_hbm, out_ref, sems = refs[-3:]
-    rows, columns = mine_ref.shape
-    head = cos_ref.shape[1]
-    place = to_column(slot_places(adapter_ref[...], me_ref[0], pool, local, depth))
-    slots = buffers * ins[0].shape[0]
-    picker = jnp.where(iota((rows, slots), 1) == place, 1.0, 0.0).astype(jnp.bfloat16)
-
-    def picked(at, size):
-        code = jnp.concatenate([x[:, at : at + size] for x in ins], axis=0).astype(jnp.int32)
-        high = (code >> 8).astype(jnp.float32).astype(jnp.bfloat16)
-        low = (code & 255).astype(jnp.float32).astype(jnp.bfloat16)
-        high = jnp.dot(picker, high, preferred_element_type=jnp.float32)
-        low = jnp.dot(picker, low, preferred_element_type=jnp.float32)
-        return high * 256.0 + low
-
+def planes(codes, at, size):
+    code = jnp.concatenate([x[:, at : at + size] for x in codes], axis=0).astype(jnp.int32)
+    high = (code >> 8).astype(jnp.float32).astype(jnp.bfloat16)
+    low = (code & 255).astype(jnp.float32).astype(jnp.bfloat16)
+    return high, low
+
+
+def decoded(picker, plane):
+    high = jnp.dot(picker, plane[0], preferred_element_type=jnp.float32)
+    low = jnp.dot(picker, plane[1], preferred_element_type=jnp.float32)
+    return high * 256.0 + low
+
+
+def scale_of(first):
     lane = iota((1, LANES), 1)
-    bits = picked(0, LANES).astype(jnp.int32) & 1
+    bits = first.astype(jnp.int32) & 1
     bits = jnp.where(lane < EXPONENT_BITS, bits << jnp.minimum(lane, EXPONENT_BITS - 1), 0)
     exponent = jnp.sum(bits.astype(jnp.float32), axis=1, keepdims=True) - EXPONENT_BIAS
-    scale = jnp.exp2(exponent - 15.0)
-    cosine, sine, gain = cos_ref[...], sin_ref[...], gain_ref[...]
-    entries = []
-    for at in range(0, columns, 2 * head):
-        projected = mine_ref[:, at : at + 2 * head] + other_ref[:, at : at + 2 * head]
-        projected = projected + picked(at, 2 * head) * scale
-        key, value = projected[:, :head], projected[:, head:]
-        mean = jnp.mean(key * key, axis=1, keepdims=True)
-        normed = key * lax.rsqrt(mean + NORM_EPS) * gain
-        rotated = normed * cosine + pltpu.roll(normed, head // 2, 1) * sine
-        entries += [rotated.astype(jnp.bfloat16), value.astype(jnp.bfloat16)]
-    kinds, block = len(entries), 16
+    return jnp.exp2(exponent - 15.0)
+
+
+def start_rows_kernel(
+    buffers, pool, local, depth, me_ref, adapter_ref, mine_ref, other_ref, own_ref, partial_ref, picker_ref
+):
+    rows, columns = mine_ref.shape
+    size = own_ref.shape[0]
+    place = to_column(slot_places(adapter_ref[...], me_ref[0], pool, local, depth))
+    picker = jnp.where(iota((rows, size), 1) == place, 1.0, 0.0).astype(jnp.bfloat16)
+    scale = scale_of(decoded(picker, planes([own_ref], 0, LANES)))
+    for at in range(0, columns, 256):
+        term = decoded(picker, planes([own_ref], at, 256)) * scale
+        partial_ref[:, at : at + 256] = (
+            mine_ref[:, at : at + 256] + other_ref[:, at : at + 256] + term
+        )
+    slots = (buffers - 1) * size
+    picker_ref[...] = jnp.where(iota((rows, slots), 1) == place - size, 1.0, 0.0).astype(
+        jnp.bfloat16
+    )
+
+
+def finish_kernel(buffers, partial_ref, picker_ref, cos_ref, sin_ref, gain_ref, *refs):
+    order = return_order(buffers)
+    ins = [refs[order.index(j)] for j in range(1, buffers)]
+    out_hbm, out_ref, sems = refs[-3:]
+    rows, columns = partial_ref.shape
+    head = cos_ref.shape[1]
+    gain = gain_ref[...]
+    kinds, block = columns // head, 16
     n = kinds * block
     source = (iota((n, n), 0) % kinds) * block + iota((n, n), 0) // kinds
-    order = jnp.where(iota((n, n), 1) == source, 1.0, 0.0).astype(jnp.bfloat16)
+    mix = jnp.where(iota((n, n), 1) == source, 1.0, 0.0).astype(jnp.bfloat16)
+    plane = [planes(ins, at, 2 * head) for at in range(0, columns, 2 * head)]
+    first = planes(ins, 0, LANES)
     copies = []
-    for i in range(rows // block):
-        stacked = jnp.concatenate([e[i * block : (i + 1) * block] for e in entries], axis=0)
-        mixed = jnp.dot(order, stacked, preferred_element_type=jnp.float32)
-        out_ref[i * n : (i + 1) * n, :] = mixed.astype(jnp.bfloat16)
-        if i % 2:
-            done = pl.ds((i - 1) * n, 2 * n)
-            copies.append(
-                pltpu.make_async_copy(out_ref.at[done, :], out_hbm.at[done, :], sems.at[i // 2])
+    part = rows // 2
+    for begin in range(0, rows, part):
+        here = slice(begin, begin + part)
+        picker = picker_ref[here, :]
+        scale = scale_of(decoded(picker, first))
+        cosine, sine = cos_ref[here, :], sin_ref[here, :]
+        entries = []
+        for at in range(0, columns, 2 * head):
+            projected = partial_ref[here, at : at + 2 * head]
+            projected = projected + decoded(picker, plane[at // (2 * head)]) * scale
+            key, value = projected[:, :head], projected[:, head:]
+            mean = jnp.mean(key * key, axis=1, keepdims=True)
+            normed = key * lax.rsqrt(mean + NORM_EPS) * gain
+            rotated = normed * cosine + pltpu.roll(normed, head // 2, 1) * sine
+            entries += [rotated.astype(jnp.bfloat16), value.astype(jnp.bfloat16)]
+        for i in range(part // block):
+            stacked = jnp.concatenate([e[i * block : (i + 1) * block] for e in entries], axis=0)
+            mixed = jnp.dot(mix, stacked, preferred_element_type=jnp.float32)
+            top = begin * kinds + i * n
+            out_ref[top : top + n, :] = mixed.astype(jnp.bfloat16)
+        done = pl.ds(begin * kinds, part * kinds)
+        copies.append(
+            pltpu.make_async_copy(
+                out_ref.at[done, :], out_hbm.at[done, :], sems.at[begin // part]
             )
-            copies[-1].start()
+        )
+        copies[-1].start()
     for copy in copies:
         copy.wait()
 
@@ -446,30 +477,33 @@
         name="up",
     )(group, low, low_other, factor, own_up, *far_ups)
     order = return_order(buffers)
-    returned = [terms[0]] + [exchange(terms[j], "pool", pool, j) for j in order]
-
+    returned = [exchange(terms[j], "pool", pool, j) for j in order]
+
+    partial, picker = pl.pallas_call(
+        functools.partial(start_rows_kernel, buffers, pool, local, depth),
+        in_specs=[SMEM] + [VMEM] * 4,
+        out_specs=[VMEM] * 2,
+        out_shape=[
+            jax.ShapeDtypeStruct((rows, columns), f32),
+            jax.ShapeDtypeStruct((rows, slots - size), bf16),
+        ],
+        compiler_params=params(),
+        cost_estimate=cost(4 * rows * size * columns, 12 * rows * columns),
+        name="start_rows",
+    )(me, adapter_row, mine, other, terms[0])
     out = pl.pallas_call(
-        functools.partial(finish_kernel, buffers, pool, local, depth),
-        in_specs=[SMEM] + [VMEM] * (6 + buffers),
+        functools.partial(finish_kernel, buffers),
+        in_specs=[VMEM] * (4 + buffers),
         out_specs=HBM,
         out_shape=jax.ShapeDtypeStruct((rows * columns // head, head), bf16),
         scratch_shapes=[
             pltpu.VMEM((rows * columns // head, head), bf16),
-            pltpu.SemaphoreType.DMA((rows // 32,)),
+            pltpu.SemaphoreType.DMA((2,)),
         ],
         compiler_params=params(),
         cost_estimate=cost(4 * rows * slots * columns, 2 * slots * columns),
         name="finish",
-    )(
-        me,
-        adapter_row,
-        mine,
-        other,
-        cosine,
-        sine,
-        key_norm_gain.astype(f32)[None, :],
-        *returned,
-    )
+    )(partial, picker, cosine, sine, key_norm_gain.astype(f32)[None, :], *returned)
     return out.reshape(rows, columns // (2 * head), 2, head)
 
 

time: 45.6 us -> 45.8 us (level)
  Pallas kernels: 11.3 us -> 12 us
  waiting for transfers between devices: 17.2 us -> 16.7 us
    pallas_call x1 -> x2, Pallas kernels: 1.66 us -> 2.37 us  [the longest x1 1.85 us: body(): pl.pallas_call(functools.partial(finish_kernel, buffers), in_specs=[VMEM]...]
    ppermute x12, waiting for transfers between devices: 17.2 us -> 16.7 us  [exchange(): return lax.ppermute(x, axis, [(p, p ^ j) for p in range(count)])]
  transfers between devices with their start and end apart: 12 -> 12, of which waited for: 8 -> 8; matrix products, arithmetic and copies ran while one was open for 2% -> 2% of each run, Pallas kernels for 17% -> 18%
where the time goes in v17:
time: 45.8 us; the launch traced here: 45.7 us
  waiting for transfers between devices  16.7 us (36%)
  starting transfers between devices  15.1 us (33%)
  Pallas kernels  12 us (26%)
  other arithmetic  1.08 us (2%)
  between operations  0.75 us (2%)
    ppermute x12, waiting for transfers between devices, exchange(): return lax.ppermute(x, axis, [(p, p ^ j) for p in range(count)])  16.7 us
    ppermute x12, starting transfers between devices, exchange(): return lax.ppermute(x, axis, [(p, p ^ j) for p in range(count)])  15.1 us
    pallas_call x1, Pallas kernels, body(): pl.pallas_call(base_kernel, in_specs=[SMEM] + [HBM] * 4, out_specs=[VMEM]...  5.63 us
    pallas_call x1, Pallas kernels, body(): pl.pallas_call(functools.partial(finish_kernel, buffers), in_specs=[VMEM]...  1.85 us
    pallas_call x1, Pallas kernels, body(): pl.pallas_call(functools.partial(pick_kernel, pool, local, depth), in_spe...  1.78 us
    pallas_call x1, Pallas kernels, body(): pl.pallas_call(functools.partial(up_share_kernel, cores), in_specs=[SMEM]...  0.95 us
  transfers between devices with their start and end apart: 12, of which 8 were waited for; matrix products, arithmetic and copies ran while one was open for 2% of the time, Pallas kernels for 18%

profile of v17, /device:TPU:0, one launch (start us, length us, event | category | flops | bytes accessed | tf_op | source)
XLA Modules:
  0.0 45.7 jit_solution(6358265854928570867)
XLA Ops:
  0.0 0.0 copy-start
  0.0 0.0 copy-start.1
  0.0 1.8 %pick.1 = (bf16[1,1280,128]{2,1,0:T(8,128)(2,1)S(1)}, bf16[64,2560]{1,0:T(8,128)(2,1)S(1)}, bf16[64,2560]{1,0:T(8,128)(2,1)S(1)}, bf16[64,2560]{1,0:T(8,128)(2,1)S(1)}, bf16[64,2560]{1,0:T(8,128)(2,1)S(1)}) custom-call(s32[1]{0:T(128)} %bitcast.me_ref, s32[1]{0:T(128)} %bitcast.2.group_ref, s32[1,128]{1,0:T(1,128)} %bitcast.8, bf16[128,2560]{1,0:T(8,128)(2,1)} %tokens_hbm.3, ...), custom_call_target="tpu_custom_call" | custom-call | flops 167772160 | bytes 1966080 | tf_op jit(solution)/shard_map/pick/pallas_call | solution.py:372
  1.8 4.1 %collective-permute-start.1 = (bf16[1,1280,128]{2,1,0:T(8,128)(2,1)S(1)}, bf16[1,1280,128]{2,1,0:T(8,128)(2,1)S(1)}, u32[]{:S(2)}, u32[]{:S(2)}) collective-permute-start(bf16[1,1280,128]{2,1,0:T(8,128)(2,1)S(1)} %get-tuple-element.45), channel_id=1, source_target_pairs={{0,8},{2,10},{4,12},{6,14},{8,0},{10,2},{12,4},{14,6},{1,9},{3,11}... | collective-permute-start | bytes 983048 | tf_op jit(solution)/shard_map/ppermute | solution.py:364
  5.9 2.5 %collective-permute-start.2 = (bf16[64,2560]{1,0:T(8,128)(2,1)S(1)}, bf16[64,2560]{1,0:T(8,128)(2,1)S(1)}, u32[]{:S(2)}, u32[]{:S(2)}) collective-permute-start(bf16[64,2560]{1,0:T(8,128)(2,1)S(1)} %get-tuple-element.41), channel_id=1, source_target_pairs={{0,6},{2,4},{4,2},{6,0},{8,14},{10,12},{12,10},{14,8},{1,7},{3,5},... | collective-permute-start | bytes 983048 | tf_op jit(solution)/shard_map/ppermute | solution.py:364
  9.1 0.9 %up_share.1 = (bf16[1,128,512]{2,1,0:T(8,128)(2,1)S(1)}, f32[1,128]{1,0:T(1,128)S(1)}) custom-call(s32[1]{0:T(128)} %bitcast.2.group_ref, s32[1]{0:T(128)} %bitcast.3.core_ref, s32[1]{0:T(128)S(6)} %copy.9.ranks_ref, bf16[1,128,2048]{2,1,0:T(8,128)(2,1)} %up_hbm.2), custom_call_target="tpu_custom_call" | custom-call | flops 65536 | bytes 262144 | tf_op jit(solution)/shard_map/up_share/pallas_call | solution.py:391
  10.0 0.4 collective-permute-start
  10.4 0.4 collective-permute-start.3
  10.9 0.3 collective-permute-start.4
  11.1 0.7 %convert_element_type.4 = f32[128]{0:T(128)S(1)} convert(s32[128]{0:T(128)} %param.10) | non-fusion elementwise | flops 128 | bytes 1024 | tf_op jit(solution)/shard_map/convert_element_type | solution.py:449
  11.8 5.6 %base.1 = (f32[128,1024]{1,0:T(8,128)S(1)}, f32[128,1024]{1,0:T(8,128)S(1)}, bf16[1,2560,128]{2,1,0:T(8,128)(2,1)S(1)}, bf16[1,128,1024]{2,1,0:T(8,128)(2,1)S(1)}) custom-call(s32[1]{0:T(128)} %bitcast.3.core_ref, bf16[128,2560]{1,0:T(8,128)(2,1)} %tokens_hbm.3, bf16[2560,2048]{1,0:T(8,128)(2,1)} %weight_hbm.1, bf16[1,2560,128]{2,1,0:T(8,128)(2,1)} %down_hbm.3, ...), custom_call_target="tpu_custom_call" | custom-call | flops 1342177280 | bytes 10485760 | tf_op jit(solution)/shard_map/base/pallas_call | solution.py:416
  17.5 4.9 %collective-permute-done.1.refs_4_ = bf16[1,1280,128]{2,1,0:T(8,128)(2,1)S(1)} collective-permute-done((bf16[1,1280,128]{2,1,0:T(8,128)(2,1)S(1)}, bf16[1,1280,128]{2,1,0:T(8,128)(2,1)S(1)}, u32[]{:S(2)}, u32[]{:S(2)}) %collective-permute-start.1) | collective-permute-done | bytes 327712 | tf_op jit(solution)/shard_map/ppermute | solution.py:364
  22.3 2.1 %collective-permute-start.6 = (bf16[1,1280,128]{2,1,0:T(8,128)(2,1)S(1)}, bf16[1,1280,128]{2,1,0:T(8,128)(2,1)S(1)}, u32[]{:S(2)}, u32[]{:S(2)}) collective-permute-start(bf16[1,1280,128]{2,1,0:T(8,128)(2,1)S(1)} %collective-permute-done.1.refs_4_), channel_id=1, source_target_pairs={{0,16},{16,0},{1,17},{17,1},{2,18},{18,2},{3,19},{19,3},{4,20},{20... | collective-permute-start | bytes 983048 | tf_op jit(solution)/shard_map/ppermute | solution.py:364
  24.5 0.3 fusion
  24.8 1.6 %collective-permute-done.refs_0_ = bf16[1,128,512]{2,1,0:T(8,128)(2,1)S(1)} collective-permute-done((bf16[1,128,512]{2,1,0:T(8,128)(2,1)S(1)}, bf16[1,128,512]{2,1,0:T(8,128)(2,1)S(1)}, u32[]{:S(2)}, u32[]{:S(2)}) %collective-permute-start) | collective-permute-done | bytes 131104 | tf_op jit(solution)/shard_map/ppermute | solution.py:364
  26.4 0.0 collective-permute-done.2.refs_1_
  26.4 0.0 collective-permute-start.5
  26.4 0.1 pad_maximum_fusion
  26.5 1.6 %collective-permute-start.8 = (bf16[1,128,512]{2,1,0:T(8,128)(2,1)S(1)}, bf16[1,128,512]{2,1,0:T(8,128)(2,1)S(1)}, u32[]{:S(2)}, u32[]{:S(2)}) collective-permute-start(bf16[1,128,512]{2,1,0:T(8,128)(2,1)S(1)} %collective-permute-done.refs_0_), channel_id=1, source_target_pairs={{0,16},{16,0},{1,17},{17,1},{2,18},{18,2},{3,19},{19,3},{4,20},{20... | collective-permute-start | bytes 393224 | tf_op jit(solution)/shard_map/ppermute | solution.py:364
  28.1 3.6 %collective-permute-done.3.refs_2_ = bf16[64,2560]{1,0:T(8,128)(2,1)S(1)} collective-permute-done((bf16[64,2560]{1,0:T(8,128)(2,1)S(1)}, bf16[64,2560]{1,0:T(8,128)(2,1)S(1)}, u32[]{:S(2)}, u32[]{:S(2)}) %collective-permute-start.3) | collective-permute-done | bytes 327712 | tf_op jit(solution)/shard_map/ppermute | solution.py:364
  31.8 0.0 collective-permute-done.4.refs_3_
  31.8 0.0 collective-permute-done.6.refs_5_
  31.8 0.5 %down.1.low_ref = f32[256,128]{1,0:T(8,128)S(1)} custom-call(s32[1]{0:T(128)} %bitcast.2.group_ref, bf16[1,2560,128]{2,1,0:T(8,128)(2,1)S(1)} %get-tuple-element.56.down_ref, bf16[64,2560]{1,0:T(8,128)(2,1)S(1)} %get-tuple-element.57.refs_0_, bf16[64,2560]{1,0:T(8,128)(2,1)S(1)} %collective-permute-done.2.refs_1_, ...), custom_call_target="tpu_custom_call" | custom-call | flops 335544320 | bytes 1966080 | tf_op jit(solution)/shard_map/down/pallas_call | solution.py:458
  32.3 0.1 collective-permute-start.7
  32.4 0.1 collective-permute-done.8.refs_1_
  32.5 1.2 %collective-permute-done.7.other_ref = f32[256,128]{1,0:T(8,128)S(1)} collective-permute-done((f32[256,128]{1,0:T(8,128)S(1)}, f32[256,128]{1,0:T(8,128)S(1)}, u32[]{:S(2)}, u32[]{:S(2)}) %collective-permute-start.7) | collective-permute-done | bytes 131104 | tf_op jit(solution)/shard_map/ppermute | solution.py:364
  33.7 0.8 %up.1 = (s16[64,1024]{1,0:T(8,128)(2,1)S(1)}, s16[64,1024]{1,0:T(8,128)(2,1)S(1)}, s16[64,1024]{1,0:T(8,128)(2,1)S(1)}, s16[64,1024]{1,0:T(8,128)(2,1)S(1)}) custom-call(s32[1]{0:T(128)} %bitcast.2.group_ref, f32[256,128]{1,0:T(8,128)S(1)} %down.1.low_ref, f32[256,128]{1,0:T(8,128)S(1)} %collective-permute-done.7.other_ref, ...), custom_call_target="tpu_custom_call" | custom-call | flops 268435456 | bytes 524288 | tf_op jit(solution)/shard_map/up/pallas_call | solution.py:469
  34.5 1.9 %collective-permute-start.10 = (s16[64,1024]{1,0:T(8,128)(2,1)S(1)}, s16[64,1024]{1,0:T(8,128)(2,1)S(1)}, u32[]{:S(2)}, u32[]{:S(2)}) collective-permute-start(s16[64,1024]{1,0:T(8,128)(2,1)S(1)} %get-tuple-element.69), channel_id=1, source_target_pairs={{0,6},{2,4},{4,2},{6,0},{8,14},{10,12},{12,10},{14,8},{1,7},{3,5},... | collective-permute-start | bytes 393224 | tf_op jit(solution)/shard_map/ppermute | solution.py:364
  36.4 0.2 collective-permute-start.11
  36.7 1.4 %collective-permute-start.9 = (s16[64,1024]{1,0:T(8,128)(2,1)S(1)}, s16[64,1024]{1,0:T(8,128)(2,1)S(1)}, u32[]{:S(2)}, u32[]{:S(2)}) collective-permute-start(s16[64,1024]{1,0:T(8,128)(2,1)S(1)} %get-tuple-element.68), channel_id=1, source_target_pairs={{0,2},{2,0},{4,6},{6,4},{8,10},{10,8},{12,14},{14,12},{1,3},{3,1},... | collective-permute-start | bytes 393224 | tf_op jit(solution)/shard_map/ppermute | solution.py:364
  38.0 0.0 copy-done.1
  38.1 0.0 collective-permute-done.5.other_ref
  38.1 0.0 copy-done
  38.1 0.5 %start_rows.1 = (f32[128,1024]{1,0:T(8,128)S(1)}, bf16[128,192]{1,0:T(8,128)(2,1)S(1)}) custom-call(s32[1]{0:T(128)} %bitcast.me_ref, s32[1,128]{1,0:T(1,128)S(1)} %bitcast.9, f32[128,1024]{1,0:T(8,128)S(1)} %get-tuple-element.54.mine_ref, f32[128,1024]{1,0:T(8,128)S(1)} %collective-permute-done.5.other_ref, s16[64,1024]{1,0:T(8,128)(2,1)S(1)} %get-tuple-element.63.own_ref), custom_call_target="tpu_custom_call" | custom-call | flops 33554432 | bytes 1572864 | tf_op jit(solution)/shard_map/start_rows/pallas_call | solution.py:482
  38.6 3.2 %collective-permute-done.10.refs_1_ = s16[64,1024]{1,0:T(8,128)(2,1)S(1)} collective-permute-done((s16[64,1024]{1,0:T(8,128)(2,1)S(1)}, s16[64,1024]{1,0:T(8,128)(2,1)S(1)}, u32[]{:S(2)}, u32[]{:S(2)}) %collective-permute-start.10) | collective-permute-done | bytes 131104 | tf_op jit(solution)/shard_map/ppermute | solution.py:364
  41.8 1.1 %collective-permute-done.11.refs_2_ = s16[64,1024]{1,0:T(8,128)(2,1)S(1)} collective-permute-done((s16[64,1024]{1,0:T(8,128)(2,1)S(1)}, s16[64,1024]{1,0:T(8,128)(2,1)S(1)}, u32[]{:S(2)}, u32[]{:S(2)}) %collective-permute-start.11) | collective-permute-done | bytes 131104 | tf_op jit(solution)/shard_map/ppermute | solution.py:364
  42.9 0.9 %collective-permute-done.9.refs_0_ = s16[64,1024]{1,0:T(8,128)(2,1)S(1)} collective-permute-done((s16[64,1024]{1,0:T(8,128)(2,1)S(1)}, s16[64,1024]{1,0:T(8,128)(2,1)S(1)}, u32[]{:S(2)}, u32[]{:S(2)}) %collective-permute-start.9) | collective-permute-done | bytes 131104 | tf_op jit(solution)/shard_map/ppermute | solution.py:364
  43.8 1.9 %finish.1 = bf16[1024,128]{1,0:T(8,128)(2,1)} custom-call(f32[128,1024]{1,0:T(8,128)S(1)} %get-tuple-element.64.partial_ref, bf16[128,192]{1,0:T(8,128)(2,1)S(1)} %get-tuple-element.65.picker_ref, f32[128,128]{1,0:T(8,128)S(1)} %get-tuple-element.66.cos_ref, f32[128,128]{1,0:T(8,128)S(1)} %get-tuple-element.67.sin_ref, ...), custom_call_target="tpu_custom_call" | custom-call | flops 134217728 | bytes 524288 | tf_op jit(solution)/shard_map/finish/pallas_call | solution.py:494
  (2 shorter events, 0.0 us)
Async XLA Ops:
  0.0 38.1 %copy-start = (s32[128,1]{0,1:T(1,128)S(1)}, s32[128,1]{0,1:T(1,128)}, u32[]{:S(2)}) copy-start(s32[128,1]{0,1:T(1,128)} %param.9) | copy-start | bytes 1540
  0.0 38.0 %copy-start.1 = (bf16[128]{0:T(256)(128)(2,1)S(1)}, bf16[128]{0:T(256)(128)(2,1)}, u32[]{:S(2)}) copy-start(bf16[128]{0:T(256)(128)(2,1)} %param.15) | copy-start | bytes 772
  1.8 20.5 %collective-permute-start.1 = (bf16[1,1280,128]{2,1,0:T(8,128)(2,1)S(1)}, bf16[1,1280,128]{2,1,0:T(8,128)(2,1)S(1)}, u32[]{:S(2)}, u32[]{:S(2)}) collective-permute-start(bf16[1,1280,128]{2,1,0:T(8,128)(2,1)S(1)} %get-tuple-element.45), channel_id=1, source_target_pairs={{0,8},{2,10},{4,12},{6,14},{8,0},{10,2},{12,4},{14,6},{1,9},{3,11}... | collective-permute-start | bytes 983048 | tf_op jit(solution)/shard_map/ppermute | solution.py:364
  5.9 20.5 %collective-permute-start.2 = (bf16[64,2560]{1,0:T(8,128)(2,1)S(1)}, bf16[64,2560]{1,0:T(8,128)(2,1)S(1)}, u32[]{:S(2)}, u32[]{:S(2)}) collective-permute-start(bf16[64,2560]{1,0:T(8,128)(2,1)S(1)} %get-tuple-element.41), channel_id=1, source_target_pairs={{0,6},{2,4},{4,2},{6,0},{8,14},{10,12},{12,10},{14,8},{1,7},{3,5},... | collective-permute-start | bytes 983048 | tf_op jit(solution)/shard_map/ppermute | solution.py:364
  10.0 16.4 %collective-permute-start = (bf16[1,128,512]{2,1,0:T(8,128)(2,1)S(1)}, bf16[1,128,512]{2,1,0:T(8,128)(2,1)S(1)}, u32[]{:S(2)}, u32[]{:S(2)}) collective-permute-start(bf16[1,128,512]{2,1,0:T(8,128)(2,1)S(1)} %get-tuple-element.44), channel_id=1, source_target_pairs={{0,8},{2,10},{4,12},{6,14},{8,0},{10,2},{12,4},{14,6},{1,9},{3,11}... | collective-permute-start | bytes 393224 | tf_op jit(solution)/shard_map/ppermute | solution.py:364
  10.4 21.3 %collective-permute-start.3 = (bf16[64,2560]{1,0:T(8,128)(2,1)S(1)}, bf16[64,2560]{1,0:T(8,128)(2,1)S(1)}, u32[]{:S(2)}, u32[]{:S(2)}) collective-permute-start(bf16[64,2560]{1,0:T(8,128)(2,1)S(1)} %get-tuple-element.51), channel_id=1, source_target_pairs={{0,4},{2,6},{4,0},{6,2},{8,12},{10,14},{12,8},{14,10},{1,5},{3,7},... | collective-permute-start | bytes 983048 | tf_op jit(solution)/shard_map/ppermute | solution.py:364
  10.9 20.9 %collective-permute-start.4 = (bf16[64,2560]{1,0:T(8,128)(2,1)S(1)}, bf16[64,2560]{1,0:T(8,128)(2,1)S(1)}, u32[]{:S(2)}, u32[]{:S(2)}) collective-permute-start(bf16[64,2560]{1,0:T(8,128)(2,1)S(1)} %get-tuple-element.52), channel_id=1, source_target_pairs={{0,2},{2,0},{4,6},{6,4},{8,10},{10,8},{12,14},{14,12},{1,3},{3,1},... | collective-permute-start | bytes 983048 | tf_op jit(solution)/shard_map/ppermute | solution.py:364
  22.3 9.4 %collective-permute-start.6 = (bf16[1,1280,128]{2,1,0:T(8,128)(2,1)S(1)}, bf16[1,1280,128]{2,1,0:T(8,128)(2,1)S(1)}, u32[]{:S(2)}, u32[]{:S(2)}) collective-permute-start(bf16[1,1280,128]{2,1,0:T(8,128)(2,1)S(1)} %collective-permute-done.1.refs_4_), channel_id=1, source_target_pairs={{0,16},{16,0},{1,17},{17,1},{2,18},{18,2},{3,19},{19,3},{4,20},{20... | collective-permute-start | bytes 983048 | tf_op jit(solution)/shard_map/ppermute | solution.py:364
  26.4 11.7 %collective-permute-start.5 = (f32[128,1024]{1,0:T(8,128)S(1)}, f32[128,1024]{1,0:T(8,128)S(1)}, u32[]{:S(2)}, u32[]{:S(2)}) collective-permute-start(f32[128,1024]{1,0:T(8,128)S(1)} %get-tuple-element.55), channel_id=1, source_target_pairs={{0,1},{1,0},{2,3},{3,2},{4,5},{5,4},{6,7},{7,6},{8,9},{9,8},{10,11... | collective-permute-start | bytes 1572872 | tf_op jit(solution)/shard_map/ppermute | solution.py:364
  26.5 6.0 %collective-permute-start.8 = (bf16[1,128,512]{2,1,0:T(8,128)(2,1)S(1)}, bf16[1,128,512]{2,1,0:T(8,128)(2,1)S(1)}, u32[]{:S(2)}, u32[]{:S(2)}) collective-permute-start(bf16[1,128,512]{2,1,0:T(8,128)(2,1)S(1)} %collective-permute-done.refs_0_), channel_id=1, source_target_pairs={{0,16},{16,0},{1,17},{17,1},{2,18},{18,2},{3,19},{19,3},{4,20},{20... | collective-permute-start | bytes 393224 | tf_op jit(solution)/shard_map/ppermute | solution.py:364
  32.3 1.4 %collective-permute-start.7 = (f32[256,128]{1,0:T(8,128)S(1)}, f32[256,128]{1,0:T(8,128)S(1)}, u32[]{:S(2)}, u32[]{:S(2)}) collective-permute-start(f32[256,128]{1,0:T(8,128)S(1)} %down.1.low_ref), channel_id=1, source_target_pairs={{0,1},{1,0},{2,3},{3,2},{4,5},{5,4},{6,7},{7,6},{8,9},{9,8},{10,11... | collective-permute-start | bytes 393224 | tf_op jit(solution)/shard_map/ppermute | solution.py:364
  34.5 7.3 %collective-permute-start.10 = (s16[64,1024]{1,0:T(8,128)(2,1)S(1)}, s16[64,1024]{1,0:T(8,128)(2,1)S(1)}, u32[]{:S(2)}, u32[]{:S(2)}) collective-permute-start(s16[64,1024]{1,0:T(8,128)(2,1)S(1)} %get-tuple-element.69), channel_id=1, source_target_pairs={{0,6},{2,4},{4,2},{6,0},{8,14},{10,12},{12,10},{14,8},{1,7},{3,5},... | collective-permute-start | bytes 393224 | tf_op jit(solution)/shard_map/ppermute | solution.py:364
  36.4 6.5 %collective-permute-start.11 = (s16[64,1024]{1,0:T(8,128)(2,1)S(1)}, s16[64,1024]{1,0:T(8,128)(2,1)S(1)}, u32[]{:S(2)}, u32[]{:S(2)}) collective-permute-start(s16[64,1024]{1,0:T(8,128)(2,1)S(1)} %get-tuple-element.70), channel_id=1, source_target_pairs={{0,4},{2,6},{4,0},{6,2},{8,12},{10,14},{12,8},{14,10},{1,5},{3,7},... | collective-permute-start | bytes 393224 | tf_op jit(solution)/shard_map/ppermute | solution.py:364
  36.7 7.1 %collective-permute-start.9 = (s16[64,1024]{1,0:T(8,128)(2,1)S(1)}, s16[64,1024]{1,0:T(8,128)(2,1)S(1)}, u32[]{:S(2)}, u32[]{:S(2)}) collective-permute-start(s16[64,1024]{1,0:T(8,128)(2,1)S(1)} %get-tuple-element.68), channel_id=1, source_target_pairs={{0,2},{2,0},{4,6},{6,4},{8,10},{10,8},{12,14},{14,12},{1,3},{3,1},... | collective-permute-start | bytes 393224 | tf_op jit(solution)/shard_map/ppermute | solution.py:364

commit v18 on v17

--- a/solution.py
+++ b/solution.py
@@ -290,43 +290,27 @@
 def finish_kernel(buffers, partial_ref, picker_ref, cos_ref, sin_ref, gain_ref, *refs):
     order = return_order(buffers)
     ins = [refs[order.index(j)] for j in range(1, buffers)]
-    out_hbm, out_ref, sems = refs[-3:]
+    out_hbm, entry_ref, out_ref, sems = refs[-4:]
     rows, columns = partial_ref.shape
     head = cos_ref.shape[1]
-    gain = gain_ref[...]
-    kinds, block = columns // head, 16
-    n = kinds * block
-    source = (iota((n, n), 0) % kinds) * block + iota((n, n), 0) // kinds
-    mix = jnp.where(iota((n, n), 1) == source, 1.0, 0.0).astype(jnp.bfloat16)
-    plane = [planes(ins, at, 2 * head) for at in range(0, columns, 2 * head)]
-    first = planes(ins, 0, LANES)
+    kinds = columns // head
+    gain, cosine, sine, picker = gain_ref[...], cos_ref[...], sin_ref[...], picker_ref[...]
+    scale = scale_of(decoded(picker, planes(ins, 0, LANES)))
+    for at in range(0, columns, 2 * head):
+        projected = partial_ref[:, at : at + 2 * head]
+        projected = projected + decoded(picker, planes(ins, at, 2 * head)) * scale
+        key, value = projected[:, :head], projected[:, head:]
+        mean = jnp.mean(key * key, axis=1, keepdims=True)
+        normed = key * lax.rsqrt(mean + NORM_EPS) * gain
+        rotated = normed * cosine + pltpu.roll(normed, head // 2, 1) * sine
+        entry_ref[pl.ds(at // head, rows, stride=kinds), :] = rotated
+        entry_ref[pl.ds(at // head + 1, rows, stride=kinds), :] = value
     copies = []
-    part = rows // 2
-    for begin in range(0, rows, part):
-        here = slice(begin, begin + part)
-        picker = picker_ref[here, :]
-        scale = scale_of(decoded(picker, first))
-        cosine, sine = cos_ref[here, :], sin_ref[here, :]
-        entries = []
-        for at in range(0, columns, 2 * head):
-            projected = partial_ref[here, at : at + 2 * head]
-            projected = projected + decoded(picker, plane[at // (2 * head)]) * scale
-            key, value = projected[:, :head], projected[:, head:]
-            mean = jnp.mean(key * key, axis=1, keepdims=True)
-            normed = key * lax.rsqrt(mean + NORM_EPS) * gain
-            rotated = normed * cosine + pltpu.roll(normed, head // 2, 1) * sine
-            entries += [rotated.astype(jnp.bfloat16), value.astype(jnp.bfloat16)]
-        for i in range(part // block):
-            stacked = jnp.concatenate([e[i * block : (i + 1) * block] for e in entries], axis=0)
-            mixed = jnp.dot(mix, stacked, preferred_element_type=jnp.float32)
-            top = begin * kinds + i * n
-            out_ref[top : top + n, :] = mixed.astype(jnp.bfloat16)
-        done = pl.ds(begin * kinds, part * kinds)
-        copies.append(
-            pltpu.make_async_copy(
-                out_ref.at[done, :], out_hbm.at[done, :], sems.at[begin // part]
-            )
-        )
+    part = rows * kinds // sems.shape[0]
+    for i in range(sems.shape[0]):
+        done = pl.ds(i * part, part)
+        out_ref[done, :] = entry_ref[done, :].astype(jnp.bfloat16)
+        copies.append(pltpu.make_async_copy(out_ref.at[done, :], out_hbm.at[done, :], sems.at[i]))
         copies[-1].start()
     for copy in copies:
         copy.wait()
@@ -497,8 +481,9 @@
         out_specs=HBM,
         out_shape=jax.ShapeDtypeStruct((rows * columns // head, head), bf16),
         scratch_shapes=[
+            pltpu.VMEM((rows * columns // head, head), f32),
             pltpu.VMEM((rows * columns // head, head), bf16),
-            pltpu.SemaphoreType.DMA((2,)),
+            pltpu.SemaphoreType.DMA((4,)),
         ],
         compiler_params=params(),
         cost_estimate=cost(4 * rows * slots * columns, 2 * slots * columns),

time: 45.8 us -> 45.3 us (0.989)
  Pallas kernels: 12 us -> 11.5 us
    pallas_call x1, Pallas kernels: 1.85 us -> 1.29 us  [body(): pl.pallas_call(functools.partial(finish_kernel, buffers), in_specs=[VMEM]...]
  transfers between devices with their start and end apart: 12 -> 12, of which waited for: 8 -> 8; matrix products, arithmetic and copies ran while one was open for 2% -> 2% of each run, Pallas kernels for 18% -> 19%
where the time goes in v18:
time: 45.3 us; the launch traced here: 45.1 us
  waiting for transfers between devices  16.7 us (37%)
  starting transfers between devices  15.1 us (33%)
  Pallas kernels  11.5 us (25%)
  other arithmetic  1.08 us (2%)
  between operations  0.75 us (2%)
    ppermute x12, waiting for transfers between devices, exchange(): return lax.ppermute(x, axis, [(p, p ^ j) for p in range(count)])  16.7 us
    ppermute x12, starting transfers between devices, exchange(): return lax.ppermute(x, axis, [(p, p ^ j) for p in range(count)])  15.1 us
    pallas_call x1, Pallas kernels, body(): pl.pallas_call(base_kernel, in_specs=[SMEM] + [HBM] * 4, out_specs=[VMEM]...  5.63 us
    pallas_call x1, Pallas kernels, body(): pl.pallas_call(functools.partial(pick_kernel, pool, local, depth), in_spe...  1.78 us
    pallas_call x1, Pallas kernels, body(): pl.pallas_call(functools.partial(finish_kernel, buffers), in_specs=[VMEM]...  1.29 us
    pallas_call x1, Pallas kernels, body(): pl.pallas_call(functools.partial(up_share_kernel, cores), in_specs=[SMEM]...  0.95 us
  transfers between devices with their start and end apart: 12, of which 8 were waited for; matrix products, arithmetic and copies ran while one was open for 2% of the time, Pallas kernels for 19%

profile of v18, /device:TPU:0, one launch (start us, length us, event | category | flops | bytes accessed | tf_op | source)
XLA Modules:
  0.0 45.1 jit_solution(5088349925299361794)
XLA Ops:
  0.0 0.0 copy-start
  0.0 0.0 copy-start.1
  0.0 1.8 %pick.1 = (bf16[1,1280,128]{2,1,0:T(8,128)(2,1)S(1)}, bf16[64,2560]{1,0:T(8,128)(2,1)S(1)}, bf16[64,2560]{1,0:T(8,128)(2,1)S(1)}, bf16[64,2560]{1,0:T(8,128)(2,1)S(1)}, bf16[64,2560]{1,0:T(8,128)(2,1)S(1)}) custom-call(s32[1]{0:T(128)} %bitcast.me_ref, s32[1]{0:T(128)} %bitcast.2.group_ref, s32[1,128]{1,0:T(1,128)} %bitcast.8, bf16[128,2560]{1,0:T(8,128)(2,1)} %tokens_hbm.3, ...), custom_call_target="tpu_custom_call" | custom-call | flops 167772160 | bytes 1966080 | tf_op jit(solution)/shard_map/pick/pallas_call | solution.py:356
  1.8 4.1 %collective-permute-start.1 = (bf16[1,1280,128]{2,1,0:T(8,128)(2,1)S(1)}, bf16[1,1280,128]{2,1,0:T(8,128)(2,1)S(1)}, u32[]{:S(2)}, u32[]{:S(2)}) collective-permute-start(bf16[1,1280,128]{2,1,0:T(8,128)(2,1)S(1)} %get-tuple-element.45), channel_id=1, source_target_pairs={{0,8},{2,10},{4,12},{6,14},{8,0},{10,2},{12,4},{14,6},{1,9},{3,11}... | collective-permute-start | bytes 983048 | tf_op jit(solution)/shard_map/ppermute | solution.py:348
  5.9 2.5 %collective-permute-start.2 = (bf16[64,2560]{1,0:T(8,128)(2,1)S(1)}, bf16[64,2560]{1,0:T(8,128)(2,1)S(1)}, u32[]{:S(2)}, u32[]{:S(2)}) collective-permute-start(bf16[64,2560]{1,0:T(8,128)(2,1)S(1)} %get-tuple-element.41), channel_id=1, source_target_pairs={{0,6},{2,4},{4,2},{6,0},{8,14},{10,12},{12,10},{14,8},{1,7},{3,5},... | collective-permute-start | bytes 983048 | tf_op jit(solution)/shard_map/ppermute | solution.py:348
  9.1 0.9 %up_share.1 = (bf16[1,128,512]{2,1,0:T(8,128)(2,1)S(1)}, f32[1,128]{1,0:T(1,128)S(1)}) custom-call(s32[1]{0:T(128)} %bitcast.2.group_ref, s32[1]{0:T(128)} %bitcast.3.core_ref, s32[1]{0:T(128)S(6)} %copy.9.ranks_ref, bf16[1,128,2048]{2,1,0:T(8,128)(2,1)} %up_hbm.2), custom_call_target="tpu_custom_call" | custom-call | flops 65536 | bytes 262144 | tf_op jit(solution)/shard_map/up_share/pallas_call | solution.py:375
  10.0 0.4 collective-permute-start
  10.4 0.4 collective-permute-start.3
  10.9 0.3 collective-permute-start.4
  11.1 0.7 %convert_element_type.4 = f32[128]{0:T(128)S(1)} convert(s32[128]{0:T(128)} %param.10) | non-fusion elementwise | flops 128 | bytes 1024 | tf_op jit(solution)/shard_map/convert_element_type | solution.py:433
  11.8 5.6 %base.1 = (f32[128,1024]{1,0:T(8,128)S(1)}, f32[128,1024]{1,0:T(8,128)S(1)}, bf16[1,2560,128]{2,1,0:T(8,128)(2,1)S(1)}, bf16[1,128,1024]{2,1,0:T(8,128)(2,1)S(1)}) custom-call(s32[1]{0:T(128)} %bitcast.3.core_ref, bf16[128,2560]{1,0:T(8,128)(2,1)} %tokens_hbm.3, bf16[2560,2048]{1,0:T(8,128)(2,1)} %weight_hbm.1, bf16[1,2560,128]{2,1,0:T(8,128)(2,1)} %down_hbm.3, ...), custom_call_target="tpu_custom_call" | custom-call | flops 1342177280 | bytes 10485760 | tf_op jit(solution)/shard_map/base/pallas_call | solution.py:400
  17.5 4.9 %collective-permute-done.1.refs_4_ = bf16[1,1280,128]{2,1,0:T(8,128)(2,1)S(1)} collective-permute-done((bf16[1,1280,128]{2,1,0:T(8,128)(2,1)S(1)}, bf16[1,1280,128]{2,1,0:T(8,128)(2,1)S(1)}, u32[]{:S(2)}, u32[]{:S(2)}) %collective-permute-start.1) | collective-permute-done | bytes 327712 | tf_op jit(solution)/shard_map/ppermute | solution.py:348
  22.3 2.1 %collective-permute-start.6 = (bf16[1,1280,128]{2,1,0:T(8,128)(2,1)S(1)}, bf16[1,1280,128]{2,1,0:T(8,128)(2,1)S(1)}, u32[]{:S(2)}, u32[]{:S(2)}) collective-permute-start(bf16[1,1280,128]{2,1,0:T(8,128)(2,1)S(1)} %collective-permute-done.1.refs_4_), channel_id=1, source_target_pairs={{0,16},{16,0},{1,17},{17,1},{2,18},{18,2},{3,19},{19,3},{4,20},{20... | collective-permute-start | bytes 983048 | tf_op jit(solution)/shard_map/ppermute | solution.py:348
  24.5 0.3 fusion
  24.8 1.6 %collective-permute-done.refs_0_ = bf16[1,128,512]{2,1,0:T(8,128)(2,1)S(1)} collective-permute-done((bf16[1,128,512]{2,1,0:T(8,128)(2,1)S(1)}, bf16[1,128,512]{2,1,0:T(8,128)(2,1)S(1)}, u32[]{:S(2)}, u32[]{:S(2)}) %collective-permute-start) | collective-permute-done | bytes 131104 | tf_op jit(solution)/shard_map/ppermute | solution.py:348
  26.4 0.0 collective-permute-done.2.refs_1_
  26.4 0.0 collective-permute-start.5
  26.4 0.1 pad_maximum_fusion
  26.5 1.6 %collective-permute-start.8 = (bf16[1,128,512]{2,1,0:T(8,128)(2,1)S(1)}, bf16[1,128,512]{2,1,0:T(8,128)(2,1)S(1)}, u32[]{:S(2)}, u32[]{:S(2)}) collective-permute-start(bf16[1,128,512]{2,1,0:T(8,128)(2,1)S(1)} %collective-permute-done.refs_0_), channel_id=1, source_target_pairs={{0,16},{16,0},{1,17},{17,1},{2,18},{18,2},{3,19},{19,3},{4,20},{20... | collective-permute-start | bytes 393224 | tf_op jit(solution)/shard_map/ppermute | solution.py:348
  28.1 3.6 %collective-permute-done.3.refs_2_ = bf16[64,2560]{1,0:T(8,128)(2,1)S(1)} collective-permute-done((bf16[64,2560]{1,0:T(8,128)(2,1)S(1)}, bf16[64,2560]{1,0:T(8,128)(2,1)S(1)}, u32[]{:S(2)}, u32[]{:S(2)}) %collective-permute-start.3) | collective-permute-done | bytes 327712 | tf_op jit(solution)/shard_map/ppermute | solution.py:348
  31.8 0.0 collective-permute-done.4.refs_3_
  31.8 0.0 collective-permute-done.6.refs_5_
  31.8 0.5 %down.1.low_ref = f32[256,128]{1,0:T(8,128)S(1)} custom-call(s32[1]{0:T(128)} %bitcast.2.group_ref, bf16[1,2560,128]{2,1,0:T(8,128)(2,1)S(1)} %get-tuple-element.56.down_ref, bf16[64,2560]{1,0:T(8,128)(2,1)S(1)} %get-tuple-element.57.refs_0_, bf16[64,2560]{1,0:T(8,128)(2,1)S(1)} %collective-permute-done.2.refs_1_, ...), custom_call_target="tpu_custom_call" | custom-call | flops 335544320 | bytes 1966080 | tf_op jit(solution)/shard_map/down/pallas_call | solution.py:442
  32.3 0.1 collective-permute-start.7
  32.4 0.1 collective-permute-done.8.refs_1_
  32.5 1.2 %collective-permute-done.7.other_ref = f32[256,128]{1,0:T(8,128)S(1)} collective-permute-done((f32[256,128]{1,0:T(8,128)S(1)}, f32[256,128]{1,0:T(8,128)S(1)}, u32[]{:S(2)}, u32[]{:S(2)}) %collective-permute-start.7) | collective-permute-done | bytes 131104 | tf_op jit(solution)/shard_map/ppermute | solution.py:348
  33.7 0.8 %up.1 = (s16[64,1024]{1,0:T(8,128)(2,1)S(1)}, s16[64,1024]{1,0:T(8,128)(2,1)S(1)}, s16[64,1024]{1,0:T(8,128)(2,1)S(1)}, s16[64,1024]{1,0:T(8,128)(2,1)S(1)}) custom-call(s32[1]{0:T(128)} %bitcast.2.group_ref, f32[256,128]{1,0:T(8,128)S(1)} %down.1.low_ref, f32[256,128]{1,0:T(8,128)S(1)} %collective-permute-done.7.other_ref, ...), custom_call_target="tpu_custom_call" | custom-call | flops 268435456 | bytes 524288 | tf_op jit(solution)/shard_map/up/pallas_call | solution.py:453
  34.5 1.9 %collective-permute-start.10 = (s16[64,1024]{1,0:T(8,128)(2,1)S(1)}, s16[64,1024]{1,0:T(8,128)(2,1)S(1)}, u32[]{:S(2)}, u32[]{:S(2)}) collective-permute-start(s16[64,1024]{1,0:T(8,128)(2,1)S(1)} %get-tuple-element.69), channel_id=1, source_target_pairs={{0,6},{2,4},{4,2},{6,0},{8,14},{10,12},{12,10},{14,8},{1,7},{3,5},... | collective-permute-start | bytes 393224 | tf_op jit(solution)/shard_map/ppermute | solution.py:348
  36.4 0.2 collective-permute-start.11
  36.7 1.4 %collective-permute-start.9 = (s16[64,1024]{1,0:T(8,128)(2,1)S(1)}, s16[64,1024]{1,0:T(8,128)(2,1)S(1)}, u32[]{:S(2)}, u32[]{:S(2)}) collective-permute-start(s16[64,1024]{1,0:T(8,128)(2,1)S(1)} %get-tuple-element.68), channel_id=1, source_target_pairs={{0,2},{2,0},{4,6},{6,4},{8,10},{10,8},{12,14},{14,12},{1,3},{3,1},... | collective-permute-start | bytes 393224 | tf_op jit(solution)/shard_map/ppermute | solution.py:348
  38.0 0.0 copy-done.1
  38.1 0.0 collective-permute-done.5.other_ref
  38.1 0.0 copy-done
  38.1 0.5 %start_rows.1 = (f32[128,1024]{1,0:T(8,128)S(1)}, bf16[128,192]{1,0:T(8,128)(2,1)S(1)}) custom-call(s32[1]{0:T(128)} %bitcast.me_ref, s32[1,128]{1,0:T(1,128)S(1)} %bitcast.9, f32[128,1024]{1,0:T(8,128)S(1)} %get-tuple-element.54.mine_ref, f32[128,1024]{1,0:T(8,128)S(1)} %collective-permute-done.5.other_ref, s16[64,1024]{1,0:T(8,128)(2,1)S(1)} %get-tuple-element.63.own_ref), custom_call_target="tpu_custom_call" | custom-call | flops 33554432 | bytes 1572864 | tf_op jit(solution)/shard_map/start_rows/pallas_call | solution.py:466
  38.6 3.2 %collective-permute-done.10.refs_1_ = s16[64,1024]{1,0:T(8,128)(2,1)S(1)} collective-permute-done((s16[64,1024]{1,0:T(8,128)(2,1)S(1)}, s16[64,1024]{1,0:T(8,128)(2,1)S(1)}, u32[]{:S(2)}, u32[]{:S(2)}) %collective-permute-start.10) | collective-permute-done | bytes 131104 | tf_op jit(solution)/shard_map/ppermute | solution.py:348
  41.8 1.1 %collective-permute-done.11.refs_2_ = s16[64,1024]{1,0:T(8,128)(2,1)S(1)} collective-permute-done((s16[64,1024]{1,0:T(8,128)(2,1)S(1)}, s16[64,1024]{1,0:T(8,128)(2,1)S(1)}, u32[]{:S(2)}, u32[]{:S(2)}) %collective-permute-start.11) | collective-permute-done | bytes 131104 | tf_op jit(solution)/shard_map/ppermute | solution.py:348
  42.9 0.9 %collective-permute-done.9.refs_0_ = s16[64,1024]{1,0:T(8,128)(2,1)S(1)} collective-permute-done((s16[64,1024]{1,0:T(8,128)(2,1)S(1)}, s16[64,1024]{1,0:T(8,128)(2,1)S(1)}, u32[]{:S(2)}, u32[]{:S(2)}) %collective-permute-start.9) | collective-permute-done | bytes 131104 | tf_op jit(solution)/shard_map/ppermute | solution.py:348
  43.8 1.3 %finish.1 = bf16[1024,128]{1,0:T(8,128)(2,1)} custom-call(f32[128,1024]{1,0:T(8,128)S(1)} %get-tuple-element.64.partial_ref, bf16[128,192]{1,0:T(8,128)(2,1)S(1)} %get-tuple-element.65.picker_ref, f32[128,128]{1,0:T(8,128)S(1)} %get-tuple-element.66.cos_ref, f32[128,128]{1,0:T(8,128)S(1)} %get-tuple-element.67.sin_ref, ...), custom_call_target="tpu_custom_call" | custom-call | flops 134217728 | bytes 524288 | tf_op jit(solution)/shard_map/finish/pallas_call | solution.py:478
  (2 shorter events, 0.0 us)
Async XLA Ops:
  0.0 38.1 %copy-start = (s32[128,1]{0,1:T(1,128)S(1)}, s32[128,1]{0,1:T(1,128)}, u32[]{:S(2)}) copy-start(s32[128,1]{0,1:T(1,128)} %param.9) | copy-start | bytes 1540
  0.0 38.0 %copy-start.1 = (bf16[128]{0:T(256)(128)(2,1)S(1)}, bf16[128]{0:T(256)(128)(2,1)}, u32[]{:S(2)}) copy-start(bf16[128]{0:T(256)(128)(2,1)} %param.15) | copy-start | bytes 772
  1.8 20.5 %collective-permute-start.1 = (bf16[1,1280,128]{2,1,0:T(8,128)(2,1)S(1)}, bf16[1,1280,128]{2,1,0:T(8,128)(2,1)S(1)}, u32[]{:S(2)}, u32[]{:S(2)}) collective-permute-start(bf16[1,1280,128]{2,1,0:T(8,128)(2,1)S(1)} %get-tuple-element.45), channel_id=1, source_target_pairs={{0,8},{2,10},{4,12},{6,14},{8,0},{10,2},{12,4},{14,6},{1,9},{3,11}... | collective-permute-start | bytes 983048 | tf_op jit(solution)/shard_map/ppermute | solution.py:348
  5.9 20.5 %collective-permute-start.2 = (bf16[64,2560]{1,0:T(8,128)(2,1)S(1)}, bf16[64,2560]{1,0:T(8,128)(2,1)S(1)}, u32[]{:S(2)}, u32[]{:S(2)}) collective-permute-start(bf16[64,2560]{1,0:T(8,128)(2,1)S(1)} %get-tuple-element.41), channel_id=1, source_target_pairs={{0,6},{2,4},{4,2},{6,0},{8,14},{10,12},{12,10},{14,8},{1,7},{3,5},... | collective-permute-start | bytes 983048 | tf_op jit(solution)/shard_map/ppermute | solution.py:348
  10.0 16.4 %collective-permute-start = (bf16[1,128,512]{2,1,0:T(8,128)(2,1)S(1)}, bf16[1,128,512]{2,1,0:T(8,128)(2,1)S(1)}, u32[]{:S(2)}, u32[]{:S(2)}) collective-permute-start(bf16[1,128,512]{2,1,0:T(8,128)(2,1)S(1)} %get-tuple-element.44), channel_id=1, source_target_pairs={{0,8},{2,10},{4,12},{6,14},{8,0},{10,2},{12,4},{14,6},{1,9},{3,11}... | collective-permute-start | bytes 393224 | tf_op jit(solution)/shard_map/ppermute | solution.py:348
  10.4 21.3 %collective-permute-start.3 = (bf16[64,2560]{1,0:T(8,128)(2,1)S(1)}, bf16[64,2560]{1,0:T(8,128)(2,1)S(1)}, u32[]{:S(2)}, u32[]{:S(2)}) collective-permute-start(bf16[64,2560]{1,0:T(8,128)(2,1)S(1)} %get-tuple-element.51), channel_id=1, source_target_pairs={{0,4},{2,6},{4,0},{6,2},{8,12},{10,14},{12,8},{14,10},{1,5},{3,7},... | collective-permute-start | bytes 983048 | tf_op jit(solution)/shard_map/ppermute | solution.py:348
  10.9 20.9 %collective-permute-start.4 = (bf16[64,2560]{1,0:T(8,128)(2,1)S(1)}, bf16[64,2560]{1,0:T(8,128)(2,1)S(1)}, u32[]{:S(2)}, u32[]{:S(2)}) collective-permute-start(bf16[64,2560]{1,0:T(8,128)(2,1)S(1)} %get-tuple-element.52), channel_id=1, source_target_pairs={{0,2},{2,0},{4,6},{6,4},{8,10},{10,8},{12,14},{14,12},{1,3},{3,1},... | collective-permute-start | bytes 983048 | tf_op jit(solution)/shard_map/ppermute | solution.py:348
  22.3 9.4 %collective-permute-start.6 = (bf16[1,1280,128]{2,1,0:T(8,128)(2,1)S(1)}, bf16[1,1280,128]{2,1,0:T(8,128)(2,1)S(1)}, u32[]{:S(2)}, u32[]{:S(2)}) collective-permute-start(bf16[1,1280,128]{2,1,0:T(8,128)(2,1)S(1)} %collective-permute-done.1.refs_4_), channel_id=1, source_target_pairs={{0,16},{16,0},{1,17},{17,1},{2,18},{18,2},{3,19},{19,3},{4,20},{20... | collective-permute-start | bytes 983048 | tf_op jit(solution)/shard_map/ppermute | solution.py:348
  26.4 11.7 %collective-permute-start.5 = (f32[128,1024]{1,0:T(8,128)S(1)}, f32[128,1024]{1,0:T(8,128)S(1)}, u32[]{:S(2)}, u32[]{:S(2)}) collective-permute-start(f32[128,1024]{1,0:T(8,128)S(1)} %get-tuple-element.55), channel_id=1, source_target_pairs={{0,1},{1,0},{2,3},{3,2},{4,5},{5,4},{6,7},{7,6},{8,9},{9,8},{10,11... | collective-permute-start | bytes 1572872 | tf_op jit(solution)/shard_map/ppermute | solution.py:348
  26.5 6.0 %collective-permute-start.8 = (bf16[1,128,512]{2,1,0:T(8,128)(2,1)S(1)}, bf16[1,128,512]{2,1,0:T(8,128)(2,1)S(1)}, u32[]{:S(2)}, u32[]{:S(2)}) collective-permute-start(bf16[1,128,512]{2,1,0:T(8,128)(2,1)S(1)} %collective-permute-done.refs_0_), channel_id=1, source_target_pairs={{0,16},{16,0},{1,17},{17,1},{2,18},{18,2},{3,19},{19,3},{4,20},{20... | collective-permute-start | bytes 393224 | tf_op jit(solution)/shard_map/ppermute | solution.py:348
  32.3 1.4 %collective-permute-start.7 = (f32[256,128]{1,0:T(8,128)S(1)}, f32[256,128]{1,0:T(8,128)S(1)}, u32[]{:S(2)}, u32[]{:S(2)}) collective-permute-start(f32[256,128]{1,0:T(8,128)S(1)} %down.1.low_ref), channel_id=1, source_target_pairs={{0,1},{1,0},{2,3},{3,2},{4,5},{5,4},{6,7},{7,6},{8,9},{9,8},{10,11... | collective-permute-start | bytes 393224 | tf_op jit(solution)/shard_map/ppermute | solution.py:348
  34.5 7.3 %collective-permute-start.10 = (s16[64,1024]{1,0:T(8,128)(2,1)S(1)}, s16[64,1024]{1,0:T(8,128)(2,1)S(1)}, u32[]{:S(2)}, u32[]{:S(2)}) collective-permute-start(s16[64,1024]{1,0:T(8,128)(2,1)S(1)} %get-tuple-element.69), channel_id=1, source_target_pairs={{0,6},{2,4},{4,2},{6,0},{8,14},{10,12},{12,10},{14,8},{1,7},{3,5},... | collective-permute-start | bytes 393224 | tf_op jit(solution)/shard_map/ppermute | solution.py:348
  36.4 6.5 %collective-permute-start.11 = (s16[64,1024]{1,0:T(8,128)(2,1)S(1)}, s16[64,1024]{1,0:T(8,128)(2,1)S(1)}, u32[]{:S(2)}, u32[]{:S(2)}) collective-permute-start(s16[64,1024]{1,0:T(8,128)(2,1)S(1)} %get-tuple-element.70), channel_id=1, source_target_pairs={{0,4},{2,6},{4,0},{6,2},{8,12},{10,14},{12,8},{14,10},{1,5},{3,7},... | collective-permute-start | bytes 393224 | tf_op jit(solution)/shard_map/ppermute | solution.py:348
  36.7 7.1 %collective-permute-start.9 = (s16[64,1024]{1,0:T(8,128)(2,1)S(1)}, s16[64,1024]{1,0:T(8,128)(2,1)S(1)}, u32[]{:S(2)}, u32[]{:S(2)}) collective-permute-start(s16[64,1024]{1,0:T(8,128)(2,1)S(1)} %get-tuple-element.68), channel_id=1, source_target_pairs={{0,2},{2,0},{4,6},{6,4},{8,10},{10,8},{12,14},{14,12},{1,3},{3,1},... | collective-permute-start | bytes 393224 | tf_op jit(solution)/shard_map/ppermute | solution.py:348

commit v19 on v18

--- a/solution.py
+++ b/solution.py
@@ -424,7 +424,7 @@
     )
     far_down, theirs = lax.optimization_barrier((far_down, theirs))
     far_downs = hand_round(far_down)
-    far_up, _ = lax.optimization_barrier((far_up, far_down))
+    far_up, arrived[-1] = lax.optimization_barrier((far_up, arrived[-1]))
     far_ups = hand_round(far_up)
     half_dim = head // 2
     frequency = jnp.power(
@@ -435,7 +435,7 @@
     cosine = jnp.concatenate([cosine, cosine], axis=1)
     sine = jnp.concatenate([-sine, sine], axis=1)
 
-    far_up, arrived[1], theirs = lax.optimization_barrier((far_up, arrived[1], theirs))
+    far_up, arrived[-1], theirs = lax.optimization_barrier((far_up, arrived[-1], theirs))
     other = exchange(theirs, "tp", cores, 1)
     arrived, mine, cosine, sine = lax.optimization_barrier((arrived, mine, cosine, sine))
     slots = buffers * size

time: 45.3 us -> 45.3 us (level)
  no operation moved by 1% of the time
where the time goes in v19:
time: 45.3 us; the launch traced here: 45.1 us
  waiting for transfers between devices  16.7 us (37%)
  starting transfers between devices  15.1 us (33%)
  Pallas kernels  11.5 us (25%)
  other arithmetic  1.08 us (2%)
  between operations  0.75 us (2%)
    ppermute x12, waiting for transfers between devices, exchange(): return lax.ppermute(x, axis, [(p, p ^ j) for p in range(count)])  16.7 us
    ppermute x12, starting transfers between devices, exchange(): return lax.ppermute(x, axis, [(p, p ^ j) for p in range(count)])  15.1 us
    pallas_call x1, Pallas kernels, body(): pl.pallas_call(base_kernel, in_specs=[SMEM] + [HBM] * 4, out_specs=[VMEM]...  5.63 us
    pallas_call x1, Pallas kernels, body(): pl.pallas_call(functools.partial(pick_kernel, pool, local, depth), in_spe...  1.78 us
    pallas_call x1, Pallas kernels, body(): pl.pallas_call(functools.partial(finish_kernel, buffers), in_specs=[VMEM]...  1.29 us
    pallas_call x1, Pallas kernels, body(): pl.pallas_call(functools.partial(up_share_kernel, cores), in_specs=[SMEM]...  0.95 us
  transfers between devices with their start and end apart: 12, of which 8 were waited for; matrix products, arithmetic and copies ran while one was open for 2% of the time, Pallas kernels for 19%

profile of v19, /device:TPU:0, one launch (start us, length us, event | category | flops | bytes accessed | tf_op | source)
XLA Modules:
  0.0 45.1 jit_solution(15920162929015678404)
XLA Ops:
  0.0 0.0 copy-start
  0.0 0.0 copy-start.1
  0.0 1.8 %pick.1 = (bf16[1,1280,128]{2,1,0:T(8,128)(2,1)S(1)}, bf16[64,2560]{1,0:T(8,128)(2,1)S(1)}, bf16[64,2560]{1,0:T(8,128)(2,1)S(1)}, bf16[64,2560]{1,0:T(8,128)(2,1)S(1)}, bf16[64,2560]{1,0:T(8,128)(2,1)S(1)}) custom-call(s32[1]{0:T(128)} %bitcast.me_ref, s32[1]{0:T(128)} %bitcast.2.group_ref, s32[1,128]{1,0:T(1,128)} %bitcast.8, bf16[128,2560]{1,0:T(8,128)(2,1)} %tokens_hbm.3, ...), custom_call_target="tpu_custom_call" | custom-call | flops 167772160 | bytes 1966080 | tf_op jit(solution)/shard_map/pick/pallas_call | solution.py:356
  1.8 4.1 %collective-permute-start.4 = (bf16[1,1280,128]{2,1,0:T(8,128)(2,1)S(1)}, bf16[1,1280,128]{2,1,0:T(8,128)(2,1)S(1)}, u32[]{:S(2)}, u32[]{:S(2)}) collective-permute-start(bf16[1,1280,128]{2,1,0:T(8,128)(2,1)S(1)} %get-tuple-element.50), channel_id=1, source_target_pairs={{0,8},{2,10},{4,12},{6,14},{8,0},{10,2},{12,4},{14,6},{1,9},{3,11}... | collective-permute-start | bytes 983048 | tf_op jit(solution)/shard_map/ppermute | solution.py:348
  5.9 2.5 %collective-permute-start = (bf16[64,2560]{1,0:T(8,128)(2,1)S(1)}, bf16[64,2560]{1,0:T(8,128)(2,1)S(1)}, u32[]{:S(2)}, u32[]{:S(2)}) collective-permute-start(bf16[64,2560]{1,0:T(8,128)(2,1)S(1)} %get-tuple-element.40), channel_id=1, source_target_pairs={{0,6},{2,4},{4,2},{6,0},{8,14},{10,12},{12,10},{14,8},{1,7},{3,5},... | collective-permute-start | bytes 983048 | tf_op jit(solution)/shard_map/ppermute | solution.py:348
  9.1 0.9 %up_share.1 = (bf16[1,128,512]{2,1,0:T(8,128)(2,1)S(1)}, f32[1,128]{1,0:T(1,128)S(1)}) custom-call(s32[1]{0:T(128)} %bitcast.2.group_ref, s32[1]{0:T(128)} %bitcast.3.core_ref, s32[1]{0:T(128)S(6)} %copy.9.ranks_ref, bf16[1,128,2048]{2,1,0:T(8,128)(2,1)} %up_hbm.2), custom_call_target="tpu_custom_call" | custom-call | flops 65536 | bytes 262144 | tf_op jit(solution)/shard_map/up_share/pallas_call | solution.py:375
  10.0 0.4 collective-permute-start.2
  10.4 0.5 %collective-permute-start.3 = (bf16[64,2560]{1,0:T(8,128)(2,1)S(1)}, bf16[64,2560]{1,0:T(8,128)(2,1)S(1)}, u32[]{:S(2)}, u32[]{:S(2)}) collective-permute-start(bf16[64,2560]{1,0:T(8,128)(2,1)S(1)} %get-tuple-element.47), channel_id=1, source_target_pairs={{0,2},{2,0},{4,6},{6,4},{8,10},{10,8},{12,14},{14,12},{1,3},{3,1},... | collective-permute-start | bytes 983048 | tf_op jit(solution)/shard_map/ppermute | solution.py:348
  10.9 0.2 collective-permute-start.1
  11.1 0.7 %convert_element_type.4 = f32[128]{0:T(128)S(1)} convert(s32[128]{0:T(128)} %param.10) | non-fusion elementwise | flops 128 | bytes 1024 | tf_op jit(solution)/shard_map/convert_element_type | solution.py:433
  11.8 5.6 %base.1 = (f32[128,1024]{1,0:T(8,128)S(1)}, f32[128,1024]{1,0:T(8,128)S(1)}, bf16[1,2560,128]{2,1,0:T(8,128)(2,1)S(1)}, bf16[1,128,1024]{2,1,0:T(8,128)(2,1)S(1)}) custom-call(s32[1]{0:T(128)} %bitcast.3.core_ref, bf16[128,2560]{1,0:T(8,128)(2,1)} %tokens_hbm.3, bf16[2560,2048]{1,0:T(8,128)(2,1)} %weight_hbm.1, bf16[1,2560,128]{2,1,0:T(8,128)(2,1)} %down_hbm.3, ...), custom_call_target="tpu_custom_call" | custom-call | flops 1342177280 | bytes 10485760 | tf_op jit(solution)/shard_map/base/pallas_call | solution.py:400
  17.5 4.9 %collective-permute-done.4.refs_4_ = bf16[1,1280,128]{2,1,0:T(8,128)(2,1)S(1)} collective-permute-done((bf16[1,1280,128]{2,1,0:T(8,128)(2,1)S(1)}, bf16[1,1280,128]{2,1,0:T(8,128)(2,1)S(1)}, u32[]{:S(2)}, u32[]{:S(2)}) %collective-permute-start.4) | collective-permute-done | bytes 327712 | tf_op jit(solution)/shard_map/ppermute | solution.py:348
  22.3 2.1 %collective-permute-start.6 = (bf16[1,1280,128]{2,1,0:T(8,128)(2,1)S(1)}, bf16[1,1280,128]{2,1,0:T(8,128)(2,1)S(1)}, u32[]{:S(2)}, u32[]{:S(2)}) collective-permute-start(bf16[1,1280,128]{2,1,0:T(8,128)(2,1)S(1)} %collective-permute-done.4.refs_4_), channel_id=1, source_target_pairs={{0,16},{16,0},{1,17},{17,1},{2,18},{18,2},{3,19},{19,3},{4,20},{20... | collective-permute-start | bytes 983048 | tf_op jit(solution)/shard_map/ppermute | solution.py:348
  24.5 0.3 fusion
  24.8 1.6 %collective-permute-done.2.refs_0_ = bf16[1,128,512]{2,1,0:T(8,128)(2,1)S(1)} collective-permute-done((bf16[1,128,512]{2,1,0:T(8,128)(2,1)S(1)}, bf16[1,128,512]{2,1,0:T(8,128)(2,1)S(1)}, u32[]{:S(2)}, u32[]{:S(2)}) %collective-permute-start.2) | collective-permute-done | bytes 131104 | tf_op jit(solution)/shard_map/ppermute | solution.py:348
  26.4 0.0 collective-permute-done.3.refs_3_
  26.4 0.0 collective-permute-start.5
  26.4 0.1 pad_maximum_fusion
  26.5 1.6 %collective-permute-start.8 = (bf16[1,128,512]{2,1,0:T(8,128)(2,1)S(1)}, bf16[1,128,512]{2,1,0:T(8,128)(2,1)S(1)}, u32[]{:S(2)}, u32[]{:S(2)}) collective-permute-start(bf16[1,128,512]{2,1,0:T(8,128)(2,1)S(1)} %collective-permute-done.2.refs_0_), channel_id=1, source_target_pairs={{0,16},{16,0},{1,17},{17,1},{2,18},{18,2},{3,19},{19,3},{4,20},{20... | collective-permute-start | bytes 393224 | tf_op jit(solution)/shard_map/ppermute | solution.py:348
  28.1 3.6 %collective-permute-done.1.refs_2_ = bf16[64,2560]{1,0:T(8,128)(2,1)S(1)} collective-permute-done((bf16[64,2560]{1,0:T(8,128)(2,1)S(1)}, bf16[64,2560]{1,0:T(8,128)(2,1)S(1)}, u32[]{:S(2)}, u32[]{:S(2)}) %collective-permute-start.1) | collective-permute-done | bytes 327712 | tf_op jit(solution)/shard_map/ppermute | solution.py:348
  31.8 0.0 collective-permute-done.refs_1_
  31.8 0.0 collective-permute-done.6.refs_5_
  31.8 0.5 %down.1.low_ref = f32[256,128]{1,0:T(8,128)S(1)} custom-call(s32[1]{0:T(128)} %bitcast.2.group_ref, bf16[1,2560,128]{2,1,0:T(8,128)(2,1)S(1)} %get-tuple-element.57.down_ref, bf16[64,2560]{1,0:T(8,128)(2,1)S(1)} %get-tuple-element.58.refs_0_, bf16[64,2560]{1,0:T(8,128)(2,1)S(1)} %collective-permute-done.refs_1_, ...), custom_call_target="tpu_custom_call" | custom-call | flops 335544320 | bytes 1966080 | tf_op jit(solution)/shard_map/down/pallas_call | solution.py:442
  32.3 0.1 collective-permute-start.7
  32.4 0.1 collective-permute-done.8.refs_1_
  32.5 1.2 %collective-permute-done.7.other_ref = f32[256,128]{1,0:T(8,128)S(1)} collective-permute-done((f32[256,128]{1,0:T(8,128)S(1)}, f32[256,128]{1,0:T(8,128)S(1)}, u32[]{:S(2)}, u32[]{:S(2)}) %collective-permute-start.7) | collective-permute-done | bytes 131104 | tf_op jit(solution)/shard_map/ppermute | solution.py:348
  33.7 0.8 %up.1 = (s16[64,1024]{1,0:T(8,128)(2,1)S(1)}, s16[64,1024]{1,0:T(8,128)(2,1)S(1)}, s16[64,1024]{1,0:T(8,128)(2,1)S(1)}, s16[64,1024]{1,0:T(8,128)(2,1)S(1)}) custom-call(s32[1]{0:T(128)} %bitcast.2.group_ref, f32[256,128]{1,0:T(8,128)S(1)} %down.1.low_ref, f32[256,128]{1,0:T(8,128)S(1)} %collective-permute-done.7.other_ref, ...), custom_call_target="tpu_custom_call" | custom-call | flops 268435456 | bytes 524288 | tf_op jit(solution)/shard_map/up/pallas_call | solution.py:453
  34.5 1.9 %collective-permute-start.10 = (s16[64,1024]{1,0:T(8,128)(2,1)S(1)}, s16[64,1024]{1,0:T(8,128)(2,1)S(1)}, u32[]{:S(2)}, u32[]{:S(2)}) collective-permute-start(s16[64,1024]{1,0:T(8,128)(2,1)S(1)} %get-tuple-element.71), channel_id=1, source_target_pairs={{0,6},{2,4},{4,2},{6,0},{8,14},{10,12},{12,10},{14,8},{1,7},{3,5},... | collective-permute-start | bytes 393224 | tf_op jit(solution)/shard_map/ppermute | solution.py:348
  36.4 0.3 collective-permute-start.11
  36.7 1.4 %collective-permute-start.9 = (s16[64,1024]{1,0:T(8,128)(2,1)S(1)}, s16[64,1024]{1,0:T(8,128)(2,1)S(1)}, u32[]{:S(2)}, u32[]{:S(2)}) collective-permute-start(s16[64,1024]{1,0:T(8,128)(2,1)S(1)} %get-tuple-element.70), channel_id=1, source_target_pairs={{0,2},{2,0},{4,6},{6,4},{8,10},{10,8},{12,14},{14,12},{1,3},{3,1},... | collective-permute-start | bytes 393224 | tf_op jit(solution)/shard_map/ppermute | solution.py:348
  38.0 0.0 copy-done.1
  38.1 0.0 collective-permute-done.5.other_ref
  38.1 0.0 copy-done
  38.1 0.5 %start_rows.1 = (f32[128,1024]{1,0:T(8,128)S(1)}, bf16[128,192]{1,0:T(8,128)(2,1)S(1)}) custom-call(s32[1]{0:T(128)} %bitcast.me_ref, s32[1,128]{1,0:T(1,128)S(1)} %bitcast.9, f32[128,1024]{1,0:T(8,128)S(1)} %get-tuple-element.55.mine_ref, f32[128,1024]{1,0:T(8,128)S(1)} %collective-permute-done.5.other_ref, s16[64,1024]{1,0:T(8,128)(2,1)S(1)} %get-tuple-element.65.own_ref), custom_call_target="tpu_custom_call" | custom-call | flops 33554432 | bytes 1572864 | tf_op jit(solution)/shard_map/start_rows/pallas_call | solution.py:466
  38.6 3.2 %collective-permute-done.10.refs_1_ = s16[64,1024]{1,0:T(8,128)(2,1)S(1)} collective-permute-done((s16[64,1024]{1,0:T(8,128)(2,1)S(1)}, s16[64,1024]{1,0:T(8,128)(2,1)S(1)}, u32[]{:S(2)}, u32[]{:S(2)}) %collective-permute-start.10) | collective-permute-done | bytes 131104 | tf_op jit(solution)/shard_map/ppermute | solution.py:348
  41.8 1.1 %collective-permute-done.11.refs_2_ = s16[64,1024]{1,0:T(8,128)(2,1)S(1)} collective-permute-done((s16[64,1024]{1,0:T(8,128)(2,1)S(1)}, s16[64,1024]{1,0:T(8,128)(2,1)S(1)}, u32[]{:S(2)}, u32[]{:S(2)}) %collective-permute-start.11) | collective-permute-done | bytes 131104 | tf_op jit(solution)/shard_map/ppermute | solution.py:348
  42.9 0.9 %collective-permute-done.9.refs_0_ = s16[64,1024]{1,0:T(8,128)(2,1)S(1)} collective-permute-done((s16[64,1024]{1,0:T(8,128)(2,1)S(1)}, s16[64,1024]{1,0:T(8,128)(2,1)S(1)}, u32[]{:S(2)}, u32[]{:S(2)}) %collective-permute-start.9) | collective-permute-done | bytes 131104 | tf_op jit(solution)/shard_map/ppermute | solution.py:348
  43.8 1.3 %finish.1 = bf16[1024,128]{1,0:T(8,128)(2,1)} custom-call(f32[128,1024]{1,0:T(8,128)S(1)} %get-tuple-element.66.partial_ref, bf16[128,192]{1,0:T(8,128)(2,1)S(1)} %get-tuple-element.67.picker_ref, f32[128,128]{1,0:T(8,128)S(1)} %get-tuple-element.68.cos_ref, f32[128,128]{1,0:T(8,128)S(1)} %get-tuple-element.69.sin_ref, ...), custom_call_target="tpu_custom_call" | custom-call | flops 134217728 | bytes 524288 | tf_op jit(solution)/shard_map/finish/pallas_call | solution.py:478
  (2 shorter events, 0.0 us)
Async XLA Ops:
  0.0 38.1 %copy-start = (s32[128,1]{0,1:T(1,128)S(1)}, s32[128,1]{0,1:T(1,128)}, u32[]{:S(2)}) copy-start(s32[128,1]{0,1:T(1,128)} %param.9) | copy-start | bytes 1540
  0.0 38.0 %copy-start.1 = (bf16[128]{0:T(256)(128)(2,1)S(1)}, bf16[128]{0:T(256)(128)(2,1)}, u32[]{:S(2)}) copy-start(bf16[128]{0:T(256)(128)(2,1)} %param.15) | copy-start | bytes 772
  1.8 20.5 %collective-permute-start.4 = (bf16[1,1280,128]{2,1,0:T(8,128)(2,1)S(1)}, bf16[1,1280,128]{2,1,0:T(8,128)(2,1)S(1)}, u32[]{:S(2)}, u32[]{:S(2)}) collective-permute-start(bf16[1,1280,128]{2,1,0:T(8,128)(2,1)S(1)} %get-tuple-element.50), channel_id=1, source_target_pairs={{0,8},{2,10},{4,12},{6,14},{8,0},{10,2},{12,4},{14,6},{1,9},{3,11}... | collective-permute-start | bytes 983048 | tf_op jit(solution)/shard_map/ppermute | solution.py:348
  5.9 25.9 %collective-permute-start = (bf16[64,2560]{1,0:T(8,128)(2,1)S(1)}, bf16[64,2560]{1,0:T(8,128)(2,1)S(1)}, u32[]{:S(2)}, u32[]{:S(2)}) collective-permute-start(bf16[64,2560]{1,0:T(8,128)(2,1)S(1)} %get-tuple-element.40), channel_id=1, source_target_pairs={{0,6},{2,4},{4,2},{6,0},{8,14},{10,12},{12,10},{14,8},{1,7},{3,5},... | collective-permute-start | bytes 983048 | tf_op jit(solution)/shard_map/ppermute | solution.py:348
  10.0 16.4 %collective-permute-start.2 = (bf16[1,128,512]{2,1,0:T(8,128)(2,1)S(1)}, bf16[1,128,512]{2,1,0:T(8,128)(2,1)S(1)}, u32[]{:S(2)}, u32[]{:S(2)}) collective-permute-start(bf16[1,128,512]{2,1,0:T(8,128)(2,1)S(1)} %get-tuple-element.45), channel_id=1, source_target_pairs={{0,8},{2,10},{4,12},{6,14},{8,0},{10,2},{12,4},{14,6},{1,9},{3,11}... | collective-permute-start | bytes 393224 | tf_op jit(solution)/shard_map/ppermute | solution.py:348
  10.4 16.0 %collective-permute-start.3 = (bf16[64,2560]{1,0:T(8,128)(2,1)S(1)}, bf16[64,2560]{1,0:T(8,128)(2,1)S(1)}, u32[]{:S(2)}, u32[]{:S(2)}) collective-permute-start(bf16[64,2560]{1,0:T(8,128)(2,1)S(1)} %get-tuple-element.47), channel_id=1, source_target_pairs={{0,2},{2,0},{4,6},{6,4},{8,10},{10,8},{12,14},{14,12},{1,3},{3,1},... | collective-permute-start | bytes 983048 | tf_op jit(solution)/shard_map/ppermute | solution.py:348
  10.9 20.8 %collective-permute-start.1 = (bf16[64,2560]{1,0:T(8,128)(2,1)S(1)}, bf16[64,2560]{1,0:T(8,128)(2,1)S(1)}, u32[]{:S(2)}, u32[]{:S(2)}) collective-permute-start(bf16[64,2560]{1,0:T(8,128)(2,1)S(1)} %get-tuple-element.46), channel_id=1, source_target_pairs={{0,4},{2,6},{4,0},{6,2},{8,12},{10,14},{12,8},{14,10},{1,5},{3,7},... | collective-permute-start | bytes 983048 | tf_op jit(solution)/shard_map/ppermute | solution.py:348
  22.3 9.4 %collective-permute-start.6 = (bf16[1,1280,128]{2,1,0:T(8,128)(2,1)S(1)}, bf16[1,1280,128]{2,1,0:T(8,128)(2,1)S(1)}, u32[]{:S(2)}, u32[]{:S(2)}) collective-permute-start(bf16[1,1280,128]{2,1,0:T(8,128)(2,1)S(1)} %collective-permute-done.4.refs_4_), channel_id=1, source_target_pairs={{0,16},{16,0},{1,17},{17,1},{2,18},{18,2},{3,19},{19,3},{4,20},{20... | collective-permute-start | bytes 983048 | tf_op jit(solution)/shard_map/ppermute | solution.py:348
  26.4 11.7 %collective-permute-start.5 = (f32[128,1024]{1,0:T(8,128)S(1)}, f32[128,1024]{1,0:T(8,128)S(1)}, u32[]{:S(2)}, u32[]{:S(2)}) collective-permute-start(f32[128,1024]{1,0:T(8,128)S(1)} %get-tuple-element.56), channel_id=1, source_target_pairs={{0,1},{1,0},{2,3},{3,2},{4,5},{5,4},{6,7},{7,6},{8,9},{9,8},{10,11... | collective-permute-start | bytes 1572872 | tf_op jit(solution)/shard_map/ppermute | solution.py:348
  26.5 6.0 %collective-permute-start.8 = (bf16[1,128,512]{2,1,0:T(8,128)(2,1)S(1)}, bf16[1,128,512]{2,1,0:T(8,128)(2,1)S(1)}, u32[]{:S(2)}, u32[]{:S(2)}) collective-permute-start(bf16[1,128,512]{2,1,0:T(8,128)(2,1)S(1)} %collective-permute-done.2.refs_0_), channel_id=1, source_target_pairs={{0,16},{16,0},{1,17},{17,1},{2,18},{18,2},{3,19},{19,3},{4,20},{20... | collective-permute-start | bytes 393224 | tf_op jit(solution)/shard_map/ppermute | solution.py:348
  32.3 1.4 %collective-permute-start.7 = (f32[256,128]{1,0:T(8,128)S(1)}, f32[256,128]{1,0:T(8,128)S(1)}, u32[]{:S(2)}, u32[]{:S(2)}) collective-permute-start(f32[256,128]{1,0:T(8,128)S(1)} %down.1.low_ref), channel_id=1, source_target_pairs={{0,1},{1,0},{2,3},{3,2},{4,5},{5,4},{6,7},{7,6},{8,9},{9,8},{10,11... | collective-permute-start | bytes 393224 | tf_op jit(solution)/shard_map/ppermute | solution.py:348
  34.5 7.3 %collective-permute-start.10 = (s16[64,1024]{1,0:T(8,128)(2,1)S(1)}, s16[64,1024]{1,0:T(8,128)(2,1)S(1)}, u32[]{:S(2)}, u32[]{:S(2)}) collective-permute-start(s16[64,1024]{1,0:T(8,128)(2,1)S(1)} %get-tuple-element.71), channel_id=1, source_target_pairs={{0,6},{2,4},{4,2},{6,0},{8,14},{10,12},{12,10},{14,8},{1,7},{3,5},... | collective-permute-start | bytes 393224 | tf_op jit(solution)/shard_map/ppermute | solution.py:348
  36.4 6.5 %collective-permute-start.11 = (s16[64,1024]{1,0:T(8,128)(2,1)S(1)}, s16[64,1024]{1,0:T(8,128)(2,1)S(1)}, u32[]{:S(2)}, u32[]{:S(2)}) collective-permute-start(s16[64,1024]{1,0:T(8,128)(2,1)S(1)} %get-tuple-element.72), channel_id=1, source_target_pairs={{0,4},{2,6},{4,0},{6,2},{8,12},{10,14},{12,8},{14,10},{1,5},{3,7},... | collective-permute-start | bytes 393224 | tf_op jit(solution)/shard_map/ppermute | solution.py:348
  36.7 7.1 %collective-permute-start.9 = (s16[64,1024]{1,0:T(8,128)(2,1)S(1)}, s16[64,1024]{1,0:T(8,128)(2,1)S(1)}, u32[]{:S(2)}, u32[]{:S(2)}) collective-permute-start(s16[64,1024]{1,0:T(8,128)(2,1)S(1)} %get-tuple-element.70), channel_id=1, source_target_pairs={{0,2},{2,0},{4,6},{6,4},{8,10},{10,8},{12,14},{14,12},{1,3},{3,1},... | collective-permute-start | bytes 393224 | tf_op jit(solution)/shard_map/ppermute | solution.py:348

commit v20 on v18

--- a/solution.py
+++ b/solution.py
@@ -88,13 +88,19 @@
         out_ref[a] = (own_ref[a].astype(jnp.float32) * factor((rank, 1), 0)).astype(jnp.bfloat16)
 
 
+def down_share_kernel(group_ref, down_hbm, out_ref, sem):
+    share = out_ref.shape[1]
+    at = pl.multiple_of(group_ref[0] * share, share)
+    copy = pltpu.make_async_copy(down_hbm.at[:, pl.ds(at, share), :], out_ref, sem)
+    copy.start()
+    copy.wait()
+
+
 def pick_kernel(
-    pool, local, depth, me_ref, group_ref, adapter_hbm, tokens_hbm, down_hbm, *refs
+    pool, local, depth, me_ref, adapter_hbm, tokens_hbm, *refs
 ):
-    share_ref, outs = refs[0], refs[1:-4]
-    adapter_ref, tokens_ref, share_sem, sems = refs[-4:]
+    outs, (adapter_ref, tokens_ref, sems) = refs[:-3], refs[-3:]
     rows, width = tokens_ref.shape
-    share = share_ref.shape[1]
     parts = sems.shape[0] - 1
     part = rows // parts
     adapter_copy = pltpu.make_async_copy(adapter_hbm, adapter_ref, sems.at[parts])
@@ -109,9 +115,6 @@
     ]
     for copy in copies:
         copy.start()
-    at = pl.multiple_of(group_ref[0] * share, share)
-    share_copy = pltpu.make_async_copy(down_hbm.at[:, pl.ds(at, share), :], share_ref, share_sem)
-    share_copy.start()
     adapter_copy.wait()
     place = slot_places(adapter_ref[...], me_ref[0], pool, local, depth)
     size = outs[0].shape[0]
@@ -126,7 +129,6 @@
         )
         for j, out in enumerate(outs):
             out[:, at : at + step] = block[j * size : (j + 1) * size].astype(jnp.bfloat16)
-    share_copy.wait()
 
 
 def base_kernel(
@@ -353,22 +355,31 @@
     adapter_row = row_adapters.reshape(1, rows)
     down_share = width // groups
     parts = rows // 16
-    down_part, *picked = pl.pallas_call(
+    down_part = pl.pallas_call(
+        down_share_kernel,
+        in_specs=[SMEM, HBM],
+        out_specs=VMEM,
+        out_shape=jax.ShapeDtypeStruct((local, down_share, rank), bf16),
+        scratch_shapes=[pltpu.SemaphoreType.DMA],
+        compiler_params=params(),
+        cost_estimate=cost(0, 4 * local * rank * down_share),
+        name="down_share",
+    )(group, in_hbm(adapter_down))
+    tokens_now, _ = lax.optimization_barrier((tokens, down_part))
+    picked = pl.pallas_call(
         functools.partial(pick_kernel, pool, local, depth),
-        in_specs=[SMEM] * 2 + [HBM] * 3,
-        out_specs=[VMEM] * (1 + buffers),
-        out_shape=[jax.ShapeDtypeStruct((local, down_share, rank), bf16)]
-        + [jax.ShapeDtypeStruct((size, width), bf16)] * buffers,
+        in_specs=[SMEM] + [HBM] * 2,
+        out_specs=[VMEM] * buffers,
+        out_shape=[jax.ShapeDtypeStruct((size, width), bf16)] * buffers,
         scratch_shapes=[
             pltpu.VMEM((1, rows), jnp.int32),
             pltpu.VMEM((rows, width), bf16),
-            pltpu.SemaphoreType.DMA,
             pltpu.SemaphoreType.DMA((parts + 1,)),
         ],
         compiler_params=params(),
         cost_estimate=cost(2 * buffers * size * rows * width, 2 * (rows + buffers * size) * width),
         name="pick",
-    )(me, group, in_hbm(adapter_row), in_hbm(tokens), in_hbm(adapter_down))
+    )(me, in_hbm(adapter_row), in_hbm(tokens_now))
     far_down = exchange(down_part, "pool", pool, pool // 2)
     up_share = columns // groups
     ranks_now, adapter_up_now, _ = lax.optimization_barrier((ranks, adapter_up, picked))

time: 45.3 us -> 46.3 us (1.022)
  Pallas kernels: 11.5 us -> 12.4 us
    pallas_call x0 -> x1, Pallas kernels: none -> 1.01 us  [body(): pl.pallas_call(down_share_kernel, in_specs=[SMEM, HBM], out_specs=VMEM, o...]
  transfers between devices with their start and end apart: 12 -> 12, of which waited for: 8 -> 8; matrix products, arithmetic and copies ran while one was open for 2% -> 2% of each run, Pallas kernels for 19% -> 22%
where the time goes in v20:
time: 46.3 us; the launch traced here: 46.1 us
  waiting for transfers between devices  16.7 us (36%)
  starting transfers between devices  15.1 us (33%)
  Pallas kernels  12.4 us (27%)
  other arithmetic  1.08 us (2%)
  between operations  0.77 us (2%)
    ppermute x12, waiting for transfers between devices, exchange(): return lax.ppermute(x, axis, [(p, p ^ j) for p in range(count)])  16.7 us
    ppermute x12, starting transfers between devices, exchange(): return lax.ppermute(x, axis, [(p, p ^ j) for p in range(count)])  15.1 us
    pallas_call x1, Pallas kernels, body(): pl.pallas_call(base_kernel, in_specs=[SMEM] + [HBM] * 4, out_specs=[VMEM]...  5.63 us
    pallas_call x1, Pallas kernels, body(): pl.pallas_call(functools.partial(pick_kernel, pool, local, depth), in_spe...  1.74 us
    pallas_call x1, Pallas kernels, body(): pl.pallas_call(functools.partial(finish_kernel, buffers), in_specs=[VMEM]...  1.29 us
    pallas_call x1, Pallas kernels, body(): pl.pallas_call(down_share_kernel, in_specs=[SMEM, HBM], out_specs=VMEM, o...  1.01 us
    pallas_call x1, Pallas kernels, body(): pl.pallas_call(functools.partial(up_share_kernel, cores), in_specs=[SMEM]...  0.95 us
  transfers between devices with their start and end apart: 12, of which 8 were waited for; matrix products, arithmetic and copies ran while one was open for 2% of the time, Pallas kernels for 22%

profile of v20, /device:TPU:0, one launch (start us, length us, event | category | flops | bytes accessed | tf_op | source)
XLA Modules:
  0.0 46.1 jit_solution(1397553228512121674)
XLA Ops:
  0.0 0.0 copy-start
  0.0 0.0 copy-start.1
  0.0 1.0 %down_share.1 = bf16[1,1280,128]{2,1,0:T(8,128)(2,1)S(1)} custom-call(s32[1]{0:T(128)} %bitcast.2.group_ref, bf16[1,2560,128]{2,1,0:T(8,128)(2,1)} %down_hbm.3), custom_call_target="tpu_custom_call" | custom-call | bytes 655360 | tf_op jit(solution)/shard_map/down_share/pallas_call | solution.py:358
  1.0 4.1 %collective-permute-start.1 = (bf16[1,1280,128]{2,1,0:T(8,128)(2,1)S(1)}, bf16[1,1280,128]{2,1,0:T(8,128)(2,1)S(1)}, u32[]{:S(2)}, u32[]{:S(2)}) collective-permute-start(bf16[1,1280,128]{2,1,0:T(8,128)(2,1)S(1)} %down_share.1), channel_id=1, source_target_pairs={{0,8},{2,10},{4,12},{6,14},{8,0},{10,2},{12,4},{14,6},{1,9},{3,11}... | collective-permute-start | bytes 983048 | tf_op jit(solution)/shard_map/ppermute | solution.py:350
  5.1 1.7 %pick.1 = (bf16[64,2560]{1,0:T(8,128)(2,1)S(1)}, bf16[64,2560]{1,0:T(8,128)(2,1)S(1)}, bf16[64,2560]{1,0:T(8,128)(2,1)S(1)}, bf16[64,2560]{1,0:T(8,128)(2,1)S(1)}) custom-call(s32[1]{0:T(128)} %bitcast.me_ref, s32[1,128]{1,0:T(1,128)} %bitcast.8, bf16[128,2560]{1,0:T(8,128)(2,1)} %tokens_hbm.2), custom_call_target="tpu_custom_call" | custom-call | flops 167772160 | bytes 1966080 | tf_op jit(solution)/shard_map/pick/pallas_call | solution.py:369
  6.9 2.6 %collective-permute-start.2 = (bf16[64,2560]{1,0:T(8,128)(2,1)S(1)}, bf16[64,2560]{1,0:T(8,128)(2,1)S(1)}, u32[]{:S(2)}, u32[]{:S(2)}) collective-permute-start(bf16[64,2560]{1,0:T(8,128)(2,1)S(1)} %get-tuple-element.42), channel_id=1, source_target_pairs={{0,6},{2,4},{4,2},{6,0},{8,14},{10,12},{12,10},{14,8},{1,7},{3,5},... | collective-permute-start | bytes 983048 | tf_op jit(solution)/shard_map/ppermute | solution.py:350
  10.1 0.9 %up_share.1 = (bf16[1,128,512]{2,1,0:T(8,128)(2,1)S(1)}, f32[1,128]{1,0:T(1,128)S(1)}) custom-call(s32[1]{0:T(128)} %bitcast.2.group_ref, s32[1]{0:T(128)} %bitcast.3.core_ref, s32[1]{0:T(128)S(6)} %copy.9.ranks_ref, bf16[1,128,2048]{2,1,0:T(8,128)(2,1)} %up_hbm.2), custom_call_target="tpu_custom_call" | custom-call | flops 65536 | bytes 262144 | tf_op jit(solution)/shard_map/up_share/pallas_call | solution.py:386
  11.1 0.4 collective-permute-start
  11.5 0.4 collective-permute-start.3
  11.9 0.2 collective-permute-start.4
  12.2 0.7 %convert_element_type.4 = f32[128]{0:T(128)S(1)} convert(s32[128]{0:T(128)} %param.10) | non-fusion elementwise | flops 128 | bytes 1024 | tf_op jit(solution)/shard_map/convert_element_type | solution.py:444
  12.8 5.6 %base.1 = (f32[128,1024]{1,0:T(8,128)S(1)}, f32[128,1024]{1,0:T(8,128)S(1)}, bf16[1,2560,128]{2,1,0:T(8,128)(2,1)S(1)}, bf16[1,128,1024]{2,1,0:T(8,128)(2,1)S(1)}) custom-call(s32[1]{0:T(128)} %bitcast.3.core_ref, bf16[128,2560]{1,0:T(8,128)(2,1)} %tokens_hbm.2, bf16[2560,2048]{1,0:T(8,128)(2,1)} %weight_hbm.1, bf16[1,2560,128]{2,1,0:T(8,128)(2,1)} %down_hbm.3, ...), custom_call_target="tpu_custom_call" | custom-call | flops 1342177280 | bytes 10485760 | tf_op jit(solution)/shard_map/base/pallas_call | solution.py:411
  18.5 3.1 %collective-permute-done.1.refs_4_ = bf16[1,1280,128]{2,1,0:T(8,128)(2,1)S(1)} collective-permute-done((bf16[1,1280,128]{2,1,0:T(8,128)(2,1)S(1)}, bf16[1,1280,128]{2,1,0:T(8,128)(2,1)S(1)}, u32[]{:S(2)}, u32[]{:S(2)}) %collective-permute-start.1) | collective-permute-done | bytes 327712 | tf_op jit(solution)/shard_map/ppermute | solution.py:350
  21.5 2.1 %collective-permute-start.6 = (bf16[1,1280,128]{2,1,0:T(8,128)(2,1)S(1)}, bf16[1,1280,128]{2,1,0:T(8,128)(2,1)S(1)}, u32[]{:S(2)}, u32[]{:S(2)}) collective-permute-start(bf16[1,1280,128]{2,1,0:T(8,128)(2,1)S(1)} %collective-permute-done.1.refs_4_), channel_id=1, source_target_pairs={{0,16},{16,0},{1,17},{17,1},{2,18},{18,2},{3,19},{19,3},{4,20},{20... | collective-permute-start | bytes 983048 | tf_op jit(solution)/shard_map/ppermute | solution.py:350
  23.7 0.3 fusion
  24.0 1.6 %collective-permute-done.refs_0_ = bf16[1,128,512]{2,1,0:T(8,128)(2,1)S(1)} collective-permute-done((bf16[1,128,512]{2,1,0:T(8,128)(2,1)S(1)}, bf16[1,128,512]{2,1,0:T(8,128)(2,1)S(1)}, u32[]{:S(2)}, u32[]{:S(2)}) %collective-permute-start) | collective-permute-done | bytes 131104 | tf_op jit(solution)/shard_map/ppermute | solution.py:350
  25.6 1.6 %collective-permute-done.2.refs_1_ = bf16[64,2560]{1,0:T(8,128)(2,1)S(1)} collective-permute-done((bf16[64,2560]{1,0:T(8,128)(2,1)S(1)}, bf16[64,2560]{1,0:T(8,128)(2,1)S(1)}, u32[]{:S(2)}, u32[]{:S(2)}) %collective-permute-start.2) | collective-permute-done | bytes 327712 | tf_op jit(solution)/shard_map/ppermute | solution.py:350
  27.2 0.0 collective-permute-start.5
  27.2 0.1 pad_maximum_fusion
  27.3 1.6 %collective-permute-start.8 = (bf16[1,128,512]{2,1,0:T(8,128)(2,1)S(1)}, bf16[1,128,512]{2,1,0:T(8,128)(2,1)S(1)}, u32[]{:S(2)}, u32[]{:S(2)}) collective-permute-start(bf16[1,128,512]{2,1,0:T(8,128)(2,1)S(1)} %collective-permute-done.refs_0_), channel_id=1, source_target_pairs={{0,16},{16,0},{1,17},{17,1},{2,18},{18,2},{3,19},{19,3},{4,20},{20... | collective-permute-start | bytes 393224 | tf_op jit(solution)/shard_map/ppermute | solution.py:350
  28.9 3.9 %collective-permute-done.3.refs_2_ = bf16[64,2560]{1,0:T(8,128)(2,1)S(1)} collective-permute-done((bf16[64,2560]{1,0:T(8,128)(2,1)S(1)}, bf16[64,2560]{1,0:T(8,128)(2,1)S(1)}, u32[]{:S(2)}, u32[]{:S(2)}) %collective-permute-start.3) | collective-permute-done | bytes 327712 | tf_op jit(solution)/shard_map/ppermute | solution.py:350
  32.8 0.0 collective-permute-done.4.refs_3_
  32.8 0.0 collective-permute-done.6.refs_5_
  32.8 0.5 %down.1.low_ref = f32[256,128]{1,0:T(8,128)S(1)} custom-call(s32[1]{0:T(128)} %bitcast.2.group_ref, bf16[1,2560,128]{2,1,0:T(8,128)(2,1)S(1)} %get-tuple-element.56.down_ref, bf16[64,2560]{1,0:T(8,128)(2,1)S(1)} %get-tuple-element.57.refs_0_, bf16[64,2560]{1,0:T(8,128)(2,1)S(1)} %collective-permute-done.2.refs_1_, ...), custom_call_target="tpu_custom_call" | custom-call | flops 335544320 | bytes 1966080 | tf_op jit(solution)/shard_map/down/pallas_call | solution.py:453
  33.3 0.1 collective-permute-start.7
  33.4 0.0 collective-permute-done.8.refs_1_
  33.4 1.3 %collective-permute-done.7.other_ref = f32[256,128]{1,0:T(8,128)S(1)} collective-permute-done((f32[256,128]{1,0:T(8,128)S(1)}, f32[256,128]{1,0:T(8,128)S(1)}, u32[]{:S(2)}, u32[]{:S(2)}) %collective-permute-start.7) | collective-permute-done | bytes 131104 | tf_op jit(solution)/shard_map/ppermute | solution.py:350
  34.7 0.8 %up.1 = (s16[64,1024]{1,0:T(8,128)(2,1)S(1)}, s16[64,1024]{1,0:T(8,128)(2,1)S(1)}, s16[64,1024]{1,0:T(8,128)(2,1)S(1)}, s16[64,1024]{1,0:T(8,128)(2,1)S(1)}) custom-call(s32[1]{0:T(128)} %bitcast.2.group_ref, f32[256,128]{1,0:T(8,128)S(1)} %down.1.low_ref, f32[256,128]{1,0:T(8,128)S(1)} %collective-permute-done.7.other_ref, ...), custom_call_target="tpu_custom_call" | custom-call | flops 268435456 | bytes 524288 | tf_op jit(solution)/shard_map/up/pallas_call | solution.py:464
  35.5 0.2 collective-permute-start.10
  35.6 1.9 %collective-permute-start.11 = (s16[64,1024]{1,0:T(8,128)(2,1)S(1)}, s16[64,1024]{1,0:T(8,128)(2,1)S(1)}, u32[]{:S(2)}, u32[]{:S(2)}) collective-permute-start(s16[64,1024]{1,0:T(8,128)(2,1)S(1)} %get-tuple-element.70), channel_id=1, source_target_pairs={{0,4},{2,6},{4,0},{6,2},{8,12},{10,14},{12,8},{14,10},{1,5},{3,7},... | collective-permute-start | bytes 393224 | tf_op jit(solution)/shard_map/ppermute | solution.py:350
  37.6 1.5 %collective-permute-start.9 = (s16[64,1024]{1,0:T(8,128)(2,1)S(1)}, s16[64,1024]{1,0:T(8,128)(2,1)S(1)}, u32[]{:S(2)}, u32[]{:S(2)}) collective-permute-start(s16[64,1024]{1,0:T(8,128)(2,1)S(1)} %get-tuple-element.68), channel_id=1, source_target_pairs={{0,2},{2,0},{4,6},{6,4},{8,10},{10,8},{12,14},{14,12},{1,3},{3,1},... | collective-permute-start | bytes 393224 | tf_op jit(solution)/shard_map/ppermute | solution.py:350
  39.0 0.0 copy-done.1
  39.0 0.0 collective-permute-done.5.other_ref
  39.0 0.0 copy-done
  39.1 0.5 %start_rows.1 = (f32[128,1024]{1,0:T(8,128)S(1)}, bf16[128,192]{1,0:T(8,128)(2,1)S(1)}) custom-call(s32[1]{0:T(128)} %bitcast.me_ref, s32[1,128]{1,0:T(1,128)S(1)} %bitcast.9, f32[128,1024]{1,0:T(8,128)S(1)} %get-tuple-element.54.mine_ref, f32[128,1024]{1,0:T(8,128)S(1)} %collective-permute-done.5.other_ref, s16[64,1024]{1,0:T(8,128)(2,1)S(1)} %get-tuple-element.63.own_ref), custom_call_target="tpu_custom_call" | custom-call | flops 33554432 | bytes 1572864 | tf_op jit(solution)/shard_map/start_rows/pallas_call | solution.py:477
  39.6 3.2 %collective-permute-done.10.refs_1_ = s16[64,1024]{1,0:T(8,128)(2,1)S(1)} collective-permute-done((s16[64,1024]{1,0:T(8,128)(2,1)S(1)}, s16[64,1024]{1,0:T(8,128)(2,1)S(1)}, u32[]{:S(2)}, u32[]{:S(2)}) %collective-permute-start.10) | collective-permute-done | bytes 131104 | tf_op jit(solution)/shard_map/ppermute | solution.py:350
  42.8 1.1 %collective-permute-done.11.refs_2_ = s16[64,1024]{1,0:T(8,128)(2,1)S(1)} collective-permute-done((s16[64,1024]{1,0:T(8,128)(2,1)S(1)}, s16[64,1024]{1,0:T(8,128)(2,1)S(1)}, u32[]{:S(2)}, u32[]{:S(2)}) %collective-permute-start.11) | collective-permute-done | bytes 131104 | tf_op jit(solution)/shard_map/ppermute | solution.py:350
  43.9 0.9 %collective-permute-done.9.refs_0_ = s16[64,1024]{1,0:T(8,128)(2,1)S(1)} collective-permute-done((s16[64,1024]{1,0:T(8,128)(2,1)S(1)}, s16[64,1024]{1,0:T(8,128)(2,1)S(1)}, u32[]{:S(2)}, u32[]{:S(2)}) %collective-permute-start.9) | collective-permute-done | bytes 131104 | tf_op jit(solution)/shard_map/ppermute | solution.py:350
  44.8 1.3 %finish.1 = bf16[1024,128]{1,0:T(8,128)(2,1)} custom-call(f32[128,1024]{1,0:T(8,128)S(1)} %get-tuple-element.64.partial_ref, bf16[128,192]{1,0:T(8,128)(2,1)S(1)} %get-tuple-element.65.picker_ref, f32[128,128]{1,0:T(8,128)S(1)} %get-tuple-element.66.cos_ref, f32[128,128]{1,0:T(8,128)S(1)} %get-tuple-element.67.sin_ref, ...), custom_call_target="tpu_custom_call" | custom-call | flops 134217728 | bytes 524288 | tf_op jit(solution)/shard_map/finish/pallas_call | solution.py:489
  (2 shorter events, 0.0 us)
Async XLA Ops:
  0.0 39.1 %copy-start = (s32[128,1]{0,1:T(1,128)S(1)}, s32[128,1]{0,1:T(1,128)}, u32[]{:S(2)}) copy-start(s32[128,1]{0,1:T(1,128)} %param.9) | copy-start | bytes 1540
  0.0 39.0 %copy-start.1 = (bf16[128]{0:T(256)(128)(2,1)S(1)}, bf16[128]{0:T(256)(128)(2,1)}, u32[]{:S(2)}) copy-start(bf16[128]{0:T(256)(128)(2,1)} %param.15) | copy-start | bytes 772
  1.0 20.5 %collective-permute-start.1 = (bf16[1,1280,128]{2,1,0:T(8,128)(2,1)S(1)}, bf16[1,1280,128]{2,1,0:T(8,128)(2,1)S(1)}, u32[]{:S(2)}, u32[]{:S(2)}) collective-permute-start(bf16[1,1280,128]{2,1,0:T(8,128)(2,1)S(1)} %down_share.1), channel_id=1, source_target_pairs={{0,8},{2,10},{4,12},{6,14},{8,0},{10,2},{12,4},{14,6},{1,9},{3,11}... | collective-permute-start | bytes 983048 | tf_op jit(solution)/shard_map/ppermute | solution.py:350
  6.9 20.3 %collective-permute-start.2 = (bf16[64,2560]{1,0:T(8,128)(2,1)S(1)}, bf16[64,2560]{1,0:T(8,128)(2,1)S(1)}, u32[]{:S(2)}, u32[]{:S(2)}) collective-permute-start(bf16[64,2560]{1,0:T(8,128)(2,1)S(1)} %get-tuple-element.42), channel_id=1, source_target_pairs={{0,6},{2,4},{4,2},{6,0},{8,14},{10,12},{12,10},{14,8},{1,7},{3,5},... | collective-permute-start | bytes 983048 | tf_op jit(solution)/shard_map/ppermute | solution.py:350
  11.1 14.5 %collective-permute-start = (bf16[1,128,512]{2,1,0:T(8,128)(2,1)S(1)}, bf16[1,128,512]{2,1,0:T(8,128)(2,1)S(1)}, u32[]{:S(2)}, u32[]{:S(2)}) collective-permute-start(bf16[1,128,512]{2,1,0:T(8,128)(2,1)S(1)} %get-tuple-element.45), channel_id=1, source_target_pairs={{0,8},{2,10},{4,12},{6,14},{8,0},{10,2},{12,4},{14,6},{1,9},{3,11}... | collective-permute-start | bytes 393224 | tf_op jit(solution)/shard_map/ppermute | solution.py:350
  11.5 21.3 %collective-permute-start.3 = (bf16[64,2560]{1,0:T(8,128)(2,1)S(1)}, bf16[64,2560]{1,0:T(8,128)(2,1)S(1)}, u32[]{:S(2)}, u32[]{:S(2)}) collective-permute-start(bf16[64,2560]{1,0:T(8,128)(2,1)S(1)} %get-tuple-element.51), channel_id=1, source_target_pairs={{0,4},{2,6},{4,0},{6,2},{8,12},{10,14},{12,8},{14,10},{1,5},{3,7},... | collective-permute-start | bytes 983048 | tf_op jit(solution)/shard_map/ppermute | solution.py:350
  11.9 20.8 %collective-permute-start.4 = (bf16[64,2560]{1,0:T(8,128)(2,1)S(1)}, bf16[64,2560]{1,0:T(8,128)(2,1)S(1)}, u32[]{:S(2)}, u32[]{:S(2)}) collective-permute-start(bf16[64,2560]{1,0:T(8,128)(2,1)S(1)} %get-tuple-element.52), channel_id=1, source_target_pairs={{0,2},{2,0},{4,6},{6,4},{8,10},{10,8},{12,14},{14,12},{1,3},{3,1},... | collective-permute-start | bytes 983048 | tf_op jit(solution)/shard_map/ppermute | solution.py:350
  21.5 11.2 %collective-permute-start.6 = (bf16[1,1280,128]{2,1,0:T(8,128)(2,1)S(1)}, bf16[1,1280,128]{2,1,0:T(8,128)(2,1)S(1)}, u32[]{:S(2)}, u32[]{:S(2)}) collective-permute-start(bf16[1,1280,128]{2,1,0:T(8,128)(2,1)S(1)} %collective-permute-done.1.refs_4_), channel_id=1, source_target_pairs={{0,16},{16,0},{1,17},{17,1},{2,18},{18,2},{3,19},{19,3},{4,20},{20... | collective-permute-start | bytes 983048 | tf_op jit(solution)/shard_map/ppermute | solution.py:350
  27.2 11.9 %collective-permute-start.5 = (f32[128,1024]{1,0:T(8,128)S(1)}, f32[128,1024]{1,0:T(8,128)S(1)}, u32[]{:S(2)}, u32[]{:S(2)}) collective-permute-start(f32[128,1024]{1,0:T(8,128)S(1)} %get-tuple-element.55), channel_id=1, source_target_pairs={{0,1},{1,0},{2,3},{3,2},{4,5},{5,4},{6,7},{7,6},{8,9},{9,8},{10,11... | collective-permute-start | bytes 1572872 | tf_op jit(solution)/shard_map/ppermute | solution.py:350
  27.3 6.1 %collective-permute-start.8 = (bf16[1,128,512]{2,1,0:T(8,128)(2,1)S(1)}, bf16[1,128,512]{2,1,0:T(8,128)(2,1)S(1)}, u32[]{:S(2)}, u32[]{:S(2)}) collective-permute-start(bf16[1,128,512]{2,1,0:T(8,128)(2,1)S(1)} %collective-permute-done.refs_0_), channel_id=1, source_target_pairs={{0,16},{16,0},{1,17},{17,1},{2,18},{18,2},{3,19},{19,3},{4,20},{20... | collective-permute-start | bytes 393224 | tf_op jit(solution)/shard_map/ppermute | solution.py:350
  33.3 1.4 %collective-permute-start.7 = (f32[256,128]{1,0:T(8,128)S(1)}, f32[256,128]{1,0:T(8,128)S(1)}, u32[]{:S(2)}, u32[]{:S(2)}) collective-permute-start(f32[256,128]{1,0:T(8,128)S(1)} %down.1.low_ref), channel_id=1, source_target_pairs={{0,1},{1,0},{2,3},{3,2},{4,5},{5,4},{6,7},{7,6},{8,9},{9,8},{10,11... | collective-permute-start | bytes 393224 | tf_op jit(solution)/shard_map/ppermute | solution.py:350
  35.5 7.3 %collective-permute-start.10 = (s16[64,1024]{1,0:T(8,128)(2,1)S(1)}, s16[64,1024]{1,0:T(8,128)(2,1)S(1)}, u32[]{:S(2)}, u32[]{:S(2)}) collective-permute-start(s16[64,1024]{1,0:T(8,128)(2,1)S(1)} %get-tuple-element.69), channel_id=1, source_target_pairs={{0,6},{2,4},{4,2},{6,0},{8,14},{10,12},{12,10},{14,8},{1,7},{3,5},... | collective-permute-start | bytes 393224 | tf_op jit(solution)/shard_map/ppermute | solution.py:350
  35.6 8.3 %collective-permute-start.11 = (s16[64,1024]{1,0:T(8,128)(2,1)S(1)}, s16[64,1024]{1,0:T(8,128)(2,1)S(1)}, u32[]{:S(2)}, u32[]{:S(2)}) collective-permute-start(s16[64,1024]{1,0:T(8,128)(2,1)S(1)} %get-tuple-element.70), channel_id=1, source_target_pairs={{0,4},{2,6},{4,0},{6,2},{8,12},{10,14},{12,8},{14,10},{1,5},{3,7},... | collective-permute-start | bytes 393224 | tf_op jit(solution)/shard_map/ppermute | solution.py:350
  37.6 7.2 %collective-permute-start.9 = (s16[64,1024]{1,0:T(8,128)(2,1)S(1)}, s16[64,1024]{1,0:T(8,128)(2,1)S(1)}, u32[]{:S(2)}, u32[]{:S(2)}) collective-permute-start(s16[64,1024]{1,0:T(8,128)(2,1)S(1)} %get-tuple-element.68), channel_id=1, source_target_pairs={{0,2},{2,0},{4,6},{6,4},{8,10},{10,8},{12,14},{14,12},{1,3},{3,1},... | collective-permute-start | bytes 393224 | tf_op jit(solution)/shard_map/ppermute | solution.py:350

commit v21 on v18

--- a/solution.py
+++ b/solution.py
@@ -96,13 +96,13 @@
     rows, width = tokens_ref.shape
     share = share_ref.shape[1]
     parts = sems.shape[0] - 1
-    part = rows // parts
+    part = width // parts
     adapter_copy = pltpu.make_async_copy(adapter_hbm, adapter_ref, sems.at[parts])
     adapter_copy.start()
     copies = [
         pltpu.make_async_copy(
-            tokens_hbm.at[pl.ds(i * part, part), :],
-            tokens_ref.at[pl.ds(i * part, part), :],
+            tokens_hbm.at[:, pl.ds(i * part, part)],
+            tokens_ref.at[:, pl.ds(i * part, part)],
             sems.at[i],
         )
         for i in range(parts)
@@ -117,15 +117,12 @@
     size = outs[0].shape[0]
     slots = len(outs) * size
     picker = jnp.where(iota((slots, rows), 0) == place, 1.0, 0.0).astype(jnp.bfloat16)
-    for copy in copies:
+    for i, copy in enumerate(copies):
         copy.wait()
-    step = 512
-    for at in range(0, width, step):
-        block = jnp.dot(
-            picker, tokens_ref[:, at : at + step], preferred_element_type=jnp.float32
-        )
+        here = slice(i * part, (i + 1) * part)
+        block = jnp.dot(picker, tokens_ref[:, here], preferred_element_type=jnp.float32)
         for j, out in enumerate(outs):
-            out[:, at : at + step] = block[j * size : (j + 1) * size].astype(jnp.bfloat16)
+            out[:, here] = block[j * size : (j + 1) * size].astype(jnp.bfloat16)
     share_copy.wait()
 
 
@@ -352,7 +349,7 @@
 
     adapter_row = row_adapters.reshape(1, rows)
     down_share = width // groups
-    parts = rows // 16
+    parts = 10
     down_part, *picked = pl.pallas_call(
         functools.partial(pick_kernel, pool, local, depth),
         in_specs=[SMEM] * 2 + [HBM] * 3,

time: 45.3 us -> 46.5 us (1.026)
  Pallas kernels: 11.5 us -> 12.7 us
    pallas_call x1, Pallas kernels: 1.78 us -> 2.99 us  [body(): pl.pallas_call(functools.partial(pick_kernel, pool, local, depth), in_spe...]
  transfers between devices with their start and end apart: 12 -> 12, of which waited for: 8 -> 8; matrix products, arithmetic and copies ran while one was open for 2% -> 2% of each run, Pallas kernels for 19% -> 18%
where the time goes in v21:
time: 46.5 us; the launch traced here: 46.3 us
  waiting for transfers between devices  16.7 us (36%)
  starting transfers between devices  15.1 us (32%)
  Pallas kernels  12.7 us (27%)
  other arithmetic  1.08 us (2%)
  between operations  0.75 us (2%)
    ppermute x12, waiting for transfers between devices, exchange(): return lax.ppermute(x, axis, [(p, p ^ j) for p in range(count)])  16.7 us
    ppermute x12, starting transfers between devices, exchange(): return lax.ppermute(x, axis, [(p, p ^ j) for p in range(count)])  15.1 us
    pallas_call x1, Pallas kernels, body(): pl.pallas_call(base_kernel, in_specs=[SMEM] + [HBM] * 4, out_specs=[VMEM]...  5.63 us
    pallas_call x1, Pallas kernels, body(): pl.pallas_call(functools.partial(pick_kernel, pool, local, depth), in_spe...  2.99 us
    pallas_call x1, Pallas kernels, body(): pl.pallas_call(functools.partial(finish_kernel, buffers), in_specs=[VMEM]...  1.28 us
    pallas_call x1, Pallas kernels, body(): pl.pallas_call(functools.partial(up_share_kernel, cores), in_specs=[SMEM]...  0.95 us
  transfers between devices with their start and end apart: 12, of which 8 were waited for; matrix products, arithmetic and copies ran while one was open for 2% of the time, Pallas kernels for 18%

profile of v21, /device:TPU:0, one launch (start us, length us, event | category | flops | bytes accessed | tf_op | source)
XLA Modules:
  0.0 46.3 jit_solution(8514822744238137199)
XLA Ops:
  0.0 0.0 copy-start
  0.0 0.0 copy-start.1
  0.0 3.0 %pick.1 = (bf16[1,1280,128]{2,1,0:T(8,128)(2,1)S(1)}, bf16[64,2560]{1,0:T(8,128)(2,1)S(1)}, bf16[64,2560]{1,0:T(8,128)(2,1)S(1)}, bf16[64,2560]{1,0:T(8,128)(2,1)S(1)}, bf16[64,2560]{1,0:T(8,128)(2,1)S(1)}) custom-call(s32[1]{0:T(128)} %bitcast.me_ref, s32[1]{0:T(128)} %bitcast.2.group_ref, s32[1,128]{1,0:T(1,128)} %bitcast.8, bf16[128,2560]{1,0:T(8,128)(2,1)} %tokens_hbm.3, ...), custom_call_target="tpu_custom_call" | custom-call | flops 167772160 | bytes 1966080 | tf_op jit(solution)/shard_map/pick/pallas_call | solution.py:353
  3.0 4.1 %collective-permute-start.1 = (bf16[1,1280,128]{2,1,0:T(8,128)(2,1)S(1)}, bf16[1,1280,128]{2,1,0:T(8,128)(2,1)S(1)}, u32[]{:S(2)}, u32[]{:S(2)}) collective-permute-start(bf16[1,1280,128]{2,1,0:T(8,128)(2,1)S(1)} %get-tuple-element.45), channel_id=1, source_target_pairs={{0,8},{2,10},{4,12},{6,14},{8,0},{10,2},{12,4},{14,6},{1,9},{3,11}... | collective-permute-start | bytes 983048 | tf_op jit(solution)/shard_map/ppermute | solution.py:345
  7.1 2.5 %collective-permute-start.2 = (bf16[64,2560]{1,0:T(8,128)(2,1)S(1)}, bf16[64,2560]{1,0:T(8,128)(2,1)S(1)}, u32[]{:S(2)}, u32[]{:S(2)}) collective-permute-start(bf16[64,2560]{1,0:T(8,128)(2,1)S(1)} %get-tuple-element.41), channel_id=1, source_target_pairs={{0,6},{2,4},{4,2},{6,0},{8,14},{10,12},{12,10},{14,8},{1,7},{3,5},... | collective-permute-start | bytes 983048 | tf_op jit(solution)/shard_map/ppermute | solution.py:345
  10.3 0.9 %up_share.1 = (bf16[1,128,512]{2,1,0:T(8,128)(2,1)S(1)}, f32[1,128]{1,0:T(1,128)S(1)}) custom-call(s32[1]{0:T(128)} %bitcast.2.group_ref, s32[1]{0:T(128)} %bitcast.3.core_ref, s32[1]{0:T(128)S(6)} %copy.9.ranks_ref, bf16[1,128,2048]{2,1,0:T(8,128)(2,1)} %up_hbm.2), custom_call_target="tpu_custom_call" | custom-call | flops 65536 | bytes 262144 | tf_op jit(solution)/shard_map/up_share/pallas_call | solution.py:372
  11.2 0.4 collective-permute-start
  11.6 0.5 collective-permute-start.3
  12.1 0.2 collective-permute-start.4
  12.3 0.7 %convert_element_type.4 = f32[128]{0:T(128)S(1)} convert(s32[128]{0:T(128)} %param.10) | non-fusion elementwise | flops 128 | bytes 1024 | tf_op jit(solution)/shard_map/convert_element_type | solution.py:430
  13.0 5.6 %base.1 = (f32[128,1024]{1,0:T(8,128)S(1)}, f32[128,1024]{1,0:T(8,128)S(1)}, bf16[1,2560,128]{2,1,0:T(8,128)(2,1)S(1)}, bf16[1,128,1024]{2,1,0:T(8,128)(2,1)S(1)}) custom-call(s32[1]{0:T(128)} %bitcast.3.core_ref, bf16[128,2560]{1,0:T(8,128)(2,1)} %tokens_hbm.3, bf16[2560,2048]{1,0:T(8,128)(2,1)} %weight_hbm.1, bf16[1,2560,128]{2,1,0:T(8,128)(2,1)} %down_hbm.3, ...), custom_call_target="tpu_custom_call" | custom-call | flops 1342177280 | bytes 10485760 | tf_op jit(solution)/shard_map/base/pallas_call | solution.py:397
  18.7 4.9 %collective-permute-done.1.refs_4_ = bf16[1,1280,128]{2,1,0:T(8,128)(2,1)S(1)} collective-permute-done((bf16[1,1280,128]{2,1,0:T(8,128)(2,1)S(1)}, bf16[1,1280,128]{2,1,0:T(8,128)(2,1)S(1)}, u32[]{:S(2)}, u32[]{:S(2)}) %collective-permute-start.1) | collective-permute-done | bytes 327712 | tf_op jit(solution)/shard_map/ppermute | solution.py:345
  23.5 2.1 %collective-permute-start.6 = (bf16[1,1280,128]{2,1,0:T(8,128)(2,1)S(1)}, bf16[1,1280,128]{2,1,0:T(8,128)(2,1)S(1)}, u32[]{:S(2)}, u32[]{:S(2)}) collective-permute-start(bf16[1,1280,128]{2,1,0:T(8,128)(2,1)S(1)} %collective-permute-done.1.refs_4_), channel_id=1, source_target_pairs={{0,16},{16,0},{1,17},{17,1},{2,18},{18,2},{3,19},{19,3},{4,20},{20... | collective-permute-start | bytes 983048 | tf_op jit(solution)/shard_map/ppermute | solution.py:345
  25.7 0.3 fusion
  26.0 1.6 %collective-permute-done.refs_0_ = bf16[1,128,512]{2,1,0:T(8,128)(2,1)S(1)} collective-permute-done((bf16[1,128,512]{2,1,0:T(8,128)(2,1)S(1)}, bf16[1,128,512]{2,1,0:T(8,128)(2,1)S(1)}, u32[]{:S(2)}, u32[]{:S(2)}) %collective-permute-start) | collective-permute-done | bytes 131104 | tf_op jit(solution)/shard_map/ppermute | solution.py:345
  27.6 0.0 collective-permute-done.2.refs_1_
  27.6 0.0 collective-permute-start.5
  27.6 0.1 pad_maximum_fusion
  27.7 1.6 %collective-permute-start.8 = (bf16[1,128,512]{2,1,0:T(8,128)(2,1)S(1)}, bf16[1,128,512]{2,1,0:T(8,128)(2,1)S(1)}, u32[]{:S(2)}, u32[]{:S(2)}) collective-permute-start(bf16[1,128,512]{2,1,0:T(8,128)(2,1)S(1)} %collective-permute-done.refs_0_), channel_id=1, source_target_pairs={{0,16},{16,0},{1,17},{17,1},{2,18},{18,2},{3,19},{19,3},{4,20},{20... | collective-permute-start | bytes 393224 | tf_op jit(solution)/shard_map/ppermute | solution.py:345
  29.3 3.6 %collective-permute-done.3.refs_2_ = bf16[64,2560]{1,0:T(8,128)(2,1)S(1)} collective-permute-done((bf16[64,2560]{1,0:T(8,128)(2,1)S(1)}, bf16[64,2560]{1,0:T(8,128)(2,1)S(1)}, u32[]{:S(2)}, u32[]{:S(2)}) %collective-permute-start.3) | collective-permute-done | bytes 327712 | tf_op jit(solution)/shard_map/ppermute | solution.py:345
  33.0 0.0 collective-permute-done.4.refs_3_
  33.0 0.0 collective-permute-done.6.refs_5_
  33.0 0.5 %down.1.low_ref = f32[256,128]{1,0:T(8,128)S(1)} custom-call(s32[1]{0:T(128)} %bitcast.2.group_ref, bf16[1,2560,128]{2,1,0:T(8,128)(2,1)S(1)} %get-tuple-element.56.down_ref, bf16[64,2560]{1,0:T(8,128)(2,1)S(1)} %get-tuple-element.57.refs_0_, bf16[64,2560]{1,0:T(8,128)(2,1)S(1)} %collective-permute-done.2.refs_1_, ...), custom_call_target="tpu_custom_call" | custom-call | flops 335544320 | bytes 1966080 | tf_op jit(solution)/shard_map/down/pallas_call | solution.py:439
  33.5 0.1 collective-permute-start.7
  33.6 0.1 collective-permute-done.8.refs_1_
  33.7 1.2 %collective-permute-done.7.other_ref = f32[256,128]{1,0:T(8,128)S(1)} collective-permute-done((f32[256,128]{1,0:T(8,128)S(1)}, f32[256,128]{1,0:T(8,128)S(1)}, u32[]{:S(2)}, u32[]{:S(2)}) %collective-permute-start.7) | collective-permute-done | bytes 131104 | tf_op jit(solution)/shard_map/ppermute | solution.py:345
  34.9 0.8 %up.1 = (s16[64,1024]{1,0:T(8,128)(2,1)S(1)}, s16[64,1024]{1,0:T(8,128)(2,1)S(1)}, s16[64,1024]{1,0:T(8,128)(2,1)S(1)}, s16[64,1024]{1,0:T(8,128)(2,1)S(1)}) custom-call(s32[1]{0:T(128)} %bitcast.2.group_ref, f32[256,128]{1,0:T(8,128)S(1)} %down.1.low_ref, f32[256,128]{1,0:T(8,128)S(1)} %collective-permute-done.7.other_ref, ...), custom_call_target="tpu_custom_call" | custom-call | flops 268435456 | bytes 524288 | tf_op jit(solution)/shard_map/up/pallas_call | solution.py:450
  35.7 1.9 %collective-permute-start.10 = (s16[64,1024]{1,0:T(8,128)(2,1)S(1)}, s16[64,1024]{1,0:T(8,128)(2,1)S(1)}, u32[]{:S(2)}, u32[]{:S(2)}) collective-permute-start(s16[64,1024]{1,0:T(8,128)(2,1)S(1)} %get-tuple-element.69), channel_id=1, source_target_pairs={{0,6},{2,4},{4,2},{6,0},{8,14},{10,12},{12,10},{14,8},{1,7},{3,5},... | collective-permute-start | bytes 393224 | tf_op jit(solution)/shard_map/ppermute | solution.py:345
  37.7 0.2 collective-permute-start.11
  37.9 1.4 %collective-permute-start.9 = (s16[64,1024]{1,0:T(8,128)(2,1)S(1)}, s16[64,1024]{1,0:T(8,128)(2,1)S(1)}, u32[]{:S(2)}, u32[]{:S(2)}) collective-permute-start(s16[64,1024]{1,0:T(8,128)(2,1)S(1)} %get-tuple-element.68), channel_id=1, source_target_pairs={{0,2},{2,0},{4,6},{6,4},{8,10},{10,8},{12,14},{14,12},{1,3},{3,1},... | collective-permute-start | bytes 393224 | tf_op jit(solution)/shard_map/ppermute | solution.py:345
  39.3 0.0 copy-done.1
  39.3 0.0 collective-permute-done.5.other_ref
  39.3 0.0 copy-done
  39.3 0.5 %start_rows.1 = (f32[128,1024]{1,0:T(8,128)S(1)}, bf16[128,192]{1,0:T(8,128)(2,1)S(1)}) custom-call(s32[1]{0:T(128)} %bitcast.me_ref, s32[1,128]{1,0:T(1,128)S(1)} %bitcast.9, f32[128,1024]{1,0:T(8,128)S(1)} %get-tuple-element.54.mine_ref, f32[128,1024]{1,0:T(8,128)S(1)} %collective-permute-done.5.other_ref, s16[64,1024]{1,0:T(8,128)(2,1)S(1)} %get-tuple-element.63.own_ref), custom_call_target="tpu_custom_call" | custom-call | flops 33554432 | bytes 1572864 | tf_op jit(solution)/shard_map/start_rows/pallas_call | solution.py:463
  39.8 3.2 %collective-permute-done.10.refs_1_ = s16[64,1024]{1,0:T(8,128)(2,1)S(1)} collective-permute-done((s16[64,1024]{1,0:T(8,128)(2,1)S(1)}, s16[64,1024]{1,0:T(8,128)(2,1)S(1)}, u32[]{:S(2)}, u32[]{:S(2)}) %collective-permute-start.10) | collective-permute-done | bytes 131104 | tf_op jit(solution)/shard_map/ppermute | solution.py:345
  43.0 1.1 %collective-permute-done.11.refs_2_ = s16[64,1024]{1,0:T(8,128)(2,1)S(1)} collective-permute-done((s16[64,1024]{1,0:T(8,128)(2,1)S(1)}, s16[64,1024]{1,0:T(8,128)(2,1)S(1)}, u32[]{:S(2)}, u32[]{:S(2)}) %collective-permute-start.11) | collective-permute-done | bytes 131104 | tf_op jit(solution)/shard_map/ppermute | solution.py:345
  44.1 0.9 %collective-permute-done.9.refs_0_ = s16[64,1024]{1,0:T(8,128)(2,1)S(1)} collective-permute-done((s16[64,1024]{1,0:T(8,128)(2,1)S(1)}, s16[64,1024]{1,0:T(8,128)(2,1)S(1)}, u32[]{:S(2)}, u32[]{:S(2)}) %collective-permute-start.9) | collective-permute-done | bytes 131104 | tf_op jit(solution)/shard_map/ppermute | solution.py:345
  45.0 1.3 %finish.1 = bf16[1024,128]{1,0:T(8,128)(2,1)} custom-call(f32[128,1024]{1,0:T(8,128)S(1)} %get-tuple-element.64.partial_ref, bf16[128,192]{1,0:T(8,128)(2,1)S(1)} %get-tuple-element.65.picker_ref, f32[128,128]{1,0:T(8,128)S(1)} %get-tuple-element.66.cos_ref, f32[128,128]{1,0:T(8,128)S(1)} %get-tuple-element.67.sin_ref, ...), custom_call_target="tpu_custom_call" | custom-call | flops 134217728 | bytes 524288 | tf_op jit(solution)/shard_map/finish/pallas_call | solution.py:475
  (2 shorter events, 0.0 us)
Async XLA Ops:
  0.0 39.3 %copy-start = (s32[128,1]{0,1:T(1,128)S(1)}, s32[128,1]{0,1:T(1,128)}, u32[]{:S(2)}) copy-start(s32[128,1]{0,1:T(1,128)} %param.9) | copy-start | bytes 1540
  0.0 39.3 %copy-start.1 = (bf16[128]{0:T(256)(128)(2,1)S(1)}, bf16[128]{0:T(256)(128)(2,1)}, u32[]{:S(2)}) copy-start(bf16[128]{0:T(256)(128)(2,1)} %param.15) | copy-start | bytes 772
  3.0 20.5 %collective-permute-start.1 = (bf16[1,1280,128]{2,1,0:T(8,128)(2,1)S(1)}, bf16[1,1280,128]{2,1,0:T(8,128)(2,1)S(1)}, u32[]{:S(2)}, u32[]{:S(2)}) collective-permute-start(bf16[1,1280,128]{2,1,0:T(8,128)(2,1)S(1)} %get-tuple-element.45), channel_id=1, source_target_pairs={{0,8},{2,10},{4,12},{6,14},{8,0},{10,2},{12,4},{14,6},{1,9},{3,11}... | collective-permute-start | bytes 983048 | tf_op jit(solution)/shard_map/ppermute | solution.py:345
  7.1 20.5 %collective-permute-start.2 = (bf16[64,2560]{1,0:T(8,128)(2,1)S(1)}, bf16[64,2560]{1,0:T(8,128)(2,1)S(1)}, u32[]{:S(2)}, u32[]{:S(2)}) collective-permute-start(bf16[64,2560]{1,0:T(8,128)(2,1)S(1)} %get-tuple-element.41), channel_id=1, source_target_pairs={{0,6},{2,4},{4,2},{6,0},{8,14},{10,12},{12,10},{14,8},{1,7},{3,5},... | collective-permute-start | bytes 983048 | tf_op jit(solution)/shard_map/ppermute | solution.py:345
  11.2 16.4 %collective-permute-start = (bf16[1,128,512]{2,1,0:T(8,128)(2,1)S(1)}, bf16[1,128,512]{2,1,0:T(8,128)(2,1)S(1)}, u32[]{:S(2)}, u32[]{:S(2)}) collective-permute-start(bf16[1,128,512]{2,1,0:T(8,128)(2,1)S(1)} %get-tuple-element.44), channel_id=1, source_target_pairs={{0,8},{2,10},{4,12},{6,14},{8,0},{10,2},{12,4},{14,6},{1,9},{3,11}... | collective-permute-start | bytes 393224 | tf_op jit(solution)/shard_map/ppermute | solution.py:345
  11.6 21.3 %collective-permute-start.3 = (bf16[64,2560]{1,0:T(8,128)(2,1)S(1)}, bf16[64,2560]{1,0:T(8,128)(2,1)S(1)}, u32[]{:S(2)}, u32[]{:S(2)}) collective-permute-start(bf16[64,2560]{1,0:T(8,128)(2,1)S(1)} %get-tuple-element.51), channel_id=1, source_target_pairs={{0,4},{2,6},{4,0},{6,2},{8,12},{10,14},{12,8},{14,10},{1,5},{3,7},... | collective-permute-start | bytes 983048 | tf_op jit(solution)/shard_map/ppermute | solution.py:345
  12.1 20.9 %collective-permute-start.4 = (bf16[64,2560]{1,0:T(8,128)(2,1)S(1)}, bf16[64,2560]{1,0:T(8,128)(2,1)S(1)}, u32[]{:S(2)}, u32[]{:S(2)}) collective-permute-start(bf16[64,2560]{1,0:T(8,128)(2,1)S(1)} %get-tuple-element.52), channel_id=1, source_target_pairs={{0,2},{2,0},{4,6},{6,4},{8,10},{10,8},{12,14},{14,12},{1,3},{3,1},... | collective-permute-start | bytes 983048 | tf_op jit(solution)/shard_map/ppermute | solution.py:345
  23.5 9.4 %collective-permute-start.6 = (bf16[1,1280,128]{2,1,0:T(8,128)(2,1)S(1)}, bf16[1,1280,128]{2,1,0:T(8,128)(2,1)S(1)}, u32[]{:S(2)}, u32[]{:S(2)}) collective-permute-start(bf16[1,1280,128]{2,1,0:T(8,128)(2,1)S(1)} %collective-permute-done.1.refs_4_), channel_id=1, source_target_pairs={{0,16},{16,0},{1,17},{17,1},{2,18},{18,2},{3,19},{19,3},{4,20},{20... | collective-permute-start | bytes 983048 | tf_op jit(solution)/shard_map/ppermute | solution.py:345
  27.6 11.7 %collective-permute-start.5 = (f32[128,1024]{1,0:T(8,128)S(1)}, f32[128,1024]{1,0:T(8,128)S(1)}, u32[]{:S(2)}, u32[]{:S(2)}) collective-permute-start(f32[128,1024]{1,0:T(8,128)S(1)} %get-tuple-element.55), channel_id=1, source_target_pairs={{0,1},{1,0},{2,3},{3,2},{4,5},{5,4},{6,7},{7,6},{8,9},{9,8},{10,11... | collective-permute-start | bytes 1572872 | tf_op jit(solution)/shard_map/ppermute | solution.py:345
  27.7 6.0 %collective-permute-start.8 = (bf16[1,128,512]{2,1,0:T(8,128)(2,1)S(1)}, bf16[1,128,512]{2,1,0:T(8,128)(2,1)S(1)}, u32[]{:S(2)}, u32[]{:S(2)}) collective-permute-start(bf16[1,128,512]{2,1,0:T(8,128)(2,1)S(1)} %collective-permute-done.refs_0_), channel_id=1, source_target_pairs={{0,16},{16,0},{1,17},{17,1},{2,18},{18,2},{3,19},{19,3},{4,20},{20... | collective-permute-start | bytes 393224 | tf_op jit(solution)/shard_map/ppermute | solution.py:345
  33.5 1.4 %collective-permute-start.7 = (f32[256,128]{1,0:T(8,128)S(1)}, f32[256,128]{1,0:T(8,128)S(1)}, u32[]{:S(2)}, u32[]{:S(2)}) collective-permute-start(f32[256,128]{1,0:T(8,128)S(1)} %down.1.low_ref), channel_id=1, source_target_pairs={{0,1},{1,0},{2,3},{3,2},{4,5},{5,4},{6,7},{7,6},{8,9},{9,8},{10,11... | collective-permute-start | bytes 393224 | tf_op jit(solution)/shard_map/ppermute | solution.py:345
  35.7 7.3 %collective-permute-start.10 = (s16[64,1024]{1,0:T(8,128)(2,1)S(1)}, s16[64,1024]{1,0:T(8,128)(2,1)S(1)}, u32[]{:S(2)}, u32[]{:S(2)}) collective-permute-start(s16[64,1024]{1,0:T(8,128)(2,1)S(1)} %get-tuple-element.69), channel_id=1, source_target_pairs={{0,6},{2,4},{4,2},{6,0},{8,14},{10,12},{12,10},{14,8},{1,7},{3,5},... | collective-permute-start | bytes 393224 | tf_op jit(solution)/shard_map/ppermute | solution.py:345
  37.7 6.5 %collective-permute-start.11 = (s16[64,1024]{1,0:T(8,128)(2,1)S(1)}, s16[64,1024]{1,0:T(8,128)(2,1)S(1)}, u32[]{:S(2)}, u32[]{:S(2)}) collective-permute-start(s16[64,1024]{1,0:T(8,128)(2,1)S(1)} %get-tuple-element.70), channel_id=1, source_target_pairs={{0,4},{2,6},{4,0},{6,2},{8,12},{10,14},{12,8},{14,10},{1,5},{3,7},... | collective-permute-start | bytes 393224 | tf_op jit(solution)/shard_map/ppermute | solution.py:345
  37.9 7.1 %collective-permute-start.9 = (s16[64,1024]{1,0:T(8,128)(2,1)S(1)}, s16[64,1024]{1,0:T(8,128)(2,1)S(1)}, u32[]{:S(2)}, u32[]{:S(2)}) collective-permute-start(s16[64,1024]{1,0:T(8,128)(2,1)S(1)} %get-tuple-element.68), channel_id=1, source_target_pairs={{0,2},{2,0},{4,6},{6,4},{8,10},{10,8},{12,14},{14,12},{1,3},{3,1},... | collective-permute-start | bytes 393224 | tf_op jit(solution)/shard_map/ppermute | solution.py:345

commit v22 on v18

--- a/solution.py
+++ b/solution.py
@@ -88,37 +88,32 @@
         out_ref[a] = (own_ref[a].astype(jnp.float32) * factor((rank, 1), 0)).astype(jnp.bfloat16)
 
 
-def pick_kernel(
-    pool, local, depth, me_ref, group_ref, adapter_hbm, tokens_hbm, down_hbm, *refs
-):
-    share_ref, outs = refs[0], refs[1:-4]
-    adapter_ref, tokens_ref, share_sem, sems = refs[-4:]
-    rows, width = tokens_ref.shape
+def fetch_kernel(group_ref, down_hbm, adapter_hbm, tokens_hbm, share_ref, adapter_ref, tokens_ref, sems):
     share = share_ref.shape[1]
-    parts = sems.shape[0] - 1
-    part = rows // parts
-    adapter_copy = pltpu.make_async_copy(adapter_hbm, adapter_ref, sems.at[parts])
-    adapter_copy.start()
+    at = pl.multiple_of(group_ref[0] * share, share)
     copies = [
-        pltpu.make_async_copy(
-            tokens_hbm.at[pl.ds(i * part, part), :],
-            tokens_ref.at[pl.ds(i * part, part), :],
-            sems.at[i],
+        pltpu.make_async_copy(down_hbm.at[:, pl.ds(at, share), :], share_ref, sems.at[0]),
+        pltpu.make_async_copy(adapter_hbm, adapter_ref, sems.at[1]),
+    ]
+    parts = sems.shape[0] - 2
+    part = tokens_ref.shape[0] // parts
+    for i in range(parts):
+        here = pl.ds(i * part, part)
+        copies.append(
+            pltpu.make_async_copy(tokens_hbm.at[here, :], tokens_ref.at[here, :], sems.at[2 + i])
         )
-        for i in range(parts)
-    ]
     for copy in copies:
         copy.start()
-    at = pl.multiple_of(group_ref[0] * share, share)
-    share_copy = pltpu.make_async_copy(down_hbm.at[:, pl.ds(at, share), :], share_ref, share_sem)
-    share_copy.start()
-    adapter_copy.wait()
+    for copy in copies:
+        copy.wait()
+
+
+def pick_kernel(pool, local, depth, me_ref, adapter_ref, tokens_ref, *outs):
+    rows, width = tokens_ref.shape
     place = slot_places(adapter_ref[...], me_ref[0], pool, local, depth)
     size = outs[0].shape[0]
     slots = len(outs) * size
     picker = jnp.where(iota((slots, rows), 0) == place, 1.0, 0.0).astype(jnp.bfloat16)
-    for copy in copies:
-        copy.wait()
     step = 512
     for at in range(0, width, step):
         block = jnp.dot(
@@ -126,7 +121,6 @@
         )
         for j, out in enumerate(outs):
             out[:, at : at + step] = block[j * size : (j + 1) * size].astype(jnp.bfloat16)
-    share_copy.wait()
 
 
 def base_kernel(
@@ -353,22 +347,29 @@
     adapter_row = row_adapters.reshape(1, rows)
     down_share = width // groups
     parts = rows // 16
-    down_part, *picked = pl.pallas_call(
+    down_part, adapter_now, tokens_now = pl.pallas_call(
+        fetch_kernel,
+        in_specs=[SMEM] + [HBM] * 3,
+        out_specs=[VMEM] * 3,
+        out_shape=[
+            jax.ShapeDtypeStruct((local, down_share, rank), bf16),
+            jax.ShapeDtypeStruct((1, rows), jnp.int32),
+            jax.ShapeDtypeStruct((rows, width), bf16),
+        ],
+        scratch_shapes=[pltpu.SemaphoreType.DMA((parts + 2,))],
+        compiler_params=params(),
+        cost_estimate=cost(0, 4 * (local * rank * down_share + rows * width)),
+        name="fetch",
+    )(group, in_hbm(adapter_down), in_hbm(adapter_row), in_hbm(tokens))
+    picked = pl.pallas_call(
         functools.partial(pick_kernel, pool, local, depth),
-        in_specs=[SMEM] * 2 + [HBM] * 3,
-        out_specs=[VMEM] * (1 + buffers),
-        out_shape=[jax.ShapeDtypeStruct((local, down_share, rank), bf16)]
-        + [jax.ShapeDtypeStruct((size, width), bf16)] * buffers,
-        scratch_shapes=[
-            pltpu.VMEM((1, rows), jnp.int32),
-            pltpu.VMEM((rows, width), bf16),
-            pltpu.SemaphoreType.DMA,
-            pltpu.SemaphoreType.DMA((parts + 1,)),
-        ],
+        in_specs=[SMEM] + [VMEM] * 2,
+        out_specs=[VMEM] * buffers,
+        out_shape=[jax.ShapeDtypeStruct((size, width), bf16)] * buffers,
         compiler_params=params(),
         cost_estimate=cost(2 * buffers * size * rows * width, 2 * (rows + buffers * size) * width),
         name="pick",
-    )(me, group, in_hbm(adapter_row), in_hbm(tokens), in_hbm(adapter_down))
+    )(me, adapter_now, tokens_now)
     far_down = exchange(down_part, "pool", pool, pool // 2)
     up_share = columns // groups
     ranks_now, adapter_up_now, _ = lax.optimization_barrier((ranks, adapter_up, picked))

time: 45.3 us -> 45.5 us (level)
    pallas_call x0 -> x1, Pallas kernels: none -> 1.33 us  [body(): pl.pallas_call(fetch_kernel, in_specs=[SMEM] + [HBM] * 3, out_specs=[VMEM...]
    pallas_call x1, Pallas kernels: 1.78 us -> 0.59 us  [body(): pl.pallas_call(functools.partial(pick_kernel, pool, local, depth), in_spe...]
  transfers between devices with their start and end apart: 12 -> 12, of which waited for: 8 -> 7; matrix products, arithmetic and copies ran while one was open for 2% -> 2% of each run, Pallas kernels for 19% -> 20%
where the time goes in v22:
time: 45.5 us; the launch traced here: 45.3 us
  waiting for transfers between devices  16.7 us (37%)
  starting transfers between devices  15.2 us (33%)
  Pallas kernels  11.6 us (25%)
  other arithmetic  1.08 us (2%)
  between operations  0.76 us (2%)
    ppermute x12, waiting for transfers between devices, exchange(): return lax.ppermute(x, axis, [(p, p ^ j) for p in range(count)])  16.7 us
    ppermute x12, starting transfers between devices, exchange(): return lax.ppermute(x, axis, [(p, p ^ j) for p in range(count)])  15.2 us
    pallas_call x1, Pallas kernels, body(): pl.pallas_call(base_kernel, in_specs=[SMEM] + [HBM] * 4, out_specs=[VMEM]...  5.63 us
    pallas_call x1, Pallas kernels, body(): pl.pallas_call(fetch_kernel, in_specs=[SMEM] + [HBM] * 3, out_specs=[VMEM...  1.33 us
    pallas_call x1, Pallas kernels, body(): pl.pallas_call(functools.partial(finish_kernel, buffers), in_specs=[VMEM]...  1.29 us
    pallas_call x1, Pallas kernels, body(): pl.pallas_call(functools.partial(up_share_kernel, cores), in_specs=[SMEM]...  0.95 us
  transfers between devices with their start and end apart: 12, of which 7 were waited for; matrix products, arithmetic and copies ran while one was open for 2% of the time, Pallas kernels for 20%

profile of v22, /device:TPU:0, one launch (start us, length us, event | category | flops | bytes accessed | tf_op | source)
XLA Modules:
  0.0 45.3 jit_solution(13291345333878761538)
XLA Ops:
  0.0 0.0 copy-start
  0.0 0.0 copy-start.1
  0.0 1.3 %fetch.1 = (bf16[1,1280,128]{2,1,0:T(8,128)(2,1)S(1)}, s32[1,128]{1,0:T(1,128)S(1)}, bf16[128,2560]{1,0:T(8,128)(2,1)S(1)}) custom-call(s32[1]{0:T(128)} %bitcast.2.group_ref, bf16[1,2560,128]{2,1,0:T(8,128)(2,1)} %down_hbm.3, s32[1,128]{1,0:T(1,128)} %bitcast.8, bf16[128,2560]{1,0:T(8,128)(2,1)} %tokens_hbm.3), custom_call_target="tpu_custom_call" | custom-call | bytes 1966080 | tf_op jit(solution)/shard_map/fetch/pallas_call | solution.py:350
  1.3 4.1 %collective-permute-start.1 = (bf16[1,1280,128]{2,1,0:T(8,128)(2,1)S(1)}, bf16[1,1280,128]{2,1,0:T(8,128)(2,1)S(1)}, u32[]{:S(2)}, u32[]{:S(2)}) collective-permute-start(bf16[1,1280,128]{2,1,0:T(8,128)(2,1)S(1)} %get-tuple-element.49), channel_id=1, source_target_pairs={{0,8},{2,10},{4,12},{6,14},{8,0},{10,2},{12,4},{14,6},{1,9},{3,11}... | collective-permute-start | bytes 983048 | tf_op jit(solution)/shard_map/ppermute | solution.py:342
  5.4 0.6 %pick.1 = (bf16[64,2560]{1,0:T(8,128)(2,1)S(1)}, bf16[64,2560]{1,0:T(8,128)(2,1)S(1)}, bf16[64,2560]{1,0:T(8,128)(2,1)S(1)}, bf16[64,2560]{1,0:T(8,128)(2,1)S(1)}) custom-call(s32[1]{0:T(128)} %bitcast.me_ref, s32[1,128]{1,0:T(1,128)S(1)} %get-tuple-element.40.adapter_ref, bf16[128,2560]{1,0:T(8,128)(2,1)S(1)} %get-tuple-element.41.tokens_ref), custom_call_target="tpu_custom_call" | custom-call | flops 167772160 | bytes 1966080 | tf_op jit(solution)/shard_map/pick/pallas_call | solution.py:364
  6.0 2.6 %collective-permute-start.2 = (bf16[64,2560]{1,0:T(8,128)(2,1)S(1)}, bf16[64,2560]{1,0:T(8,128)(2,1)S(1)}, u32[]{:S(2)}, u32[]{:S(2)}) collective-permute-start(bf16[64,2560]{1,0:T(8,128)(2,1)S(1)} %get-tuple-element.45), channel_id=1, source_target_pairs={{0,6},{2,4},{4,2},{6,0},{8,14},{10,12},{12,10},{14,8},{1,7},{3,5},... | collective-permute-start | bytes 983048 | tf_op jit(solution)/shard_map/ppermute | solution.py:342
  9.3 0.9 %up_share.1 = (bf16[1,128,512]{2,1,0:T(8,128)(2,1)S(1)}, f32[1,128]{1,0:T(1,128)S(1)}) custom-call(s32[1]{0:T(128)} %bitcast.2.group_ref, s32[1]{0:T(128)} %bitcast.3.core_ref, s32[1]{0:T(128)S(6)} %copy.9.ranks_ref, bf16[1,128,2048]{2,1,0:T(8,128)(2,1)} %up_hbm.2), custom_call_target="tpu_custom_call" | custom-call | flops 65536 | bytes 262144 | tf_op jit(solution)/shard_map/up_share/pallas_call | solution.py:376
  10.2 0.4 collective-permute-start
  10.7 0.4 collective-permute-start.3
  11.1 0.2 collective-permute-start.4
  11.4 0.7 %convert_element_type.4 = f32[128]{0:T(128)S(1)} convert(s32[128]{0:T(128)} %param.10) | non-fusion elementwise | flops 128 | bytes 1024 | tf_op jit(solution)/shard_map/convert_element_type | solution.py:434
  12.0 5.6 %base.1 = (f32[128,1024]{1,0:T(8,128)S(1)}, f32[128,1024]{1,0:T(8,128)S(1)}, bf16[1,2560,128]{2,1,0:T(8,128)(2,1)S(1)}, bf16[1,128,1024]{2,1,0:T(8,128)(2,1)S(1)}) custom-call(s32[1]{0:T(128)} %bitcast.3.core_ref, bf16[128,2560]{1,0:T(8,128)(2,1)} %tokens_hbm.3, bf16[2560,2048]{1,0:T(8,128)(2,1)} %weight_hbm.1, bf16[1,2560,128]{2,1,0:T(8,128)(2,1)} %down_hbm.3, ...), custom_call_target="tpu_custom_call" | custom-call | flops 1342177280 | bytes 10485760 | tf_op jit(solution)/shard_map/base/pallas_call | solution.py:401
  17.7 4.2 %collective-permute-done.1.refs_4_ = bf16[1,1280,128]{2,1,0:T(8,128)(2,1)S(1)} collective-permute-done((bf16[1,1280,128]{2,1,0:T(8,128)(2,1)S(1)}, bf16[1,1280,128]{2,1,0:T(8,128)(2,1)S(1)}, u32[]{:S(2)}, u32[]{:S(2)}) %collective-permute-start.1) | collective-permute-done | bytes 327712 | tf_op jit(solution)/shard_map/ppermute | solution.py:342
  21.9 2.1 %collective-permute-start.6 = (bf16[1,1280,128]{2,1,0:T(8,128)(2,1)S(1)}, bf16[1,1280,128]{2,1,0:T(8,128)(2,1)S(1)}, u32[]{:S(2)}, u32[]{:S(2)}) collective-permute-start(bf16[1,1280,128]{2,1,0:T(8,128)(2,1)S(1)} %collective-permute-done.1.refs_4_), channel_id=1, source_target_pairs={{0,16},{16,0},{1,17},{17,1},{2,18},{18,2},{3,19},{19,3},{4,20},{20... | collective-permute-start | bytes 983048 | tf_op jit(solution)/shard_map/ppermute | solution.py:342
  24.0 0.3 fusion
  24.3 1.6 %collective-permute-done.refs_0_ = bf16[1,128,512]{2,1,0:T(8,128)(2,1)S(1)} collective-permute-done((bf16[1,128,512]{2,1,0:T(8,128)(2,1)S(1)}, bf16[1,128,512]{2,1,0:T(8,128)(2,1)S(1)}, u32[]{:S(2)}, u32[]{:S(2)}) %collective-permute-start) | collective-permute-done | bytes 131104 | tf_op jit(solution)/shard_map/ppermute | solution.py:342
  25.9 0.0 collective-permute-done.2.refs_1_
  25.9 0.0 collective-permute-start.5
  25.9 0.1 pad_maximum_fusion
  26.1 1.6 %collective-permute-start.8 = (bf16[1,128,512]{2,1,0:T(8,128)(2,1)S(1)}, bf16[1,128,512]{2,1,0:T(8,128)(2,1)S(1)}, u32[]{:S(2)}, u32[]{:S(2)}) collective-permute-start(bf16[1,128,512]{2,1,0:T(8,128)(2,1)S(1)} %collective-permute-done.refs_0_), channel_id=1, source_target_pairs={{0,16},{16,0},{1,17},{17,1},{2,18},{18,2},{3,19},{19,3},{4,20},{20... | collective-permute-start | bytes 393224 | tf_op jit(solution)/shard_map/ppermute | solution.py:342
  27.7 4.3 %collective-permute-done.3.refs_2_ = bf16[64,2560]{1,0:T(8,128)(2,1)S(1)} collective-permute-done((bf16[64,2560]{1,0:T(8,128)(2,1)S(1)}, bf16[64,2560]{1,0:T(8,128)(2,1)S(1)}, u32[]{:S(2)}, u32[]{:S(2)}) %collective-permute-start.3) | collective-permute-done | bytes 327712 | tf_op jit(solution)/shard_map/ppermute | solution.py:342
  32.0 0.0 collective-permute-done.4.refs_3_
  32.0 0.0 collective-permute-done.6.refs_5_
  32.0 0.5 %down.1.low_ref = f32[256,128]{1,0:T(8,128)S(1)} custom-call(s32[1]{0:T(128)} %bitcast.2.group_ref, bf16[1,2560,128]{2,1,0:T(8,128)(2,1)S(1)} %get-tuple-element.60.down_ref, bf16[64,2560]{1,0:T(8,128)(2,1)S(1)} %get-tuple-element.61.refs_0_, bf16[64,2560]{1,0:T(8,128)(2,1)S(1)} %collective-permute-done.2.refs_1_, ...), custom_call_target="tpu_custom_call" | custom-call | flops 335544320 | bytes 1966080 | tf_op jit(solution)/shard_map/down/pallas_call | solution.py:443
  32.5 0.1 collective-permute-start.7
  32.6 0.0 collective-permute-done.8.refs_1_
  32.6 1.3 %collective-permute-done.7.other_ref = f32[256,128]{1,0:T(8,128)S(1)} collective-permute-done((f32[256,128]{1,0:T(8,128)S(1)}, f32[256,128]{1,0:T(8,128)S(1)}, u32[]{:S(2)}, u32[]{:S(2)}) %collective-permute-start.7) | collective-permute-done | bytes 131104 | tf_op jit(solution)/shard_map/ppermute | solution.py:342
  33.9 0.8 %up.1 = (s16[64,1024]{1,0:T(8,128)(2,1)S(1)}, s16[64,1024]{1,0:T(8,128)(2,1)S(1)}, s16[64,1024]{1,0:T(8,128)(2,1)S(1)}, s16[64,1024]{1,0:T(8,128)(2,1)S(1)}) custom-call(s32[1]{0:T(128)} %bitcast.2.group_ref, f32[256,128]{1,0:T(8,128)S(1)} %down.1.low_ref, f32[256,128]{1,0:T(8,128)S(1)} %collective-permute-done.7.other_ref, ...), custom_call_target="tpu_custom_call" | custom-call | flops 268435456 | bytes 524288 | tf_op jit(solution)/shard_map/up/pallas_call | solution.py:454
  34.7 1.3 %collective-permute-start.10 = (s16[64,1024]{1,0:T(8,128)(2,1)S(1)}, s16[64,1024]{1,0:T(8,128)(2,1)S(1)}, u32[]{:S(2)}, u32[]{:S(2)}) collective-permute-start(s16[64,1024]{1,0:T(8,128)(2,1)S(1)} %get-tuple-element.73), channel_id=1, source_target_pairs={{0,6},{2,4},{4,2},{6,0},{8,14},{10,12},{12,10},{14,8},{1,7},{3,5},... | collective-permute-start | bytes 393224 | tf_op jit(solution)/shard_map/ppermute | solution.py:342
  36.0 0.8 %collective-permute-start.11 = (s16[64,1024]{1,0:T(8,128)(2,1)S(1)}, s16[64,1024]{1,0:T(8,128)(2,1)S(1)}, u32[]{:S(2)}, u32[]{:S(2)}) collective-permute-start(s16[64,1024]{1,0:T(8,128)(2,1)S(1)} %get-tuple-element.74), channel_id=1, source_target_pairs={{0,4},{2,6},{4,0},{6,2},{8,12},{10,14},{12,8},{14,10},{1,5},{3,7},... | collective-permute-start | bytes 393224 | tf_op jit(solution)/shard_map/ppermute | solution.py:342
  36.8 1.5 %collective-permute-start.9 = (s16[64,1024]{1,0:T(8,128)(2,1)S(1)}, s16[64,1024]{1,0:T(8,128)(2,1)S(1)}, u32[]{:S(2)}, u32[]{:S(2)}) collective-permute-start(s16[64,1024]{1,0:T(8,128)(2,1)S(1)} %get-tuple-element.72), channel_id=1, source_target_pairs={{0,2},{2,0},{4,6},{6,4},{8,10},{10,8},{12,14},{14,12},{1,3},{3,1},... | collective-permute-start | bytes 393224 | tf_op jit(solution)/shard_map/ppermute | solution.py:342
  38.2 0.0 copy-done.1
  38.3 0.0 collective-permute-done.5.other_ref
  38.3 0.0 copy-done
  38.3 0.5 %start_rows.1 = (f32[128,1024]{1,0:T(8,128)S(1)}, bf16[128,192]{1,0:T(8,128)(2,1)S(1)}) custom-call(s32[1]{0:T(128)} %bitcast.me_ref, s32[1,128]{1,0:T(1,128)S(1)} %bitcast.9, f32[128,1024]{1,0:T(8,128)S(1)} %get-tuple-element.58.mine_ref, f32[128,1024]{1,0:T(8,128)S(1)} %collective-permute-done.5.other_ref, s16[64,1024]{1,0:T(8,128)(2,1)S(1)} %get-tuple-element.67.own_ref), custom_call_target="tpu_custom_call" | custom-call | flops 33554432 | bytes 1572864 | tf_op jit(solution)/shard_map/start_rows/pallas_call | solution.py:467
  38.8 3.2 %collective-permute-done.10.refs_1_ = s16[64,1024]{1,0:T(8,128)(2,1)S(1)} collective-permute-done((s16[64,1024]{1,0:T(8,128)(2,1)S(1)}, s16[64,1024]{1,0:T(8,128)(2,1)S(1)}, u32[]{:S(2)}, u32[]{:S(2)}) %collective-permute-start.10) | collective-permute-done | bytes 131104 | tf_op jit(solution)/shard_map/ppermute | solution.py:342
  42.0 1.1 %collective-permute-done.11.refs_2_ = s16[64,1024]{1,0:T(8,128)(2,1)S(1)} collective-permute-done((s16[64,1024]{1,0:T(8,128)(2,1)S(1)}, s16[64,1024]{1,0:T(8,128)(2,1)S(1)}, u32[]{:S(2)}, u32[]{:S(2)}) %collective-permute-start.11) | collective-permute-done | bytes 131104 | tf_op jit(solution)/shard_map/ppermute | solution.py:342
  43.1 0.9 %collective-permute-done.9.refs_0_ = s16[64,1024]{1,0:T(8,128)(2,1)S(1)} collective-permute-done((s16[64,1024]{1,0:T(8,128)(2,1)S(1)}, s16[64,1024]{1,0:T(8,128)(2,1)S(1)}, u32[]{:S(2)}, u32[]{:S(2)}) %collective-permute-start.9) | collective-permute-done | bytes 131104 | tf_op jit(solution)/shard_map/ppermute | solution.py:342
  44.0 1.3 %finish.1 = bf16[1024,128]{1,0:T(8,128)(2,1)} custom-call(f32[128,1024]{1,0:T(8,128)S(1)} %get-tuple-element.68.partial_ref, bf16[128,192]{1,0:T(8,128)(2,1)S(1)} %get-tuple-element.69.picker_ref, f32[128,128]{1,0:T(8,128)S(1)} %get-tuple-element.70.cos_ref, f32[128,128]{1,0:T(8,128)S(1)} %get-tuple-element.71.sin_ref, ...), custom_call_target="tpu_custom_call" | custom-call | flops 134217728 | bytes 524288 | tf_op jit(solution)/shard_map/finish/pallas_call | solution.py:479
  (2 shorter events, 0.0 us)
Async XLA Ops:
  0.0 38.3 %copy-start = (s32[128,1]{0,1:T(1,128)S(1)}, s32[128,1]{0,1:T(1,128)}, u32[]{:S(2)}) copy-start(s32[128,1]{0,1:T(1,128)} %param.9) | copy-start | bytes 1540
  0.0 38.2 %copy-start.1 = (bf16[128]{0:T(256)(128)(2,1)S(1)}, bf16[128]{0:T(256)(128)(2,1)}, u32[]{:S(2)}) copy-start(bf16[128]{0:T(256)(128)(2,1)} %param.15) | copy-start | bytes 772
  1.3 20.5 %collective-permute-start.1 = (bf16[1,1280,128]{2,1,0:T(8,128)(2,1)S(1)}, bf16[1,1280,128]{2,1,0:T(8,128)(2,1)S(1)}, u32[]{:S(2)}, u32[]{:S(2)}) collective-permute-start(bf16[1,1280,128]{2,1,0:T(8,128)(2,1)S(1)} %get-tuple-element.49), channel_id=1, source_target_pairs={{0,8},{2,10},{4,12},{6,14},{8,0},{10,2},{12,4},{14,6},{1,9},{3,11}... | collective-permute-start | bytes 983048 | tf_op jit(solution)/shard_map/ppermute | solution.py:342
  6.0 19.9 %collective-permute-start.2 = (bf16[64,2560]{1,0:T(8,128)(2,1)S(1)}, bf16[64,2560]{1,0:T(8,128)(2,1)S(1)}, u32[]{:S(2)}, u32[]{:S(2)}) collective-permute-start(bf16[64,2560]{1,0:T(8,128)(2,1)S(1)} %get-tuple-element.45), channel_id=1, source_target_pairs={{0,6},{2,4},{4,2},{6,0},{8,14},{10,12},{12,10},{14,8},{1,7},{3,5},... | collective-permute-start | bytes 983048 | tf_op jit(solution)/shard_map/ppermute | solution.py:342
  10.2 15.7 %collective-permute-start = (bf16[1,128,512]{2,1,0:T(8,128)(2,1)S(1)}, bf16[1,128,512]{2,1,0:T(8,128)(2,1)S(1)}, u32[]{:S(2)}, u32[]{:S(2)}) collective-permute-start(bf16[1,128,512]{2,1,0:T(8,128)(2,1)S(1)} %get-tuple-element.48), channel_id=1, source_target_pairs={{0,8},{2,10},{4,12},{6,14},{8,0},{10,2},{12,4},{14,6},{1,9},{3,11}... | collective-permute-start | bytes 393224 | tf_op jit(solution)/shard_map/ppermute | solution.py:342
  10.7 21.3 %collective-permute-start.3 = (bf16[64,2560]{1,0:T(8,128)(2,1)S(1)}, bf16[64,2560]{1,0:T(8,128)(2,1)S(1)}, u32[]{:S(2)}, u32[]{:S(2)}) collective-permute-start(bf16[64,2560]{1,0:T(8,128)(2,1)S(1)} %get-tuple-element.55), channel_id=1, source_target_pairs={{0,4},{2,6},{4,0},{6,2},{8,12},{10,14},{12,8},{14,10},{1,5},{3,7},... | collective-permute-start | bytes 983048 | tf_op jit(solution)/shard_map/ppermute | solution.py:342
  11.1 20.9 %collective-permute-start.4 = (bf16[64,2560]{1,0:T(8,128)(2,1)S(1)}, bf16[64,2560]{1,0:T(8,128)(2,1)S(1)}, u32[]{:S(2)}, u32[]{:S(2)}) collective-permute-start(bf16[64,2560]{1,0:T(8,128)(2,1)S(1)} %get-tuple-element.56), channel_id=1, source_target_pairs={{0,2},{2,0},{4,6},{6,4},{8,10},{10,8},{12,14},{14,12},{1,3},{3,1},... | collective-permute-start | bytes 983048 | tf_op jit(solution)/shard_map/ppermute | solution.py:342
  21.9 10.1 %collective-permute-start.6 = (bf16[1,1280,128]{2,1,0:T(8,128)(2,1)S(1)}, bf16[1,1280,128]{2,1,0:T(8,128)(2,1)S(1)}, u32[]{:S(2)}, u32[]{:S(2)}) collective-permute-start(bf16[1,1280,128]{2,1,0:T(8,128)(2,1)S(1)} %collective-permute-done.1.refs_4_), channel_id=1, source_target_pairs={{0,16},{16,0},{1,17},{17,1},{2,18},{18,2},{3,19},{19,3},{4,20},{20... | collective-permute-start | bytes 983048 | tf_op jit(solution)/shard_map/ppermute | solution.py:342
  25.9 12.3 %collective-permute-start.5 = (f32[128,1024]{1,0:T(8,128)S(1)}, f32[128,1024]{1,0:T(8,128)S(1)}, u32[]{:S(2)}, u32[]{:S(2)}) collective-permute-start(f32[128,1024]{1,0:T(8,128)S(1)} %get-tuple-element.59), channel_id=1, source_target_pairs={{0,1},{1,0},{2,3},{3,2},{4,5},{5,4},{6,7},{7,6},{8,9},{9,8},{10,11... | collective-permute-start | bytes 1572872 | tf_op jit(solution)/shard_map/ppermute | solution.py:342
  26.1 6.5 %collective-permute-start.8 = (bf16[1,128,512]{2,1,0:T(8,128)(2,1)S(1)}, bf16[1,128,512]{2,1,0:T(8,128)(2,1)S(1)}, u32[]{:S(2)}, u32[]{:S(2)}) collective-permute-start(bf16[1,128,512]{2,1,0:T(8,128)(2,1)S(1)} %collective-permute-done.refs_0_), channel_id=1, source_target_pairs={{0,16},{16,0},{1,17},{17,1},{2,18},{18,2},{3,19},{19,3},{4,20},{20... | collective-permute-start | bytes 393224 | tf_op jit(solution)/shard_map/ppermute | solution.py:342
  32.5 1.4 %collective-permute-start.7 = (f32[256,128]{1,0:T(8,128)S(1)}, f32[256,128]{1,0:T(8,128)S(1)}, u32[]{:S(2)}, u32[]{:S(2)}) collective-permute-start(f32[256,128]{1,0:T(8,128)S(1)} %down.1.low_ref), channel_id=1, source_target_pairs={{0,1},{1,0},{2,3},{3,2},{4,5},{5,4},{6,7},{7,6},{8,9},{9,8},{10,11... | collective-permute-start | bytes 393224 | tf_op jit(solution)/shard_map/ppermute | solution.py:342
  34.7 7.3 %collective-permute-start.10 = (s16[64,1024]{1,0:T(8,128)(2,1)S(1)}, s16[64,1024]{1,0:T(8,128)(2,1)S(1)}, u32[]{:S(2)}, u32[]{:S(2)}) collective-permute-start(s16[64,1024]{1,0:T(8,128)(2,1)S(1)} %get-tuple-element.73), channel_id=1, source_target_pairs={{0,6},{2,4},{4,2},{6,0},{8,14},{10,12},{12,10},{14,8},{1,7},{3,5},... | collective-permute-start | bytes 393224 | tf_op jit(solution)/shard_map/ppermute | solution.py:342
  36.0 7.1 %collective-permute-start.11 = (s16[64,1024]{1,0:T(8,128)(2,1)S(1)}, s16[64,1024]{1,0:T(8,128)(2,1)S(1)}, u32[]{:S(2)}, u32[]{:S(2)}) collective-permute-start(s16[64,1024]{1,0:T(8,128)(2,1)S(1)} %get-tuple-element.74), channel_id=1, source_target_pairs={{0,4},{2,6},{4,0},{6,2},{8,12},{10,14},{12,8},{14,10},{1,5},{3,7},... | collective-permute-start | bytes 393224 | tf_op jit(solution)/shard_map/ppermute | solution.py:342
  36.8 7.2 %collective-permute-start.9 = (s16[64,1024]{1,0:T(8,128)(2,1)S(1)}, s16[64,1024]{1,0:T(8,128)(2,1)S(1)}, u32[]{:S(2)}, u32[]{:S(2)}) collective-permute-start(s16[64,1024]{1,0:T(8,128)(2,1)S(1)} %get-tuple-element.72), channel_id=1, source_target_pairs={{0,2},{2,0},{4,6},{6,4},{8,10},{10,8},{12,14},{14,12},{1,3},{3,1},... | collective-permute-start | bytes 393224 | tf_op jit(solution)/shard_map/ppermute | solution.py:342

commit v23 on v22

--- a/solution.py
+++ b/solution.py
@@ -392,7 +392,7 @@
     far_up = exchange(up_part, "pool", pool, pool // 2)
 
     order = far_first(buffers)
-    early, late = order[:1], order[1:]
+    early, late = order[:-1], order[-1:]
     late_rows, _ = lax.optimization_barrier(([picked[j] for j in late], up_part))
     leaving = [picked[j] for j in early] + late_rows
     arrived = [picked[0]] + [exchange(x, "pool", pool, j) for x, j in zip(leaving, order)]

time: 45.5 us -> 47.3 us (1.040)
  waiting for transfers between devices: 16.7 us -> 18.3 us
    ppermute x12, waiting for transfers between devices: 16.7 us -> 18.3 us  [exchange(): return lax.ppermute(x, axis, [(p, p ^ j) for p in range(count)])]
  transfers between devices with their start and end apart: 12 -> 12, of which waited for: 7 -> 7; matrix products, arithmetic and copies ran while one was open for 2% -> 2% of each run, Pallas kernels for 20% -> 19%
where the time goes in v23:
time: 47.3 us; the launch traced here: 47.1 us
  waiting for transfers between devices  18.3 us (39%)
  starting transfers between devices  15.3 us (32%)
  Pallas kernels  11.6 us (25%)
  other arithmetic  1.08 us (2%)
  between operations  0.76 us (2%)
    ppermute x12, waiting for transfers between devices, exchange(): return lax.ppermute(x, axis, [(p, p ^ j) for p in range(count)])  18.3 us
    ppermute x12, starting transfers between devices, exchange(): return lax.ppermute(x, axis, [(p, p ^ j) for p in range(count)])  15.3 us
    pallas_call x1, Pallas kernels, body(): pl.pallas_call(base_kernel, in_specs=[SMEM] + [HBM] * 4, out_specs=[VMEM]...  5.63 us
    pallas_call x1, Pallas kernels, body(): pl.pallas_call(fetch_kernel, in_specs=[SMEM] + [HBM] * 3, out_specs=[VMEM...  1.33 us
    pallas_call x1, Pallas kernels, body(): pl.pallas_call(functools.partial(finish_kernel, buffers), in_specs=[VMEM]...  1.29 us
    pallas_call x1, Pallas kernels, body(): pl.pallas_call(functools.partial(up_share_kernel, cores), in_specs=[SMEM]...  0.95 us
  transfers between devices with their start and end apart: 12, of which 7 were waited for; matrix products, arithmetic and copies ran while one was open for 2% of the time, Pallas kernels for 19%

profile of v23, /device:TPU:0, one launch (start us, length us, event | category | flops | bytes accessed | tf_op | source)
XLA Modules:
  0.0 47.1 jit_solution(11182252409067542002)
XLA Ops:
  0.0 0.0 copy-start
  0.0 0.0 copy-start.1
  0.0 1.3 %fetch.1 = (bf16[1,1280,128]{2,1,0:T(8,128)(2,1)S(1)}, s32[1,128]{1,0:T(1,128)S(1)}, bf16[128,2560]{1,0:T(8,128)(2,1)S(1)}) custom-call(s32[1]{0:T(128)} %bitcast.2.group_ref, bf16[1,2560,128]{2,1,0:T(8,128)(2,1)} %down_hbm.3, s32[1,128]{1,0:T(1,128)} %bitcast.8, bf16[128,2560]{1,0:T(8,128)(2,1)} %tokens_hbm.3), custom_call_target="tpu_custom_call" | custom-call | bytes 1966080 | tf_op jit(solution)/shard_map/fetch/pallas_call | solution.py:350
  1.3 4.1 %collective-permute-start.1 = (bf16[1,1280,128]{2,1,0:T(8,128)(2,1)S(1)}, bf16[1,1280,128]{2,1,0:T(8,128)(2,1)S(1)}, u32[]{:S(2)}, u32[]{:S(2)}) collective-permute-start(bf16[1,1280,128]{2,1,0:T(8,128)(2,1)S(1)} %get-tuple-element.48), channel_id=1, source_target_pairs={{0,8},{2,10},{4,12},{6,14},{8,0},{10,2},{12,4},{14,6},{1,9},{3,11}... | collective-permute-start | bytes 983048 | tf_op jit(solution)/shard_map/ppermute | solution.py:342
  5.4 0.6 %pick.1 = (bf16[64,2560]{1,0:T(8,128)(2,1)S(1)}, bf16[64,2560]{1,0:T(8,128)(2,1)S(1)}, bf16[64,2560]{1,0:T(8,128)(2,1)S(1)}, bf16[64,2560]{1,0:T(8,128)(2,1)S(1)}) custom-call(s32[1]{0:T(128)} %bitcast.me_ref, s32[1,128]{1,0:T(1,128)S(1)} %get-tuple-element.39.adapter_ref, bf16[128,2560]{1,0:T(8,128)(2,1)S(1)} %get-tuple-element.40.tokens_ref), custom_call_target="tpu_custom_call" | custom-call | flops 167772160 | bytes 1966080 | tf_op jit(solution)/shard_map/pick/pallas_call | solution.py:364
  6.0 2.6 %collective-permute-start.2 = (bf16[64,2560]{1,0:T(8,128)(2,1)S(1)}, bf16[64,2560]{1,0:T(8,128)(2,1)S(1)}, u32[]{:S(2)}, u32[]{:S(2)}) collective-permute-start(bf16[64,2560]{1,0:T(8,128)(2,1)S(1)} %get-tuple-element.44), channel_id=1, source_target_pairs={{0,6},{2,4},{4,2},{6,0},{8,14},{10,12},{12,10},{14,8},{1,7},{3,5},... | collective-permute-start | bytes 983048 | tf_op jit(solution)/shard_map/ppermute | solution.py:342
  8.6 0.5 collective-permute-start.3
  9.7 0.9 %up_share.1 = (bf16[1,128,512]{2,1,0:T(8,128)(2,1)S(1)}, f32[1,128]{1,0:T(1,128)S(1)}) custom-call(s32[1]{0:T(128)} %bitcast.2.group_ref, s32[1]{0:T(128)} %bitcast.3.core_ref, s32[1]{0:T(128)S(6)} %copy.9.ranks_ref, bf16[1,128,2048]{2,1,0:T(8,128)(2,1)} %up_hbm.2), custom_call_target="tpu_custom_call" | custom-call | flops 65536 | bytes 262144 | tf_op jit(solution)/shard_map/up_share/pallas_call | solution.py:376
  10.7 0.4 collective-permute-start
  11.1 0.2 collective-permute-start.4
  11.4 0.7 %convert_element_type.4 = f32[128]{0:T(128)S(1)} convert(s32[128]{0:T(128)} %param.10) | non-fusion elementwise | flops 128 | bytes 1024 | tf_op jit(solution)/shard_map/convert_element_type | solution.py:434
  12.0 5.6 %base.1 = (f32[128,1024]{1,0:T(8,128)S(1)}, f32[128,1024]{1,0:T(8,128)S(1)}, bf16[1,2560,128]{2,1,0:T(8,128)(2,1)S(1)}, bf16[1,128,1024]{2,1,0:T(8,128)(2,1)S(1)}) custom-call(s32[1]{0:T(128)} %bitcast.3.core_ref, bf16[128,2560]{1,0:T(8,128)(2,1)} %tokens_hbm.3, bf16[2560,2048]{1,0:T(8,128)(2,1)} %weight_hbm.1, bf16[1,2560,128]{2,1,0:T(8,128)(2,1)} %down_hbm.3, ...), custom_call_target="tpu_custom_call" | custom-call | flops 1342177280 | bytes 10485760 | tf_op jit(solution)/shard_map/base/pallas_call | solution.py:401
  17.7 3.4 %collective-permute-done.1.refs_4_ = bf16[1,1280,128]{2,1,0:T(8,128)(2,1)S(1)} collective-permute-done((bf16[1,1280,128]{2,1,0:T(8,128)(2,1)S(1)}, bf16[1,1280,128]{2,1,0:T(8,128)(2,1)S(1)}, u32[]{:S(2)}, u32[]{:S(2)}) %collective-permute-start.1) | collective-permute-done | bytes 327712 | tf_op jit(solution)/shard_map/ppermute | solution.py:342
  21.1 1.8 %collective-permute-start.6 = (bf16[1,1280,128]{2,1,0:T(8,128)(2,1)S(1)}, bf16[1,1280,128]{2,1,0:T(8,128)(2,1)S(1)}, u32[]{:S(2)}, u32[]{:S(2)}) collective-permute-start(bf16[1,1280,128]{2,1,0:T(8,128)(2,1)S(1)} %collective-permute-done.1.refs_4_), channel_id=1, source_target_pairs={{0,16},{16,0},{1,17},{17,1},{2,18},{18,2},{3,19},{19,3},{4,20},{20... | collective-permute-start | bytes 983048 | tf_op jit(solution)/shard_map/ppermute | solution.py:342
  22.9 0.3 fusion
  23.3 6.1 %collective-permute-done.refs_0_ = bf16[1,128,512]{2,1,0:T(8,128)(2,1)S(1)} collective-permute-done((bf16[1,128,512]{2,1,0:T(8,128)(2,1)S(1)}, bf16[1,128,512]{2,1,0:T(8,128)(2,1)S(1)}, u32[]{:S(2)}, u32[]{:S(2)}) %collective-permute-start) | collective-permute-done | bytes 131104 | tf_op jit(solution)/shard_map/ppermute | solution.py:342
  29.4 0.0 collective-permute-done.2.refs_1_
  29.4 0.0 collective-permute-start.5
  29.4 0.1 pad_maximum_fusion
  29.5 1.6 %collective-permute-start.8 = (bf16[1,128,512]{2,1,0:T(8,128)(2,1)S(1)}, bf16[1,128,512]{2,1,0:T(8,128)(2,1)S(1)}, u32[]{:S(2)}, u32[]{:S(2)}) collective-permute-start(bf16[1,128,512]{2,1,0:T(8,128)(2,1)S(1)} %collective-permute-done.refs_0_), channel_id=1, source_target_pairs={{0,16},{16,0},{1,17},{17,1},{2,18},{18,2},{3,19},{19,3},{4,20},{20... | collective-permute-start | bytes 393224 | tf_op jit(solution)/shard_map/ppermute | solution.py:342
  31.0 0.0 collective-permute-done.4.refs_3_
  31.0 0.9 %collective-permute-done.3.refs_2_ = bf16[64,2560]{1,0:T(8,128)(2,1)S(1)} collective-permute-done((bf16[64,2560]{1,0:T(8,128)(2,1)S(1)}, bf16[64,2560]{1,0:T(8,128)(2,1)S(1)}, u32[]{:S(2)}, u32[]{:S(2)}) %collective-permute-start.3) | collective-permute-done | bytes 327712 | tf_op jit(solution)/shard_map/ppermute | solution.py:342
  32.0 0.0 collective-permute-done.6.refs_5_
  32.0 0.5 %down.1.low_ref = f32[256,128]{1,0:T(8,128)S(1)} custom-call(s32[1]{0:T(128)} %bitcast.2.group_ref, bf16[1,2560,128]{2,1,0:T(8,128)(2,1)S(1)} %get-tuple-element.58.down_ref, bf16[64,2560]{1,0:T(8,128)(2,1)S(1)} %get-tuple-element.59.refs_0_, bf16[64,2560]{1,0:T(8,128)(2,1)S(1)} %collective-permute-done.2.refs_1_, ...), custom_call_target="tpu_custom_call" | custom-call | flops 335544320 | bytes 1966080 | tf_op jit(solution)/shard_map/down/pallas_call | solution.py:443
  32.5 0.1 collective-permute-start.7
  32.6 2.9 %collective-permute-done.8.refs_1_ = bf16[1,128,512]{2,1,0:T(8,128)(2,1)S(1)} collective-permute-done((bf16[1,128,512]{2,1,0:T(8,128)(2,1)S(1)}, bf16[1,128,512]{2,1,0:T(8,128)(2,1)S(1)}, u32[]{:S(2)}, u32[]{:S(2)}) %collective-permute-start.8) | collective-permute-done | bytes 131104 | tf_op jit(solution)/shard_map/ppermute | solution.py:342
  35.4 0.0 collective-permute-done.7.other_ref
  35.4 0.8 %up.1 = (s16[64,1024]{1,0:T(8,128)(2,1)S(1)}, s16[64,1024]{1,0:T(8,128)(2,1)S(1)}, s16[64,1024]{1,0:T(8,128)(2,1)S(1)}, s16[64,1024]{1,0:T(8,128)(2,1)S(1)}) custom-call(s32[1]{0:T(128)} %bitcast.2.group_ref, f32[256,128]{1,0:T(8,128)S(1)} %down.1.low_ref, f32[256,128]{1,0:T(8,128)S(1)} %collective-permute-done.7.other_ref, ...), custom_call_target="tpu_custom_call" | custom-call | flops 268435456 | bytes 524288 | tf_op jit(solution)/shard_map/up/pallas_call | solution.py:454
  36.2 3.4 %collective-permute-start.10 = (s16[64,1024]{1,0:T(8,128)(2,1)S(1)}, s16[64,1024]{1,0:T(8,128)(2,1)S(1)}, u32[]{:S(2)}, u32[]{:S(2)}) collective-permute-start(s16[64,1024]{1,0:T(8,128)(2,1)S(1)} %get-tuple-element.71), channel_id=1, source_target_pairs={{0,6},{2,4},{4,2},{6,0},{8,14},{10,12},{12,10},{14,8},{1,7},{3,5},... | collective-permute-start | bytes 393224 | tf_op jit(solution)/shard_map/ppermute | solution.py:342
  39.6 0.0 collective-permute-start.11
  39.6 0.6 %collective-permute-start.9 = (s16[64,1024]{1,0:T(8,128)(2,1)S(1)}, s16[64,1024]{1,0:T(8,128)(2,1)S(1)}, u32[]{:S(2)}, u32[]{:S(2)}) collective-permute-start(s16[64,1024]{1,0:T(8,128)(2,1)S(1)} %get-tuple-element.70), channel_id=1, source_target_pairs={{0,2},{2,0},{4,6},{6,4},{8,10},{10,8},{12,14},{14,12},{1,3},{3,1},... | collective-permute-start | bytes 393224 | tf_op jit(solution)/shard_map/ppermute | solution.py:342
  40.3 0.0 copy-done.1
  40.3 0.0 collective-permute-done.5.other_ref
  40.3 0.0 copy-done
  40.3 0.5 %start_rows.1 = (f32[128,1024]{1,0:T(8,128)S(1)}, bf16[128,192]{1,0:T(8,128)(2,1)S(1)}) custom-call(s32[1]{0:T(128)} %bitcast.me_ref, s32[1,128]{1,0:T(1,128)S(1)} %bitcast.9, f32[128,1024]{1,0:T(8,128)S(1)} %get-tuple-element.56.mine_ref, f32[128,1024]{1,0:T(8,128)S(1)} %collective-permute-done.5.other_ref, s16[64,1024]{1,0:T(8,128)(2,1)S(1)} %get-tuple-element.65.own_ref), custom_call_target="tpu_custom_call" | custom-call | flops 33554432 | bytes 1572864 | tf_op jit(solution)/shard_map/start_rows/pallas_call | solution.py:467
  40.8 3.1 %collective-permute-done.10.refs_1_ = s16[64,1024]{1,0:T(8,128)(2,1)S(1)} collective-permute-done((s16[64,1024]{1,0:T(8,128)(2,1)S(1)}, s16[64,1024]{1,0:T(8,128)(2,1)S(1)}, u32[]{:S(2)}, u32[]{:S(2)}) %collective-permute-start.10) | collective-permute-done | bytes 131104 | tf_op jit(solution)/shard_map/ppermute | solution.py:342
  44.0 1.2 %collective-permute-done.11.refs_2_ = s16[64,1024]{1,0:T(8,128)(2,1)S(1)} collective-permute-done((s16[64,1024]{1,0:T(8,128)(2,1)S(1)}, s16[64,1024]{1,0:T(8,128)(2,1)S(1)}, u32[]{:S(2)}, u32[]{:S(2)}) %collective-permute-start.11) | collective-permute-done | bytes 131104 | tf_op jit(solution)/shard_map/ppermute | solution.py:342
  45.2 0.6 %collective-permute-done.9.refs_0_ = s16[64,1024]{1,0:T(8,128)(2,1)S(1)} collective-permute-done((s16[64,1024]{1,0:T(8,128)(2,1)S(1)}, s16[64,1024]{1,0:T(8,128)(2,1)S(1)}, u32[]{:S(2)}, u32[]{:S(2)}) %collective-permute-start.9) | collective-permute-done | bytes 131104 | tf_op jit(solution)/shard_map/ppermute | solution.py:342
  45.8 1.3 %finish.1 = bf16[1024,128]{1,0:T(8,128)(2,1)} custom-call(f32[128,1024]{1,0:T(8,128)S(1)} %get-tuple-element.66.partial_ref, bf16[128,192]{1,0:T(8,128)(2,1)S(1)} %get-tuple-element.67.picker_ref, f32[128,128]{1,0:T(8,128)S(1)} %get-tuple-element.68.cos_ref, f32[128,128]{1,0:T(8,128)S(1)} %get-tuple-element.69.sin_ref, ...), custom_call_target="tpu_custom_call" | custom-call | flops 134217728 | bytes 524288 | tf_op jit(solution)/shard_map/finish/pallas_call | solution.py:479
  (2 shorter events, 0.0 us)
Async XLA Ops:
  0.0 40.3 %copy-start = (s32[128,1]{0,1:T(1,128)S(1)}, s32[128,1]{0,1:T(1,128)}, u32[]{:S(2)}) copy-start(s32[128,1]{0,1:T(1,128)} %param.9) | copy-start | bytes 1540
  0.0 40.3 %copy-start.1 = (bf16[128]{0:T(256)(128)(2,1)S(1)}, bf16[128]{0:T(256)(128)(2,1)}, u32[]{:S(2)}) copy-start(bf16[128]{0:T(256)(128)(2,1)} %param.15) | copy-start | bytes 772
  1.3 19.8 %collective-permute-start.1 = (bf16[1,1280,128]{2,1,0:T(8,128)(2,1)S(1)}, bf16[1,1280,128]{2,1,0:T(8,128)(2,1)S(1)}, u32[]{:S(2)}, u32[]{:S(2)}) collective-permute-start(bf16[1,1280,128]{2,1,0:T(8,128)(2,1)S(1)} %get-tuple-element.48), channel_id=1, source_target_pairs={{0,8},{2,10},{4,12},{6,14},{8,0},{10,2},{12,4},{14,6},{1,9},{3,11}... | collective-permute-start | bytes 983048 | tf_op jit(solution)/shard_map/ppermute | solution.py:342
  6.0 23.3 %collective-permute-start.2 = (bf16[64,2560]{1,0:T(8,128)(2,1)S(1)}, bf16[64,2560]{1,0:T(8,128)(2,1)S(1)}, u32[]{:S(2)}, u32[]{:S(2)}) collective-permute-start(bf16[64,2560]{1,0:T(8,128)(2,1)S(1)} %get-tuple-element.44), channel_id=1, source_target_pairs={{0,6},{2,4},{4,2},{6,0},{8,14},{10,12},{12,10},{14,8},{1,7},{3,5},... | collective-permute-start | bytes 983048 | tf_op jit(solution)/shard_map/ppermute | solution.py:342
  8.6 23.3 %collective-permute-start.3 = (bf16[64,2560]{1,0:T(8,128)(2,1)S(1)}, bf16[64,2560]{1,0:T(8,128)(2,1)S(1)}, u32[]{:S(2)}, u32[]{:S(2)}) collective-permute-start(bf16[64,2560]{1,0:T(8,128)(2,1)S(1)} %get-tuple-element.43), channel_id=1, source_target_pairs={{0,4},{2,6},{4,0},{6,2},{8,12},{10,14},{12,8},{14,10},{1,5},{3,7},... | collective-permute-start | bytes 983048 | tf_op jit(solution)/shard_map/ppermute | solution.py:342
  10.7 18.7 %collective-permute-start = (bf16[1,128,512]{2,1,0:T(8,128)(2,1)S(1)}, bf16[1,128,512]{2,1,0:T(8,128)(2,1)S(1)}, u32[]{:S(2)}, u32[]{:S(2)}) collective-permute-start(bf16[1,128,512]{2,1,0:T(8,128)(2,1)S(1)} %get-tuple-element.47), channel_id=1, source_target_pairs={{0,8},{2,10},{4,12},{6,14},{8,0},{10,2},{12,4},{14,6},{1,9},{3,11}... | collective-permute-start | bytes 393224 | tf_op jit(solution)/shard_map/ppermute | solution.py:342
  11.1 19.9 %collective-permute-start.4 = (bf16[64,2560]{1,0:T(8,128)(2,1)S(1)}, bf16[64,2560]{1,0:T(8,128)(2,1)S(1)}, u32[]{:S(2)}, u32[]{:S(2)}) collective-permute-start(bf16[64,2560]{1,0:T(8,128)(2,1)S(1)} %get-tuple-element.54), channel_id=1, source_target_pairs={{0,2},{2,0},{4,6},{6,4},{8,10},{10,8},{12,14},{14,12},{1,3},{3,1},... | collective-permute-start | bytes 983048 | tf_op jit(solution)/shard_map/ppermute | solution.py:342
  21.1 10.8 %collective-permute-start.6 = (bf16[1,1280,128]{2,1,0:T(8,128)(2,1)S(1)}, bf16[1,1280,128]{2,1,0:T(8,128)(2,1)S(1)}, u32[]{:S(2)}, u32[]{:S(2)}) collective-permute-start(bf16[1,1280,128]{2,1,0:T(8,128)(2,1)S(1)} %collective-permute-done.1.refs_4_), channel_id=1, source_target_pairs={{0,16},{16,0},{1,17},{17,1},{2,18},{18,2},{3,19},{19,3},{4,20},{20... | collective-permute-start | bytes 983048 | tf_op jit(solution)/shard_map/ppermute | solution.py:342
  29.4 10.9 %collective-permute-start.5 = (f32[128,1024]{1,0:T(8,128)S(1)}, f32[128,1024]{1,0:T(8,128)S(1)}, u32[]{:S(2)}, u32[]{:S(2)}) collective-permute-start(f32[128,1024]{1,0:T(8,128)S(1)} %get-tuple-element.57), channel_id=1, source_target_pairs={{0,1},{1,0},{2,3},{3,2},{4,5},{5,4},{6,7},{7,6},{8,9},{9,8},{10,11... | collective-permute-start | bytes 1572872 | tf_op jit(solution)/shard_map/ppermute | solution.py:342
  29.5 6.0 %collective-permute-start.8 = (bf16[1,128,512]{2,1,0:T(8,128)(2,1)S(1)}, bf16[1,128,512]{2,1,0:T(8,128)(2,1)S(1)}, u32[]{:S(2)}, u32[]{:S(2)}) collective-permute-start(bf16[1,128,512]{2,1,0:T(8,128)(2,1)S(1)} %collective-permute-done.refs_0_), channel_id=1, source_target_pairs={{0,16},{16,0},{1,17},{17,1},{2,18},{18,2},{3,19},{19,3},{4,20},{20... | collective-permute-start | bytes 393224 | tf_op jit(solution)/shard_map/ppermute | solution.py:342
  32.5 3.0 %collective-permute-start.7 = (f32[256,128]{1,0:T(8,128)S(1)}, f32[256,128]{1,0:T(8,128)S(1)}, u32[]{:S(2)}, u32[]{:S(2)}) collective-permute-start(f32[256,128]{1,0:T(8,128)S(1)} %down.1.low_ref), channel_id=1, source_target_pairs={{0,1},{1,0},{2,3},{3,2},{4,5},{5,4},{6,7},{7,6},{8,9},{9,8},{10,11... | collective-permute-start | bytes 393224 | tf_op jit(solution)/shard_map/ppermute | solution.py:342
  36.2 7.7 %collective-permute-start.10 = (s16[64,1024]{1,0:T(8,128)(2,1)S(1)}, s16[64,1024]{1,0:T(8,128)(2,1)S(1)}, u32[]{:S(2)}, u32[]{:S(2)}) collective-permute-start(s16[64,1024]{1,0:T(8,128)(2,1)S(1)} %get-tuple-element.71), channel_id=1, source_target_pairs={{0,6},{2,4},{4,2},{6,0},{8,14},{10,12},{12,10},{14,8},{1,7},{3,5},... | collective-permute-start | bytes 393224 | tf_op jit(solution)/shard_map/ppermute | solution.py:342
  39.6 5.6 %collective-permute-start.11 = (s16[64,1024]{1,0:T(8,128)(2,1)S(1)}, s16[64,1024]{1,0:T(8,128)(2,1)S(1)}, u32[]{:S(2)}, u32[]{:S(2)}) collective-permute-start(s16[64,1024]{1,0:T(8,128)(2,1)S(1)} %get-tuple-element.72), channel_id=1, source_target_pairs={{0,4},{2,6},{4,0},{6,2},{8,12},{10,14},{12,8},{14,10},{1,5},{3,7},... | collective-permute-start | bytes 393224 | tf_op jit(solution)/shard_map/ppermute | solution.py:342
  39.6 6.2 %collective-permute-start.9 = (s16[64,1024]{1,0:T(8,128)(2,1)S(1)}, s16[64,1024]{1,0:T(8,128)(2,1)S(1)}, u32[]{:S(2)}, u32[]{:S(2)}) collective-permute-start(s16[64,1024]{1,0:T(8,128)(2,1)S(1)} %get-tuple-element.70), channel_id=1, source_target_pairs={{0,2},{2,0},{4,6},{6,4},{8,10},{10,8},{12,14},{14,12},{1,3},{3,1},... | collective-permute-start | bytes 393224 | tf_op jit(solution)/shard_map/ppermute | solution.py:342

commit v24 on v22

--- a/solution.py
+++ b/solution.py
@@ -69,14 +69,8 @@
     return high, low
 
 
-def up_share_kernel(cores, group_ref, core_ref, ranks_ref, up_hbm, out_ref, factor_ref, own_ref, sem):
-    local, rank, share = out_ref.shape
-    at = core_ref[0] * (up_hbm.shape[2] // cores) + group_ref[0] * share
-    copy = pltpu.make_async_copy(
-        up_hbm.at[:, :, pl.ds(pl.multiple_of(at, share), share)], own_ref, sem
-    )
-    copy.start()
-    copy.wait()
+def scale_up_kernel(ranks_ref, own_ref, out_ref, factor_ref):
+    local, rank, _ = out_ref.shape
     for a in range(local):
         used = ranks_ref[a]
 
@@ -88,20 +82,37 @@
         out_ref[a] = (own_ref[a].astype(jnp.float32) * factor((rank, 1), 0)).astype(jnp.bfloat16)
 
 
-def fetch_kernel(group_ref, down_hbm, adapter_hbm, tokens_hbm, share_ref, adapter_ref, tokens_ref, sems):
-    share = share_ref.shape[1]
+def fetch_kernel(
+    columns,
+    group_ref,
+    core_ref,
+    down_hbm,
+    up_hbm,
+    adapter_hbm,
+    tokens_hbm,
+    share_ref,
+    up_ref,
+    adapter_ref,
+    tokens_ref,
+    sems,
+):
+    share, up_share = share_ref.shape[1], up_ref.shape[2]
+    up_at = pl.multiple_of(core_ref[0] * columns + group_ref[0] * up_share, up_share)
     at = pl.multiple_of(group_ref[0] * share, share)
     copies = [
         pltpu.make_async_copy(down_hbm.at[:, pl.ds(at, share), :], share_ref, sems.at[0]),
         pltpu.make_async_copy(adapter_hbm, adapter_ref, sems.at[1]),
     ]
-    parts = sems.shape[0] - 2
+    parts = sems.shape[0] - 3
     part = tokens_ref.shape[0] // parts
     for i in range(parts):
         here = pl.ds(i * part, part)
         copies.append(
-            pltpu.make_async_copy(tokens_hbm.at[here, :], tokens_ref.at[here, :], sems.at[2 + i])
+            pltpu.make_async_copy(tokens_hbm.at[here, :], tokens_ref.at[here, :], sems.at[3 + i])
         )
+    copies.append(
+        pltpu.make_async_copy(up_hbm.at[:, :, pl.ds(up_at, up_share)], up_ref, sems.at[2])
+    )
     for copy in copies:
         copy.start()
     for copy in copies:
@@ -347,20 +358,29 @@
     adapter_row = row_adapters.reshape(1, rows)
     down_share = width // groups
     parts = rows // 16
-    down_part, adapter_now, tokens_now = pl.pallas_call(
-        fetch_kernel,
-        in_specs=[SMEM] + [HBM] * 3,
-        out_specs=[VMEM] * 3,
+    up_share = columns // groups
+    down_part, up_own, adapter_now, tokens_now = pl.pallas_call(
+        functools.partial(fetch_kernel, columns),
+        in_specs=[SMEM] * 2 + [HBM] * 4,
+        out_specs=[VMEM] * 4,
         out_shape=[
             jax.ShapeDtypeStruct((local, down_share, rank), bf16),
+            jax.ShapeDtypeStruct((local, rank, up_share), bf16),
             jax.ShapeDtypeStruct((1, rows), jnp.int32),
             jax.ShapeDtypeStruct((rows, width), bf16),
         ],
-        scratch_shapes=[pltpu.SemaphoreType.DMA((parts + 2,))],
+        scratch_shapes=[pltpu.SemaphoreType.DMA((parts + 3,))],
         compiler_params=params(),
         cost_estimate=cost(0, 4 * (local * rank * down_share + rows * width)),
         name="fetch",
-    )(group, in_hbm(adapter_down), in_hbm(adapter_row), in_hbm(tokens))
+    )(
+        group,
+        core,
+        in_hbm(adapter_down),
+        in_hbm(adapter_up),
+        in_hbm(adapter_row),
+        in_hbm(tokens),
+    )
     picked = pl.pallas_call(
         functools.partial(pick_kernel, pool, local, depth),
         in_specs=[SMEM] + [VMEM] * 2,
@@ -371,24 +391,19 @@
         name="pick",
     )(me, adapter_now, tokens_now)
     far_down = exchange(down_part, "pool", pool, pool // 2)
-    up_share = columns // groups
-    ranks_now, adapter_up_now, _ = lax.optimization_barrier((ranks, adapter_up, picked))
+    ranks_now, up_own, _ = lax.optimization_barrier((ranks, up_own, picked))
     up_part, factor = pl.pallas_call(
-        functools.partial(up_share_kernel, cores),
-        in_specs=[SMEM] * 3 + [HBM],
+        scale_up_kernel,
+        in_specs=[SMEM, VMEM],
         out_specs=[VMEM] * 2,
         out_shape=[
             jax.ShapeDtypeStruct((local, rank, up_share), bf16),
             jax.ShapeDtypeStruct((local, rank), f32),
         ],
-        scratch_shapes=[
-            pltpu.VMEM((local, rank, up_share), bf16),
-            pltpu.SemaphoreType.DMA,
-        ],
         compiler_params=params(),
         cost_estimate=cost(local * rank * up_share, 4 * local * rank * up_share),
-        name="up_share",
-    )(group, core, ranks_now, in_hbm(adapter_up_now))
+        name="scale_up",
+    )(ranks_now, up_own)
     far_up = exchange(up_part, "pool", pool, pool // 2)
 
     order = far_first(buffers)

time: 45.5 us -> 45.5 us (level)
  waiting for transfers between devices: 16.7 us -> 17.6 us
  Pallas kernels: 11.6 us -> 10.7 us
    ppermute x12, waiting for transfers between devices: 16.7 us -> 17.6 us  [exchange(): return lax.ppermute(x, axis, [(p, p ^ j) for p in range(count)])]
    pallas_call x2, Pallas kernels: 2.28 us -> 1.42 us  [the longest x1 1.38 us: body(): pl.pallas_call(functools.partial(fetch_kernel, columns), in_specs=[SMEM]...]
  transfers between devices with their start and end apart: 12 -> 12, of which waited for: 7 -> 7; matrix products, arithmetic and copies ran while one was open for 2% -> 2% of each run, Pallas kernels for 20% -> 18%
where the time goes in v24:
time: 45.5 us; the launch traced here: 45.4 us
  waiting for transfers between devices  17.6 us (39%)
  starting transfers between devices  15.2 us (33%)
  Pallas kernels  10.7 us (24%)
  other arithmetic  1.08 us (2%)
  between operations  0.76 us (2%)
    ppermute x12, waiting for transfers between devices, exchange(): return lax.ppermute(x, axis, [(p, p ^ j) for p in range(count)])  17.6 us
    ppermute x12, starting transfers between devices, exchange(): return lax.ppermute(x, axis, [(p, p ^ j) for p in range(count)])  15.2 us
    pallas_call x1, Pallas kernels, body(): pl.pallas_call(base_kernel, in_specs=[SMEM] + [HBM] * 4, out_specs=[VMEM]...  5.63 us
    pallas_call x1, Pallas kernels, body(): pl.pallas_call(functools.partial(fetch_kernel, columns), in_specs=[SMEM]...  1.38 us
    pallas_call x1, Pallas kernels, body(): pl.pallas_call(functools.partial(finish_kernel, buffers), in_specs=[VMEM]...  1.29 us
  transfers between devices with their start and end apart: 12, of which 7 were waited for; matrix products, arithmetic and copies ran while one was open for 2% of the time, Pallas kernels for 18%

profile of v24, /device:TPU:0, one launch (start us, length us, event | category | flops | bytes accessed | tf_op | source)
XLA Modules:
  0.0 45.4 jit_solution(283464510458120879)
XLA Ops:
  0.0 0.0 copy-start
  0.0 0.0 copy-start.1
  0.0 1.4 %fetch.1 = (bf16[1,1280,128]{2,1,0:T(8,128)(2,1)S(1)}, bf16[1,128,512]{2,1,0:T(8,128)(2,1)S(1)}, s32[1,128]{1,0:T(1,128)S(1)}, bf16[128,2560]{1,0:T(8,128)(2,1)S(1)}) custom-call(s32[1]{0:T(128)} %bitcast.2.group_ref, s32[1]{0:T(128)} %bitcast.3.core_ref, bf16[1,2560,128]{2,1,0:T(8,128)(2,1)} %down_hbm.3, bf16[1,128,2048]{2,1,0:T(8,128)(2,1)} %up_hbm.3, ...), custom_call_target="tpu_custom_call" | custom-call | bytes 1966080 | tf_op jit(solution)/shard_map/fetch/pallas_call | solution.py:362
  1.4 4.1 %collective-permute-start.1 = (bf16[1,1280,128]{2,1,0:T(8,128)(2,1)S(1)}, bf16[1,1280,128]{2,1,0:T(8,128)(2,1)S(1)}, u32[]{:S(2)}, u32[]{:S(2)}) collective-permute-start(bf16[1,1280,128]{2,1,0:T(8,128)(2,1)S(1)} %get-tuple-element.51), channel_id=1, source_target_pairs={{0,8},{2,10},{4,12},{6,14},{8,0},{10,2},{12,4},{14,6},{1,9},{3,11}... | collective-permute-start | bytes 983048 | tf_op jit(solution)/shard_map/ppermute | solution.py:353
  5.5 0.6 %pick.1 = (bf16[64,2560]{1,0:T(8,128)(2,1)S(1)}, bf16[64,2560]{1,0:T(8,128)(2,1)S(1)}, bf16[64,2560]{1,0:T(8,128)(2,1)S(1)}, bf16[64,2560]{1,0:T(8,128)(2,1)S(1)}) custom-call(s32[1]{0:T(128)} %bitcast.me_ref, s32[1,128]{1,0:T(1,128)S(1)} %get-tuple-element.41.adapter_ref, bf16[128,2560]{1,0:T(8,128)(2,1)S(1)} %get-tuple-element.42.tokens_ref), custom_call_target="tpu_custom_call" | custom-call | flops 167772160 | bytes 1966080 | tf_op jit(solution)/shard_map/pick/pallas_call | solution.py:384
  6.1 2.6 %collective-permute-start.2 = (bf16[64,2560]{1,0:T(8,128)(2,1)S(1)}, bf16[64,2560]{1,0:T(8,128)(2,1)S(1)}, u32[]{:S(2)}, u32[]{:S(2)}) collective-permute-start(bf16[64,2560]{1,0:T(8,128)(2,1)S(1)} %get-tuple-element.47), channel_id=1, source_target_pairs={{0,6},{2,4},{4,2},{6,0},{8,14},{10,12},{12,10},{14,8},{1,7},{3,5},... | collective-permute-start | bytes 983048 | tf_op jit(solution)/shard_map/ppermute | solution.py:353
  9.4 0.4 collective-permute-start
  9.8 0.4 collective-permute-start.3
  10.2 0.2 collective-permute-start.4
  10.5 0.7 %convert_element_type.4 = f32[128]{0:T(128)S(1)} convert(s32[128]{0:T(128)} %param.10) | non-fusion elementwise | flops 128 | bytes 1024 | tf_op jit(solution)/shard_map/convert_element_type | solution.py:449
  11.1 5.6 %base.1 = (f32[128,1024]{1,0:T(8,128)S(1)}, f32[128,1024]{1,0:T(8,128)S(1)}, bf16[1,2560,128]{2,1,0:T(8,128)(2,1)S(1)}, bf16[1,128,1024]{2,1,0:T(8,128)(2,1)S(1)}) custom-call(s32[1]{0:T(128)} %bitcast.3.core_ref, bf16[128,2560]{1,0:T(8,128)(2,1)} %tokens_hbm.3, bf16[2560,2048]{1,0:T(8,128)(2,1)} %weight_hbm.1, bf16[1,2560,128]{2,1,0:T(8,128)(2,1)} %down_hbm.3, ...), custom_call_target="tpu_custom_call" | custom-call | flops 1342177280 | bytes 10485760 | tf_op jit(solution)/shard_map/base/pallas_call | solution.py:416
  16.8 5.1 %collective-permute-done.1.refs_4_ = bf16[1,1280,128]{2,1,0:T(8,128)(2,1)S(1)} collective-permute-done((bf16[1,1280,128]{2,1,0:T(8,128)(2,1)S(1)}, bf16[1,1280,128]{2,1,0:T(8,128)(2,1)S(1)}, u32[]{:S(2)}, u32[]{:S(2)}) %collective-permute-start.1) | collective-permute-done | bytes 327712 | tf_op jit(solution)/shard_map/ppermute | solution.py:353
  21.9 2.1 %collective-permute-start.6 = (bf16[1,1280,128]{2,1,0:T(8,128)(2,1)S(1)}, bf16[1,1280,128]{2,1,0:T(8,128)(2,1)S(1)}, u32[]{:S(2)}, u32[]{:S(2)}) collective-permute-start(bf16[1,1280,128]{2,1,0:T(8,128)(2,1)S(1)} %collective-permute-done.1.refs_4_), channel_id=1, source_target_pairs={{0,16},{16,0},{1,17},{17,1},{2,18},{18,2},{3,19},{19,3},{4,20},{20... | collective-permute-start | bytes 983048 | tf_op jit(solution)/shard_map/ppermute | solution.py:353
  24.1 0.3 fusion
  24.4 1.6 %collective-permute-done.refs_0_ = bf16[1,128,512]{2,1,0:T(8,128)(2,1)S(1)} collective-permute-done((bf16[1,128,512]{2,1,0:T(8,128)(2,1)S(1)}, bf16[1,128,512]{2,1,0:T(8,128)(2,1)S(1)}, u32[]{:S(2)}, u32[]{:S(2)}) %collective-permute-start) | collective-permute-done | bytes 131104 | tf_op jit(solution)/shard_map/ppermute | solution.py:353
  26.0 0.0 collective-permute-done.2.refs_1_
  26.0 0.0 collective-permute-start.5
  26.0 0.1 pad_maximum_fusion
  26.1 1.6 %collective-permute-start.8 = (bf16[1,128,512]{2,1,0:T(8,128)(2,1)S(1)}, bf16[1,128,512]{2,1,0:T(8,128)(2,1)S(1)}, u32[]{:S(2)}, u32[]{:S(2)}) collective-permute-start(bf16[1,128,512]{2,1,0:T(8,128)(2,1)S(1)} %collective-permute-done.refs_0_), channel_id=1, source_target_pairs={{0,16},{16,0},{1,17},{17,1},{2,18},{18,2},{3,19},{19,3},{4,20},{20... | collective-permute-start | bytes 393224 | tf_op jit(solution)/shard_map/ppermute | solution.py:353
  27.7 4.3 %collective-permute-done.3.refs_2_ = bf16[64,2560]{1,0:T(8,128)(2,1)S(1)} collective-permute-done((bf16[64,2560]{1,0:T(8,128)(2,1)S(1)}, bf16[64,2560]{1,0:T(8,128)(2,1)S(1)}, u32[]{:S(2)}, u32[]{:S(2)}) %collective-permute-start.3) | collective-permute-done | bytes 327712 | tf_op jit(solution)/shard_map/ppermute | solution.py:353
  32.0 0.0 collective-permute-done.4.refs_3_
  32.0 0.0 collective-permute-done.6.refs_5_
  32.0 0.5 %down.1.low_ref = f32[256,128]{1,0:T(8,128)S(1)} custom-call(s32[1]{0:T(128)} %bitcast.2.group_ref, bf16[1,2560,128]{2,1,0:T(8,128)(2,1)S(1)} %get-tuple-element.62.down_ref, bf16[64,2560]{1,0:T(8,128)(2,1)S(1)} %get-tuple-element.63.refs_0_, bf16[64,2560]{1,0:T(8,128)(2,1)S(1)} %collective-permute-done.2.refs_1_, ...), custom_call_target="tpu_custom_call" | custom-call | flops 335544320 | bytes 1966080 | tf_op jit(solution)/shard_map/down/pallas_call | solution.py:458
  32.6 0.1 collective-permute-start.7
  32.6 0.0 collective-permute-done.8.refs_1_
  32.6 1.3 %collective-permute-done.7.other_ref = f32[256,128]{1,0:T(8,128)S(1)} collective-permute-done((f32[256,128]{1,0:T(8,128)S(1)}, f32[256,128]{1,0:T(8,128)S(1)}, u32[]{:S(2)}, u32[]{:S(2)}) %collective-permute-start.7) | collective-permute-done | bytes 131104 | tf_op jit(solution)/shard_map/ppermute | solution.py:353
  34.0 0.8 %up.1 = (s16[64,1024]{1,0:T(8,128)(2,1)S(1)}, s16[64,1024]{1,0:T(8,128)(2,1)S(1)}, s16[64,1024]{1,0:T(8,128)(2,1)S(1)}, s16[64,1024]{1,0:T(8,128)(2,1)S(1)}) custom-call(s32[1]{0:T(128)} %bitcast.2.group_ref, f32[256,128]{1,0:T(8,128)S(1)} %down.1.low_ref, f32[256,128]{1,0:T(8,128)S(1)} %collective-permute-done.7.other_ref, ...), custom_call_target="tpu_custom_call" | custom-call | flops 268435456 | bytes 524288 | tf_op jit(solution)/shard_map/up/pallas_call | solution.py:469
  34.8 1.3 %collective-permute-start.10 = (s16[64,1024]{1,0:T(8,128)(2,1)S(1)}, s16[64,1024]{1,0:T(8,128)(2,1)S(1)}, u32[]{:S(2)}, u32[]{:S(2)}) collective-permute-start(s16[64,1024]{1,0:T(8,128)(2,1)S(1)} %get-tuple-element.75), channel_id=1, source_target_pairs={{0,6},{2,4},{4,2},{6,0},{8,14},{10,12},{12,10},{14,8},{1,7},{3,5},... | collective-permute-start | bytes 393224 | tf_op jit(solution)/shard_map/ppermute | solution.py:353
  36.0 0.8 %collective-permute-start.11 = (s16[64,1024]{1,0:T(8,128)(2,1)S(1)}, s16[64,1024]{1,0:T(8,128)(2,1)S(1)}, u32[]{:S(2)}, u32[]{:S(2)}) collective-permute-start(s16[64,1024]{1,0:T(8,128)(2,1)S(1)} %get-tuple-element.76), channel_id=1, source_target_pairs={{0,4},{2,6},{4,0},{6,2},{8,12},{10,14},{12,8},{14,10},{1,5},{3,7},... | collective-permute-start | bytes 393224 | tf_op jit(solution)/shard_map/ppermute | solution.py:353
  36.8 1.5 %collective-permute-start.9 = (s16[64,1024]{1,0:T(8,128)(2,1)S(1)}, s16[64,1024]{1,0:T(8,128)(2,1)S(1)}, u32[]{:S(2)}, u32[]{:S(2)}) collective-permute-start(s16[64,1024]{1,0:T(8,128)(2,1)S(1)} %get-tuple-element.74), channel_id=1, source_target_pairs={{0,2},{2,0},{4,6},{6,4},{8,10},{10,8},{12,14},{14,12},{1,3},{3,1},... | collective-permute-start | bytes 393224 | tf_op jit(solution)/shard_map/ppermute | solution.py:353
  38.3 0.0 copy-done.1
  38.3 0.0 collective-permute-done.5.other_ref
  38.3 0.0 copy-done
  38.3 0.5 %start_rows.1 = (f32[128,1024]{1,0:T(8,128)S(1)}, bf16[128,192]{1,0:T(8,128)(2,1)S(1)}) custom-call(s32[1]{0:T(128)} %bitcast.me_ref, s32[1,128]{1,0:T(1,128)S(1)} %bitcast.9, f32[128,1024]{1,0:T(8,128)S(1)} %get-tuple-element.60.mine_ref, f32[128,1024]{1,0:T(8,128)S(1)} %collective-permute-done.5.other_ref, s16[64,1024]{1,0:T(8,128)(2,1)S(1)} %get-tuple-element.69.own_ref), custom_call_target="tpu_custom_call" | custom-call | flops 33554432 | bytes 1572864 | tf_op jit(solution)/shard_map/start_rows/pallas_call | solution.py:482
  38.9 3.2 %collective-permute-done.10.refs_1_ = s16[64,1024]{1,0:T(8,128)(2,1)S(1)} collective-permute-done((s16[64,1024]{1,0:T(8,128)(2,1)S(1)}, s16[64,1024]{1,0:T(8,128)(2,1)S(1)}, u32[]{:S(2)}, u32[]{:S(2)}) %collective-permute-start.10) | collective-permute-done | bytes 131104 | tf_op jit(solution)/shard_map/ppermute | solution.py:353
  42.1 1.1 %collective-permute-done.11.refs_2_ = s16[64,1024]{1,0:T(8,128)(2,1)S(1)} collective-permute-done((s16[64,1024]{1,0:T(8,128)(2,1)S(1)}, s16[64,1024]{1,0:T(8,128)(2,1)S(1)}, u32[]{:S(2)}, u32[]{:S(2)}) %collective-permute-start.11) | collective-permute-done | bytes 131104 | tf_op jit(solution)/shard_map/ppermute | solution.py:353
  43.2 0.9 %collective-permute-done.9.refs_0_ = s16[64,1024]{1,0:T(8,128)(2,1)S(1)} collective-permute-done((s16[64,1024]{1,0:T(8,128)(2,1)S(1)}, s16[64,1024]{1,0:T(8,128)(2,1)S(1)}, u32[]{:S(2)}, u32[]{:S(2)}) %collective-permute-start.9) | collective-permute-done | bytes 131104 | tf_op jit(solution)/shard_map/ppermute | solution.py:353
  44.1 1.3 %finish.1 = bf16[1024,128]{1,0:T(8,128)(2,1)} custom-call(f32[128,1024]{1,0:T(8,128)S(1)} %get-tuple-element.70.partial_ref, bf16[128,192]{1,0:T(8,128)(2,1)S(1)} %get-tuple-element.71.picker_ref, f32[128,128]{1,0:T(8,128)S(1)} %get-tuple-element.72.cos_ref, f32[128,128]{1,0:T(8,128)S(1)} %get-tuple-element.73.sin_ref, ...), custom_call_target="tpu_custom_call" | custom-call | flops 134217728 | bytes 524288 | tf_op jit(solution)/shard_map/finish/pallas_call | solution.py:494
  (3 shorter events, 0.0 us)
Async XLA Ops:
  0.0 38.3 %copy-start = (s32[128,1]{0,1:T(1,128)S(1)}, s32[128,1]{0,1:T(1,128)}, u32[]{:S(2)}) copy-start(s32[128,1]{0,1:T(1,128)} %param.9) | copy-start | bytes 1540
  0.0 38.3 %copy-start.1 = (bf16[128]{0:T(256)(128)(2,1)S(1)}, bf16[128]{0:T(256)(128)(2,1)}, u32[]{:S(2)}) copy-start(bf16[128]{0:T(256)(128)(2,1)} %param.15) | copy-start | bytes 772
  1.4 20.5 %collective-permute-start.1 = (bf16[1,1280,128]{2,1,0:T(8,128)(2,1)S(1)}, bf16[1,1280,128]{2,1,0:T(8,128)(2,1)S(1)}, u32[]{:S(2)}, u32[]{:S(2)}) collective-permute-start(bf16[1,1280,128]{2,1,0:T(8,128)(2,1)S(1)} %get-tuple-element.51), channel_id=1, source_target_pairs={{0,8},{2,10},{4,12},{6,14},{8,0},{10,2},{12,4},{14,6},{1,9},{3,11}... | collective-permute-start | bytes 983048 | tf_op jit(solution)/shard_map/ppermute | solution.py:353
  6.1 19.9 %collective-permute-start.2 = (bf16[64,2560]{1,0:T(8,128)(2,1)S(1)}, bf16[64,2560]{1,0:T(8,128)(2,1)S(1)}, u32[]{:S(2)}, u32[]{:S(2)}) collective-permute-start(bf16[64,2560]{1,0:T(8,128)(2,1)S(1)} %get-tuple-element.47), channel_id=1, source_target_pairs={{0,6},{2,4},{4,2},{6,0},{8,14},{10,12},{12,10},{14,8},{1,7},{3,5},... | collective-permute-start | bytes 983048 | tf_op jit(solution)/shard_map/ppermute | solution.py:353
  9.4 16.6 %collective-permute-start = (bf16[1,128,512]{2,1,0:T(8,128)(2,1)S(1)}, bf16[1,128,512]{2,1,0:T(8,128)(2,1)S(1)}, u32[]{:S(2)}, u32[]{:S(2)}) collective-permute-start(bf16[1,128,512]{2,1,0:T(8,128)(2,1)S(1)} %get-tuple-element.50), channel_id=1, source_target_pairs={{0,8},{2,10},{4,12},{6,14},{8,0},{10,2},{12,4},{14,6},{1,9},{3,11}... | collective-permute-start | bytes 393224 | tf_op jit(solution)/shard_map/ppermute | solution.py:353
  9.8 22.2 %collective-permute-start.3 = (bf16[64,2560]{1,0:T(8,128)(2,1)S(1)}, bf16[64,2560]{1,0:T(8,128)(2,1)S(1)}, u32[]{:S(2)}, u32[]{:S(2)}) collective-permute-start(bf16[64,2560]{1,0:T(8,128)(2,1)S(1)} %get-tuple-element.57), channel_id=1, source_target_pairs={{0,4},{2,6},{4,0},{6,2},{8,12},{10,14},{12,8},{14,10},{1,5},{3,7},... | collective-permute-start | bytes 983048 | tf_op jit(solution)/shard_map/ppermute | solution.py:353
  10.2 21.8 %collective-permute-start.4 = (bf16[64,2560]{1,0:T(8,128)(2,1)S(1)}, bf16[64,2560]{1,0:T(8,128)(2,1)S(1)}, u32[]{:S(2)}, u32[]{:S(2)}) collective-permute-start(bf16[64,2560]{1,0:T(8,128)(2,1)S(1)} %get-tuple-element.58), channel_id=1, source_target_pairs={{0,2},{2,0},{4,6},{6,4},{8,10},{10,8},{12,14},{14,12},{1,3},{3,1},... | collective-permute-start | bytes 983048 | tf_op jit(solution)/shard_map/ppermute | solution.py:353
  21.9 10.1 %collective-permute-start.6 = (bf16[1,1280,128]{2,1,0:T(8,128)(2,1)S(1)}, bf16[1,1280,128]{2,1,0:T(8,128)(2,1)S(1)}, u32[]{:S(2)}, u32[]{:S(2)}) collective-permute-start(bf16[1,1280,128]{2,1,0:T(8,128)(2,1)S(1)} %collective-permute-done.1.refs_4_), channel_id=1, source_target_pairs={{0,16},{16,0},{1,17},{17,1},{2,18},{18,2},{3,19},{19,3},{4,20},{20... | collective-permute-start | bytes 983048 | tf_op jit(solution)/shard_map/ppermute | solution.py:353
  26.0 12.3 %collective-permute-start.5 = (f32[128,1024]{1,0:T(8,128)S(1)}, f32[128,1024]{1,0:T(8,128)S(1)}, u32[]{:S(2)}, u32[]{:S(2)}) collective-permute-start(f32[128,1024]{1,0:T(8,128)S(1)} %get-tuple-element.61), channel_id=1, source_target_pairs={{0,1},{1,0},{2,3},{3,2},{4,5},{5,4},{6,7},{7,6},{8,9},{9,8},{10,11... | collective-permute-start | bytes 1572872 | tf_op jit(solution)/shard_map/ppermute | solution.py:353
  26.1 6.5 %collective-permute-start.8 = (bf16[1,128,512]{2,1,0:T(8,128)(2,1)S(1)}, bf16[1,128,512]{2,1,0:T(8,128)(2,1)S(1)}, u32[]{:S(2)}, u32[]{:S(2)}) collective-permute-start(bf16[1,128,512]{2,1,0:T(8,128)(2,1)S(1)} %collective-permute-done.refs_0_), channel_id=1, source_target_pairs={{0,16},{16,0},{1,17},{17,1},{2,18},{18,2},{3,19},{19,3},{4,20},{20... | collective-permute-start | bytes 393224 | tf_op jit(solution)/shard_map/ppermute | solution.py:353
  32.6 1.4 %collective-permute-start.7 = (f32[256,128]{1,0:T(8,128)S(1)}, f32[256,128]{1,0:T(8,128)S(1)}, u32[]{:S(2)}, u32[]{:S(2)}) collective-permute-start(f32[256,128]{1,0:T(8,128)S(1)} %down.1.low_ref), channel_id=1, source_target_pairs={{0,1},{1,0},{2,3},{3,2},{4,5},{5,4},{6,7},{7,6},{8,9},{9,8},{10,11... | collective-permute-start | bytes 393224 | tf_op jit(solution)/shard_map/ppermute | solution.py:353
  34.8 7.3 %collective-permute-start.10 = (s16[64,1024]{1,0:T(8,128)(2,1)S(1)}, s16[64,1024]{1,0:T(8,128)(2,1)S(1)}, u32[]{:S(2)}, u32[]{:S(2)}) collective-permute-start(s16[64,1024]{1,0:T(8,128)(2,1)S(1)} %get-tuple-element.75), channel_id=1, source_target_pairs={{0,6},{2,4},{4,2},{6,0},{8,14},{10,12},{12,10},{14,8},{1,7},{3,5},... | collective-permute-start | bytes 393224 | tf_op jit(solution)/shard_map/ppermute | solution.py:353
  36.0 7.2 %collective-permute-start.11 = (s16[64,1024]{1,0:T(8,128)(2,1)S(1)}, s16[64,1024]{1,0:T(8,128)(2,1)S(1)}, u32[]{:S(2)}, u32[]{:S(2)}) collective-permute-start(s16[64,1024]{1,0:T(8,128)(2,1)S(1)} %get-tuple-element.76), channel_id=1, source_target_pairs={{0,4},{2,6},{4,0},{6,2},{8,12},{10,14},{12,8},{14,10},{1,5},{3,7},... | collective-permute-start | bytes 393224 | tf_op jit(solution)/shard_map/ppermute | solution.py:353
  36.8 7.2 %collective-permute-start.9 = (s16[64,1024]{1,0:T(8,128)(2,1)S(1)}, s16[64,1024]{1,0:T(8,128)(2,1)S(1)}, u32[]{:S(2)}, u32[]{:S(2)}) collective-permute-start(s16[64,1024]{1,0:T(8,128)(2,1)S(1)} %get-tuple-element.74), channel_id=1, source_target_pairs={{0,2},{2,0},{4,6},{6,4},{8,10},{10,8},{12,14},{14,12},{1,3},{3,1},... | collective-permute-start | bytes 393224 | tf_op jit(solution)/shard_map/ppermute | solution.py:353

commit v25 on v24

--- a/solution.py
+++ b/solution.py
@@ -242,8 +242,7 @@
         term = term_ref[j * size : (j + 1) * size, :]
         top = jnp.max(jnp.abs(term), axis=1, keepdims=True)
         exponent = jnp.ceil(jnp.log2(jnp.maximum(top, 1e-30)) + 1e-3)
-        code = jnp.clip(jnp.round(term * jnp.exp2(15.0 - exponent)), -32767.0, 32767.0)
-        code = code.astype(jnp.int32)
+        code = jnp.round(term * jnp.exp2(15.0 - exponent)).astype(jnp.int32)
         biased = exponent.astype(jnp.int32) + EXPONENT_BIAS
         first = code[:, :LANES]
         marked = (first & -2) | ((biased >> jnp.minimum(lane, EXPONENT_BITS - 1)) & 1)

time: 45.5 us -> 45.5 us (level)
  no operation moved by 1% of the time
where the time goes in v25:
time: 45.5 us; the launch traced here: 45.3 us
  waiting for transfers between devices  17.6 us (39%)
  starting transfers between devices  15.2 us (33%)
  Pallas kernels  10.7 us (24%)
  other arithmetic  1.08 us (2%)
  between operations  0.76 us (2%)
    ppermute x12, waiting for transfers between devices, exchange(): return lax.ppermute(x, axis, [(p, p ^ j) for p in range(count)])  17.6 us
    ppermute x12, starting transfers between devices, exchange(): return lax.ppermute(x, axis, [(p, p ^ j) for p in range(count)])  15.2 us
    pallas_call x1, Pallas kernels, body(): pl.pallas_call(base_kernel, in_specs=[SMEM] + [HBM] * 4, out_specs=[VMEM]...  5.63 us
    pallas_call x1, Pallas kernels, body(): pl.pallas_call(functools.partial(fetch_kernel, columns), in_specs=[SMEM]...  1.38 us
    pallas_call x1, Pallas kernels, body(): pl.pallas_call(functools.partial(finish_kernel, buffers), in_specs=[VMEM]...  1.29 us
  transfers between devices with their start and end apart: 12, of which 7 were waited for; matrix products, arithmetic and copies ran while one was open for 2% of the time, Pallas kernels for 18%

profile of v25, /device:TPU:0, one launch (start us, length us, event | category | flops | bytes accessed | tf_op | source)
XLA Modules:
  0.0 45.3 jit_solution(10929264582317450738)
XLA Ops:
  0.0 0.0 copy-start
  0.0 0.0 copy-start.1
  0.0 1.4 %fetch.1 = (bf16[1,1280,128]{2,1,0:T(8,128)(2,1)S(1)}, bf16[1,128,512]{2,1,0:T(8,128)(2,1)S(1)}, s32[1,128]{1,0:T(1,128)S(1)}, bf16[128,2560]{1,0:T(8,128)(2,1)S(1)}) custom-call(s32[1]{0:T(128)} %bitcast.2.group_ref, s32[1]{0:T(128)} %bitcast.3.core_ref, bf16[1,2560,128]{2,1,0:T(8,128)(2,1)} %down_hbm.3, bf16[1,128,2048]{2,1,0:T(8,128)(2,1)} %up_hbm.3, ...), custom_call_target="tpu_custom_call" | custom-call | bytes 1966080 | tf_op jit(solution)/shard_map/fetch/pallas_call | solution.py:361
  1.4 4.1 %collective-permute-start.1 = (bf16[1,1280,128]{2,1,0:T(8,128)(2,1)S(1)}, bf16[1,1280,128]{2,1,0:T(8,128)(2,1)S(1)}, u32[]{:S(2)}, u32[]{:S(2)}) collective-permute-start(bf16[1,1280,128]{2,1,0:T(8,128)(2,1)S(1)} %get-tuple-element.51), channel_id=1, source_target_pairs={{0,8},{2,10},{4,12},{6,14},{8,0},{10,2},{12,4},{14,6},{1,9},{3,11}... | collective-permute-start | bytes 983048 | tf_op jit(solution)/shard_map/ppermute | solution.py:352
  5.5 0.6 %pick.1 = (bf16[64,2560]{1,0:T(8,128)(2,1)S(1)}, bf16[64,2560]{1,0:T(8,128)(2,1)S(1)}, bf16[64,2560]{1,0:T(8,128)(2,1)S(1)}, bf16[64,2560]{1,0:T(8,128)(2,1)S(1)}) custom-call(s32[1]{0:T(128)} %bitcast.me_ref, s32[1,128]{1,0:T(1,128)S(1)} %get-tuple-element.41.adapter_ref, bf16[128,2560]{1,0:T(8,128)(2,1)S(1)} %get-tuple-element.42.tokens_ref), custom_call_target="tpu_custom_call" | custom-call | flops 167772160 | bytes 1966080 | tf_op jit(solution)/shard_map/pick/pallas_call | solution.py:383
  6.1 2.6 %collective-permute-start.2 = (bf16[64,2560]{1,0:T(8,128)(2,1)S(1)}, bf16[64,2560]{1,0:T(8,128)(2,1)S(1)}, u32[]{:S(2)}, u32[]{:S(2)}) collective-permute-start(bf16[64,2560]{1,0:T(8,128)(2,1)S(1)} %get-tuple-element.47), channel_id=1, source_target_pairs={{0,6},{2,4},{4,2},{6,0},{8,14},{10,12},{12,10},{14,8},{1,7},{3,5},... | collective-permute-start | bytes 983048 | tf_op jit(solution)/shard_map/ppermute | solution.py:352
  9.4 0.4 collective-permute-start
  9.8 0.4 collective-permute-start.3
  10.2 0.2 collective-permute-start.4
  10.5 0.7 %convert_element_type.4 = f32[128]{0:T(128)S(1)} convert(s32[128]{0:T(128)} %param.10) | non-fusion elementwise | flops 128 | bytes 1024 | tf_op jit(solution)/shard_map/convert_element_type | solution.py:448
  11.1 5.6 %base.1 = (f32[128,1024]{1,0:T(8,128)S(1)}, f32[128,1024]{1,0:T(8,128)S(1)}, bf16[1,2560,128]{2,1,0:T(8,128)(2,1)S(1)}, bf16[1,128,1024]{2,1,0:T(8,128)(2,1)S(1)}) custom-call(s32[1]{0:T(128)} %bitcast.3.core_ref, bf16[128,2560]{1,0:T(8,128)(2,1)} %tokens_hbm.3, bf16[2560,2048]{1,0:T(8,128)(2,1)} %weight_hbm.1, bf16[1,2560,128]{2,1,0:T(8,128)(2,1)} %down_hbm.3, ...), custom_call_target="tpu_custom_call" | custom-call | flops 1342177280 | bytes 10485760 | tf_op jit(solution)/shard_map/base/pallas_call | solution.py:415
  16.8 5.1 %collective-permute-done.1.refs_4_ = bf16[1,1280,128]{2,1,0:T(8,128)(2,1)S(1)} collective-permute-done((bf16[1,1280,128]{2,1,0:T(8,128)(2,1)S(1)}, bf16[1,1280,128]{2,1,0:T(8,128)(2,1)S(1)}, u32[]{:S(2)}, u32[]{:S(2)}) %collective-permute-start.1) | collective-permute-done | bytes 327712 | tf_op jit(solution)/shard_map/ppermute | solution.py:352
  21.9 2.1 %collective-permute-start.6 = (bf16[1,1280,128]{2,1,0:T(8,128)(2,1)S(1)}, bf16[1,1280,128]{2,1,0:T(8,128)(2,1)S(1)}, u32[]{:S(2)}, u32[]{:S(2)}) collective-permute-start(bf16[1,1280,128]{2,1,0:T(8,128)(2,1)S(1)} %collective-permute-done.1.refs_4_), channel_id=1, source_target_pairs={{0,16},{16,0},{1,17},{17,1},{2,18},{18,2},{3,19},{19,3},{4,20},{20... | collective-permute-start | bytes 983048 | tf_op jit(solution)/shard_map/ppermute | solution.py:352
  24.1 0.3 fusion
  24.4 1.6 %collective-permute-done.refs_0_ = bf16[1,128,512]{2,1,0:T(8,128)(2,1)S(1)} collective-permute-done((bf16[1,128,512]{2,1,0:T(8,128)(2,1)S(1)}, bf16[1,128,512]{2,1,0:T(8,128)(2,1)S(1)}, u32[]{:S(2)}, u32[]{:S(2)}) %collective-permute-start) | collective-permute-done | bytes 131104 | tf_op jit(solution)/shard_map/ppermute | solution.py:352
  26.0 0.0 collective-permute-done.2.refs_1_
  26.0 0.0 collective-permute-start.5
  26.0 0.1 pad_maximum_fusion
  26.1 1.6 %collective-permute-start.8 = (bf16[1,128,512]{2,1,0:T(8,128)(2,1)S(1)}, bf16[1,128,512]{2,1,0:T(8,128)(2,1)S(1)}, u32[]{:S(2)}, u32[]{:S(2)}) collective-permute-start(bf16[1,128,512]{2,1,0:T(8,128)(2,1)S(1)} %collective-permute-done.refs_0_), channel_id=1, source_target_pairs={{0,16},{16,0},{1,17},{17,1},{2,18},{18,2},{3,19},{19,3},{4,20},{20... | collective-permute-start | bytes 393224 | tf_op jit(solution)/shard_map/ppermute | solution.py:352
  27.7 4.3 %collective-permute-done.3.refs_2_ = bf16[64,2560]{1,0:T(8,128)(2,1)S(1)} collective-permute-done((bf16[64,2560]{1,0:T(8,128)(2,1)S(1)}, bf16[64,2560]{1,0:T(8,128)(2,1)S(1)}, u32[]{:S(2)}, u32[]{:S(2)}) %collective-permute-start.3) | collective-permute-done | bytes 327712 | tf_op jit(solution)/shard_map/ppermute | solution.py:352
  32.0 0.0 collective-permute-done.4.refs_3_
  32.0 0.0 collective-permute-done.6.refs_5_
  32.0 0.5 %down.1.low_ref = f32[256,128]{1,0:T(8,128)S(1)} custom-call(s32[1]{0:T(128)} %bitcast.2.group_ref, bf16[1,2560,128]{2,1,0:T(8,128)(2,1)S(1)} %get-tuple-element.62.down_ref, bf16[64,2560]{1,0:T(8,128)(2,1)S(1)} %get-tuple-element.63.refs_0_, bf16[64,2560]{1,0:T(8,128)(2,1)S(1)} %collective-permute-done.2.refs_1_, ...), custom_call_target="tpu_custom_call" | custom-call | flops 335544320 | bytes 1966080 | tf_op jit(solution)/shard_map/down/pallas_call | solution.py:457
  32.6 0.1 collective-permute-start.7
  32.6 0.0 collective-permute-done.8.refs_1_
  32.6 1.3 %collective-permute-done.7.other_ref = f32[256,128]{1,0:T(8,128)S(1)} collective-permute-done((f32[256,128]{1,0:T(8,128)S(1)}, f32[256,128]{1,0:T(8,128)S(1)}, u32[]{:S(2)}, u32[]{:S(2)}) %collective-permute-start.7) | collective-permute-done | bytes 131104 | tf_op jit(solution)/shard_map/ppermute | solution.py:352
  34.0 0.7 %up.1 = (s16[64,1024]{1,0:T(8,128)(2,1)S(1)}, s16[64,1024]{1,0:T(8,128)(2,1)S(1)}, s16[64,1024]{1,0:T(8,128)(2,1)S(1)}, s16[64,1024]{1,0:T(8,128)(2,1)S(1)}) custom-call(s32[1]{0:T(128)} %bitcast.2.group_ref, f32[256,128]{1,0:T(8,128)S(1)} %down.1.low_ref, f32[256,128]{1,0:T(8,128)S(1)} %collective-permute-done.7.other_ref, ...), custom_call_target="tpu_custom_call" | custom-call | flops 268435456 | bytes 524288 | tf_op jit(solution)/shard_map/up/pallas_call | solution.py:468
  34.7 1.3 %collective-permute-start.10 = (s16[64,1024]{1,0:T(8,128)(2,1)S(1)}, s16[64,1024]{1,0:T(8,128)(2,1)S(1)}, u32[]{:S(2)}, u32[]{:S(2)}) collective-permute-start(s16[64,1024]{1,0:T(8,128)(2,1)S(1)} %get-tuple-element.75), channel_id=1, source_target_pairs={{0,6},{2,4},{4,2},{6,0},{8,14},{10,12},{12,10},{14,8},{1,7},{3,5},... | collective-permute-start | bytes 393224 | tf_op jit(solution)/shard_map/ppermute | solution.py:352
  36.0 0.8 %collective-permute-start.11 = (s16[64,1024]{1,0:T(8,128)(2,1)S(1)}, s16[64,1024]{1,0:T(8,128)(2,1)S(1)}, u32[]{:S(2)}, u32[]{:S(2)}) collective-permute-start(s16[64,1024]{1,0:T(8,128)(2,1)S(1)} %get-tuple-element.76), channel_id=1, source_target_pairs={{0,4},{2,6},{4,0},{6,2},{8,12},{10,14},{12,8},{14,10},{1,5},{3,7},... | collective-permute-start | bytes 393224 | tf_op jit(solution)/shard_map/ppermute | solution.py:352
  36.8 1.5 %collective-permute-start.9 = (s16[64,1024]{1,0:T(8,128)(2,1)S(1)}, s16[64,1024]{1,0:T(8,128)(2,1)S(1)}, u32[]{:S(2)}, u32[]{:S(2)}) collective-permute-start(s16[64,1024]{1,0:T(8,128)(2,1)S(1)} %get-tuple-element.74), channel_id=1, source_target_pairs={{0,2},{2,0},{4,6},{6,4},{8,10},{10,8},{12,14},{14,12},{1,3},{3,1},... | collective-permute-start | bytes 393224 | tf_op jit(solution)/shard_map/ppermute | solution.py:352
  38.3 0.0 copy-done.1
  38.3 0.0 collective-permute-done.5.other_ref
  38.3 0.0 copy-done
  38.3 0.5 %start_rows.1 = (f32[128,1024]{1,0:T(8,128)S(1)}, bf16[128,192]{1,0:T(8,128)(2,1)S(1)}) custom-call(s32[1]{0:T(128)} %bitcast.me_ref, s32[1,128]{1,0:T(1,128)S(1)} %bitcast.9, f32[128,1024]{1,0:T(8,128)S(1)} %get-tuple-element.60.mine_ref, f32[128,1024]{1,0:T(8,128)S(1)} %collective-permute-done.5.other_ref, s16[64,1024]{1,0:T(8,128)(2,1)S(1)} %get-tuple-element.69.own_ref), custom_call_target="tpu_custom_call" | custom-call | flops 33554432 | bytes 1572864 | tf_op jit(solution)/shard_map/start_rows/pallas_call | solution.py:481
  38.8 3.2 %collective-permute-done.10.refs_1_ = s16[64,1024]{1,0:T(8,128)(2,1)S(1)} collective-permute-done((s16[64,1024]{1,0:T(8,128)(2,1)S(1)}, s16[64,1024]{1,0:T(8,128)(2,1)S(1)}, u32[]{:S(2)}, u32[]{:S(2)}) %collective-permute-start.10) | collective-permute-done | bytes 131104 | tf_op jit(solution)/shard_map/ppermute | solution.py:352
  42.0 1.1 %collective-permute-done.11.refs_2_ = s16[64,1024]{1,0:T(8,128)(2,1)S(1)} collective-permute-done((s16[64,1024]{1,0:T(8,128)(2,1)S(1)}, s16[64,1024]{1,0:T(8,128)(2,1)S(1)}, u32[]{:S(2)}, u32[]{:S(2)}) %collective-permute-start.11) | collective-permute-done | bytes 131104 | tf_op jit(solution)/shard_map/ppermute | solution.py:352
  43.1 0.9 %collective-permute-done.9.refs_0_ = s16[64,1024]{1,0:T(8,128)(2,1)S(1)} collective-permute-done((s16[64,1024]{1,0:T(8,128)(2,1)S(1)}, s16[64,1024]{1,0:T(8,128)(2,1)S(1)}, u32[]{:S(2)}, u32[]{:S(2)}) %collective-permute-start.9) | collective-permute-done | bytes 131104 | tf_op jit(solution)/shard_map/ppermute | solution.py:352
  44.0 1.3 %finish.1 = bf16[1024,128]{1,0:T(8,128)(2,1)} custom-call(f32[128,1024]{1,0:T(8,128)S(1)} %get-tuple-element.70.partial_ref, bf16[128,192]{1,0:T(8,128)(2,1)S(1)} %get-tuple-element.71.picker_ref, f32[128,128]{1,0:T(8,128)S(1)} %get-tuple-element.72.cos_ref, f32[128,128]{1,0:T(8,128)S(1)} %get-tuple-element.73.sin_ref, ...), custom_call_target="tpu_custom_call" | custom-call | flops 134217728 | bytes 524288 | tf_op jit(solution)/shard_map/finish/pallas_call | solution.py:493
  (3 shorter events, 0.0 us)
Async XLA Ops:
  0.0 38.3 %copy-start = (s32[128,1]{0,1:T(1,128)S(1)}, s32[128,1]{0,1:T(1,128)}, u32[]{:S(2)}) copy-start(s32[128,1]{0,1:T(1,128)} %param.9) | copy-start | bytes 1540
  0.0 38.3 %copy-start.1 = (bf16[128]{0:T(256)(128)(2,1)S(1)}, bf16[128]{0:T(256)(128)(2,1)}, u32[]{:S(2)}) copy-start(bf16[128]{0:T(256)(128)(2,1)} %param.15) | copy-start | bytes 772
  1.4 20.5 %collective-permute-start.1 = (bf16[1,1280,128]{2,1,0:T(8,128)(2,1)S(1)}, bf16[1,1280,128]{2,1,0:T(8,128)(2,1)S(1)}, u32[]{:S(2)}, u32[]{:S(2)}) collective-permute-start(bf16[1,1280,128]{2,1,0:T(8,128)(2,1)S(1)} %get-tuple-element.51), channel_id=1, source_target_pairs={{0,8},{2,10},{4,12},{6,14},{8,0},{10,2},{12,4},{14,6},{1,9},{3,11}... | collective-permute-start | bytes 983048 | tf_op jit(solution)/shard_map/ppermute | solution.py:352
  6.1 19.9 %collective-permute-start.2 = (bf16[64,2560]{1,0:T(8,128)(2,1)S(1)}, bf16[64,2560]{1,0:T(8,128)(2,1)S(1)}, u32[]{:S(2)}, u32[]{:S(2)}) collective-permute-start(bf16[64,2560]{1,0:T(8,128)(2,1)S(1)} %get-tuple-element.47), channel_id=1, source_target_pairs={{0,6},{2,4},{4,2},{6,0},{8,14},{10,12},{12,10},{14,8},{1,7},{3,5},... | collective-permute-start | bytes 983048 | tf_op jit(solution)/shard_map/ppermute | solution.py:352
  9.4 16.6 %collective-permute-start = (bf16[1,128,512]{2,1,0:T(8,128)(2,1)S(1)}, bf16[1,128,512]{2,1,0:T(8,128)(2,1)S(1)}, u32[]{:S(2)}, u32[]{:S(2)}) collective-permute-start(bf16[1,128,512]{2,1,0:T(8,128)(2,1)S(1)} %get-tuple-element.50), channel_id=1, source_target_pairs={{0,8},{2,10},{4,12},{6,14},{8,0},{10,2},{12,4},{14,6},{1,9},{3,11}... | collective-permute-start | bytes 393224 | tf_op jit(solution)/shard_map/ppermute | solution.py:352
  9.8 22.2 %collective-permute-start.3 = (bf16[64,2560]{1,0:T(8,128)(2,1)S(1)}, bf16[64,2560]{1,0:T(8,128)(2,1)S(1)}, u32[]{:S(2)}, u32[]{:S(2)}) collective-permute-start(bf16[64,2560]{1,0:T(8,128)(2,1)S(1)} %get-tuple-element.57), channel_id=1, source_target_pairs={{0,4},{2,6},{4,0},{6,2},{8,12},{10,14},{12,8},{14,10},{1,5},{3,7},... | collective-permute-start | bytes 983048 | tf_op jit(solution)/shard_map/ppermute | solution.py:352
  10.2 21.8 %collective-permute-start.4 = (bf16[64,2560]{1,0:T(8,128)(2,1)S(1)}, bf16[64,2560]{1,0:T(8,128)(2,1)S(1)}, u32[]{:S(2)}, u32[]{:S(2)}) collective-permute-start(bf16[64,2560]{1,0:T(8,128)(2,1)S(1)} %get-tuple-element.58), channel_id=1, source_target_pairs={{0,2},{2,0},{4,6},{6,4},{8,10},{10,8},{12,14},{14,12},{1,3},{3,1},... | collective-permute-start | bytes 983048 | tf_op jit(solution)/shard_map/ppermute | solution.py:352
  21.9 10.1 %collective-permute-start.6 = (bf16[1,1280,128]{2,1,0:T(8,128)(2,1)S(1)}, bf16[1,1280,128]{2,1,0:T(8,128)(2,1)S(1)}, u32[]{:S(2)}, u32[]{:S(2)}) collective-permute-start(bf16[1,1280,128]{2,1,0:T(8,128)(2,1)S(1)} %collective-permute-done.1.refs_4_), channel_id=1, source_target_pairs={{0,16},{16,0},{1,17},{17,1},{2,18},{18,2},{3,19},{19,3},{4,20},{20... | collective-permute-start | bytes 983048 | tf_op jit(solution)/shard_map/ppermute | solution.py:352
  26.0 12.3 %collective-permute-start.5 = (f32[128,1024]{1,0:T(8,128)S(1)}, f32[128,1024]{1,0:T(8,128)S(1)}, u32[]{:S(2)}, u32[]{:S(2)}) collective-permute-start(f32[128,1024]{1,0:T(8,128)S(1)} %get-tuple-element.61), channel_id=1, source_target_pairs={{0,1},{1,0},{2,3},{3,2},{4,5},{5,4},{6,7},{7,6},{8,9},{9,8},{10,11... | collective-permute-start | bytes 1572872 | tf_op jit(solution)/shard_map/ppermute | solution.py:352
  26.1 6.5 %collective-permute-start.8 = (bf16[1,128,512]{2,1,0:T(8,128)(2,1)S(1)}, bf16[1,128,512]{2,1,0:T(8,128)(2,1)S(1)}, u32[]{:S(2)}, u32[]{:S(2)}) collective-permute-start(bf16[1,128,512]{2,1,0:T(8,128)(2,1)S(1)} %collective-permute-done.refs_0_), channel_id=1, source_target_pairs={{0,16},{16,0},{1,17},{17,1},{2,18},{18,2},{3,19},{19,3},{4,20},{20... | collective-permute-start | bytes 393224 | tf_op jit(solution)/shard_map/ppermute | solution.py:352
  32.6 1.4 %collective-permute-start.7 = (f32[256,128]{1,0:T(8,128)S(1)}, f32[256,128]{1,0:T(8,128)S(1)}, u32[]{:S(2)}, u32[]{:S(2)}) collective-permute-start(f32[256,128]{1,0:T(8,128)S(1)} %down.1.low_ref), channel_id=1, source_target_pairs={{0,1},{1,0},{2,3},{3,2},{4,5},{5,4},{6,7},{7,6},{8,9},{9,8},{10,11... | collective-permute-start | bytes 393224 | tf_op jit(solution)/shard_map/ppermute | solution.py:352
  34.7 7.3 %collective-permute-start.10 = (s16[64,1024]{1,0:T(8,128)(2,1)S(1)}, s16[64,1024]{1,0:T(8,128)(2,1)S(1)}, u32[]{:S(2)}, u32[]{:S(2)}) collective-permute-start(s16[64,1024]{1,0:T(8,128)(2,1)S(1)} %get-tuple-element.75), channel_id=1, source_target_pairs={{0,6},{2,4},{4,2},{6,0},{8,14},{10,12},{12,10},{14,8},{1,7},{3,5},... | collective-permute-start | bytes 393224 | tf_op jit(solution)/shard_map/ppermute | solution.py:352
  36.0 7.2 %collective-permute-start.11 = (s16[64,1024]{1,0:T(8,128)(2,1)S(1)}, s16[64,1024]{1,0:T(8,128)(2,1)S(1)}, u32[]{:S(2)}, u32[]{:S(2)}) collective-permute-start(s16[64,1024]{1,0:T(8,128)(2,1)S(1)} %get-tuple-element.76), channel_id=1, source_target_pairs={{0,4},{2,6},{4,0},{6,2},{8,12},{10,14},{12,8},{14,10},{1,5},{3,7},... | collective-permute-start | bytes 393224 | tf_op jit(solution)/shard_map/ppermute | solution.py:352
  36.8 7.2 %collective-permute-start.9 = (s16[64,1024]{1,0:T(8,128)(2,1)S(1)}, s16[64,1024]{1,0:T(8,128)(2,1)S(1)}, u32[]{:S(2)}, u32[]{:S(2)}) collective-permute-start(s16[64,1024]{1,0:T(8,128)(2,1)S(1)} %get-tuple-element.74), channel_id=1, source_target_pairs={{0,2},{2,0},{4,6},{6,4},{8,10},{10,8},{12,14},{14,12},{1,3},{3,1},... | collective-permute-start | bytes 393224 | tf_op jit(solution)/shard_map/ppermute | solution.py:352
